TPU v7x, 32 devices: a whole 2x2x4 slice. The times are simulated.
32 devices in a mesh: wide: 8 (over y, x, core), narrow: 4 (over z).
Axes of the slice: x: 2, y: 2, z: 4, core: 2. Of those that a mesh axis runs over, the one named last changes fastest.
Arguments:
- enc_in: bfloat16 [16384, 1024], P(('wide', 'narrow')), may hold values from -6 to 6
- dec_in: bfloat16 [16384, 1024], P(('wide', 'narrow')), may hold values from -6 to 6
- segment_ids: int32 [16384], P(('wide', 'narrow')), may hold values from 0 to 8, as said below
- enc_cot: bfloat16 [16384, 1024], P(('wide', 'narrow'))
- dec_cot: bfloat16 [16384, 1024], P(('wide', 'narrow'))
- enc_qkv: bfloat16 [3, 1024, 1024], P(None, 'wide'), may hold values from -0.1875 to 0.1875
- enc_wo: bfloat16 [1024, 1024], P('wide'), may hold values from -0.75 to 0.75
- enc_w_in: bfloat16 [1024, 4096], P('wide'), may hold values from -0.1875 to 0.1875
- enc_w_out: bfloat16 [4096, 1024], P('wide'), may hold values from -0.09375 to 0.09375
- enc_gains: bfloat16 [2, 1024], P(None, 'wide'), may hold values from 0.25 to 1.75
- dec_qkv: bfloat16 [6, 1024, 1024], P(None, 'wide'), may hold values from -0.1875 to 0.1875
- dec_wo: bfloat16 [2, 1024, 1024], P(None, 'wide'), may hold values from -0.75 to 0.75
- dec_w_in: bfloat16 [1024, 4096], P('wide'), may hold values from -0.1875 to 0.1875
- dec_w_out: bfloat16 [4096, 1024], P('wide'), may hold values from -0.09375 to 0.09375
- dec_gains: bfloat16 [3, 1024], P(None, 'wide'), may hold values from 0.25 to 1.75
- adapter_weights: float32 [4, 1024, 512], P(None, ('wide', 'narrow')), may hold values from -0.25 to 0.25
- adapter_momenta: float32 [4, 1024, 512], P(None, ('wide', 'narrow'))
- bias_in: float32 [2, 512], replicated, may hold values from -3 to 3
- bias_out: float32 [2, 1024], replicated, may hold values from -2 to 2
Outputs:
- enc_out: bfloat16 [16384, 1024], P(('wide', 'narrow'))
- dec_out: bfloat16 [16384, 1024], P(('wide', 'narrow'))
- grad_enc_in: float32 [16384, 1024], P(('wide', 'narrow'))
- grad_dec_in: float32 [16384, 1024], P(('wide', 'narrow'))
- grad_bias_in: float32 [2, 512], P(None, ('wide', 'narrow'))
- grad_bias_out: float32 [2, 1024], P(None, ('wide', 'narrow'))
- new_momenta: float32 [4, 1024, 512], P(None, ('wide', 'narrow'))
- new_weights: float32 [4, 1024, 512], P(None, ('wide', 'narrow'))
Inputs may be any that keep to these rules, and one draw needn't show every extreme that they name: `segment_ids`: within each sequence of 1024 consecutive tokens the ids never fall, equal ids mark one document, and a sequence holds at most 9 documents.
All inputs are finite; a program needn't handle non-finite values.
Results may differ from a plain program's by a relative error of at most 0.02.
Values may be sent and summed in bfloat16 or wider, within the bound.
A program may use at most 448 MiB of HBM per device.

v0:
```python
import math

import jax
import jax.numpy as jnp
from jax import lax
from jax.sharding import PartitionSpec as P

D = 1024
HD = 64
ADAPT = 512
NS_ITERS = 5


EPSILON = 1e-05
MASKED = -1e30
NEWTON_LINEAR = 3.4445
NEWTON_QUADRATIC = -4.775
NEWTON_CUBIC = 2.0315
RATE = 0.7
DECAY = 0.5
FULL_PRECISION = lax.Precision.HIGHEST


def from_partner(array, axis, distance):
    return lax.ppermute(array, axis, [(i, i ^ 1 << distance) for i in range(lax.axis_size(axis))])


def bfloat(tensor):
    return tensor.astype(jnp.bfloat16)


def product(left_side, right_side):
    return jnp.dot(left_side, right_side, preferred_element_type=jnp.float32)


def product_t(left_side, right_side):
    return lax.dot_general(
        left_side, right_side, (((1,), (1,)), ((), ())), preferred_element_type=jnp.float32
    )


def product_rows(left_side, right_side):
    return lax.dot_general(
        left_side, right_side, (((0,), (0,)), ((), ())), preferred_element_type=jnp.float32
    )


def layer_norm(tensor, gain_vector):
    gain_full = gain_vector.astype(jnp.float32)
    average = jnp.mean(tensor, axis=-1, keepdims=True)
    centred = tensor - average
    inverse = lax.rsqrt(jnp.mean(centred * centred, axis=-1, keepdims=True) + EPSILON)
    normed = centred * inverse
    return (normed * gain_full, (normed, inverse, gain_full))


def norm_back(grad_out, stored):
    normed, inverse, gain_full = stored
    scaled = grad_out * gain_full
    return inverse * (
        scaled
        - jnp.mean(scaled, axis=-1, keepdims=True)
        - normed * jnp.mean(scaled * normed, axis=-1, keepdims=True)
    )


def gelu_value(tensor):
    return jax.nn.gelu(tensor, approximate=False)


def gelu_slope(tensor):
    return (
        0.5 * (1.0 + lax.erf(tensor * 0.7071067811865476))
        + tensor * jnp.exp(-0.5 * tensor * tensor) * 0.3989422804014327
    )


def split_heads(tensor):
    return tensor.reshape(tensor.shape[0], -1, HD)


def head_scores(queries, key_rows, allowed):
    scores = jnp.einsum(
        "qhd,khd->hqk",
        split_heads(queries),
        split_heads(key_rows),
        preferred_element_type=jnp.float32,
    )
    return jnp.where(allowed[None], scores * HD ** (-0.5), MASKED)


def attend(queries, key_rows, value_rows, allowed):
    scores = head_scores(queries, key_rows, allowed)
    peak_score = jnp.max(scores, axis=-1, keepdims=True)
    raised = jnp.exp(scores - peak_score)
    totals = jnp.sum(raised, axis=-1, keepdims=True)
    weights = bfloat(raised / totals)
    mixture = jnp.einsum(
        "hqk,khd->qhd", weights, split_heads(value_rows), preferred_element_type=jnp.float32
    )
    return (bfloat(mixture.reshape(queries.shape)), peak_score + jnp.log(totals))


def attend_back(grad_out, queries, key_rows, value_rows, allowed, log_totals):
    probabilities = jnp.exp(head_scores(queries, key_rows, allowed) - log_totals)
    grad_heads = split_heads(grad_out)
    grad_probs = jnp.einsum(
        "qhd,khd->hqk", grad_heads, split_heads(value_rows), preferred_element_type=jnp.float32
    )
    inner_sum = jnp.sum(grad_probs * probabilities, axis=-1, keepdims=True)
    grad_scores = bfloat(probabilities * (grad_probs - inner_sum))
    score_scale = HD ** (-0.5)
    grad_query = (
        jnp.einsum(
            "hqk,khd->qhd", grad_scores, split_heads(key_rows), preferred_element_type=jnp.float32
        )
        * score_scale
    )
    grad_keys = (
        jnp.einsum(
            "hqk,qhd->khd", grad_scores, split_heads(queries), preferred_element_type=jnp.float32
        )
        * score_scale
    )
    grad_values = jnp.einsum(
        "hqk,qhd->khd", bfloat(probabilities), grad_heads, preferred_element_type=jnp.float32
    )
    return (
        grad_query.reshape(queries.shape),
        grad_keys.reshape(key_rows.shape),
        grad_values.reshape(key_rows.shape),
    )


def tail_forward(hidden, up_proj, down_proj, adapt_in, adapt_out_t, bias_first, bias_second):
    hidden_low = bfloat(hidden)
    upward = product(hidden_low, up_proj)
    inner_low = bfloat(gelu_value(upward))
    ffn_out = product(inner_low, down_proj)
    adapt_pre = product(hidden_low, adapt_in) + bias_first
    adapt_low = bfloat(gelu_value(adapt_pre))
    adapt_out = product_t(adapt_low, adapt_out_t) + bias_second
    return (hidden + ffn_out + 4.0 * adapt_out, (hidden_low, upward, adapt_pre, adapt_low))


def tail_back(grad_total, stored, up_proj, down_proj, adapt_in, adapt_out_t):
    hidden_low, upward, adapt_pre, adapt_low = stored
    grad_low = bfloat(grad_total)
    grad_up_low = bfloat(product_t(grad_low, down_proj) * gelu_slope(upward))
    grad_adapt = bfloat(4.0 * grad_total)
    grad_out_matrix = product_rows(grad_adapt, adapt_low)
    grad_second = jnp.sum(grad_adapt.astype(jnp.float32), axis=0)
    grad_pre_low = bfloat(product(grad_adapt, adapt_out_t) * gelu_slope(adapt_pre))
    grad_in_matrix = product_rows(hidden_low, grad_pre_low)
    grad_first = jnp.sum(grad_pre_low.astype(jnp.float32), axis=0)
    grad_hidden = grad_total + product_t(grad_up_low, up_proj) + product_t(grad_pre_low, adapt_in)
    return (grad_hidden, grad_in_matrix, grad_out_matrix, grad_first, grad_second)


def gram_sum(present_iterate):
    partial_gram = jnp.einsum(
        "esn,esk->enk", present_iterate, present_iterate, precision=FULL_PRECISION
    )
    return lax.psum(partial_gram, ("wide", "narrow"))


def partial_gram(present_iterate):
    return jnp.einsum("esn,esk->enk", present_iterate, present_iterate, precision=FULL_PRECISION)


def schulz_step(present_iterate, gram_product):
    gram_squared = jnp.einsum("mab,mbc->mac", gram_product, gram_product, precision=FULL_PRECISION)
    return NEWTON_LINEAR * present_iterate + jnp.einsum(
        "wik,wkn->win",
        present_iterate,
        NEWTON_QUADRATIC * gram_product + NEWTON_CUBIC * gram_squared,
        precision=FULL_PRECISION,
    )


def shards(
    enc_in,
    dec_in,
    segment_ids,
    enc_cot,
    dec_cot,
    enc_qkv,
    enc_wo,
    enc_w_in,
    enc_w_out,
    enc_gains,
    dec_qkv,
    dec_wo,
    dec_w_in,
    dec_w_out,
    dec_gains,
    adapter_weights,
    adapter_momenta,
    bias_in,
    bias_out,
):
    adapters = lax.all_gather(bfloat(adapter_weights), ("wide", "narrow"), axis=1, tiled=True)
    enc_proj, enc_out_proj, enc_up, enc_down, enc_gain_rows = (
        lax.all_gather(enc_qkv, "wide", axis=1, tiled=True),
        lax.all_gather(enc_wo, "wide", axis=0, tiled=True),
        lax.all_gather(enc_w_in, "wide", axis=0, tiled=True),
        lax.all_gather(enc_w_out, "wide", axis=0, tiled=True),
        lax.all_gather(enc_gains, "wide", axis=1, tiled=True),
    )
    dec_proj, dec_out_proj, dec_up, dec_down, dec_gain_rows = (
        lax.all_gather(dec_qkv, "wide", axis=1, tiled=True),
        lax.all_gather(dec_wo, "wide", axis=1, tiled=True),
        lax.all_gather(dec_w_in, "wide", axis=0, tiled=True),
        lax.all_gather(dec_w_out, "wide", axis=0, tiled=True),
        lax.all_gather(dec_gains, "wide", axis=1, tiled=True),
    )
    other_ids = from_partner(segment_ids, "narrow", 0)
    row_count = enc_in.shape[0]
    half_index = lax.axis_index("narrow") % 2
    offsets = jnp.arange(row_count, dtype=jnp.int32)
    own_places = half_index * row_count + offsets
    key_places = jnp.concatenate([own_places, (1 - half_index) * row_count + offsets])
    key_ids = jnp.concatenate([segment_ids, other_ids])
    same_doc = segment_ids[:, None] == key_ids[None, :]
    causal = same_doc & (key_places[None, :] <= own_places[:, None])
    enc_query = bfloat(product(enc_in, enc_proj[0]))
    enc_key = bfloat(product(enc_in, enc_proj[1]))
    enc_value = bfloat(product(enc_in, enc_proj[2]))
    self_query = bfloat(product(dec_in, dec_proj[0]))
    self_key = bfloat(product(dec_in, dec_proj[1]))
    self_value = bfloat(product(dec_in, dec_proj[2]))
    enc_key_far, enc_value_far, self_key_far, self_value_far = from_partner(
        (enc_key, enc_value, self_key, self_value), "narrow", 0
    )
    enc_keys = jnp.concatenate([enc_key, enc_key_far])
    enc_values = jnp.concatenate([enc_value, enc_value_far])
    self_keys = jnp.concatenate([self_key, self_key_far])
    self_values = jnp.concatenate([self_value, self_value_far])
    enc_mix, enc_lse = attend(enc_query, enc_keys, enc_values, same_doc)
    enc_z1 = enc_in.astype(jnp.float32) + product(enc_mix, enc_out_proj)
    enc_h1, enc_norm1 = layer_norm(enc_z1, enc_gain_rows[0])
    enc_z2, enc_tail = tail_forward(
        enc_h1, enc_up, enc_down, adapters[0], adapters[1], bias_in[0], bias_out[0]
    )
    encoded, enc_norm2 = layer_norm(enc_z2, enc_gain_rows[1])
    enc_low = bfloat(encoded)
    cross_key = bfloat(product(enc_low, dec_proj[4]))
    cross_value = bfloat(product(enc_low, dec_proj[5]))
    cross_key_far, cross_value_far = from_partner((cross_key, cross_value), "narrow", 0)
    cross_keys = jnp.concatenate([cross_key, cross_key_far])
    cross_values = jnp.concatenate([cross_value, cross_value_far])
    self_mix, self_lse = attend(self_query, self_keys, self_values, causal)
    dec_z1 = dec_in.astype(jnp.float32) + product(self_mix, dec_out_proj[0])
    dec_y1, dec_norm1 = layer_norm(dec_z1, dec_gain_rows[0])
    cross_query = bfloat(product(bfloat(dec_y1), dec_proj[3]))
    cross_mix, cross_lse = attend(cross_query, cross_keys, cross_values, same_doc)
    dec_z2 = dec_y1 + product(cross_mix, dec_out_proj[1])
    dec_y2, dec_norm2 = layer_norm(dec_z2, dec_gain_rows[1])
    dec_z3, dec_tail = tail_forward(
        dec_y2, dec_up, dec_down, adapters[2], adapters[3], bias_in[1], bias_out[1]
    )
    decoded, dec_norm3 = layer_norm(dec_z3, dec_gain_rows[2])
    dec_proj, dec_out_proj, dec_up, dec_down, dec_gain_rows = (
        lax.all_gather(dec_qkv, "wide", axis=1, tiled=True),
        lax.all_gather(dec_wo, "wide", axis=1, tiled=True),
        lax.all_gather(dec_w_in, "wide", axis=0, tiled=True),
        lax.all_gather(dec_w_out, "wide", axis=0, tiled=True),
        lax.all_gather(dec_gains, "wide", axis=1, tiled=True),
    )
    grad_z3 = norm_back(dec_cot.astype(jnp.float32), dec_norm3)
    grad_y2, grad_dec_down, grad_dec_up, grad_dec_first, grad_dec_second = tail_back(
        grad_z3, dec_tail, dec_up, dec_down, adapters[2], adapters[3]
    )
    grad_z2 = norm_back(grad_y2, dec_norm2)
    grad_cross_mix = bfloat(product_t(bfloat(grad_z2), dec_out_proj[1]))
    grad_cross_q, grad_cross_k, grad_cross_v = attend_back(
        grad_cross_mix, cross_query, cross_keys, cross_values, same_doc, cross_lse
    )
    grad_y1 = grad_z2 + product_t(bfloat(grad_cross_q), dec_proj[3])
    grad_z1 = norm_back(grad_y1, dec_norm1)
    grad_self_mix = bfloat(product_t(bfloat(grad_z1), dec_out_proj[0]))
    grad_self_q, grad_self_k, grad_self_v = attend_back(
        grad_self_mix, self_query, self_keys, self_values, causal, self_lse
    )
    back_cross_k, back_cross_v, back_self_k, back_self_v = (
        from_partner(grad_cross_k[row_count:].astype(jnp.bfloat16), "narrow", 0).astype(
            jnp.float32
        ),
        from_partner(grad_cross_v[row_count:].astype(jnp.bfloat16), "narrow", 0).astype(
            jnp.float32
        ),
        from_partner(grad_self_k[row_count:].astype(jnp.bfloat16), "narrow", 0).astype(jnp.float32),
        from_partner(grad_self_v[row_count:].astype(jnp.bfloat16), "narrow", 0).astype(jnp.float32),
    )
    self_k_low = bfloat(grad_self_k[:row_count] + back_self_k)
    self_v_low = bfloat(grad_self_v[:row_count] + back_self_v)
    grad_dec = (
        grad_z1
        + product_t(bfloat(grad_self_q), dec_proj[0])
        + product_t(self_k_low, dec_proj[1])
        + product_t(self_v_low, dec_proj[2])
    )
    cross_k_low = bfloat(grad_cross_k[:row_count] + back_cross_k)
    cross_v_low = bfloat(grad_cross_v[:row_count] + back_cross_v)
    grad_encoded = (
        enc_cot.astype(jnp.float32)
        + product_t(cross_k_low, dec_proj[4])
        + product_t(cross_v_low, dec_proj[5])
    )
    enc_proj, enc_out_proj, enc_up, enc_down, enc_gain_rows = (
        lax.all_gather(enc_qkv, "wide", axis=1, tiled=True),
        lax.all_gather(enc_wo, "wide", axis=0, tiled=True),
        lax.all_gather(enc_w_in, "wide", axis=0, tiled=True),
        lax.all_gather(enc_w_out, "wide", axis=0, tiled=True),
        lax.all_gather(enc_gains, "wide", axis=1, tiled=True),
    )
    grad_ez2 = norm_back(grad_encoded, enc_norm2)
    grad_eh1, grad_enc_down, grad_enc_up, grad_enc_first, grad_enc_second = tail_back(
        grad_ez2, enc_tail, enc_up, enc_down, adapters[0], adapters[1]
    )
    grad_ez1 = norm_back(grad_eh1, enc_norm1)
    grad_enc_mix = bfloat(product_t(bfloat(grad_ez1), enc_out_proj))
    grad_enc_q, grad_enc_k, grad_enc_v = attend_back(
        grad_enc_mix, enc_query, enc_keys, enc_values, same_doc, enc_lse
    )
    back_enc_k, back_enc_v = (
        from_partner(grad_enc_k[row_count:].astype(jnp.bfloat16), "narrow", 0).astype(jnp.float32),
        from_partner(grad_enc_v[row_count:].astype(jnp.bfloat16), "narrow", 0).astype(jnp.float32),
    )
    enc_k_low = bfloat(grad_enc_k[:row_count] + back_enc_k)
    enc_v_low = bfloat(grad_enc_v[:row_count] + back_enc_v)
    grad_enc = (
        grad_ez1
        + product_t(bfloat(grad_enc_q), enc_proj[0])
        + product_t(enc_k_low, enc_proj[1])
        + product_t(enc_v_low, enc_proj[2])
    )
    stacked = jnp.stack([grad_enc_down, grad_enc_up, grad_dec_down, grad_dec_up])
    first_grads = jnp.stack([grad_enc_first, grad_dec_first])
    second_grads = jnp.stack([grad_enc_second, grad_dec_second])
    summed_grads, grad_bias_in, grad_bias_out = (
        lax.psum_scatter(stacked, ("wide", "narrow"), scatter_dimension=1, tiled=True),
        lax.psum_scatter(first_grads, ("wide", "narrow"), scatter_dimension=1, tiled=True),
        lax.psum_scatter(second_grads, ("wide", "narrow"), scatter_dimension=1, tiled=True),
    )
    momenta = DECAY * adapter_momenta + summed_grads
    squares = lax.psum(jnp.sum(momenta * momenta, axis=(1, 2)), ("wide", "narrow"))
    present_iterate = momenta / (jnp.sqrt(squares)[:, None, None] + 1e-07)
    for iteration in range(NS_ITERS):
        present_iterate = schulz_step(present_iterate, gram_sum(present_iterate))
    new_weights = adapter_weights - RATE * math.sqrt(max(1.0, D / ADAPT)) * present_iterate
    return (
        bfloat(encoded),
        bfloat(decoded),
        grad_enc,
        grad_dec,
        grad_bias_in,
        grad_bias_out,
        momenta,
        new_weights,
    )


def solution(mesh):
    in_specs = (
        P(("wide", "narrow"), None),
        P(("wide", "narrow"), None),
        P(("wide", "narrow")),
        P(("wide", "narrow"), None),
        P(("wide", "narrow"), None),
        P(None, "wide", None),
        P("wide", None),
        P("wide", None),
        P("wide", None),
        P(None, "wide"),
        P(None, "wide", None),
        P(None, "wide", None),
        P("wide", None),
        P("wide", None),
        P(None, "wide"),
        P(None, ("wide", "narrow"), None),
        P(None, ("wide", "narrow"), None),
        P(),
        P(),
    )
    out_specs = (
        P(("wide", "narrow"), None),
        P(("wide", "narrow"), None),
        P(("wide", "narrow"), None),
        P(("wide", "narrow"), None),
        P(None, ("wide", "narrow")),
        P(None, ("wide", "narrow")),
        P(None, ("wide", "narrow"), None),
        P(None, ("wide", "narrow"), None),
    )
    return jax.shard_map(shards, mesh=mesh, in_specs=in_specs, out_specs=out_specs, check_vma=False)
```

profile of v0, /device:TPU:0, one launch (start us, length us, event | category | flops | bytes accessed | tf_op | source)
XLA Modules:
  0.0 2005.6 jit_solution(15961680240777322108)
XLA Ops:
  36.9 21.4 %all-gather.10.cloned.1.call-done = bf16[3,1024,1024]{2,1,0:T(8,128)(2,1)} async-done(((bf16[3,128,1024]{2,1,0:T(8,128)(2,1)}), bf16[3,1024,1024]{2,1,0:T(8,128)(2,1)}) %all-gather.10.cloned.1.call-update) | async-done | bytes 6291472 | tf_op jit(solution)/shard_map/all_gather | solution.py:204
  70.5 18.0 collective-permute-done
  92.8 20.2 %collective-permute-done.2 = bf16[512,1024]{1,0:T(8,128)(2,1)} collective-permute-done((bf16[512,1024]{1,0:T(8,128)(2,1)}, bf16[512,1024]{1,0:T(8,128)(2,1)}, u32[]{:S(2)}, u32[]{:S(2)}) %collective-permute-start.2) | collective-permute-done | bytes 1048608 | tf_op jit(solution)/shard_map/ppermute | solution.py:25
  173.5 36.0 %all-gather.14.cloned.1.call-done = bf16[1024,4096]{1,0:T(8,128)(2,1)} async-done(((bf16[128,4096]{1,0:T(8,128)(2,1)}), bf16[1024,4096]{1,0:T(8,128)(2,1)}) %all-gather.14.cloned.1.call-update) | async-done | bytes 8388624 | tf_op jit(solution)/shard_map/all_gather | solution.py:206
  219.7 45.9 %all-gather.16.cloned.1.call-done = bf16[4096,1024]{1,0:T(8,128)(2,1)} async-done(((bf16[512,1024]{1,0:T(8,128)(2,1)}), bf16[4096,1024]{1,0:T(8,128)(2,1)}) %all-gather.16.cloned.1.call-update) | async-done | bytes 8388624 | tf_op jit(solution)/shard_map/all_gather | solution.py:207
  265.6 26.0 %fusion.72 = f32[512,1024]{1,0:T(8,128)S(1)} fusion(bf16[4096,1024]{1,0:T(8,128)(2,1)} %all-gather.16.cloned.1.call-done, f32[512,4096]{1,0:T(8,128)} %fusion.280), kind=kOutput, calls=%fused_computation.110 | convolution fusion | flops 4431282176 | bytes 18874368 | tf_op jit(solution)/shard_map/dot_general | solution.py:33
  295.6 43.9 %all-gather.20.cloned.1.call-done = bf16[6,1024,1024]{2,1,0:T(8,128)(2,1)} async-done(((bf16[6,128,1024]{2,1,0:T(8,128)(2,1)}), bf16[6,1024,1024]{2,1,0:T(8,128)(2,1)}) %all-gather.20.cloned.1.call-update) | async-done | bytes 12582928 | tf_op jit(solution)/shard_map/all_gather | solution.py:211
  373.9 18.2 collective-permute-done.4
  398.0 16.2 fusion.275
  461.8 15.2 fusion.277
  524.2 26.2 %fusion.70 = f32[512,1024]{1,0:T(8,128)S(1)} fusion(bf16[4096,1024]{1,0:T(8,128)(2,1)} %all-gather.26.cloned.1.call-done, f32[512,4096]{1,0:T(8,128)} %fusion.281), kind=kOutput, calls=%fused_computation.109 | convolution fusion | flops 4431282176 | bytes 18874368 | tf_op jit(solution)/shard_map/dot_general | solution.py:33
  557.0 17.1 fusion.282
  585.7 23.5 %multiply_reduce_fusion.2 = (f32[16,512]{1,0:T(8,128)S(1)}, f32[16,512,1024]{2,1,0:T(8,128)}) fusion(f32[16,512,1024]{2,1,0:T(8,128)} %get-tuple-element.49, f32[16,512]{1,0:T(8,128)S(1)} %log_add_fusion.2, bf16[512,16,64]{0,2,1:T(8,128)(2,1)S(1)} %bitcast.341, bf16[1024,16,64]{0,2,1:T(8,128)(2,1)} %bitcast.337), kind=kOutput, calls=%fused_computation.7 | convolution fusion | flops 1098899456 | bytes 70320128 | tf_op jit(solution)/shard_map/qhd,khd->hqk/dot_general | solution.py:107
  609.2 28.1 %multiply_convert_fusion.2 = bf16[16,512,1024]{2,1,0:T(8,128)(2,1)} fusion(f32[16,512,1024]{2,1,0:T(8,128)} %get-tuple-element.58, f32[16,512,1024]{2,1,0:T(8,128)} %get-tuple-element.49, f32[16,512]{1,0:T(8,128)S(1)} %get-tuple-element.57, f32[16,512]{1,0:T(8,128)S(1)} %log_add_fusion.2), kind=kLoop, calls=%fused_computation.6 | loop fusion | flops 33554432 | bytes 83951616 | tf_op jit(solution)/shard_map/convert_element_type | solution.py:29
  649.9 15.4 fusion.74
  679.5 15.3 collective-permute-done.8
  731.0 15.6 fusion.80
  752.6 22.5 %multiply_reduce_fusion = (f32[16,512]{1,0:T(8,128)S(1)}, f32[16,512,1024]{2,1,0:T(8,128)}) fusion(f32[16,512,1024]{2,1,0:T(8,128)} %get-tuple-element.45, f32[16,512]{1,0:T(8,128)S(1)} %log_add_fusion, bf16[512,16,64]{0,2,1:T(8,128)(2,1)S(1)} %bitcast.344, bf16[1024,16,64]{0,2,1:T(8,128)(2,1)S(1)} %bitcast.336), kind=kOutput, calls=%fused_computation.1 | convolution fusion | flops 1098899456 | bytes 70320128 | tf_op jit(solution)/shard_map/qhd,khd->hqk/dot_general | solution.py:107
  775.2 28.2 %multiply_convert_fusion = bf16[16,512,1024]{2,1,0:T(8,128)(2,1)} fusion(f32[16,512,1024]{2,1,0:T(8,128)} %get-tuple-element.65, f32[16,512,1024]{2,1,0:T(8,128)} %get-tuple-element.45, f32[16,512]{1,0:T(8,128)S(1)} %get-tuple-element.64, f32[16,512]{1,0:T(8,128)S(1)} %log_add_fusion), kind=kLoop, calls=%fused_computation | loop fusion | flops 33554432 | bytes 83951616 | tf_op jit(solution)/shard_map/convert_element_type | solution.py:29
  803.3 91.9 %reduce-scatter.8.cloned.1.call-done = f32[4,32,512]{2,1,0:T(8,128)} async-done(((f32[4,1024,512]{2,1,0:T(8,128)}), f32[4,32,512]{2,1,0:T(8,128)}) %reduce-scatter.8.cloned.1.call-update) | async-done | bytes 262160 | tf_op jit(solution)/shard_map/reduce_scatter | solution.py:342
  896.3 37.6 %psum.42 = f32[4]{0:T(128)S(1)} all-reduce(f32[4]{0:T(128)S(1)} %get-tuple-element.18), channel_id=1, replica_groups=mesh['wide'=8,'narrow'=4] {'wide','narrow'}, use_global_device_ids=true, to_apply=%region_37.38 | all-reduce | flops 4 | bytes 32 | tf_op jit(solution)/shard_map/psum | solution.py:347
  970.4 122.1 %all-reduce.6.cloned.1.call-done = f32[4,512,512]{2,1,0:T(8,128)} async-done(((f32[4,512,512]{2,1,0:T(8,128)}), f32[4,512,512]{2,1,0:T(8,128)}) %all-reduce.6.cloned.1.call-update) | async-done | bytes 4194320 | tf_op jit(solution)/shard_map/psum | solution.py:164
  1111.2 18.1 fusion.283
  1134.2 117.8 %all-reduce.8.cloned.1.call-done = f32[4,512,512]{2,1,0:T(8,128)} async-done(((f32[4,512,512]{2,1,0:T(8,128)}), f32[4,512,512]{2,1,0:T(8,128)}) %all-reduce.8.cloned.1.call-update) | async-done | bytes 4194320 | tf_op jit(solution)/shard_map/psum | solution.py:164
  1277.3 15.8 fusion.77
  1293.1 118.6 %all-reduce.10.cloned.1.call-done = f32[4,512,512]{2,1,0:T(8,128)} async-done(((f32[4,512,512]{2,1,0:T(8,128)}), f32[4,512,512]{2,1,0:T(8,128)}) %all-reduce.10.cloned.1.call-update) | async-done | bytes 4194320 | tf_op jit(solution)/shard_map/psum | solution.py:164
  1431.2 23.9 %multiply_reduce_fusion.1 = (f32[16,512]{1,0:T(8,128)S(1)}, f32[16,512,1024]{2,1,0:T(8,128)}) fusion(f32[16,512,1024]{2,1,0:T(8,128)} %get-tuple-element.37, f32[16,512]{1,0:T(8,128)S(1)} %log_add_fusion.1, bf16[512,16,64]{0,2,1:T(8,128)(2,1)S(1)} %bitcast.340, bf16[1024,16,64]{0,2,1:T(8,128)(2,1)} %bitcast.333), kind=kOutput, calls=%fused_computation.4 | convolution fusion | flops 1098899456 | bytes 70320128 | tf_op jit(solution)/shard_map/qhd,khd->hqk/dot_general | solution.py:107
  1455.2 28.5 %multiply_convert_fusion.1 = bf16[16,512,1024]{2,1,0:T(8,128)(2,1)} fusion(f32[16,512,1024]{2,1,0:T(8,128)} %get-tuple-element.62, f32[16,512,1024]{2,1,0:T(8,128)} %get-tuple-element.37, f32[16,512]{1,0:T(8,128)S(1)} %get-tuple-element.61, f32[16,512]{1,0:T(8,128)S(1)} %log_add_fusion.1), kind=kLoop, calls=%fused_computation.3 | loop fusion | flops 33554432 | bytes 83951616 | tf_op jit(solution)/shard_map/convert_element_type | solution.py:29
  1528.8 44.3 %all-reduce.12.cloned.1.call-done = f32[4,512,512]{2,1,0:T(8,128)} async-done(((f32[4,512,512]{2,1,0:T(8,128)}), f32[4,512,512]{2,1,0:T(8,128)}) %all-reduce.12.cloned.1.call-update) | async-done | bytes 4194320 | tf_op jit(solution)/shard_map/psum | solution.py:164
  1596.2 112.0 %reduce-scatter.10.cloned.1.call-done = f32[16,2]{1,0:T(8,128)} async-done(((f32[512,2]{1,0:T(8,128)}), f32[16,2]{1,0:T(8,128)}) %reduce-scatter.10.cloned.1.call-update) | async-done | bytes 144
  1709.5 131.6 %reduce-scatter.12.cloned.1.call-done = f32[32,2]{1,0:T(8,128)} async-done(((f32[1024,2]{1,0:T(8,128)}), f32[32,2]{1,0:T(8,128)}) %reduce-scatter.12.cloned.1.call-update) | async-done | bytes 272
  1855.2 129.8 %all-reduce.14.cloned.1.call-done = f32[4,512,512]{2,1,0:T(8,128)} async-done(((f32[4,512,512]{2,1,0:T(8,128)}), f32[4,512,512]{2,1,0:T(8,128)}) %all-reduce.14.cloned.1.call-update) | async-done | bytes 4194320 | tf_op jit(solution)/shard_map/psum | solution.py:164
  (454 shorter events, 545.1 us)
Async XLA Ops:
  7.2 51.0 %all-gather.10.cloned.1.call-start = ((), (), s32[]{:S(2)}) async-start(), calls=%async_computation.3 | async-start | bytes 7077888 | tf_op jit(solution)/shard_map/all_gather | solution.py:204
  8.0 155.7 %all-gather.12.cloned.1.call-start = ((), (), s32[]{:S(2)}) async-start(), calls=%async_computation.4 | async-start | bytes 2359296 | tf_op jit(solution)/shard_map/all_gather | solution.py:205
  8.7 159.2 %all-gather.18.cloned.1.call-start = ((), (), s32[]{:S(2)}) async-start(), calls=%async_computation.7 | async-start | bytes 4325376 | tf_op jit(solution)/shard_map/all_gather | solution.py:202
  10.4 199.0 %all-gather.14.cloned.1.call-start = ((), (), s32[]{:S(2)}) async-start(), calls=%async_computation.5 | async-start | bytes 9437184 | tf_op jit(solution)/shard_map/all_gather | solution.py:206
  11.0 254.6 %all-gather.16.cloned.1.call-start = ((), (), s32[]{:S(2)}) async-start(), calls=%async_computation.6 | async-start | bytes 9437184 | tf_op jit(solution)/shard_map/all_gather | solution.py:207
  11.6 327.9 %all-gather.20.cloned.1.call-start = ((), (), s32[]{:S(2)}) async-start(), calls=%async_computation.8 | async-start | bytes 14155776 | tf_op jit(solution)/shard_map/all_gather | solution.py:211
  12.2 430.9 %all-gather.22.cloned.1.call-start = ((), (), s32[]{:S(2)}) async-start(), calls=%async_computation.9 | async-start | bytes 4718592 | tf_op jit(solution)/shard_map/all_gather | solution.py:212
  12.9 501.2 %all-gather.24.cloned.1.call-start = ((), (), s32[]{:S(2)}) async-start(), calls=%async_computation.10 | async-start | bytes 9437184 | tf_op jit(solution)/shard_map/all_gather | solution.py:213
  13.7 510.5 %all-gather.26.cloned.1.call-start = ((), (), s32[]{:S(2)}) async-start(), calls=%async_computation.11 | async-start | bytes 9437184 | tf_op jit(solution)/shard_map/all_gather | solution.py:214
  13.7 52.8 %collective-permute-start.1 = (s32[512]{0:T(512)S(1)}, s32[512]{0:T(512)S(1)}, u32[]{:S(2)}, u32[]{:S(2)}) collective-permute-start(s32[512]{0:T(512)S(1)} %copy-done.98), channel_id=1, source_target_pairs={{0,1},{1,0},{2,3},{3,2},{4,5},{5,4},{6,7},{7,6},{8,9},{9,8},{10,11... | collective-permute-start | bytes 6152 | tf_op jit(solution)/shard_map/ppermute | solution.py:25
  16.8 878.4 %reduce-scatter.8.cloned.1.call-start = ((), (), s32[]{:S(2)}) async-start(), calls=%async_computation.12 | async-start | bytes 8650752 | tf_op jit(solution)/shard_map/reduce_scatter | solution.py:342
  26.3 265.3 %copy-start.72 = (f32[1,1024]{1,0:T(1,128)}, f32[1,1024]{1,0:T(1,128)S(1)}, u32[]{:S(2)}) copy-start(f32[1,1024]{1,0:T(1,128)S(1)} %get-tuple-element.35) | copy-start | bytes 12292
  62.2 26.3 %collective-permute-start = (bf16[512,1024]{1,0:T(8,128)(2,1)}, bf16[512,1024]{1,0:T(8,128)(2,1)}, u32[]{:S(2)}, u32[]{:S(2)}) collective-permute-start(bf16[512,1024]{1,0:T(8,128)(2,1)} %fusion.132), channel_id=1, source_target_pairs={{0,1},{1,0},{2,3},{3,2},{4,5},{5,4},{6,7},{7,6},{8,9},{9,8},{10,11... | collective-permute-start | bytes 3145736 | tf_op jit(solution)/shard_map/ppermute | solution.py:25
  66.0 47.0 %collective-permute-start.2 = (bf16[512,1024]{1,0:T(8,128)(2,1)}, bf16[512,1024]{1,0:T(8,128)(2,1)}, u32[]{:S(2)}, u32[]{:S(2)}) collective-permute-start(bf16[512,1024]{1,0:T(8,128)(2,1)} %fusion.130), channel_id=1, source_target_pairs={{0,1},{1,0},{2,3},{3,2},{4,5},{5,4},{6,7},{7,6},{8,9},{9,8},{10,11... | collective-permute-start | bytes 3145736 | tf_op jit(solution)/shard_map/ppermute | solution.py:25
  343.3 26.3 %collective-permute-start.3 = (bf16[512,1024]{1,0:T(8,128)(2,1)}, bf16[512,1024]{1,0:T(8,128)(2,1)}, u32[]{:S(2)}, u32[]{:S(2)}) collective-permute-start(bf16[512,1024]{1,0:T(8,128)(2,1)} %fusion.129), channel_id=1, source_target_pairs={{0,1},{1,0},{2,3},{3,2},{4,5},{5,4},{6,7},{7,6},{8,9},{9,8},{10,11... | collective-permute-start | bytes 3145736 | tf_op jit(solution)/shard_map/ppermute | solution.py:25
  348.7 43.4 %collective-permute-start.4 = (bf16[512,1024]{1,0:T(8,128)(2,1)}, bf16[512,1024]{1,0:T(8,128)(2,1)}, u32[]{:S(2)}, u32[]{:S(2)}) collective-permute-start(bf16[512,1024]{1,0:T(8,128)(2,1)} %fusion.127), channel_id=1, source_target_pairs={{0,1},{1,0},{2,3},{3,2},{4,5},{5,4},{6,7},{7,6},{8,9},{9,8},{10,11... | collective-permute-start | bytes 3145736 | tf_op jit(solution)/shard_map/ppermute | solution.py:25
  357.0 94.2 %collective-permute-start.5 = (bf16[512,1024]{1,0:T(8,128)(2,1)}, bf16[512,1024]{1,0:T(8,128)(2,1)}, u32[]{:S(2)}, u32[]{:S(2)}) collective-permute-start(bf16[512,1024]{1,0:T(8,128)(2,1)} %fusion.125), channel_id=1, source_target_pairs={{0,1},{1,0},{2,3},{3,2},{4,5},{5,4},{6,7},{7,6},{8,9},{9,8},{10,11... | collective-permute-start | bytes 3145736 | tf_op jit(solution)/shard_map/ppermute | solution.py:25
  362.3 93.5 %collective-permute-start.6 = (bf16[512,1024]{1,0:T(8,128)(2,1)}, bf16[512,1024]{1,0:T(8,128)(2,1)}, u32[]{:S(2)}, u32[]{:S(2)}) collective-permute-start(bf16[512,1024]{1,0:T(8,128)(2,1)} %fusion.123), channel_id=1, source_target_pairs={{0,1},{1,0},{2,3},{3,2},{4,5},{5,4},{6,7},{7,6},{8,9},{9,8},{10,11... | collective-permute-start | bytes 3145736 | tf_op jit(solution)/shard_map/ppermute | solution.py:25
  648.4 26.3 %collective-permute-start.7 = (bf16[512,1024]{0,1:T(8,128)(2,1)S(1)}, bf16[512,1024]{0,1:T(8,128)(2,1)}, u32[]{:S(2)}, u32[]{:S(2)}) collective-permute-start(bf16[512,1024]{0,1:T(8,128)(2,1)S(1)} %bitcast.349), channel_id=1, source_target_pairs={{0,1},{1,0},{2,3},{3,2},{4,5},{5,4},{6,7},{7,6},{8,9},{9,8},{10,11... | collective-permute-start | bytes 3145736 | tf_op jit(solution)/shard_map/ppermute | solution.py:25
  667.0 27.8 %collective-permute-start.8 = (bf16[512,1024]{0,1:T(8,128)(2,1)S(1)}, bf16[512,1024]{0,1:T(8,128)(2,1)S(1)}, u32[]{:S(2)}, u32[]{:S(2)}) collective-permute-start(bf16[512,1024]{0,1:T(8,128)(2,1)S(1)} %bitcast.350), channel_id=1, source_target_pairs={{0,1},{1,0},{2,3},{3,2},{4,5},{5,4},{6,7},{7,6},{8,9},{9,8},{10,11... | collective-permute-start | bytes 3145736 | tf_op jit(solution)/shard_map/ppermute | solution.py:25
  708.1 384.4 %all-reduce.6.cloned.1.call-start = ((), (), s32[]{:S(2)}) async-start(), calls=%async_computation.13 | async-start | bytes 8388608 | tf_op jit(solution)/shard_map/psum | solution.py:164
  896.3 206.7 %copy-start.43 = (f32[4,32,512]{2,1,0:T(8,128)}, f32[4,32,512]{2,1,0:T(8,128)S(1)}, u32[]{:S(2)}) copy-start(f32[4,32,512]{2,1,0:T(8,128)S(1)} %get-tuple-element.19) | copy-start | bytes 786436
  939.1 312.8 %all-reduce.8.cloned.1.call-start = ((), (), s32[]{:S(2)}) async-start(), calls=%async_computation.14 | async-start | bytes 8388608 | tf_op jit(solution)/shard_map/psum | solution.py:164
  951.4 567.9 %collective-permute-start.12 = (bf16[512,1024]{0,1:T(8,128)(2,1)}, bf16[512,1024]{0,1:T(8,128)(2,1)}, u32[]{:S(2)}, u32[]{:S(2)}) collective-permute-start(bf16[512,1024]{0,1:T(8,128)(2,1)} %bitcast.65), channel_id=1, source_target_pairs={{0,1},{1,0},{2,3},{3,2},{4,5},{5,4},{6,7},{7,6},{8,9},{9,8},{10,11... | collective-permute-start | bytes 3145736 | tf_op jit(solution)/shard_map/ppermute | solution.py:25
  953.6 546.6 %collective-permute-start.11 = (bf16[512,1024]{0,1:T(8,128)(2,1)}, bf16[512,1024]{0,1:T(8,128)(2,1)}, u32[]{:S(2)}, u32[]{:S(2)}) collective-permute-start(bf16[512,1024]{0,1:T(8,128)(2,1)} %bitcast.62), channel_id=1, source_target_pairs={{0,1},{1,0},{2,3},{3,2},{4,5},{5,4},{6,7},{7,6},{8,9},{9,8},{10,11... | collective-permute-start | bytes 3145736 | tf_op jit(solution)/shard_map/ppermute | solution.py:25
  1111.1 300.6 %all-reduce.10.cloned.1.call-start = ((), (), s32[]{:S(2)}) async-start(), calls=%async_computation.15 | async-start | bytes 8388608 | tf_op jit(solution)/shard_map/psum | solution.py:164
  1270.9 302.2 %all-reduce.12.cloned.1.call-start = ((), (), s32[]{:S(2)}) async-start(), calls=%async_computation.16 | async-start | bytes 8388608 | tf_op jit(solution)/shard_map/psum | solution.py:164
  1430.0 278.2 %reduce-scatter.10.cloned.1.call-start = ((), (), s32[]{:S(2)}) async-start(), calls=%async_computation.18 | async-start | bytes 270336
  1455.1 386.0 %reduce-scatter.12.cloned.1.call-start = ((), (), s32[]{:S(2)}) async-start(), calls=%async_computation.19 | async-start | bytes 540672
  1497.8 344.7 %collective-permute-start.10 = (bf16[512,1024]{0,1:T(8,128)(2,1)}, bf16[512,1024]{0,1:T(8,128)(2,1)}, u32[]{:S(2)}, u32[]{:S(2)}) collective-permute-start(bf16[512,1024]{0,1:T(8,128)(2,1)} %bitcast.54), channel_id=1, source_target_pairs={{0,1},{1,0},{2,3},{3,2},{4,5},{5,4},{6,7},{7,6},{8,9},{9,8},{10,11... | collective-permute-start | bytes 3145736 | tf_op jit(solution)/shard_map/ppermute | solution.py:25
  1498.1 346.7 %collective-permute-start.9 = (bf16[512,1024]{0,1:T(8,128)(2,1)}, bf16[512,1024]{0,1:T(8,128)(2,1)}, u32[]{:S(2)}, u32[]{:S(2)}) collective-permute-start(bf16[512,1024]{0,1:T(8,128)(2,1)} %bitcast.51), channel_id=1, source_target_pairs={{0,1},{1,0},{2,3},{3,2},{4,5},{5,4},{6,7},{7,6},{8,9},{9,8},{10,11... | collective-permute-start | bytes 3145736 | tf_op jit(solution)/shard_map/ppermute | solution.py:25
  1499.9 485.1 %all-reduce.14.cloned.1.call-start = ((), (), s32[]{:S(2)}) async-start(), calls=%async_computation.17 | async-start | bytes 8388608 | tf_op jit(solution)/shard_map/psum | solution.py:164
  (118 other events, 2178.8 us)
Sparse Core Ops, SparseCore 0:
  10.0 48.2 all-gather.9
  60.1 27.8 all-gather.11
  91.7 62.7 all-gather.17
  156.2 53.1 all-gather.13
  211.2 54.3 all-gather.15
  267.4 72.1 all-gather.19
  341.4 36.7 all-gather.21
  380.1 54.3 all-gather.23
  436.4 54.3 all-gather.25
  708.2 186.9 reduce-scatter.7
  939.3 153.1 all-reduce.5
  1111.2 140.7 all-reduce.7
  1271.0 140.6 all-reduce.9
  1430.1 142.9 all-reduce.11
  1575.8 132.3 reduce-scatter.9
  1710.4 130.7 reduce-scatter.11
  1846.5 138.4 all-reduce.13
where the time goes:
time: 2010 us
  waiting for transfers between devices  1100 us (55%)
  matrix products  588 us (29%)
  other arithmetic  172 us (9%)
  blocking collectives  55.2 us (3%)
  local copies, waits for them, and re-layouts  54.8 us (3%)
    psum x5, waiting for transfers between devices, gram_sum(): return lax.psum(partial_gram, ('wide', 'narrow'))  533 us
    unnamed x19, waiting for transfers between devices  248 us
    dot_general x20, matrix products, product(): return jnp.dot(left_side, right_side, preferred_element_type=jnp.float32)  127 us
    convert_element_type x13, other arithmetic, bfloat(): return tensor.astype(jnp.bfloat16)  98.1 us
    dot_general x18, matrix products, product_t(): lax.dot_general(left_side, right_side, (((1,), (1,)), ((), ())), preferre...  95.4 us
    reduce_scatter x1, waiting for transfers between devices, shards(): lax.psum_scatter(stacked, ('wide', 'narrow'), scatter_dimension=1, tiled=...  91.9 us
    ppermute x13, waiting for transfers between devices, from_partner(): lax.ppermute(array, axis, [(i, i ^ 1 << distance) for i in range(lax.axis...  82.3 us
    dot_general x3, matrix products, attend_back(): jnp.einsum('qhd,khd->hqk', grad_heads, split_heads(value_rows), preferred...  70 us
  transfers between devices with their start and end apart: 30, of which 18 were waited for; matrix products, arithmetic and copies ran while one was open for 32% of the time, Pallas kernels for 0%

commit v1 on v0

v1 whole, which is shorter than its diff:
```python
import functools
import math

import jax
import jax.numpy as jnp
from jax import lax
from jax.experimental import pallas as pl
from jax.experimental.pallas import tpu as pltpu
from jax.sharding import PartitionSpec as P

D = 1024
HD = 64
ADAPT = 512
NS_ITERS = 5

EPSILON = 1e-05
MASKED = -1e30
NEWTON_LINEAR = 3.4445
NEWTON_QUADRATIC = -4.775
NEWTON_CUBIC = 2.0315
RATE = 0.7
DECAY = 0.5
FULL_PRECISION = lax.Precision.HIGHEST
LOG2E = 1.4426950408889634
PAIR = 2 * HD
VMEM_LIMIT = 56 * 1024 * 1024


def swap(array, axis, bit):
    return lax.ppermute(array, axis, [(i, i ^ bit) for i in range(lax.axis_size(axis))])


def bfloat(tensor):
    return tensor.astype(jnp.bfloat16)


def product(left_side, right_side):
    return jnp.dot(left_side, right_side, preferred_element_type=jnp.float32)


def contract(left_side, right_side, left_dim, right_dim):
    return lax.dot_general(
        left_side,
        right_side,
        (((left_dim,), (right_dim,)), ((), ())),
        preferred_element_type=jnp.float32,
    )


def product_t(left_side, right_side):
    return contract(left_side, right_side, 1, 1)


def product_rows(left_side, right_side):
    return contract(left_side, right_side, 0, 0)


def layer_norm(tensor, gain_vector):
    gain_full = gain_vector.astype(jnp.float32)
    average = jnp.mean(tensor, axis=-1, keepdims=True)
    centred = tensor - average
    inverse = lax.rsqrt(jnp.mean(centred * centred, axis=-1, keepdims=True) + EPSILON)
    normed = centred * inverse
    return (normed * gain_full, (normed, inverse, gain_full))


def norm_back(grad_out, stored):
    normed, inverse, gain_full = stored
    scaled = grad_out * gain_full
    return inverse * (
        scaled
        - jnp.mean(scaled, axis=-1, keepdims=True)
        - normed * jnp.mean(scaled * normed, axis=-1, keepdims=True)
    )


def gelu_both(tensor):
    phi = 0.5 * (1.0 + lax.erf(tensor * 0.7071067811865476))
    slope = phi + tensor * jnp.exp(-0.5 * tensor * tensor) * 0.3989422804014327
    return tensor * phi, slope


def fill_bias(half_ref, qid_ref, kid_own_ref, kid_far_ref, bias_ref, causal):
    rows = qid_ref.shape[1]
    qid = qid_ref[...]
    for part, kid_ref in enumerate((kid_own_ref, kid_far_ref)):
        allowed = kid_ref[...] == qid
        if causal:
            if part == 0:
                key_at = lax.broadcasted_iota(jnp.int32, (rows, rows), 0)
                query_at = lax.broadcasted_iota(jnp.int32, (rows, rows), 1)
                allowed = allowed & (key_at <= query_at)
            else:
                allowed = allowed & (half_ref[0] == 1)
        bias_ref[pl.ds(part * rows, rows), :] = jnp.where(allowed, 0.0, MASKED)


def head_mask(rows, head):
    return lax.broadcasted_iota(jnp.int32, (rows, PAIR), 1) // HD == head


def attend_kernel(
    causal,
    chunk,
    half_ref,
    qid_ref,
    kid_own_ref,
    kid_far_ref,
    q_ref,
    k_own_ref,
    k_far_ref,
    v_own_ref,
    v_far_ref,
    out_ref,
    lse_ref,
    bias_ref,
    score_ref,
):
    rows = q_ref.shape[0]

    @pl.when(pl.program_id(0) == 0)
    def _():
        fill_bias(half_ref, qid_ref, kid_own_ref, kid_far_ref, bias_ref, causal)

    queries = q_ref[...] * 0.125
    steps = [
        (part, at)
        for part in range(2)
        for at in range(0, rows, chunk)
    ]
    keys = (k_own_ref, k_far_ref)
    values = (v_own_ref, v_far_ref)
    mixes = []
    for head in range(2):
        q_head = jnp.where(head_mask(rows, head), queries, jnp.zeros_like(queries))
        peak = None
        for part, at in steps:
            place = pl.ds(part * rows + at, chunk)
            scores = product_t(keys[part][pl.ds(at, chunk), :], q_head)
            scores = scores * LOG2E + bias_ref[place, :]
            score_ref[head, place, :] = scores
            top = jnp.max(scores, axis=0, keepdims=True)
            peak = top if peak is None else jnp.maximum(peak, top)
        total, mix = None, None
        for part, at in steps:
            place = pl.ds(part * rows + at, chunk)
            raised = jnp.exp2(score_ref[head, place, :] - peak)
            share = jnp.sum(raised, axis=0, keepdims=True)
            piece = product_rows(values[part][pl.ds(at, chunk), :], bfloat(raised))
            total = share if total is None else total + share
            mix = piece if mix is None else mix + piece
        mixes.append((mix * (1.0 / total))[head * HD : (head + 1) * HD, :])
        lse_ref[0, pl.ds(head, 1), :] = peak + jnp.log2(total)
    out_ref[...] = bfloat(jnp.concatenate(mixes, axis=0).T)


def attend_back_kernel(
    causal,
    chunk,
    half_ref,
    qid_ref,
    kid_own_ref,
    kid_far_ref,
    q_ref,
    k_own_ref,
    k_far_ref,
    v_own_ref,
    v_far_ref,
    out_ref,
    grad_ref,
    lse_ref,
    dq_ref,
    dk_own_ref,
    dk_far_ref,
    dv_own_ref,
    dv_far_ref,
    bias_ref,
):
    rows = q_ref.shape[0]

    @pl.when(pl.program_id(0) == 0)
    def _():
        fill_bias(half_ref, qid_ref, kid_own_ref, kid_far_ref, bias_ref, causal)

    queries = q_ref[...] * 0.125
    grads = grad_ref[...]
    products = (grads.astype(jnp.float32) * out_ref[...].astype(jnp.float32)).T
    q_heads, g_heads, deltas, lses = [], [], [], []
    for head in range(2):
        chosen = head_mask(rows, head)
        q_heads.append(jnp.where(chosen, queries, jnp.zeros_like(queries)))
        g_heads.append(jnp.where(chosen, grads, jnp.zeros_like(grads)))
        deltas.append(jnp.sum(products[head * HD : (head + 1) * HD, :], axis=0, keepdims=True))
        lses.append(lse_ref[0, pl.ds(head, 1), :])
    grad_q = [None, None]
    for part in range(2):
        key_ref = (k_own_ref, k_far_ref)[part]
        value_ref = (v_own_ref, v_far_ref)[part]
        dk_ref = (dk_own_ref, dk_far_ref)[part]
        dv_ref = (dv_own_ref, dv_far_ref)[part]
        for at in range(0, rows, chunk):
            here = pl.ds(at, chunk)
            keys, values = key_ref[here, :], value_ref[here, :]
            grad_k, grad_v = None, None
            for head in range(2):
                scores = product_t(keys, q_heads[head])
                bias = bias_ref[pl.ds(part * rows + at, chunk), :]
                weights = jnp.exp2(scores * LOG2E + (bias - lses[head]))
                grad_w = product_t(values, g_heads[head])
                grad_s = bfloat(weights * (grad_w - deltas[head]))
                piece_v = product(bfloat(weights), g_heads[head])
                piece_k = product(grad_s, q_heads[head])
                piece_q = product_rows(keys, grad_s)
                grad_v = piece_v if grad_v is None else grad_v + piece_v
                grad_k = piece_k if grad_k is None else grad_k + piece_k
                grad_q[head] = piece_q if grad_q[head] is None else grad_q[head] + piece_q
            dk_ref[here, :] = grad_k.astype(dk_ref.dtype)
            dv_ref[here, :] = grad_v.astype(dv_ref.dtype)
    joined = jnp.concatenate([grad_q[h][h * HD : (h + 1) * HD, :] for h in range(2)], axis=0)
    dq_ref[...] = bfloat((joined * 0.125).T)


def attention_specs(rows):
    whole = lambda shape: pl.BlockSpec(shape, lambda i: (0,) * len(shape))
    columns = pl.BlockSpec((rows, PAIR), lambda i: (0, i))
    fixed = [
        pl.BlockSpec(memory_space=pltpu.SMEM),
        whole((1, rows)),
        whole((rows, 1)),
        whole((rows, 1)),
    ]
    return fixed, columns, pl.BlockSpec((1, 8, rows), lambda i: (i, 0, 0))


def attend(places, queries, keys, values, causal):
    rows, width = queries.shape
    pairs = width // PAIR
    fixed, columns, stat = attention_specs(rows)
    return pl.pallas_call(
        functools.partial(attend_kernel, causal, 256),
        grid=(pairs,),
        in_specs=fixed + [columns] * 5,
        out_specs=[columns, stat],
        out_shape=[
            jax.ShapeDtypeStruct((rows, width), jnp.bfloat16),
            jax.ShapeDtypeStruct((pairs, 8, rows), jnp.float32),
        ],
        scratch_shapes=[
            pltpu.VMEM((2 * rows, rows), jnp.float32),
            pltpu.VMEM((2, 2 * rows, rows), jnp.float32),
        ],
        compiler_params=pltpu.CompilerParams(vmem_limit_bytes=VMEM_LIMIT),
        cost_estimate=pl.CostEstimate(
            flops=32 * rows * rows * width, bytes_accessed=12 * rows * width, transcendentals=0
        ),
    )(*places, queries, *keys, *values)


def attend_back(places, grad_out, queries, keys, values, mix, lse, causal):
    rows, width = queries.shape
    pairs = width // PAIR
    fixed, columns, stat = attention_specs(rows)
    return pl.pallas_call(
        functools.partial(attend_back_kernel, causal, 256),
        grid=(pairs,),
        in_specs=fixed + [columns] * 7 + [stat],
        out_specs=[columns] * 5,
        out_shape=[
            jax.ShapeDtypeStruct((rows, width), jnp.bfloat16),
            jax.ShapeDtypeStruct((rows, width), jnp.float32),
            jax.ShapeDtypeStruct((rows, width), jnp.bfloat16),
            jax.ShapeDtypeStruct((rows, width), jnp.float32),
            jax.ShapeDtypeStruct((rows, width), jnp.bfloat16),
        ],
        scratch_shapes=[pltpu.VMEM((2 * rows, rows), jnp.float32)],
        compiler_params=pltpu.CompilerParams(vmem_limit_bytes=VMEM_LIMIT),
        cost_estimate=pl.CostEstimate(
            flops=80 * rows * rows * width, bytes_accessed=24 * rows * width, transcendentals=0
        ),
    )(*places, queries, *keys, *values, mix, grad_out, lse)


def tail_forward(hidden, up_proj, down_proj, adapt_in, adapt_out_t, bias_first, bias_second):
    hidden_low = bfloat(hidden)
    inner, up_slope = gelu_both(product(hidden_low, up_proj))
    ffn_out = product(bfloat(inner), down_proj)
    adapted, pre_slope = gelu_both(product(hidden_low, adapt_in) + bias_first)
    adapt_low = bfloat(adapted)
    adapt_out = product_t(adapt_low, adapt_out_t) + bias_second
    return (
        hidden + ffn_out + 4.0 * adapt_out,
        (hidden_low, up_slope, pre_slope, adapt_low),
    )


def tail_back(grad_total, stored, up_proj, down_proj, adapt_in, adapt_out_t):
    hidden_low, up_slope, pre_slope, adapt_low = stored
    grad_low = bfloat(grad_total)
    grad_up_low = bfloat(product_t(grad_low, down_proj) * up_slope)
    grad_adapt = bfloat(4.0 * grad_total)
    grad_out_matrix = product_rows(grad_adapt, adapt_low)
    grad_second = jnp.sum(grad_adapt.astype(jnp.float32), axis=0)
    grad_pre_low = bfloat(product(grad_adapt, adapt_out_t) * pre_slope)
    grad_in_matrix = product_rows(hidden_low, grad_pre_low)
    grad_first = jnp.sum(grad_pre_low.astype(jnp.float32), axis=0)
    grad_hidden = grad_total + product_t(grad_up_low, up_proj) + product_t(grad_pre_low, adapt_in)
    return (grad_hidden, grad_in_matrix, grad_out_matrix, grad_first, grad_second)


def halve(array, dim, axis, bit):
    mine = (lax.axis_index(axis) // bit) % 2
    keep = lax.dynamic_index_in_dim(array, mine, dim, keepdims=False)
    send = lax.dynamic_index_in_dim(array, 1 - mine, dim, keepdims=False)
    return keep + swap(send, axis, bit)


def axis_bits(axis):
    return [1 << b for b in range(lax.axis_size(axis).bit_length() - 1)]


def scatter_wide(first, second):
    bits = axis_bits("wide")
    results = []
    for array, order in ((first, bits[:1] + bits[1:]), (second, bits[:1] + bits[:0:-1])):
        array = array.reshape([2] * len(bits) + [-1, array.shape[-1]])
        left = list(reversed(bits))
        for bit in order:
            array = halve(array, left.index(bit), "wide", bit)
            left.remove(bit)
        results.append(array)
    return results


def gather_any_order(array, axis):
    blocks = array[None]
    for bit in axis_bits(axis):
        blocks = jnp.concatenate([blocks, swap(blocks, axis, bit)])
    return blocks


def sum_all(array):
    for axis in ("wide", "narrow"):
        for bit in axis_bits(axis):
            array = array + swap(array, axis, bit)
    return array


def exact(left_side, right_side):
    return jnp.dot(left_side, right_side, precision=FULL_PRECISION)


def newton_schulz(gram):
    eye = jnp.eye(gram.shape[0], dtype=jnp.float32)
    factor = None
    for step in range(NS_ITERS):
        squared = exact(gram, gram)
        poly = NEWTON_LINEAR * eye + NEWTON_QUADRATIC * gram + NEWTON_CUBIC * squared
        factor = poly if factor is None else exact(factor, poly)
        if step < NS_ITERS - 1:
            gram = exact(exact(gram, poly), poly)
    return factor


def shards(
    enc_in,
    dec_in,
    segment_ids,
    enc_cot,
    dec_cot,
    enc_qkv,
    enc_wo,
    enc_w_in,
    enc_w_out,
    enc_gains,
    dec_qkv,
    dec_wo,
    dec_w_in,
    dec_w_out,
    dec_gains,
    adapter_weights,
    adapter_momenta,
    bias_in,
    bias_out,
):
    adapters = lax.all_gather(bfloat(adapter_weights), ("wide", "narrow"), axis=1, tiled=True)
    enc_proj, enc_out_proj, enc_up, enc_down, enc_gain_rows = (
        lax.all_gather(enc_qkv, "wide", axis=1, tiled=True),
        lax.all_gather(enc_wo, "wide", axis=0, tiled=True),
        lax.all_gather(enc_w_in, "wide", axis=0, tiled=True),
        lax.all_gather(enc_w_out, "wide", axis=0, tiled=True),
        lax.all_gather(enc_gains, "wide", axis=1, tiled=True),
    )
    dec_proj, dec_out_proj, dec_up, dec_down, dec_gain_rows = (
        lax.all_gather(dec_qkv, "wide", axis=1, tiled=True),
        lax.all_gather(dec_wo, "wide", axis=1, tiled=True),
        lax.all_gather(dec_w_in, "wide", axis=0, tiled=True),
        lax.all_gather(dec_w_out, "wide", axis=0, tiled=True),
        lax.all_gather(dec_gains, "wide", axis=1, tiled=True),
    )
    partner = lambda array: swap(array, "narrow", 1)
    other_ids = partner(segment_ids)
    rows = enc_in.shape[0]
    half = (lax.axis_index("narrow") % 2).astype(jnp.int32).reshape(1)
    places = (half, segment_ids.reshape(1, rows), segment_ids.reshape(rows, 1), other_ids.reshape(rows, 1))

    enc_query = bfloat(product(enc_in, enc_proj[0]))
    enc_key = bfloat(product(enc_in, enc_proj[1]))
    enc_value = bfloat(product(enc_in, enc_proj[2]))
    self_query = bfloat(product(dec_in, dec_proj[0]))
    self_key = bfloat(product(dec_in, dec_proj[1]))
    self_value = bfloat(product(dec_in, dec_proj[2]))
    enc_keys, enc_values = (enc_key, partner(enc_key)), (enc_value, partner(enc_value))
    self_keys, self_values = (self_key, partner(self_key)), (self_value, partner(self_value))

    enc_mix, enc_lse = attend(places, enc_query, enc_keys, enc_values, False)
    enc_z1 = enc_in.astype(jnp.float32) + product(enc_mix, enc_out_proj)
    enc_h1, enc_norm1 = layer_norm(enc_z1, enc_gain_rows[0])
    enc_z2, enc_tail = tail_forward(
        enc_h1, enc_up, enc_down, adapters[0], adapters[1], bias_in[0], bias_out[0]
    )
    encoded, enc_norm2 = layer_norm(enc_z2, enc_gain_rows[1])
    enc_low = bfloat(encoded)
    cross_key = bfloat(product(enc_low, dec_proj[4]))
    cross_value = bfloat(product(enc_low, dec_proj[5]))
    cross_keys, cross_values = (cross_key, partner(cross_key)), (cross_value, partner(cross_value))

    self_mix, self_lse = attend(places, self_query, self_keys, self_values, True)
    dec_z1 = dec_in.astype(jnp.float32) + product(self_mix, dec_out_proj[0])
    dec_y1, dec_norm1 = layer_norm(dec_z1, dec_gain_rows[0])
    cross_query = bfloat(product(bfloat(dec_y1), dec_proj[3]))
    cross_mix, cross_lse = attend(places, cross_query, cross_keys, cross_values, False)
    dec_z2 = dec_y1 + product(cross_mix, dec_out_proj[1])
    dec_y2, dec_norm2 = layer_norm(dec_z2, dec_gain_rows[1])
    dec_z3, dec_tail = tail_forward(
        dec_y2, dec_up, dec_down, adapters[2], adapters[3], bias_in[1], bias_out[1]
    )
    decoded, dec_norm3 = layer_norm(dec_z3, dec_gain_rows[2])

    grad_z3 = norm_back(dec_cot.astype(jnp.float32), dec_norm3)
    grad_y2, grad_dec_down, grad_dec_up, grad_dec_first, grad_dec_second = tail_back(
        grad_z3, dec_tail, dec_up, dec_down, adapters[2], adapters[3]
    )
    dec_sums = scatter_wide(grad_dec_down, grad_dec_up)
    grad_z2 = norm_back(grad_y2, dec_norm2)
    grad_cross_mix = bfloat(product_t(bfloat(grad_z2), dec_out_proj[1]))
    cross_back = attend_back(
        places, grad_cross_mix, cross_query, cross_keys, cross_values, cross_mix, cross_lse, False
    )
    own = lambda near, far: bfloat(near + partner(far).astype(jnp.float32))
    cross_k_low = own(cross_back[1], cross_back[2])
    cross_v_low = own(cross_back[3], cross_back[4])
    grad_encoded = (
        enc_cot.astype(jnp.float32)
        + product_t(cross_k_low, dec_proj[4])
        + product_t(cross_v_low, dec_proj[5])
    )
    grad_ez2 = norm_back(grad_encoded, enc_norm2)
    grad_eh1, grad_enc_down, grad_enc_up, grad_enc_first, grad_enc_second = tail_back(
        grad_ez2, enc_tail, enc_up, enc_down, adapters[0], adapters[1]
    )
    enc_sums = scatter_wide(grad_enc_down, grad_enc_up)

    repeat = lax.axis_size("narrow") // 4
    spread = lambda array: jnp.repeat(array, repeat, axis=0) if repeat > 1 else array
    stacked = spread(jnp.stack(enc_sums + dec_sums))
    for bit in reversed(axis_bits("narrow")):
        stacked = halve(stacked.reshape(2, -1, *stacked.shape[1:]), 0, "narrow", bit)
    summed = stacked[0]
    to_matrix = lambda array: lax.all_to_all(
        spread(array), "narrow", split_axis=0, concat_axis=1, tiled=True
    )[0]
    to_rows = lambda array: lax.all_to_all(
        array[None], "narrow", split_axis=1, concat_axis=0, tiled=True
    )[::repeat]
    momentum = DECAY * to_matrix(adapter_momenta) + summed
    new_momenta = to_rows(momentum)
    everything = gather_any_order(momentum, "wide").reshape(-1, ADAPT)
    gram = lax.dot_general(
        everything, everything, (((0,), (0,)), ((), ())), precision=FULL_PRECISION
    )
    scale = 1.0 / (jnp.sqrt(jnp.trace(gram)) + 1e-07)
    factor = newton_schulz(gram * (scale * scale))
    orthogonal = to_rows(exact(momentum * scale, factor))
    new_weights = adapter_weights - RATE * math.sqrt(max(1.0, D / ADAPT)) * orthogonal

    grad_y1 = grad_z2 + product_t(cross_back[0], dec_proj[3])
    grad_z1 = norm_back(grad_y1, dec_norm1)
    grad_self_mix = bfloat(product_t(bfloat(grad_z1), dec_out_proj[0]))
    self_back = attend_back(
        places, grad_self_mix, self_query, self_keys, self_values, self_mix, self_lse, True
    )
    grad_dec = (
        grad_z1
        + product_t(self_back[0], dec_proj[0])
        + product_t(own(self_back[1], self_back[2]), dec_proj[1])
        + product_t(own(self_back[3], self_back[4]), dec_proj[2])
    )
    grad_ez1 = norm_back(grad_eh1, enc_norm1)
    grad_enc_mix = bfloat(product_t(bfloat(grad_ez1), enc_out_proj))
    enc_back = attend_back(
        places, grad_enc_mix, enc_query, enc_keys, enc_values, enc_mix, enc_lse, False
    )
    grad_enc = (
        grad_ez1
        + product_t(enc_back[0], enc_proj[0])
        + product_t(own(enc_back[1], enc_back[2]), enc_proj[1])
        + product_t(own(enc_back[3], enc_back[4]), enc_proj[2])
    )

    biases = sum_all(
        jnp.concatenate([grad_enc_first, grad_dec_first, grad_enc_second, grad_dec_second])
    )
    place = lax.axis_index("wide") * lax.axis_size("narrow") + lax.axis_index("narrow")
    devices = lax.axis_size("wide") * lax.axis_size("narrow")
    slices = lambda array: lax.dynamic_slice_in_dim(
        array.reshape(2, -1), place * (array.size // 2 // devices), array.size // 2 // devices, 1
    )
    grad_bias_in, grad_bias_out = slices(biases[: 2 * ADAPT]), slices(biases[2 * ADAPT :])
    return (
        enc_low,
        bfloat(decoded),
        grad_enc,
        grad_dec,
        grad_bias_in,
        grad_bias_out,
        new_momenta,
        new_weights,
    )


def solution(mesh):
    both = ("wide", "narrow")
    tokens = P(both, None)
    rows_first, rows_second = P("wide", None), P(None, "wide", None)
    adapters = P(None, both, None)
    in_specs = (
        tokens,
        tokens,
        P(both),
        tokens,
        tokens,
        rows_second,
        rows_first,
        rows_first,
        rows_first,
        P(None, "wide"),
        rows_second,
        rows_second,
        rows_first,
        rows_first,
        P(None, "wide"),
        adapters,
        adapters,
        P(),
        P(),
    )
    out_specs = (
        tokens,
        tokens,
        tokens,
        tokens,
        P(None, both),
        P(None, both),
        adapters,
        adapters,
    )
    return jax.shard_map(shards, mesh=mesh, in_specs=in_specs, out_specs=out_specs, check_vma=False)
```

time: 2010 us -> 876 us (0.44)
  waiting for transfers between devices: 1100 us -> 385 us
  matrix products: 588 us -> 229 us
  other arithmetic: 172 us -> 17.6 us
  Pallas kernels: 0 us -> 141 us
  local copies, waits for them, and re-layouts: 54.8 us -> 15.4 us
  blocking collectives: 55.2 us -> 17.6 us
  starting transfers between devices: 17.4 us -> 49.8 us
    psum x5 -> x0, waiting for transfers between devices: 533 us -> none  [gram_sum(): return lax.psum(partial_gram, ('wide', 'narrow'))]
    dot_general x55 -> x41, matrix products: 460 us -> 141 us  [the longest x22 99.4 us: contract(): lax.dot_general(left_side, right_side, (((left_dim,), (right_dim,)), ((),...]
    unnamed x19 -> x9, waiting for transfers between devices: 248 us -> 5.07 us
    pallas_call x0 -> x6, Pallas kernels: none -> 141 us  [the longest x3 85.5 us: attend_back(): pl.pallas_call(functools.partial(attend_back_kernel, causal, 256), grid=(...]
    convert_element_type x13 -> x4, other arithmetic: 98.1 us -> 3.61 us  [bfloat(): return tensor.astype(jnp.bfloat16)]
    reduce_scatter x1 -> x0, waiting for transfers between devices: 91.9 us -> none  [shards(): lax.psum_scatter(stacked, ('wide', 'narrow'), scatter_dimension=1, tiled=...]
    ppermute x13 -> x35, waiting for transfers between devices: 82.3 us -> 165 us  [swap(): lax.ppermute(array, axis, [(i, i ^ bit) for i in range(lax.axis_size(axis...]
    reduce_sum x4 -> x0, other arithmetic: 46 us -> none  [the longest x3 44.9 us: attend(): totals = jnp.sum(raised, axis=-1, keepdims=True)]
  transfers between devices with their start and end apart: 30 -> 47, of which waited for: 18 -> 21; matrix products, arithmetic and copies ran while one was open for 32% -> 25% of each run, Pallas kernels for 0% -> 13%
where the time goes in v1:
time: 876 us; the launch traced here: 871 us
  waiting for transfers between devices  385 us (44%)
  matrix products  229 us (26%)
  Pallas kernels  141 us (16%)
  starting transfers between devices  49.8 us (6%)
  other arithmetic  17.6 us (2%)
  blocking collectives  17.6 us (2%)
  between operations  16.3 us (2%)
  local copies, waits for them, and re-layouts  15.4 us (2%)
    ppermute x35, waiting for transfers between devices, swap(): lax.ppermute(array, axis, [(i, i ^ bit) for i in range(lax.axis_size(axis...  165 us
    dot_general x22, matrix products, contract(): lax.dot_general(left_side, right_side, (((left_dim,), (right_dim,)), ((),...  99.4 us
    dot_general x20, matrix products, product(): return jnp.dot(left_side, right_side, preferred_element_type=jnp.float32)  87.9 us
    pallas_call x3, Pallas kernels, attend_back(): pl.pallas_call(functools.partial(attend_back_kernel, causal, 256), grid=(...  85.5 us
    all_gather x1, waiting for transfers between devices, shards(): lax.all_gather(dec_qkv, 'wide', axis=1, tiled=True)  60.2 us
    pallas_call x3, Pallas kernels, attend(): pl.pallas_call(functools.partial(attend_kernel, causal, 256), grid=(pairs...  55.1 us
    all_gather x1, waiting for transfers between devices, shards(): lax.all_gather(enc_w_in, 'wide', axis=0, tiled=True)  52.7 us
    all_gather x1, waiting for transfers between devices, shards(): lax.all_gather(enc_w_out, 'wide', axis=0, tiled=True)  44.4 us
  transfers between devices with their start and end apart: 47, of which 21 were waited for; matrix products, arithmetic and copies ran while one was open for 25% of the time, Pallas kernels for 13%

profile of v1, /device:TPU:0, one launch (start us, length us, event | category | flops | bytes accessed | tf_op | source)
XLA Modules:
  0.0 871.3 jit_solution(1999293618334482862)
XLA Ops:
  21.4 8.9 %all_gather.41 = bf16[3,1024]{1,0:T(4,128)(2,1)S(1)} all-gather(bf16[3,128]{1,0:T(4,128)(2,1)S(1)} %copy-done.54), channel_id=1, replica_groups=mesh['wide'=8,'narrow'=4] {'wide'}, dimensions={1}, use_global_device_ids=true | all-gather | bytes 6912 | tf_op jit(solution)/shard_map/all_gather | solution.py:398
  30.4 8.7 all_gather.35
  39.1 19.1 %all-gather.10.cloned.1.call-done = bf16[3,1024,1024]{2,1,0:T(8,128)(2,1)} async-done(((bf16[3,128,1024]{2,1,0:T(8,128)(2,1)}), bf16[3,1024,1024]{2,1,0:T(8,128)(2,1)}) %all-gather.10.cloned.1.call-update) | async-done | bytes 6291472 | tf_op jit(solution)/shard_map/all_gather | solution.py:387
  73.3 13.9 %collective-permute-done.1.k_far_ref = bf16[512,1024]{1,0:T(8,128)(2,1)} collective-permute-done((bf16[512,1024]{1,0:T(8,128)(2,1)S(1)}, bf16[512,1024]{1,0:T(8,128)(2,1)}, u32[]{:S(2)}, u32[]{:S(2)}) %collective-permute-start.1) | collective-permute-done | bytes 1048608 | tf_op jit(solution)/shard_map/ppermute | solution.py:30
  87.2 23.9 %collective-permute-done.2.v_far_ref = bf16[512,1024]{1,0:T(8,128)(2,1)} collective-permute-done((bf16[512,1024]{1,0:T(8,128)(2,1)}, bf16[512,1024]{1,0:T(8,128)(2,1)}, u32[]{:S(2)}, u32[]{:S(2)}) %collective-permute-start.2) | collective-permute-done | bytes 1048608 | tf_op jit(solution)/shard_map/ppermute | solution.py:30
  111.1 18.3 %shard_map.242 = (bf16[512,1024]{1,0:T(8,128)(2,1)}, f32[8,8,512]{2,1,0:T(8,128)}) custom-call(s32[1]{0:T(128)} %bitcast.half_ref, s32[1,512]{1,0:T(1,128)} %bitcast.320, s32[512,1]{1,0:T(8,128)} %copy.41.kid_own_ref, s32[512,1]{1,0:T(8,128)} %copy.42.kid_far_ref, bf16[512,1024]{1,0:T(8,128)(2,1)} %fusion.55.q_ref, bf16[512,1024]{1,0:T(8,128)(2,1)} %copy-done.61, ...), custom_call_target="tpu_custom_call" | custom-call | flops 8589934592 | bytes 6291456 | tf_op jit(solution)/shard_map/pallas_call | solution.py:239
  134.6 19.8 %all-gather.18.cloned.1.call-done = bf16[4,1024,512]{2,1,0:T(8,128)(2,1)} async-done(((bf16[4,32,512]{2,1,0:T(8,128)(2,1)}), bf16[4,1024,512]{2,1,0:T(8,128)(2,1)}) %all-gather.18.cloned.1.call-update) | async-done | bytes 4194320 | tf_op jit(solution)/shard_map/all_gather | solution.py:385
  156.6 52.7 %all-gather.14.cloned.1.call-done = bf16[1024,4096]{1,0:T(8,128)(2,1)} async-done(((bf16[128,4096]{1,0:T(8,128)(2,1)}), bf16[1024,4096]{1,0:T(8,128)(2,1)}) %all-gather.14.cloned.1.call-update) | async-done | bytes 8388624 | tf_op jit(solution)/shard_map/all_gather | solution.py:389
  209.3 11.8 %fusion.112 = f32[512,4096]{1,0:T(8,128)} fusion(bf16[512,1024]{1,0:T(8,128)(2,1)} %multiply_convert_fusion.10, bf16[1024,4096]{1,0:T(8,128)(2,1)} %all-gather.14.cloned.1.call-done), kind=kOutput, calls=%fused_computation.264 | convolution fusion | flops 4294967296 | bytes 17825792 | tf_op jit(solution)/shard_map/dot_general | solution.py:38
  221.1 44.4 %all-gather.16.cloned.1.call-done = bf16[4096,1024]{1,0:T(8,128)(2,1)} async-done(((bf16[512,1024]{1,0:T(8,128)(2,1)}), bf16[4096,1024]{1,0:T(8,128)(2,1)}) %all-gather.16.cloned.1.call-update) | async-done | bytes 8388624 | tf_op jit(solution)/shard_map/all_gather | solution.py:390
  265.4 9.6 %fusion.12 = f32[512,1024]{1,0:T(8,128)S(1)} fusion(bf16[4096,1024]{1,0:T(8,128)(2,1)} %all-gather.16.cloned.1.call-done, f32[512,4096]{1,0:T(8,128)} %fusion.112), kind=kOutput, calls=%fused_computation.18 | convolution fusion | flops 4305453056 | bytes 18874368 | tf_op jit(solution)/shard_map/dot_general | solution.py:38
  279.1 60.2 %all-gather.20.cloned.1.call-done = bf16[6,1024,1024]{2,1,0:T(8,128)(2,1)} async-done(((bf16[6,128,1024]{2,1,0:T(8,128)(2,1)}), bf16[6,1024,1024]{2,1,0:T(8,128)(2,1)}) %all-gather.20.cloned.1.call-update) | async-done | bytes 12582928 | tf_op jit(solution)/shard_map/all_gather | solution.py:394
  357.0 11.5 %collective-permute-done.3.k_far_ref = bf16[512,1024]{1,0:T(8,128)(2,1)S(1)} collective-permute-done((bf16[512,1024]{1,0:T(8,128)(2,1)S(1)}, bf16[512,1024]{1,0:T(8,128)(2,1)S(1)}, u32[]{:S(2)}, u32[]{:S(2)}) %collective-permute-start.3) | collective-permute-done | bytes 1048608 | tf_op jit(solution)/shard_map/ppermute | solution.py:30
  368.4 22.5 %collective-permute-done.4.v_far_ref = bf16[512,1024]{1,0:T(8,128)(2,1)S(1)} collective-permute-done((bf16[512,1024]{1,0:T(8,128)(2,1)S(1)}, bf16[512,1024]{1,0:T(8,128)(2,1)S(1)}, u32[]{:S(2)}, u32[]{:S(2)}) %collective-permute-start.4) | collective-permute-done | bytes 1048608 | tf_op jit(solution)/shard_map/ppermute | solution.py:30
  391.9 18.2 %shard_map.243 = (bf16[512,1024]{1,0:T(8,128)(2,1)}, f32[8,8,512]{2,1,0:T(8,128)}) custom-call(s32[1]{0:T(128)} %bitcast.half_ref, s32[1,512]{1,0:T(1,128)} %bitcast.321, s32[512,1]{1,0:T(8,128)} %copy.41.kid_own_ref, s32[512,1]{1,0:T(8,128)} %copy.42.kid_far_ref, bf16[512,1024]{1,0:T(8,128)(2,1)} %fusion.52.q_ref, bf16[512,1024]{1,0:T(8,128)(2,1)} %copy-done.62, ...), custom_call_target="tpu_custom_call" | custom-call | flops 8589934592 | bytes 6291456 | tf_op jit(solution)/shard_map/pallas_call | solution.py:239
  418.0 17.2 %collective-permute-done.6.v_far_ref = bf16[512,1024]{1,0:T(8,128)(2,1)S(1)} collective-permute-done((bf16[512,1024]{1,0:T(8,128)(2,1)}, bf16[512,1024]{1,0:T(8,128)(2,1)S(1)}, u32[]{:S(2)}, u32[]{:S(2)}) %collective-permute-start.6) | collective-permute-done | bytes 1048608 | tf_op jit(solution)/shard_map/ppermute | solution.py:30
  436.2 18.6 %shard_map.244 = (bf16[512,1024]{1,0:T(8,128)(2,1)}, f32[8,8,512]{2,1,0:T(8,128)}) custom-call(s32[1]{0:T(128)} %bitcast.half_ref, s32[1,512]{1,0:T(1,128)} %bitcast.322, s32[512,1]{1,0:T(8,128)} %copy.41.kid_own_ref, s32[512,1]{1,0:T(8,128)} %copy.42.kid_far_ref, bf16[512,1024]{1,0:T(8,128)(2,1)} %fusion.48.q_ref, bf16[512,1024]{1,0:T(8,128)(2,1)} %fusion.47.k_own_ref, ...), custom_call_target="tpu_custom_call" | custom-call | flops 8589934592 | bytes 6291456 | tf_op jit(solution)/shard_map/pallas_call | solution.py:239
  461.7 10.9 %fusion.113 = f32[512,4096]{1,0:T(8,128)} fusion(bf16[512,1024]{1,0:T(8,128)(2,1)S(1)} %multiply_convert_fusion.8, bf16[1024,4096]{1,0:T(8,128)(2,1)} %all-gather.24.cloned.1.call-done), kind=kOutput, calls=%fused_computation.265 | convolution fusion | flops 4294967296 | bytes 17825792 | tf_op jit(solution)/shard_map/dot_general | solution.py:38
  472.6 18.0 %all-gather.26.cloned.1.call-done = bf16[4096,1024]{1,0:T(8,128)(2,1)} async-done(((bf16[512,1024]{1,0:T(8,128)(2,1)}), bf16[4096,1024]{1,0:T(8,128)(2,1)}) %all-gather.26.cloned.1.call-update) | async-done | bytes 8388624 | tf_op jit(solution)/shard_map/all_gather | solution.py:397
  490.7 9.7 %fusion.13 = f32[512,1024]{1,0:T(8,128)S(1)} fusion(bf16[4096,1024]{1,0:T(8,128)(2,1)} %all-gather.26.cloned.1.call-done, f32[512,4096]{1,0:T(8,128)} %fusion.113), kind=kOutput, calls=%fused_computation.19 | convolution fusion | flops 4305453056 | bytes 18874368 | tf_op jit(solution)/shard_map/dot_general | solution.py:38
  511.2 17.0 %fusion.114 = f32[512,1024]{1,0:T(8,128)} fusion(bf16[1024,4096]{1,0:T(8,128)(2,1)} %all-gather.24.cloned.1.call-done, f32[512,4096]{1,0:T(8,128)} %fusion.113, bf16[4096,1024]{1,0:T(8,128)(2,1)} %all-gather.26.cloned.1.call-done, f32[512,1024]{1,0:T(8,128)} %copy-done.4), kind=kOutput, calls=%fused_computation.266 | convolution fusion | flops 8611430400 | bytes 29360128 | tf_op jit(solution)/shard_map/dot_general | solution.py:42
  534.6 28.5 %shard_map.245 = (bf16[512,1024]{1,0:T(8,128)(2,1)}, f32[512,1024]{1,0:T(8,128)}, bf16[512,1024]{1,0:T(8,128)(2,1)}, f32[512,1024]{1,0:T(8,128)}, bf16[512,1024]{1,0:T(8,128)(2,1)}) custom-call(s32[1]{0:T(128)} %bitcast.half_ref, s32[1,512]{1,0:T(1,128)} %bitcast.323, s32[512,1]{1,0:T(8,128)} %copy.41.kid_own_ref, s32[512,1]{1,0:T(8,128)} %copy.42.kid_far_ref, ...), custom_call_target="tpu_custom_call" | custom-call | flops 21474836480 | bytes 12582912 | tf_op jit(solution)/shard_map/pallas_call | solution.py:263
  574.9 28.7 %shard_map.247 = (bf16[512,1024]{1,0:T(8,128)(2,1)}, f32[512,1024]{1,0:T(8,128)}, bf16[512,1024]{1,0:T(8,128)(2,1)}, f32[512,1024]{1,0:T(8,128)}, bf16[512,1024]{1,0:T(8,128)(2,1)}) custom-call(s32[1]{0:T(128)} %bitcast.half_ref, s32[1,512]{1,0:T(1,128)} %bitcast.324, s32[512,1]{1,0:T(8,128)} %copy.41.kid_own_ref, s32[512,1]{1,0:T(8,128)} %copy.42.kid_far_ref, ...), custom_call_target="tpu_custom_call" | custom-call | flops 21474836480 | bytes 12582912 | tf_op jit(solution)/shard_map/pallas_call | solution.py:263
  627.8 9.8 %collective-permute-done.25 = f32[2,128,512]{2,1,0:T(8,128)S(1)} collective-permute-done((f32[2,128,512]{2,1,0:T(8,128)S(1)}, f32[2,128,512]{2,1,0:T(8,128)S(1)}, u32[]{:S(2)}, u32[]{:S(2)}) %collective-permute-start.25) | collective-permute-done | bytes 524320 | tf_op jit(solution)/shard_map/ppermute | solution.py:30
  643.7 6.4 collective-permute-done.26
  657.6 6.2 collective-permute-done.22
  675.0 17.2 %fusion.115 = f32[512,1024]{1,0:T(8,128)} fusion(bf16[1024,4096]{1,0:T(8,128)(2,1)} %all-gather.14.cloned.1.call-done, f32[512,4096]{1,0:T(8,128)} %fusion.112, bf16[4096,1024]{1,0:T(8,128)(2,1)} %all-gather.16.cloned.1.call-done, f32[512,1024]{1,0:T(8,128)} %copy-done.5), kind=kOutput, calls=%fused_computation.267 | convolution fusion | flops 8611430400 | bytes 29360128 | tf_op jit(solution)/shard_map/dot_general | solution.py:42
  699.4 5.8 collective-permute-done.31
  710.1 28.3 %shard_map.246 = (bf16[512,1024]{1,0:T(8,128)(2,1)}, f32[512,1024]{1,0:T(8,128)}, bf16[512,1024]{1,0:T(8,128)(2,1)}, f32[512,1024]{1,0:T(8,128)}, bf16[512,1024]{1,0:T(8,128)(2,1)}) custom-call(s32[1]{0:T(128)} %bitcast.half_ref, s32[1,512]{1,0:T(1,128)} %bitcast.325, s32[512,1]{1,0:T(8,128)} %copy.41.kid_own_ref, s32[512,1]{1,0:T(8,128)} %copy.42.kid_far_ref, ...), custom_call_target="tpu_custom_call" | custom-call | flops 21474836480 | bytes 12582912 | tf_op jit(solution)/shard_map/pallas_call | solution.py:263
  753.6 32.8 %collective-permute-done.16 = f32[3072]{0:T(1024)S(1)} collective-permute-done((f32[3072]{0:T(1024)S(1)}, f32[3072]{0:T(1024)S(1)}, u32[]{:S(2)}, u32[]{:S(2)}) %collective-permute-start.16) | collective-permute-done | bytes 12320 | tf_op jit(solution)/shard_map/ppermute | solution.py:30
  805.6 7.0 select_reduce_fusion
  854.6 7.2 add_add_fusion.1
  (367 shorter events, 242.3 us)
Async XLA Ops:
  7.2 51.0 %all-gather.10.cloned.1.call-start = ((), (), s32[]{:S(2)}) async-start(), calls=%async_computation.3 | async-start | bytes 7077888 | tf_op jit(solution)/shard_map/all_gather | solution.py:387
  7.9 121.6 %all-gather.12.cloned.1.call-start = ((), (), s32[]{:S(2)}) async-start(), calls=%async_computation.4 | async-start | bytes 2359296 | tf_op jit(solution)/shard_map/all_gather | solution.py:388
  8.6 145.7 %all-gather.18.cloned.1.call-start = ((), (), s32[]{:S(2)}) async-start(), calls=%async_computation.7 | async-start | bytes 4325376 | tf_op jit(solution)/shard_map/all_gather | solution.py:385
  10.3 198.9 %all-gather.14.cloned.1.call-start = ((), (), s32[]{:S(2)}) async-start(), calls=%async_computation.5 | async-start | bytes 9437184 | tf_op jit(solution)/shard_map/all_gather | solution.py:389
  10.9 254.5 %all-gather.16.cloned.1.call-start = ((), (), s32[]{:S(2)}) async-start(), calls=%async_computation.6 | async-start | bytes 9437184 | tf_op jit(solution)/shard_map/all_gather | solution.py:390
  11.6 327.8 %all-gather.20.cloned.1.call-start = ((), (), s32[]{:S(2)}) async-start(), calls=%async_computation.8 | async-start | bytes 14155776 | tf_op jit(solution)/shard_map/all_gather | solution.py:394
  12.2 397.9 %all-gather.22.cloned.1.call-start = ((), (), s32[]{:S(2)}) async-start(), calls=%async_computation.9 | async-start | bytes 4718592 | tf_op jit(solution)/shard_map/all_gather | solution.py:395
  12.9 448.8 %all-gather.24.cloned.1.call-start = ((), (), s32[]{:S(2)}) async-start(), calls=%async_computation.10 | async-start | bytes 9437184 | tf_op jit(solution)/shard_map/all_gather | solution.py:396
  13.7 54.2 %collective-permute-start = (s32[512]{0:T(512)S(1)}, s32[512]{0:T(512)S(1)}, u32[]{:S(2)}, u32[]{:S(2)}) collective-permute-start(s32[512]{0:T(512)S(1)} %copy-done.53), channel_id=1, source_target_pairs={{0,1},{1,0},{2,3},{3,2},{4,5},{5,4},{6,7},{7,6},{8,9},{9,8},{10,11... | collective-permute-start | bytes 6152 | tf_op jit(solution)/shard_map/ppermute | solution.py:30
  16.7 52.0 %all-to-all-start = ((f32[4,32,512]{2,1,0:T(8,128)}), f32[4,32,512]{2,1,0:T(8,128)S(1)}, u32[]{:S(2)}, u32[]{:S(2)}) async-start(f32[4,32,512]{2,1,0:T(8,128)} %param.35), calls=%async_computation | async-start | bytes 524288 | tf_op jit(solution)/shard_map/all_to_all | solution.py:469
  20.6 470.0 %all-gather.26.cloned.1.call-start = ((), (), s32[]{:S(2)}) async-start(), calls=%async_computation.11 | async-start | bytes 9437184 | tf_op jit(solution)/shard_map/all_gather | solution.py:397
  61.1 26.2 %collective-permute-start.1 = (bf16[512,1024]{1,0:T(8,128)(2,1)S(1)}, bf16[512,1024]{1,0:T(8,128)(2,1)}, u32[]{:S(2)}, u32[]{:S(2)}) collective-permute-start(bf16[512,1024]{1,0:T(8,128)(2,1)S(1)} %fusion.54.k_own_ref), channel_id=1, source_target_pairs={{0,1},{1,0},{2,3},{3,2},{4,5},{5,4},{6,7},{7,6},{8,9},{9,8},{10,11... | collective-permute-start | bytes 3145736 | tf_op jit(solution)/shard_map/ppermute | solution.py:30
  66.4 44.7 %collective-permute-start.2 = (bf16[512,1024]{1,0:T(8,128)(2,1)}, bf16[512,1024]{1,0:T(8,128)(2,1)}, u32[]{:S(2)}, u32[]{:S(2)}) collective-permute-start(bf16[512,1024]{1,0:T(8,128)(2,1)} %fusion.53.v_own_ref), channel_id=1, source_target_pairs={{0,1},{1,0},{2,3},{3,2},{4,5},{5,4},{6,7},{7,6},{8,9},{9,8},{10,11... | collective-permute-start | bytes 3145736 | tf_op jit(solution)/shard_map/ppermute | solution.py:30
  342.4 26.1 %collective-permute-start.3 = (bf16[512,1024]{1,0:T(8,128)(2,1)S(1)}, bf16[512,1024]{1,0:T(8,128)(2,1)S(1)}, u32[]{:S(2)}, u32[]{:S(2)}) collective-permute-start(bf16[512,1024]{1,0:T(8,128)(2,1)S(1)} %fusion.51.k_own_ref), channel_id=1, source_target_pairs={{0,1},{1,0},{2,3},{3,2},{4,5},{5,4},{6,7},{7,6},{8,9},{9,8},{10,11... | collective-permute-start | bytes 3145736 | tf_op jit(solution)/shard_map/ppermute | solution.py:30
  346.8 44.1 %collective-permute-start.4 = (bf16[512,1024]{1,0:T(8,128)(2,1)S(1)}, bf16[512,1024]{1,0:T(8,128)(2,1)S(1)}, u32[]{:S(2)}, u32[]{:S(2)}) collective-permute-start(bf16[512,1024]{1,0:T(8,128)(2,1)S(1)} %fusion.50.v_own_ref), channel_id=1, source_target_pairs={{0,1},{1,0},{2,3},{3,2},{4,5},{5,4},{6,7},{7,6},{8,9},{9,8},{10,11... | collective-permute-start | bytes 3145736 | tf_op jit(solution)/shard_map/ppermute | solution.py:30
  350.4 67.6 %collective-permute-start.5 = (bf16[512,1024]{1,0:T(8,128)(2,1)}, bf16[512,1024]{1,0:T(8,128)(2,1)}, u32[]{:S(2)}, u32[]{:S(2)}) collective-permute-start(bf16[512,1024]{1,0:T(8,128)(2,1)} %fusion.47.k_own_ref), channel_id=1, source_target_pairs={{0,1},{1,0},{2,3},{3,2},{4,5},{5,4},{6,7},{7,6},{8,9},{9,8},{10,11... | collective-permute-start | bytes 3145736 | tf_op jit(solution)/shard_map/ppermute | solution.py:30
  353.5 81.7 %collective-permute-start.6 = (bf16[512,1024]{1,0:T(8,128)(2,1)}, bf16[512,1024]{1,0:T(8,128)(2,1)S(1)}, u32[]{:S(2)}, u32[]{:S(2)}) collective-permute-start(bf16[512,1024]{1,0:T(8,128)(2,1)} %fusion.46.v_own_ref), channel_id=1, source_target_pairs={{0,1},{1,0},{2,3},{3,2},{4,5},{5,4},{6,7},{7,6},{8,9},{9,8},{10,11... | collective-permute-start | bytes 3145736 | tf_op jit(solution)/shard_map/ppermute | solution.py:30
  563.2 46.6 %collective-permute-start.7 = (bf16[512,1024]{1,0:T(8,128)(2,1)}, bf16[512,1024]{1,0:T(8,128)(2,1)}, u32[]{:S(2)}, u32[]{:S(2)}) collective-permute-start(bf16[512,1024]{1,0:T(8,128)(2,1)} %get-tuple-element.34), channel_id=1, source_target_pairs={{0,1},{1,0},{2,3},{3,2},{4,5},{5,4},{6,7},{7,6},{8,9},{9,8},{10,11... | collective-permute-start | bytes 3145736 | tf_op jit(solution)/shard_map/ppermute | solution.py:30
  564.8 49.0 %collective-permute-start.8 = (bf16[512,1024]{1,0:T(8,128)(2,1)}, bf16[512,1024]{1,0:T(8,128)(2,1)S(1)}, u32[]{:S(2)}, u32[]{:S(2)}) collective-permute-start(bf16[512,1024]{1,0:T(8,128)(2,1)} %get-tuple-element.36), channel_id=1, source_target_pairs={{0,1},{1,0},{2,3},{3,2},{4,5},{5,4},{6,7},{7,6},{8,9},{9,8},{10,11... | collective-permute-start | bytes 3145736 | tf_op jit(solution)/shard_map/ppermute | solution.py:30
  566.3 55.4 %collective-permute-start.24 = (f32[2,2,128,512]{3,2,1,0:T(8,128)}, f32[2,2,128,512]{3,2,1,0:T(8,128)}, u32[]{:S(2)}, u32[]{:S(2)}) collective-permute-start(f32[2,2,128,512]{3,2,1,0:T(8,128)} %dynamic-slice_bitcast_fusion.1), channel_id=1, source_target_pairs={{0,4},{4,0},{8,12},{12,8},{16,20},{20,16},{24,28},{28,24},{1,5},{5... | collective-permute-start | bytes 3145736 | tf_op jit(solution)/shard_map/ppermute | solution.py:30
  567.4 58.2 %collective-permute-start.27 = (f32[2,2,128,512]{3,2,1,0:T(8,128)}, f32[2,2,128,512]{3,2,1,0:T(8,128)}, u32[]{:S(2)}, u32[]{:S(2)}) collective-permute-start(f32[2,2,128,512]{3,2,1,0:T(8,128)} %dynamic-slice_bitcast_fusion), channel_id=1, source_target_pairs={{0,4},{4,0},{8,12},{12,8},{16,20},{20,16},{24,28},{28,24},{1,5},{5... | collective-permute-start | bytes 3145736 | tf_op jit(solution)/shard_map/ppermute | solution.py:30
  603.6 136.9 %collective-permute-start.11 = (bf16[512,1024]{1,0:T(8,128)(2,1)}, bf16[512,1024]{1,0:T(8,128)(2,1)}, u32[]{:S(2)}, u32[]{:S(2)}) collective-permute-start(bf16[512,1024]{1,0:T(8,128)(2,1)} %get-tuple-element.47), channel_id=1, source_target_pairs={{0,1},{1,0},{2,3},{3,2},{4,5},{5,4},{6,7},{7,6},{8,9},{9,8},{10,11... | collective-permute-start | bytes 3145736 | tf_op jit(solution)/shard_map/ppermute | solution.py:30
  609.8 138.7 %collective-permute-start.12 = (bf16[512,1024]{1,0:T(8,128)(2,1)}, bf16[512,1024]{1,0:T(8,128)(2,1)}, u32[]{:S(2)}, u32[]{:S(2)}) collective-permute-start(bf16[512,1024]{1,0:T(8,128)(2,1)} %get-tuple-element.49), channel_id=1, source_target_pairs={{0,1},{1,0},{2,3},{3,2},{4,5},{5,4},{6,7},{7,6},{8,9},{9,8},{10,11... | collective-permute-start | bytes 3145736 | tf_op jit(solution)/shard_map/ppermute | solution.py:30
  641.2 66.6 %collective-permute-start.13 = (f32[3072]{0:T(1024)S(1)}, f32[3072]{0:T(1024)S(1)}, u32[]{:S(2)}, u32[]{:S(2)}) collective-permute-start(f32[3072]{0:T(1024)S(1)} %pad_maximum_fusion.3), channel_id=1, source_target_pairs={{0,4},{4,0},{8,12},{12,8},{16,20},{20,16},{24,28},{28,24},{1,5},{5... | collective-permute-start | bytes 36872 | tf_op jit(solution)/shard_map/ppermute | solution.py:30
  672.5 24.1 %collective-permute-start.30 = (f32[2,128,512]{2,1,0:T(8,128)}, f32[2,128,512]{2,1,0:T(8,128)}, u32[]{:S(2)}, u32[]{:S(2)}) collective-permute-start(f32[2,128,512]{2,1,0:T(8,128)} %dynamic-slice_bitcast_fusion.4), channel_id=1, source_target_pairs={{0,2},{1,3},{2,0},{3,1},{4,6},{5,7},{6,4},{7,5},{8,10},{9,11},{10,... | collective-permute-start | bytes 1572872 | tf_op jit(solution)/shard_map/ppermute | solution.py:30
  707.9 32.0 %collective-permute-start.14 = (f32[3072]{0:T(1024)S(1)}, f32[3072]{0:T(1024)S(1)}, u32[]{:S(2)}, u32[]{:S(2)}) collective-permute-start(f32[3072]{0:T(1024)S(1)} %fusion.98), channel_id=1, source_target_pairs={{0,8},{4,12},{8,0},{12,4},{16,24},{20,28},{24,16},{28,20},{1,9},{5... | collective-permute-start | bytes 36872 | tf_op jit(solution)/shard_map/ppermute | solution.py:30
  709.0 37.7 %collective-permute-start.33 = (f32[2,128,512]{2,1,0:T(8,128)S(1)}, f32[2,128,512]{2,1,0:T(8,128)S(1)}, u32[]{:S(2)}, u32[]{:S(2)}) collective-permute-start(f32[2,128,512]{2,1,0:T(8,128)S(1)} %pad_maximum_fusion.2), channel_id=1, source_target_pairs={{0,8},{4,12},{8,0},{12,4},{16,24},{20,28},{24,16},{28,20},{1,9},{5... | collective-permute-start | bytes 1572872 | tf_op jit(solution)/shard_map/ppermute | solution.py:30
  738.4 56.5 %collective-permute-start.9 = (bf16[512,1024]{1,0:T(8,128)(2,1)}, bf16[512,1024]{1,0:T(8,128)(2,1)}, u32[]{:S(2)}, u32[]{:S(2)}) collective-permute-start(bf16[512,1024]{1,0:T(8,128)(2,1)} %get-tuple-element.40), channel_id=1, source_target_pairs={{0,1},{1,0},{2,3},{3,2},{4,5},{5,4},{6,7},{7,6},{8,9},{9,8},{10,11... | collective-permute-start | bytes 3145736 | tf_op jit(solution)/shard_map/ppermute | solution.py:30
  739.9 114.8 %collective-permute-start.10 = (bf16[512,1024]{1,0:T(8,128)(2,1)}, bf16[512,1024]{1,0:T(8,128)(2,1)}, u32[]{:S(2)}, u32[]{:S(2)}) collective-permute-start(bf16[512,1024]{1,0:T(8,128)(2,1)} %get-tuple-element.42), channel_id=1, source_target_pairs={{0,1},{1,0},{2,3},{3,2},{4,5},{5,4},{6,7},{7,6},{8,9},{9,8},{10,11... | collective-permute-start | bytes 3145736 | tf_op jit(solution)/shard_map/ppermute | solution.py:30
  745.3 41.1 %collective-permute-start.16 = (f32[3072]{0:T(1024)S(1)}, f32[3072]{0:T(1024)S(1)}, u32[]{:S(2)}, u32[]{:S(2)}) collective-permute-start(f32[3072]{0:T(1024)S(1)} %add.430), channel_id=1, source_target_pairs={{0,1},{1,0},{2,3},{3,2},{4,5},{5,4},{6,7},{7,6},{8,9},{9,8},{10,11... | collective-permute-start | bytes 36872 | tf_op jit(solution)/shard_map/ppermute | solution.py:30
  747.9 57.7 %collective-permute-start.34 = (f32[4,128,512]{2,1,0:T(8,128)}, f32[4,128,512]{2,1,0:T(8,128)}, u32[]{:S(2)}, u32[]{:S(2)}) collective-permute-start(f32[4,128,512]{2,1,0:T(8,128)} %pad_maximum_fusion.1), channel_id=1, source_target_pairs={{0,16},{4,20},{8,24},{12,28},{16,0},{20,4},{24,8},{28,12},{1,17},{... | collective-permute-start | bytes 3145736 | tf_op jit(solution)/shard_map/ppermute | solution.py:30
  801.1 48.4 %all-to-all-start.1 = ((f32[1,128,512]{2,0,1:T(1,128)}), f32[1,128,512]{2,0,1:T(1,128)}, u32[]{:S(2)}, u32[]{:S(2)}) async-start(f32[1,128,512]{2,0,1:T(1,128)} %copy.53), calls=%async_computation.1 | async-start | bytes 524288 | tf_op jit(solution)/shard_map/all_to_all | solution.py:472
  (85 other events, 1936.5 us)
Sparse Core Ops, SparseCore 0:
  9.9 48.2 all-gather.9
  60.1 27.8 all-gather.11
  91.6 62.6 all-gather.17
  156.1 53.1 all-gather.13
  211.0 54.3 all-gather.15
  267.2 72.1 all-gather.19
  341.3 36.7 all-gather.21
  379.9 54.3 all-gather.23
  436.2 54.3 all-gather.25

commit v2 on v1

v2 whole, which is shorter than its diff:
```python
import functools
import math

import jax
import jax.numpy as jnp
from jax import lax
from jax.experimental import pallas as pl
from jax.experimental.pallas import tpu as pltpu
from jax.sharding import PartitionSpec as P

D = 1024
HD = 64
ADAPT = 512
NS_ITERS = 5

EPSILON = 1e-05
MASKED = -1e30
NEWTON_LINEAR = 3.4445
NEWTON_QUADRATIC = -4.775
NEWTON_CUBIC = 2.0315
RATE = 0.7
DECAY = 0.5
LOG2E = 1.4426950408889634
PAIR = 2 * HD
VMEM_LIMIT = 58 * 1024 * 1024
MESH = pl.DeviceIdType.MESH


def swap(array, axis, bit):
    return lax.ppermute(array, axis, [(i, i ^ bit) for i in range(lax.axis_size(axis))])


def bfloat(tensor):
    return tensor.astype(jnp.bfloat16)


def product(left_side, right_side):
    return jnp.dot(left_side, right_side, preferred_element_type=jnp.float32)


def contract(left_side, right_side, left_dim, right_dim):
    return lax.dot_general(
        left_side,
        right_side,
        (((left_dim,), (right_dim,)), ((), ())),
        preferred_element_type=jnp.float32,
    )


def product_t(left_side, right_side):
    return contract(left_side, right_side, 1, 1)


def product_rows(left_side, right_side):
    return contract(left_side, right_side, 0, 0)


def gelu_both(tensor):
    phi = 0.5 * (1.0 + lax.erf(tensor * 0.7071067811865476))
    slope = phi + tensor * jnp.exp(-0.5 * tensor * tensor) * 0.3989422804014327
    return tensor * phi, slope


def fill_bias(half_ref, qid_ref, kid_own_ref, kid_far_ref, bias_ref, causal):
    rows = qid_ref.shape[1]
    qid = qid_ref[...]
    for part, kid_ref in enumerate((kid_own_ref, kid_far_ref)):
        allowed = kid_ref[...] == qid
        if causal:
            if part == 0:
                key_at = lax.broadcasted_iota(jnp.int32, (rows, rows), 0)
                query_at = lax.broadcasted_iota(jnp.int32, (rows, rows), 1)
                allowed = allowed & (key_at <= query_at)
            else:
                allowed = allowed & (half_ref[0] == 1)
        bias_ref[pl.ds(part * rows, rows), :] = jnp.where(allowed, 0.0, MASKED)


def head_mask(rows, head):
    return lax.broadcasted_iota(jnp.int32, (rows, PAIR), 1) // HD == head


def attend_kernel(
    causal,
    chunk,
    half_ref,
    qid_ref,
    kid_own_ref,
    kid_far_ref,
    q_ref,
    k_own_ref,
    k_far_ref,
    v_own_ref,
    v_far_ref,
    out_ref,
    lse_ref,
    bias_ref,
    score_ref,
):
    rows = q_ref.shape[0]

    @pl.when(pl.program_id(0) == 0)
    def _():
        fill_bias(half_ref, qid_ref, kid_own_ref, kid_far_ref, bias_ref, causal)

    queries = q_ref[...] * 0.125
    steps = [
        (part, at)
        for part in range(2)
        for at in range(0, rows, chunk)
    ]
    keys = (k_own_ref, k_far_ref)
    values = (v_own_ref, v_far_ref)
    mixes = []
    for head in range(2):
        q_head = jnp.where(head_mask(rows, head), queries, jnp.zeros_like(queries))
        peak = None
        for part, at in steps:
            place = pl.ds(part * rows + at, chunk)
            scores = product_t(keys[part][pl.ds(at, chunk), :], q_head)
            scores = scores * LOG2E + bias_ref[place, :]
            score_ref[head, place, :] = scores
            top = jnp.max(scores, axis=0, keepdims=True)
            peak = top if peak is None else jnp.maximum(peak, top)
        total, mix = None, None
        for part, at in steps:
            place = pl.ds(part * rows + at, chunk)
            raised = jnp.exp2(score_ref[head, place, :] - peak)
            share = jnp.sum(raised, axis=0, keepdims=True)
            piece = product_rows(values[part][pl.ds(at, chunk), :], bfloat(raised))
            total = share if total is None else total + share
            mix = piece if mix is None else mix + piece
        mixes.append((mix * (1.0 / total))[head * HD : (head + 1) * HD, :])
        lse_ref[0, pl.ds(head, 1), :] = peak + jnp.log2(total)
    out_ref[...] = bfloat(jnp.concatenate(mixes, axis=0).T)


def attend_back_kernel(
    causal,
    chunk,
    half_ref,
    qid_ref,
    kid_own_ref,
    kid_far_ref,
    q_ref,
    k_own_ref,
    k_far_ref,
    v_own_ref,
    v_far_ref,
    out_ref,
    grad_ref,
    lse_ref,
    dq_ref,
    dk_own_ref,
    dk_far_ref,
    dv_own_ref,
    dv_far_ref,
    bias_ref,
):
    rows = q_ref.shape[0]

    @pl.when(pl.program_id(0) == 0)
    def _():
        fill_bias(half_ref, qid_ref, kid_own_ref, kid_far_ref, bias_ref, causal)

    queries = q_ref[...] * 0.125
    grads = grad_ref[...]
    products = (grads.astype(jnp.float32) * out_ref[...].astype(jnp.float32)).T
    q_heads, g_heads, deltas, lses = [], [], [], []
    for head in range(2):
        chosen = head_mask(rows, head)
        q_heads.append(jnp.where(chosen, queries, jnp.zeros_like(queries)))
        g_heads.append(jnp.where(chosen, grads, jnp.zeros_like(grads)))
        deltas.append(jnp.sum(products[head * HD : (head + 1) * HD, :], axis=0, keepdims=True))
        lses.append(lse_ref[0, pl.ds(head, 1), :])
    grad_q = [None, None]
    for part in range(2):
        key_ref = (k_own_ref, k_far_ref)[part]
        value_ref = (v_own_ref, v_far_ref)[part]
        dk_ref = (dk_own_ref, dk_far_ref)[part]
        dv_ref = (dv_own_ref, dv_far_ref)[part]
        for at in range(0, rows, chunk):
            here = pl.ds(at, chunk)
            keys, values = key_ref[here, :], value_ref[here, :]
            grad_k, grad_v = None, None
            for head in range(2):
                scores = product_t(keys, q_heads[head])
                bias = bias_ref[pl.ds(part * rows + at, chunk), :]
                weights = jnp.exp2(scores * LOG2E + (bias - lses[head]))
                grad_w = product_t(values, g_heads[head])
                grad_s = bfloat(weights * (grad_w - deltas[head]))
                piece_v = product(bfloat(weights), g_heads[head])
                piece_k = product(grad_s, q_heads[head])
                piece_q = product_rows(keys, grad_s)
                grad_v = piece_v if grad_v is None else grad_v + piece_v
                grad_k = piece_k if grad_k is None else grad_k + piece_k
                grad_q[head] = piece_q if grad_q[head] is None else grad_q[head] + piece_q
            dk_ref[here, :] = grad_k.astype(dk_ref.dtype)
            dv_ref[here, :] = grad_v.astype(dv_ref.dtype)
    joined = jnp.concatenate([grad_q[h][h * HD : (h + 1) * HD, :] for h in range(2)], axis=0)
    dq_ref[...] = bfloat((joined * 0.125).T)


def attention_specs(rows):
    whole = lambda shape: pl.BlockSpec(shape, lambda i: (0,) * len(shape))
    columns = pl.BlockSpec((rows, PAIR), lambda i: (0, i))
    fixed = [
        pl.BlockSpec(memory_space=pltpu.SMEM),
        whole((1, rows)),
        whole((rows, 1)),
        whole((rows, 1)),
    ]
    return fixed, columns, pl.BlockSpec((1, 8, rows), lambda i: (i, 0, 0))


def attend(places, queries, keys, values, causal):
    rows, width = queries.shape
    pairs = width // PAIR
    fixed, columns, stat = attention_specs(rows)
    return pl.pallas_call(
        functools.partial(attend_kernel, causal, 256),
        grid=(pairs,),
        in_specs=fixed + [columns] * 5,
        out_specs=[columns, stat],
        out_shape=[
            jax.ShapeDtypeStruct((rows, width), jnp.bfloat16),
            jax.ShapeDtypeStruct((pairs, 8, rows), jnp.float32),
        ],
        scratch_shapes=[
            pltpu.VMEM((2 * rows, rows), jnp.float32),
            pltpu.VMEM((2, 2 * rows, rows), jnp.float32),
        ],
        compiler_params=pltpu.CompilerParams(vmem_limit_bytes=VMEM_LIMIT),
        cost_estimate=pl.CostEstimate(
            flops=32 * rows * rows * width, bytes_accessed=12 * rows * width, transcendentals=0
        ),
    )(*places, queries, *keys, *values)


def attend_back(places, grad_out, queries, keys, values, mix, lse, causal):
    rows, width = queries.shape
    pairs = width // PAIR
    fixed, columns, stat = attention_specs(rows)
    return pl.pallas_call(
        functools.partial(attend_back_kernel, causal, 256),
        grid=(pairs,),
        in_specs=fixed + [columns] * 7 + [stat],
        out_specs=[columns] * 5,
        out_shape=[
            jax.ShapeDtypeStruct((rows, width), jnp.bfloat16),
        ]
        * 5,
        scratch_shapes=[pltpu.VMEM((2 * rows, rows), jnp.float32)],
        compiler_params=pltpu.CompilerParams(vmem_limit_bytes=VMEM_LIMIT),
        cost_estimate=pl.CostEstimate(
            flops=80 * rows * rows * width, bytes_accessed=24 * rows * width, transcendentals=0
        ),
    )(*places, queries, *keys, *values, mix, grad_out, lse)


def flipped(me, bits):
    place = me
    bit = 1
    while bit <= bits:
        if bits & bit:
            place = place + bit * (1 - 2 * lax.rem(lax.div(me, bit), 2))
        bit *= 2
    return place


class Loader:
    def __init__(self, sems):
        self.local, self.send, self.recv, self.stored = sems
        self.copies, self.stores = [], []
        self.me = lax.axis_index("wide")
        self.sibling = {"wide": flipped(self.me, 1)}
        barrier = pltpu.get_barrier_semaphore()
        pl.semaphore_signal(barrier, inc=1, device_id=self.sibling, device_id_type=MESH)
        pl.semaphore_wait(barrier, 1)

    def fetch(self, pieces, offset, height, target, columns=slice(None)):
        block = len(self.copies)
        copies = []
        for i, piece in enumerate(pieces):
            at = pl.multiple_of(flipped(self.me, 2 * i) * height, height)
            source = piece.at[pl.ds(offset, height), columns]
            place = target.at[pl.ds(at, height), columns]
            near = pltpu.make_async_copy(source, place, self.local.at[block, i])
            far = pltpu.make_async_remote_copy(
                source,
                place,
                self.send.at[block, i],
                self.recv.at[block, i],
                device_id=self.sibling,
                device_id_type=MESH,
            )
            near.start()
            far.start()
            copies.append((near, far))
        self.copies.append(copies)
        return block

    def arrived(self, block, target, out):
        for near, far in self.copies[block]:
            near.wait()
            far.wait_recv()
        store = pltpu.make_async_copy(target, out, self.stored.at[block])
        store.start()
        self.stores.append(store)

    def finish(self):
        for copies in self.copies:
            for _, far in copies:
                far.wait_send()
        for store in self.stores:
            store.wait()


def loader_sems(blocks, pieces):
    dma = pltpu.SemaphoreType.DMA
    return [dma((blocks, pieces))] * 3 + [dma((blocks,))]


def load(weights, targets, sem):
    for j, (weight, target) in enumerate(zip(weights, targets)):
        pltpu.make_async_copy(weight, target, sem.at[j]).start()


def loaded(target, sem):
    pltpu.make_async_copy(target, target, sem).wait()


def tiles(body, width, step):
    @pl.loop(0, width // step)
    def _(i):
        body(pl.ds(pl.multiple_of(i * step, step), step))


ROWS = 64
TILE = 256
STAT = 128


def normalise(z_ref, n_ref, r_ref, gain, low_ref):
    def body(rows):
        z = z_ref[rows, :]
        centred = z - jnp.mean(z, axis=-1, keepdims=True)
        inverse = lax.rsqrt(jnp.mean(centred * centred, axis=-1, keepdims=True) + EPSILON)
        normed = centred * inverse
        n_ref[rows, :] = normed
        r_ref[rows, :] = jnp.broadcast_to(inverse, (ROWS, STAT))
        if low_ref is not None:
            low_ref[rows, :] = bfloat(normed * gain)

    tiles(body, z_ref.shape[0], ROWS)


def normalise_back(read_grad, n_ref, r_ref, gain, dz_ref, low_ref):
    def body(rows):
        scaled = read_grad(rows) * gain
        normed = n_ref[rows, :]
        dz = r_ref[rows, :][:, :1] * (
            scaled
            - jnp.mean(scaled, axis=-1, keepdims=True)
            - normed * jnp.mean(scaled * normed, axis=-1, keepdims=True)
        )
        dz_ref[rows, :] = dz
        low_ref[rows, :] = bfloat(dz)

    tiles(body, n_ref.shape[0], ROWS)


def project_kernel(n, height, offsets, x_ref, far_ref, *refs):
    count = len(offsets)
    pieces, outs, full, (weight, *sems) = refs[:n], refs[n:-6], refs[-6], refs[-5:]
    loader = Loader(sems)
    for j, offset in enumerate(offsets):
        loader.fetch(pieces, offset, height, weight.at[j])
    for j in range(count):
        loader.arrived(j, weight.at[j], full.at[j])
        far = outs[count + j - (count - 2)] if j >= count - 2 else None

        def body(columns):
            outs[j][:, columns] = bfloat(product(x_ref[...], weight[j, :, columns]))
            if far is not None:
                far[:, columns] = bfloat(product(far_ref[...], weight[j, :, columns]))

        tiles(body, outs[j].shape[1], TILE)
    loader.finish()


def settle_kernel(n, height, wo_at, q_at, gain_rows, x_ref, mix_ref, gains_ref, *refs):
    pieces, refs = refs[:n], refs[n:]
    if q_at is None:
        n_ref, r_ref, full, weight, z_ref, *sems = refs
        low_ref = None
    else:
        n_ref, r_ref, q_ref, full, weight, z_ref, low_ref, *sems = refs
    loader = Loader(sems)
    loader.fetch(pieces, wo_at, height, weight.at[0])
    if q_at is not None:
        loader.fetch(pieces, q_at, height, weight.at[1])
    loader.arrived(0, weight.at[0], full.at[0])

    def project(columns):
        x = x_ref[:, columns].astype(jnp.float32)
        if gain_rows[0] is not None:
            x = x * gains_ref[pl.ds(gain_rows[0], 1), columns]
        z_ref[:, columns] = x + product(mix_ref[...], weight[0, :, columns])

    tiles(project, z_ref.shape[1], TILE)
    gain = gains_ref[pl.ds(gain_rows[1], 1), :]
    normalise(z_ref, n_ref, r_ref, gain, low_ref)
    if q_at is not None:
        loader.arrived(1, weight.at[1], full.at[1])

        def query(columns):
            q_ref[:, columns] = bfloat(product(low_ref[...], weight[1, :, columns]))

        tiles(query, q_ref.shape[1], TILE)
    loader.finish()


def tail_up_kernel(n, height, up_at, gain_row, n_ref, gains_ref, *refs):
    pieces = refs[:n]
    slope_hbm, inner_hbm, full, up, low_ref, slope_ref, inner_ref, out_sem, *sems = refs[n:]
    blocks = up.shape[0]
    loader = Loader(sems)
    for j in range(blocks):
        loader.fetch(pieces, up_at + j * height, height, up.at[j])
    gain = gains_ref[pl.ds(gain_row, 1), :]

    def lower(rows):
        low_ref[rows, :] = bfloat(n_ref[rows, :] * gain)

    tiles(lower, n_ref.shape[0], ROWS)
    width = up.shape[2]
    outs = []
    for j in range(blocks):
        loader.arrived(j, up.at[j], full.at[j])

        def upward(columns):
            inner, slope = gelu_both(product(low_ref[...], up[j, :, columns]))
            place = pl.ds(pl.multiple_of(j * width + columns.start, TILE), TILE)
            inner_ref[:, place] = bfloat(inner)
            slope_ref[:, place] = bfloat(slope)

        tiles(upward, width, TILE)
        columns = pl.ds(j * width, width)
        for i, (ref, hbm) in enumerate(((inner_ref, inner_hbm), (slope_ref, slope_hbm))):
            out = pltpu.make_async_copy(ref.at[:, columns], hbm.at[:, columns], out_sem.at[i, j])
            out.start()
            outs.append(out)
    loader.finish()
    for out in outs:
        out.wait()


def tail_down_kernel(n, height, offsets, gain_rows, n_ref, inner_ref, gains_ref, first_ref, second_ref, *refs):
    pieces, refs = refs[:n], refs[n:]
    pre_slope_ref, adapt_ref, n_out_ref, r_out_ref, out_ref, down_full, adapt_full = refs[:7]
    down, adapt, low_ref, z_ref, *sems = refs[7:]
    down_at, adapt_at = offsets
    width = z_ref.shape[1]
    loader = Loader(sems)
    loader.fetch(pieces, adapt_at, height, adapt)
    for at in range(0, width, TILE):
        loader.fetch(pieces, down_at, down.shape[0] // width * height, down, pl.ds(at, TILE))
    gain = gains_ref[pl.ds(gain_rows[0], 1), :]

    def lower(rows):
        low_ref[rows, :] = bfloat(n_ref[rows, :] * gain)

    tiles(lower, n_ref.shape[0], ROWS)
    loader.arrived(0, adapt, adapt_full)

    def adapting(columns):
        pre = product(low_ref[...], adapt[:, columns]) + first_ref[:, columns]
        adapted, slope = gelu_both(pre)
        adapt_ref[:, columns] = bfloat(adapted)
        pre_slope_ref[:, columns] = bfloat(slope)

    tiles(adapting, ADAPT, TILE)
    for i, at in enumerate(range(0, width, TILE)):
        columns = pl.ds(at, TILE)
        loader.arrived(1 + i, down.at[:, columns], down_full.at[:, columns])
        h = n_ref[:, columns] * gains_ref[pl.ds(gain_rows[0], 1), columns]
        ffn = product(inner_ref[...], down[:, columns])
        adapted = product_t(adapt_ref[...], adapt[columns, ADAPT:]) + second_ref[:, columns]
        z_ref[:, columns] = h + ffn + 4.0 * adapted
    normalise(z_ref, n_out_ref, r_out_ref, gains_ref[pl.ds(gain_rows[1], 1), :], out_ref)
    loader.finish()


def tail_back_kernel(height, gain_rows, more, *refs):
    (cot_ref, n2_ref, r2_ref, n1_ref, r1_ref, gains_ref, slope_hbm, pre_slope_ref, adapt_low_ref) = refs[:9]
    refs = refs[9:]
    (up_hbm, down_hbm, adapt_hbm, wo_hbm), refs = refs[:4], refs[4:]
    if more:
        far_ref, refs = refs[0], refs[1:]
    dz_ref, dmix_ref, matrices_ref, g_first_ref, g_second_ref = refs[:5]
    up, down, adapt, wo, dt_ref, e_ref, low_ref, du_ref, dpre_ref, sem = refs[5:]
    blocks = up.shape[0]
    load(
        [adapt_hbm, down_hbm, slope_hbm, up_hbm, wo_hbm.at[0]],
        [adapt, down, du_ref, up, wo],
        sem,
    )
    gain1 = gains_ref[pl.ds(gain_rows[0], 1), :]
    gain2 = gains_ref[pl.ds(gain_rows[1], 1), :]

    def lower(rows):
        low_ref[rows, :] = bfloat(n1_ref[rows, :] * gain1)

    tiles(lower, n1_ref.shape[0], ROWS)

    def arriving(rows):
        grad = cot_ref[rows, :].astype(jnp.float32)
        return grad + far_ref[rows, :].astype(jnp.float32) if more else grad

    normalise_back(arriving, n2_ref, r2_ref, gain2, dt_ref, e_ref)
    loaded(adapt, sem.at[0])

    def adapting(columns):
        back = 4.0 * product(e_ref[...], adapt[:, pl.ds(ADAPT + columns.start, TILE)])
        dpre_ref[:, columns] = bfloat(back * pre_slope_ref[:, columns].astype(jnp.float32))

    tiles(adapting, ADAPT, TILE)
    g_first_ref[...] = jnp.sum(dpre_ref[...].astype(jnp.float32), axis=0, keepdims=True)
    g_second_ref[...] = 4.0 * jnp.sum(e_ref[...].astype(jnp.float32), axis=0, keepdims=True)

    wide = max(height, STAT)

    def matrices(columns):
        down_grad = bfloat(product_rows(low_ref[:, columns], dpre_ref[...]))
        up_grad = bfloat(4.0 * product_rows(e_ref[:, columns], adapt_low_ref[...]))
        for i in range(wide // height):
            block, rows = columns.start // height + i, slice(i * height, (i + 1) * height)
            matrices_ref[block, :height, :] = down_grad[rows, :]
            matrices_ref[block, height:, :] = up_grad[rows, :]

    tiles(matrices, low_ref.shape[1], wide)
    loaded(down, sem.at[1])
    loaded(du_ref, sem.at[2])

    def inner(columns):
        back = product_t(e_ref[...], down[columns, :])
        du_ref[:, columns] = bfloat(back * du_ref[:, columns].astype(jnp.float32))

    tiles(inner, du_ref.shape[1], TILE)
    loaded(up, sem.at[3])
    width = up.shape[2]

    def hidden(columns):
        total = dt_ref[:, columns] + product_t(dpre_ref[...], adapt[columns, :ADAPT])
        for j in range(blocks):
            total += product_t(du_ref[:, j * width : (j + 1) * width], up[j, columns, :])
        dt_ref[:, columns] = total

    tiles(hidden, dt_ref.shape[1], TILE)
    normalise_back(lambda rows: dt_ref[rows, :], n1_ref, r1_ref, gain1, dz_ref, e_ref)
    loaded(wo, sem.at[4])

    def mixing(columns):
        dmix_ref[:, columns] = bfloat(product_t(e_ref[...], wo[columns, :]))

    tiles(mixing, dmix_ref.shape[1], TILE)


def query_back_kernel(gain_row, dz_ref, dq_ref, n_ref, r_ref, gains_ref, weights, *refs):
    dz_out_ref, dmix_ref, weight, dy_ref, e_ref, sem = refs
    load([weights.at[1], weights.at[0]], [weight.at[0], weight.at[1]], sem)
    loaded(weight.at[0], sem.at[0])

    def back(columns):
        dy_ref[:, columns] = dz_ref[:, columns] + product_t(dq_ref[...], weight[0, columns, :])

    tiles(back, dy_ref.shape[1], TILE)
    gain = gains_ref[pl.ds(gain_row, 1), :]
    normalise_back(lambda rows: dy_ref[rows, :], n_ref, r_ref, gain, dz_out_ref, e_ref)
    loaded(weight.at[1], sem.at[1])

    def mixing(columns):
        dmix_ref[:, columns] = bfloat(product_t(e_ref[...], weight[1, columns, :]))

    tiles(mixing, dmix_ref.shape[1], TILE)


def back_kernel(indices, bases, *refs):
    count = len(indices)
    base_refs, grads = refs[:bases], refs[bases : bases + count]
    weights, out_ref, weight, sem = refs[bases + count :]
    load([weights.at[i] for i in indices], [weight.at[j] for j in range(count)], sem)
    for j in range(count):
        loaded(weight.at[j], sem.at[j])

    def back(columns):
        total = None
        for base in base_refs:
            part = base[:, columns].astype(jnp.float32)
            total = part if total is None else total + part
        for j in range(count):
            part = product_t(grads[j][...], weight[j, columns, :])
            total = part if total is None else total + part
        out_ref[:, columns] = total.astype(out_ref.dtype)

    tiles(back, out_ref.shape[1], TILE)


def split(value):
    high = bfloat(value)
    return high, bfloat(value - high.astype(jnp.float32))


def put_left(ref, value):
    high, low = split(value)
    ref[:, :ADAPT] = high
    ref[:, ADAPT : 2 * ADAPT] = high
    ref[:, 2 * ADAPT :] = low


def put_right(ref, value):
    high, low = split(value)
    ref[:ADAPT, :] = high
    ref[ADAPT : 2 * ADAPT, :] = low
    ref[2 * ADAPT :, :] = high


def multiply(out_ref, left, right):
    def body(columns):
        out_ref[:, columns] = product(left[...], right[:, columns])

    tiles(body, ADAPT, TILE)


def muon_kernel(parts, *refs):
    rows_refs, (out_ref, high, low, gram, poly, factor, left, right, rows_left) = refs[:parts], refs[parts:]
    rows = rows_refs[0].shape[0]
    for i, ref in enumerate(rows_refs):
        high[i * rows : (i + 1) * rows, :], low[i * rows : (i + 1) * rows, :] = split(ref[...])

    def square(columns):
        gram[:, columns] = (
            product_rows(high[...], high[:, columns])
            + product_rows(high[...], low[:, columns])
            + product_rows(low[...], high[:, columns])
        )

    tiles(square, ADAPT, TILE)
    eye = lax.broadcasted_iota(jnp.int32, (ADAPT, ADAPT), 0) == lax.broadcasted_iota(
        jnp.int32, (ADAPT, ADAPT), 1
    )
    scale = 1.0 / (jnp.sqrt(jnp.sum(jnp.where(eye, gram[...], 0.0), keepdims=True)) + 1e-07)
    gram[...] = gram[...] * (scale * scale)

    def polynomial():
        put_left(left, gram[...])
        put_right(right, gram[...])
        multiply(poly, left, right)
        poly[...] = (
            jnp.where(eye, NEWTON_LINEAR, 0.0) + NEWTON_QUADRATIC * gram[...] + NEWTON_CUBIC * poly[...]
        )
        put_right(right, poly[...])

    def advance():
        multiply(gram, left, right)
        put_left(left, gram[...])
        multiply(gram, left, right)

    polynomial()
    factor[...] = poly[...]
    advance()

    @pl.loop(0, NS_ITERS - 2)
    def _(i):
        polynomial()
        advance()
        put_left(left, factor[...])
        multiply(factor, left, right)

    polynomial()
    put_left(left, factor[...])
    multiply(factor, left, right)
    put_right(right, factor[...])
    put_left(rows_left, rows_refs[0][...] * scale)
    multiply(out_ref, rows_left, right)


HBM = pl.BlockSpec(memory_space=pltpu.HBM)
IN_VMEM = pl.BlockSpec(memory_space=pltpu.VMEM)
F32, BF16 = jnp.float32, jnp.bfloat16


def call(kernel, ins, specs, outs, scratch, flops, collective_id=None):
    return pl.pallas_call(
        kernel,
        in_specs=specs,
        out_specs=[IN_VMEM if len(out) == 2 else HBM for out in outs],
        out_shape=[jax.ShapeDtypeStruct(*out[:2]) for out in outs],
        scratch_shapes=scratch,
        compiler_params=pltpu.CompilerParams(
            vmem_limit_bytes=VMEM_LIMIT,
            collective_id=collective_id,
            has_side_effects=collective_id is not None,
        ),
        cost_estimate=pl.CostEstimate(
            flops=flops, bytes_accessed=sum(a.size * a.dtype.itemsize for a in ins), transcendentals=0
        ),
    )(*ins)


def squares(count):
    return pltpu.VMEM((count, D, D), BF16)


def stored(*shape):
    return (shape, BF16, HBM)


def project(collective_id, x, far, pieces, offsets):
    rows = x.shape[0]
    count, n = len(offsets), len(pieces.arrays)
    return call(
        functools.partial(project_kernel, n, pieces.height, offsets),
        [x, far, *pieces.arrays],
        [IN_VMEM] * 2 + [HBM] * n,
        [((rows, D), BF16)] * (count + 2) + [stored(count, D, D)],
        [squares(count), *loader_sems(count, n)],
        2 * rows * D * D * (count + 2),
        collective_id,
    )


def settle(collective_id, x, mix, gains, pieces, wo_at, q_at, gain_rows):
    rows = x.shape[0]
    n = len(pieces.arrays)
    count = 1 if q_at is None else 2
    outs = [((rows, D), F32), ((rows, STAT), F32)]
    scratch = [squares(count), pltpu.VMEM((rows, D), F32)]
    if q_at is not None:
        outs.append(((rows, D), BF16))
        scratch.append(pltpu.VMEM((rows, D), BF16))
    return call(
        functools.partial(settle_kernel, n, pieces.height, wo_at, q_at, gain_rows),
        [x, mix, gains, *pieces.arrays],
        [IN_VMEM] * 3 + [HBM] * n,
        outs + [stored(count, D, D)],
        scratch + loader_sems(count, n),
        2 * rows * D * D * count,
        collective_id,
    )


def tail_up(collective_id, normed, gains, pieces, up_at, gain_row):
    rows = normed.shape[0]
    n = len(pieces.arrays)
    blocks = 4
    hidden = blocks * D
    return call(
        functools.partial(tail_up_kernel, n, pieces.height, up_at, gain_row),
        [normed, gains, *pieces.arrays],
        [IN_VMEM] * 2 + [HBM] * n,
        [stored(rows, hidden), stored(rows, hidden), stored(blocks, D, D)],
        [
            squares(blocks),
            pltpu.VMEM((rows, D), BF16),
            pltpu.VMEM((rows, hidden), BF16),
            pltpu.VMEM((rows, hidden), BF16),
            pltpu.SemaphoreType.DMA((2, blocks)),
            *loader_sems(blocks, n),
        ],
        8 * rows * D * D,
        collective_id,
    )


def tail_down(collective_id, normed, inner, gains, bias_first, bias_second, pieces, offsets, gain_rows):
    rows, hidden = inner.shape
    n = len(pieces.arrays)
    return call(
        functools.partial(tail_down_kernel, n, pieces.height, offsets, gain_rows),
        [normed, inner, gains, bias_first[None], bias_second[None], *pieces.arrays],
        [IN_VMEM] * 5 + [HBM] * n,
        [
            ((rows, ADAPT), BF16),
            ((rows, ADAPT), BF16),
            ((rows, D), F32),
            ((rows, STAT), F32),
            ((rows, D), BF16),
            stored(hidden, D),
            stored(D, D),
        ],
        [
            pltpu.VMEM((hidden, D), BF16),
            pltpu.VMEM((D, D), BF16),
            pltpu.VMEM((rows, D), BF16),
            pltpu.VMEM((rows, D), F32),
            *loader_sems(1 + D // TILE, n),
        ],
        10 * rows * D * D,
        collective_id,
    )


def tail_back(height, cot, second, first, gains, slope, pre_slope, adapt_low, weights, gain_rows, more=()):
    rows = cot.shape[0]
    hidden = slope.shape[1]
    return call(
        functools.partial(tail_back_kernel, height, gain_rows, bool(more)),
        [cot, *second, *first, gains, slope, pre_slope, adapt_low, *weights, *more],
        [IN_VMEM] * 6 + [HBM] + [IN_VMEM] * 2 + [HBM] * 4 + [IN_VMEM] * len(more),
        [
            ((rows, D), F32),
            ((rows, D), BF16),
            ((D // height, 2 * height, ADAPT), BF16),
            ((1, ADAPT), F32),
            ((1, D), F32),
        ],
        [
            squares(hidden // D),
            pltpu.VMEM((hidden, D), BF16),
            pltpu.VMEM((D, D), BF16),
            pltpu.VMEM((D, D), BF16),
            pltpu.VMEM((rows, D), F32),
            pltpu.VMEM((rows, D), BF16),
            pltpu.VMEM((rows, D), BF16),
            pltpu.VMEM((rows, hidden), BF16),
            pltpu.VMEM((rows, ADAPT), BF16),
            pltpu.SemaphoreType.DMA((5,)),
        ],
        24 * rows * D * D,
    )


def query_back(dz, dq, first, gains, weights, gain_row):
    rows = dz.shape[0]
    return call(
        functools.partial(query_back_kernel, gain_row),
        [dz, dq, *first, gains, weights],
        [IN_VMEM] * 5 + [HBM],
        [((rows, D), F32), ((rows, D), BF16)],
        [
            squares(2),
            pltpu.VMEM((rows, D), F32),
            pltpu.VMEM((rows, D), BF16),
            pltpu.SemaphoreType.DMA((2,)),
        ],
        4 * rows * D * D,
    )


def back(bases, grads, weights, indices, dtype):
    rows = grads[0].shape[0]
    count = len(indices)
    return call(
        functools.partial(back_kernel, indices, len(bases)),
        [*bases, *grads, weights],
        [IN_VMEM] * (len(bases) + count) + [HBM],
        [((rows, D), dtype)],
        [squares(count), pltpu.SemaphoreType.DMA((count,))],
        2 * rows * D * D * count,
    )[0]


def muon(parts):
    rows = parts[0].shape[0]
    full = pltpu.VMEM((ADAPT, ADAPT), F32)
    return call(
        functools.partial(muon_kernel, len(parts)),
        parts,
        [IN_VMEM] * len(parts),
        [((rows, ADAPT), F32)],
        [
            pltpu.VMEM((rows * len(parts), ADAPT), BF16),
            pltpu.VMEM((rows * len(parts), ADAPT), BF16),
            full,
            full,
            full,
            pltpu.VMEM((ADAPT, 3 * ADAPT), BF16),
            pltpu.VMEM((3 * ADAPT, ADAPT), BF16),
            pltpu.VMEM((rows, 3 * ADAPT), BF16),
        ],
        20 * 6 * ADAPT**3,
    )[0]


def axis_bits(axis):
    return [1 << b for b in range(lax.axis_size(axis).bit_length() - 1)]


def tie(array, *others):
    return lax.optimization_barrier((array, *others))[0]


class Gather:
    def __init__(self, array, height):
        self.height = height
        self.array = array

    def begin(self, *after):
        array = tie(self.array, *after) if after else self.array
        bits = axis_bits("wide")
        self.pieces = {0: self.array}
        for bit in bits[1:3]:
            self.pieces[bit] = swap(array, "wide", bit)
        return self

    def across(self, *after):
        bits = axis_bits("wide")
        near, far = bits[1:3]
        pieces = self.pieces
        even = lax.axis_index("wide") % 2 == 0
        chosen = jnp.where(even, pieces[near], pieces[far])
        pieces[near | far] = lax.ppermute(
            tie(chosen, *after) if after else chosen,
            "wide",
            [(i, i ^ (near if i % 2 else far)) for i in range(lax.axis_size("wide"))],
        )
        for bit in bits[3:]:
            for r in list(pieces):
                pieces[r | bit] = swap(pieces[r], "wide", bit)
        self.arrays = [pieces[r] for r in range(0, lax.axis_size("wide"), 2)]
        return self

    def marks(self):
        return list(self.pieces.values())[1:3]


def gather_any_order(array, axis):
    blocks = array[None]
    for bit in axis_bits(axis):
        blocks = jnp.concatenate([blocks, swap(blocks, axis, bit)])
    return blocks


def shards(
    enc_in,
    dec_in,
    segment_ids,
    enc_cot,
    dec_cot,
    enc_qkv,
    enc_wo,
    enc_w_in,
    enc_w_out,
    enc_gains,
    dec_qkv,
    dec_wo,
    dec_w_in,
    dec_w_out,
    dec_gains,
    adapter_weights,
    adapter_momenta,
    bias_in,
    bias_out,
):
    height = enc_wo.shape[0]
    stack = lambda *arrays: jnp.concatenate([a.reshape(-1, D) for a in arrays])
    columns = lambda array: [array[:, j * D : (j + 1) * D] for j in range(array.shape[1] // D)]
    found = gather_any_order(bfloat(adapter_weights), "narrow")
    found = found[lax.axis_index("narrow") ^ jnp.arange(lax.axis_size("narrow"))]
    adapters = found.transpose(1, 0, 2, 3).reshape(4, height, ADAPT)
    beside = lambda l: jnp.concatenate([adapters[2 * l], adapters[2 * l + 1]], axis=1)
    gain_rows = jnp.concatenate([enc_gains, dec_gains])
    gain_block = jnp.pad(gain_rows, ((0, 16 - gain_rows.shape[0]), (0, D - height)))
    gather = lambda array: Gather(array, height)
    enc_first = gather(stack(enc_qkv, gain_block))
    dec_first = gather(stack(dec_qkv[:3]))
    enc_up = gather(stack(enc_wo, *columns(enc_w_in)))
    enc_down = gather(stack(enc_w_out, beside(0)))
    dec_second = gather(stack(dec_wo, dec_qkv[3:]))
    dec_up = gather(stack(*columns(dec_w_in)))
    dec_down = gather(stack(dec_w_out, beside(1)))

    partner = lambda array: swap(array, "narrow", 1)
    other_ids = partner(segment_ids)
    rows = enc_in.shape[0]
    half = (lax.axis_index("narrow") % 2).astype(jnp.int32).reshape(1)
    places = (half, segment_ids.reshape(1, rows), segment_ids.reshape(rows, 1), other_ids.reshape(rows, 1))
    at = lambda i: i * height

    enc_first.begin()
    enc_far, dec_far = partner(enc_in), partner(dec_in)
    dec_first.begin(*enc_first.marks())
    enc_first.across()
    enc_up.begin(enc_first.arrays[-1])
    enc_query, enc_key, enc_value, enc_key_far, enc_value_far, enc_qkv_full = project(
        0, enc_in, enc_far, enc_first, (at(0), at(1), at(2))
    )
    enc_keys, enc_values = (enc_key, enc_key_far), (enc_value, enc_value_far)
    count = lax.axis_size("wide")
    found = jnp.stack([p[at(3) : at(3) + 8, :height] for p in enc_first.arrays])
    found = jnp.concatenate([found, swap(found, "wide", 1)])
    order = lax.axis_index("wide") ^ jnp.arange(count)
    order = order // 2 + order % 2 * (count // 2)
    gains = found[order].transpose(1, 0, 2).reshape(8, D).astype(jnp.float32)

    dec_first.across(enc_value)
    enc_mix, enc_lse = attend(places, enc_query, enc_keys, enc_values, False)
    enc_up.across(enc_mix)
    enc_down.begin(enc_mix)
    self_query, self_key, self_value, self_key_far, self_value_far, dec_qkv_full = project(
        1, tie(dec_in, enc_mix), dec_far, dec_first, (at(0), at(1), at(2))
    )
    self_keys, self_values = (self_key, self_key_far), (self_value, self_value_far)
    dec_second.begin(self_value)
    self_mix, self_lse = attend(places, self_query, self_keys, self_values, True)
    enc_down.across(self_mix)
    *enc_norm1, enc_wo_full = settle(
        2, enc_in, tie(enc_mix, self_mix), gains, enc_up, at(0), None, (None, 0)
    )
    enc_slope, enc_inner, enc_up_full = tail_up(3, enc_norm1[0], gains, enc_up, at(1), 0)
    dec_second.across(enc_inner)
    dec_up.begin(enc_inner)
    enc_pre_slope, enc_adapt, *enc_norm2, enc_low, enc_down_full, enc_adapt_full = tail_down(
        4, enc_norm1[0], enc_inner, gains, bias_in[0], bias_out[0], enc_down, (0, at(4)), (0, 1)
    )
    *dec_norm1, cross_query, dec_q_full = settle(
        5, dec_in, tie(self_mix, enc_low), gains, dec_second, at(0), at(2), (None, 2)
    )
    dec_down.begin(cross_query)
    cross_key, cross_value, cross_key_far, cross_value_far, dec_kv_full = project(
        6, tie(enc_low, cross_query), partner(enc_low), dec_second, (at(3), at(4))
    )
    cross_keys, cross_values = (cross_key, cross_key_far), (cross_value, cross_value_far)
    dec_up.across(cross_key)
    cross_mix, cross_lse = attend(places, cross_query, cross_keys, cross_values, False)
    dec_down.across(cross_mix)
    *dec_norm2, dec_wo_full = settle(
        7, dec_norm1[0], cross_mix, gains, dec_second, at(1), None, (2, 3)
    )
    dec_slope, dec_inner, dec_up_full = tail_up(8, dec_norm2[0], gains, dec_up, at(0), 3)
    dec_pre_slope, dec_adapt, *dec_norm3, dec_low, dec_down_full, dec_adapt_full = tail_down(
        9, dec_norm2[0], dec_inner, gains, bias_in[1], bias_out[1], dec_down, (0, at(4)), (3, 4)
    )

    grad_z2, grad_cross_mix, dec_matrices, grad_dec_first, grad_dec_second = tail_back(
        height,
        dec_cot,
        dec_norm3,
        dec_norm2,
        gains,
        dec_slope,
        dec_pre_slope,
        dec_adapt,
        (dec_up_full, dec_down_full, dec_adapt_full, dec_wo_full),
        (3, 4),
    )
    exchange = lambda array, axis: lax.all_to_all(array, axis, split_axis=0, concat_axis=0, tiled=True)
    total = lambda array: jnp.sum(array.astype(jnp.float32), axis=0)
    dec_matrices = exchange(dec_matrices, "wide")
    cross_back = attend_back(
        places, grad_cross_mix, cross_query, cross_keys, cross_values, cross_mix, cross_lse, False
    )
    far_encoded = back((), (cross_back[2], cross_back[4]), dec_kv_full, (0, 1), BF16)
    near_encoded = partner(far_encoded)
    grad_encoded = back(
        (tie(enc_cot, far_encoded),), (cross_back[1], cross_back[3]), dec_kv_full, (0, 1), F32
    )
    dec_sums = total(tie(dec_matrices, cross_back[0]))
    grad_z1, grad_self_mix = query_back(
        tie(grad_z2, grad_encoded),
        cross_back[0],
        dec_norm1,
        gains,
        dec_q_full,
        2,
    )
    grad_ez1, grad_enc_mix, enc_matrices, grad_enc_first, grad_enc_second = tail_back(
        height,
        tie(grad_encoded, grad_z1),
        enc_norm2,
        enc_norm1,
        gains,
        enc_slope,
        enc_pre_slope,
        enc_adapt,
        (enc_up_full, enc_down_full, enc_adapt_full, enc_wo_full),
        (0, 1),
        (near_encoded,),
    )
    enc_matrices = exchange(enc_matrices, "wide")

    devices = lax.axis_size("wide") * lax.axis_size("narrow")
    slices = lambda first, second: jnp.concatenate([first, second]).reshape(2, devices, -1).transpose(1, 0, 2)
    firsts = slices(grad_enc_first, grad_dec_first)
    seconds = slices(grad_enc_second, grad_dec_second)
    biases = jnp.concatenate([firsts.reshape(devices, -1), seconds.reshape(devices, -1)], axis=1)
    used = biases.shape[1]
    biases = jnp.pad(biases, ((0, 0), (0, -used % STAT)))
    biases = jnp.sum(exchange(biases, ("wide", "narrow")), axis=0)[:used]
    grad_bias_in = biases[: firsts[0].size].reshape(firsts.shape[1:])
    grad_bias_out = biases[firsts[0].size :].reshape(seconds.shape[1:])

    self_back = attend_back(
        places, tie(grad_self_mix, grad_ez1), self_query, self_keys, self_values, self_mix, self_lse, True
    )

    repeat = lax.axis_size("narrow") // 4
    spread = lambda array: jnp.repeat(array, repeat, axis=0) if repeat > 1 else array
    to_matrix = lambda array: lax.all_to_all(
        spread(array), "narrow", split_axis=0, concat_axis=1, tiled=True
    )[0]
    to_rows = lambda array: lax.all_to_all(
        array[None], "narrow", split_axis=1, concat_axis=0, tiled=True
    )[::repeat]
    old_momentum = to_matrix(tie(adapter_momenta, cross_back[0]))
    sums = jnp.concatenate([total(tie(enc_matrices, self_back[0])), dec_sums])
    sums = spread(bfloat(sums).reshape(4, height, ADAPT))
    enc_back = attend_back(
        places, tie(grad_enc_mix, sums), enc_query, enc_keys, enc_values, enc_mix, enc_lse, False
    )
    summed = exchange(sums, "narrow")
    momentum = DECAY * old_momentum + total(tie(summed, enc_back[0]))
    parts = [momentum] + [swap(momentum, "wide", r) for r in range(1, lax.axis_size("wide"))]
    new_momenta = to_rows(momentum)

    far_dec = back(
        (), (tie(self_back[2], momentum), self_back[4]), dec_qkv_full, (1, 2), BF16
    )
    near_dec = partner(far_dec)
    far_enc = back((), (tie(enc_back[2], far_dec), enc_back[4]), enc_qkv_full, (1, 2), BF16)
    near_enc = partner(far_enc)
    grad_dec = back(
        (tie(grad_z1, far_enc), near_dec),
        (self_back[0], self_back[1], self_back[3]),
        dec_qkv_full,
        (0, 1, 2),
        F32,
    )
    orthogonal = muon([parts[0], tie(parts[1], grad_dec), *parts[2:]])
    grad_enc = back(
        (tie(grad_ez1, orthogonal), near_enc),
        (enc_back[0], enc_back[1], enc_back[3]),
        enc_qkv_full,
        (0, 1, 2),
        F32,
    )
    new_weights = adapter_weights - RATE * math.sqrt(max(1.0, D / ADAPT)) * to_rows(orthogonal)
    return (
        enc_low,
        dec_low,
        grad_enc,
        grad_dec,
        grad_bias_in,
        grad_bias_out,
        new_momenta,
        new_weights,
    )


def solution(mesh):
    both = ("wide", "narrow")
    tokens = P(both, None)
    rows_first, rows_second = P("wide", None), P(None, "wide", None)
    adapters = P(None, both, None)
    in_specs = (
        tokens,
        tokens,
        P(both),
        tokens,
        tokens,
        rows_second,
        rows_first,
        rows_first,
        rows_first,
        P(None, "wide"),
        rows_second,
        rows_second,
        rows_first,
        rows_first,
        P(None, "wide"),
        adapters,
        adapters,
        P(),
        P(),
    )
    out_specs = (
        tokens,
        tokens,
        tokens,
        tokens,
        P(None, both),
        P(None, both),
        adapters,
        adapters,
    )
    return jax.shard_map(shards, mesh=mesh, in_specs=in_specs, out_specs=out_specs, check_vma=False)
```

time: 876 us -> 691 us (0.79)
  Pallas kernels: 141 us -> 437 us
  waiting for transfers between devices: 385 us -> 122 us
  matrix products: 229 us -> 0 us
  starting transfers between devices: 49.8 us -> 78.5 us
  blocking collectives: 17.6 us -> 0 us
  between operations: 16.3 us -> 1.72 us
  local copies, waits for them, and re-layouts: 15.4 us -> 27.5 us
    pallas_call x0 -> x20, Pallas kernels: none -> 297 us  [call(): pl.pallas_call(kernel, in_specs=specs, out_specs=[IN_VMEM if len(out) ==...]
    dot_general x61 -> x0, matrix products: 229 us -> none  [the longest x22 99.4 us: contract(): lax.dot_general(left_side, right_side, (((left_dim,), (right_dim,)), ((),...]
    all_gather x9 -> x0, waiting for transfers between devices: 214 us -> none  [the longest x1 60.2 us: shards(): lax.all_gather(dec_qkv, 'wide', axis=1, tiled=True)]
    ppermute x35 -> x31, waiting for transfers between devices: 165 us -> 49.4 us  [swap(): lax.ppermute(array, axis, [(i, i ^ bit) for i in range(lax.axis_size(axis...]
    ppermute x0 -> x7, waiting for transfers between devices: none -> 48.4 us  [across(): lax.ppermute(tie(chosen, *after) if after else chosen, 'wide', [(i, i ^ (...]
    all_to_all x1, waiting for transfers between devices: 0.01 us -> 24.3 us  [shards(): lax.all_to_all(spread(array), 'narrow', split_axis=0, concat_axis=1, tile...]
    all_gather x2 -> x0, blocking collectives: 17.6 us -> none  [the longest x1 8.92 us: shards(): lax.all_gather(dec_gains, 'wide', axis=1, tiled=True)]
    all_to_all x0 -> x4, starting transfers between devices: none -> 17.3 us  [shards(): lax.all_to_all(array, axis, split_axis=0, concat_axis=0, tiled=True)]
  transfers between devices with their start and end apart: 47 -> 45, of which waited for: 21 -> 11; matrix products, arithmetic and copies ran while one was open for 25% -> 5% of each run, Pallas kernels for 13% -> 50%
where the time goes in v2:
time: 691 us; the launch traced here: 687 us
  Pallas kernels  437 us (63%)
  waiting for transfers between devices  122 us (18%)
  starting transfers between devices  78.5 us (11%)
  local copies, waits for them, and re-layouts  27.5 us (4%)
  other arithmetic  20.5 us (3%)
    pallas_call x20, Pallas kernels, call(): pl.pallas_call(kernel, in_specs=specs, out_specs=[IN_VMEM if len(out) ==...  297 us
    pallas_call x3, Pallas kernels, attend_back(): pl.pallas_call(functools.partial(attend_back_kernel, causal, 256), grid=(...  85.1 us
    pallas_call x3, Pallas kernels, attend(): pl.pallas_call(functools.partial(attend_kernel, causal, 256), grid=(pairs...  54.5 us
    ppermute x31, waiting for transfers between devices, swap(): lax.ppermute(array, axis, [(i, i ^ bit) for i in range(lax.axis_size(axis...  49.4 us
    ppermute x7, waiting for transfers between devices, across(): lax.ppermute(tie(chosen, *after) if after else chosen, 'wide', [(i, i ^ (...  48.4 us
    ppermute x31, starting transfers between devices, swap(): lax.ppermute(array, axis, [(i, i ^ bit) for i in range(lax.axis_size(axis...  40.6 us
    all_to_all x1, waiting for transfers between devices, shards(): lax.all_to_all(spread(array), 'narrow', split_axis=0, concat_axis=1, tile...  24.3 us
    all_to_all x4, starting transfers between devices, shards(): lax.all_to_all(array, axis, split_axis=0, concat_axis=0, tiled=True)  17.3 us
  transfers between devices with their start and end apart: 45, of which 11 were waited for; matrix products, arithmetic and copies ran while one was open for 5% of the time, Pallas kernels for 50%

profile of v2, /device:TPU:0, one launch (start us, length us, event | category | flops | bytes accessed | tf_op | source)
XLA Modules:
  0.0 687.1 jit_solution(13668482892284326963)
XLA Ops:
  24.7 17.4 %collective-permute-done.14 = bf16[2,4,32,512]{3,2,1,0:T(8,128)(2,1)} collective-permute-done((bf16[2,4,32,512]{3,2,1,0:T(8,128)(2,1)}, bf16[2,4,32,512]{3,2,1,0:T(8,128)(2,1)}, u32[]{:S(2)}, u32[]{:S(2)}) %collective-permute-start.14) | collective-permute-done | bytes 262176 | tf_op jit(solution)/shard_map/ppermute | solution.py:30
  48.5 12.3 %collective-permute-done.7.refs_2_ = bf16[384,1024]{1,0:T(8,128)(2,1)S(1)} collective-permute-done((bf16[384,1024]{1,0:T(8,128)(2,1)}, bf16[384,1024]{1,0:T(8,128)(2,1)S(1)}, u32[]{:S(2)}, u32[]{:S(2)}) %collective-permute-start.7) | collective-permute-done | bytes 786464 | tf_op jit(solution)/shard_map/ppermute | solution.py:30
  71.2 15.2 %shard_map.242 = (bf16[512,1024]{1,0:T(8,128)(2,1)}, bf16[512,1024]{1,0:T(8,128)(2,1)}, bf16[512,1024]{1,0:T(8,128)(2,1)}, bf16[512,1024]{1,0:T(8,128)(2,1)}, bf...) custom-call(bf16[512,1024]{1,0:T(8,128)(2,1)} %x_ref.5, bf16[512,1024]{1,0:T(8,128)(2,1)} %collective-permute-done.1.far_ref, ...), custom_call_target="tpu_custom_call" | custom-call | flops 5368709120 | bytes 5373952 | tf_op jit(solution)/shard_map/pallas_call | solution.py:695
  86.4 18.2 %shard_map.243 = (bf16[512,1024]{1,0:T(8,128)(2,1)}, f32[8,8,512]{2,1,0:T(8,128)}) custom-call(s32[1]{0:T(128)} %bitcast.half_ref, s32[1,512]{1,0:T(1,128)} %bitcast.77, s32[512,1]{1,0:T(8,128)} %copy.60.kid_own_ref, s32[512,1]{1,0:T(8,128)} %copy.61.kid_far_ref, bf16[512,1024]{1,0:T(8,128)(2,1)} %get-tuple-element.118.q_ref, ...), custom_call_target="tpu_custom_call" | custom-call | flops 8589934592 | bytes 6291456 | tf_op jit(solution)/shard_map/pallas_call | solution.py:220
  110.7 33.6 %collective-permute-done.8.refs_3_ = bf16[384,1024]{1,0:T(8,128)(2,1)} collective-permute-done((bf16[384,1024]{1,0:T(8,128)(2,1)S(1)}, bf16[384,1024]{1,0:T(8,128)(2,1)}, u32[]{:S(2)}, u32[]{:S(2)}) %collective-permute-start.8) | collective-permute-done | bytes 786464 | tf_op jit(solution)/shard_map/ppermute | solution.py:914
  144.3 14.9 %shard_map.244 = (bf16[512,1024]{1,0:T(8,128)(2,1)}, bf16[512,1024]{1,0:T(8,128)(2,1)}, bf16[512,1024]{1,0:T(8,128)(2,1)}, bf16[512,1024]{1,0:T(8,128)(2,1)}, bf...) custom-call(bf16[512,1024]{1,0:T(8,128)(2,1)} %x_ref.6, bf16[512,1024]{1,0:T(8,128)(2,1)} %collective-permute-done.5.far_ref, ...), custom_call_target="tpu_custom_call" | custom-call | flops 5368709120 | bytes 5242880 | tf_op jit(solution)/shard_map/pallas_call | solution.py:695
  166.4 18.2 %shard_map.245 = (bf16[512,1024]{1,0:T(8,128)(2,1)}, f32[8,8,512]{2,1,0:T(8,128)}) custom-call(s32[1]{0:T(128)} %bitcast.half_ref, s32[1,512]{1,0:T(1,128)} %bitcast.78, s32[512,1]{1,0:T(8,128)} %copy.60.kid_own_ref, s32[512,1]{1,0:T(8,128)} %copy.61.kid_far_ref, bf16[512,1024]{1,0:T(8,128)(2,1)} %get-tuple-element.127.q_ref, ...), custom_call_target="tpu_custom_call" | custom-call | flops 8589934592 | bytes 6291456 | tf_op jit(solution)/shard_map/pallas_call | solution.py:220
  193.5 11.1 %collective-permute-done.12.refs_3_ = bf16[640,1024]{1,0:T(8,128)(2,1)S(1)} collective-permute-done((bf16[640,1024]{1,0:T(8,128)(2,1)}, bf16[640,1024]{1,0:T(8,128)(2,1)S(1)}, u32[]{:S(2)}, u32[]{:S(2)}) %collective-permute-start.12) | collective-permute-done | bytes 1310752 | tf_op jit(solution)/shard_map/ppermute | solution.py:914
  205.7 9.7 %shard_map.246 = (f32[512,1024]{1,0:T(8,128)}, f32[512,128]{1,0:T(8,128)}, bf16[1,1024,1024]{2,1,0:T(8,128)(2,1)}) custom-call(bf16[512,1024]{1,0:T(8,128)(2,1)} %x_ref.5, bf16[512,1024]{1,0:T(8,128)(2,1)} %get-tuple-element.133.mix_ref.out_ref, f32[8,1024]{1,0:T(8,128)} %convert_bitcast_fusion.1.gains_ref.refs_5_, ...), custom_call_target="tpu_custom_call" | custom-call | flops 1073741824 | bytes 7372800 | tf_op jit(solution)/shard_map/pallas_call | solution.py:695
  215.4 15.5 %shard_map.247 = (bf16[512,4096]{1,0:T(8,128)(2,1)}, bf16[512,4096]{1,0:T(8,128)(2,1)}, bf16[4,1024,1024]{2,1,0:T(8,128)(2,1)}) custom-call(f32[512,1024]{1,0:T(8,128)} %get-tuple-element.136.n_ref.refs_3_, f32[8,1024]{1,0:T(8,128)} %convert_bitcast_fusion.1.gains_ref.refs_5_, bf16[640,1024]{1,0:T(8,128)(2,1)} %slice_dynamic-update-slice_fusion.refs_0_, ...), custom_call_target="tpu_custom_call" | custom-call | flops 4294967296 | bytes 7372800 | tf_op jit(solution)/shard_map/pallas_call | solution.py:695
  235.0 21.1 %shard_map.248 = (bf16[512,512]{1,0:T(8,128)(2,1)}, bf16[512,512]{1,0:T(8,128)(2,1)}, f32[512,1024]{1,0:T(8,128)}, f32[512,128]{1,0:T(8,128)}, bf16[512,1024]{1,...) custom-call(f32[512,1024]{1,0:T(8,128)} %get-tuple-element.136.n_ref.refs_3_, ...), custom_call_target="tpu_custom_call" | custom-call | flops 5368709120 | bytes 11573248 | tf_op jit(solution)/shard_map/pallas_call | solution.py:695
  262.6 11.8 %shard_map.249 = (f32[512,1024]{1,0:T(8,128)}, f32[512,128]{1,0:T(8,128)}, bf16[512,1024]{1,0:T(8,128)(2,1)}, bf16[2,1024,1024]{2,1,0:T(8,128)(2,1)}) custom-call(bf16[512,1024]{1,0:T(8,128)(2,1)} %x_ref.6, bf16[512,1024]{1,0:T(8,128)(2,1)} %get-tuple-element.141.mix_ref.out_ref, f32[8,1024]{1,0:T(8,128)} %convert_bitcast_fusion.1.gains_ref.refs_5_, ...), custom_call_target="tpu_custom_call" | custom-call | flops 2147483648 | bytes 7372800 | tf_op jit(solution)/shard_map/pallas_call | solution.py:695
  277.8 6.3 collective-permute-done.21.far_ref
  284.1 12.4 %shard_map.250 = (bf16[512,1024]{1,0:T(8,128)(2,1)}, bf16[512,1024]{1,0:T(8,128)(2,1)}, bf16[512,1024]{1,0:T(8,128)(2,1)}, bf16[512,1024]{1,0:T(8,128)(2,1)}, bf16[2,1024,1024]{2,1,0:T(8,128)(2,1)}) custom-call(bf16[512,1024]{1,0:T(8,128)(2,1)} %get-tuple-element.252.x_ref, bf16[512,1024]{1,0:T(8,128)(2,1)} %collective-permute-done.21.far_ref, ...), custom_call_target="tpu_custom_call" | custom-call | flops 4294967296 | bytes 7340032 | tf_op jit(solution)/shard_map/pallas_call | solution.py:695
  298.0 18.2 %shard_map.251 = (bf16[512,1024]{1,0:T(8,128)(2,1)}, f32[8,8,512]{2,1,0:T(8,128)}) custom-call(s32[1]{0:T(128)} %bitcast.half_ref, s32[1,512]{1,0:T(1,128)} %bitcast.79, s32[512,1]{1,0:T(8,128)} %copy.60.kid_own_ref, s32[512,1]{1,0:T(8,128)} %copy.61.kid_far_ref, bf16[512,1024]{1,0:T(8,128)(2,1)} %get-tuple-element.145.q_ref, ...), custom_call_target="tpu_custom_call" | custom-call | flops 8589934592 | bytes 6291456 | tf_op jit(solution)/shard_map/pallas_call | solution.py:220
  318.3 9.8 %shard_map.252 = (f32[512,1024]{1,0:T(8,128)}, f32[512,128]{1,0:T(8,128)}, bf16[1,1024,1024]{2,1,0:T(8,128)(2,1)}) custom-call(f32[512,1024]{1,0:T(8,128)} %get-tuple-element.144.x_ref.n_ref, bf16[512,1024]{1,0:T(8,128)(2,1)} %get-tuple-element.151.mix_ref.out_ref, f32[8,1024]{1,0:T(8,128)} %convert_bitcast_fusion.1.gains_ref.refs_5_, ...), custom_call_target="tpu_custom_call" | custom-call | flops 1073741824 | bytes 8421376 | tf_op jit(solution)/shard_map/pallas_call | solution.py:695
  329.1 15.7 %shard_map.253 = (bf16[512,4096]{1,0:T(8,128)(2,1)}, bf16[512,4096]{1,0:T(8,128)(2,1)}, bf16[4,1024,1024]{2,1,0:T(8,128)(2,1)}) custom-call(f32[512,1024]{1,0:T(8,128)} %get-tuple-element.152.n_ref.refs_3_, f32[8,1024]{1,0:T(8,128)} %convert_bitcast_fusion.1.gains_ref.refs_5_, bf16[512,1024]{1,0:T(8,128)(2,1)} %copy-done.21, ...), custom_call_target="tpu_custom_call" | custom-call | flops 4294967296 | bytes 6324224 | tf_op jit(solution)/shard_map/pallas_call | solution.py:695
  345.9 21.0 %shard_map.254 = (bf16[512,512]{1,0:T(8,128)(2,1)}, bf16[512,512]{1,0:T(8,128)(2,1)}, f32[512,1024]{1,0:T(8,128)}, f32[512,128]{1,0:T(8,128)}, bf16[512,1024]{1,...) custom-call(f32[512,1024]{1,0:T(8,128)} %get-tuple-element.152.n_ref.refs_3_, ...), custom_call_target="tpu_custom_call" | custom-call | flops 5368709120 | bytes 11573248 | tf_op jit(solution)/shard_map/pallas_call | solution.py:695
  366.9 27.1 %shard_map.255 = (f32[512,1024]{1,0:T(8,128)}, bf16[512,1024]{1,0:T(8,128)(2,1)}, bf16[8,256,512]{2,1,0:T(8,128)(2,1)}, f32[1,512]{1,0:T(1,128)}, f32[1,1024]{1,0:T(1,128)}) custom-call(bf16[512,1024]{1,0:T(8,128)(2,1)} %refs_0_.1, f32[512,1024]{1,0:T(8,128)} %get-tuple-element.159.refs_1_, f32[512,128]{1,0:T(8,128)} %get-tuple-element.160.refs_2_, ...), custom_call_target="tpu_custom_call" | custom-call | flops 12884901888 | bytes 32014336 | tf_op jit(solution)/shard_map/pallas_call | solution.py:695
  394.0 28.7 %shard_map.256 = (bf16[512,1024]{1,0:T(8,128)(2,1)}, bf16[512,1024]{1,0:T(8,128)(2,1)}, bf16[512,1024]{1,0:T(8,128)(2,1)}, bf16[512,1024]{1,0:T(8,128)(2,1)}, bf16[512,1024]{1,0:T(8,128)(2,1)}) custom-call(s32[1]{0:T(128)} %bitcast.half_ref, s32[1,512]{1,0:T(1,128)} %bitcast.80, s32[512,1]{1,0:T(8,128)} %copy.60.kid_own_ref, s32[512,1]{1,0:T(8,128)} %copy.61.kid_far_ref, ...), custom_call_target="tpu_custom_call" | custom-call | flops 21474836480 | bytes 12582912 | tf_op jit(solution)/shard_map/pallas_call | solution.py:244
  422.7 7.8 %shard_map.257 = bf16[512,1024]{1,0:T(8,128)(2,1)} custom-call(bf16[512,1024]{1,0:T(8,128)(2,1)} %get-tuple-element.171.refs_0_, bf16[512,1024]{1,0:T(8,128)(2,1)} %get-tuple-element.172.refs_1_, bf16[2,1024,1024]{2,1,0:T(8,128)(2,1)} %get-tuple-element.173.refs_2_.refs_3_), custom_call_target="tpu_custom_call" | custom-call | flops 2147483648 | bytes 6291456 | tf_op jit(solution)/shard_map/pallas_call | solution.py:695
  435.7 24.3 %all-to-all-done = f32[4,32,512]{2,1,0:T(8,128)S(1)} async-done(((f32[4,32,512]{2,1,0:T(8,128)}), f32[4,32,512]{2,1,0:T(8,128)S(1)}, u32[]{:S(2)}, u32[]{:S(2)}) %all-to-all-start) | async-done | bytes 262176 | tf_op jit(solution)/shard_map/all_to_all | solution.py:1101
  463.6 8.4 %shard_map.258.refs_0_ = f32[512,1024]{1,0:T(8,128)} custom-call(bf16[512,1024]{1,0:T(8,128)(2,1)} %refs_0_.2, bf16[512,1024]{1,0:T(8,128)(2,1)} %get-tuple-element.175.refs_1_, bf16[512,1024]{1,0:T(8,128)(2,1)} %get-tuple-element.176.refs_2_, bf16[2,1024,1024]{2,1,0:T(8,128)(2,1)} %get-tuple-element.173.refs_2_.refs_3_), custom_call_target="tpu_custom_call" | custom-call | flops 2147483648 | bytes 7340032 | tf_op jit(solution)/shard_map/pallas_call | solution.py:695
  472.0 10.5 %shard_map.259 = (f32[512,1024]{1,0:T(8,128)}, bf16[512,1024]{1,0:T(8,128)(2,1)}) custom-call(f32[512,1024]{1,0:T(8,128)} %get-tuple-element.178.dz_ref, bf16[512,1024]{1,0:T(8,128)(2,1)} %get-tuple-element.179.dq_ref, f32[512,1024]{1,0:T(8,128)} %get-tuple-element.144.x_ref.n_ref, f32[512,128]{1,0:T(8,128)} %get-tuple-element.180.r_ref, ...), custom_call_target="tpu_custom_call" | custom-call | flops 2147483648 | bytes 9732096 | tf_op jit(solution)/shard_map/pallas_call | solution.py:695
  482.6 27.7 %shard_map.260 = (f32[512,1024]{1,0:T(8,128)}, bf16[512,1024]{1,0:T(8,128)(2,1)}, bf16[8,256,512]{2,1,0:T(8,128)(2,1)}, f32[1,512]{1,0:T(1,128)}, f32[1,1024]{1,0:T(1,128)}) custom-call(f32[512,1024]{1,0:T(8,128)} %shard_map.258.refs_0_, f32[512,1024]{1,0:T(8,128)} %get-tuple-element.184.refs_1_, f32[512,128]{1,0:T(8,128)} %get-tuple-element.185.refs_2_, ...), custom_call_target="tpu_custom_call" | custom-call | flops 12884901888 | bytes 34111488 | tf_op jit(solution)/shard_map/pallas_call | solution.py:695
  514.8 28.3 %shard_map.261 = (bf16[512,1024]{1,0:T(8,128)(2,1)}, bf16[512,1024]{1,0:T(8,128)(2,1)}, bf16[512,1024]{1,0:T(8,128)(2,1)}, bf16[512,1024]{1,0:T(8,128)(2,1)}, bf16[512,1024]{1,0:T(8,128)(2,1)}) custom-call(s32[1]{0:T(128)} %bitcast.half_ref, s32[1,512]{1,0:T(1,128)} %bitcast.81, s32[512,1]{1,0:T(8,128)} %copy.60.kid_own_ref, s32[512,1]{1,0:T(8,128)} %copy.61.kid_far_ref, ...), custom_call_target="tpu_custom_call" | custom-call | flops 21474836480 | bytes 12582912 | tf_op jit(solution)/shard_map/pallas_call | solution.py:244
  550.4 28.2 %shard_map.262 = (bf16[512,1024]{1,0:T(8,128)(2,1)}, bf16[512,1024]{1,0:T(8,128)(2,1)}, bf16[512,1024]{1,0:T(8,128)(2,1)}, bf16[512,1024]{1,0:T(8,128)(2,1)}, bf16[512,1024]{1,0:T(8,128)(2,1)}) custom-call(s32[1]{0:T(128)} %bitcast.half_ref, s32[1,512]{1,0:T(1,128)} %bitcast.82, s32[512,1]{1,0:T(8,128)} %copy.60.kid_own_ref, s32[512,1]{1,0:T(8,128)} %copy.61.kid_far_ref, ...), custom_call_target="tpu_custom_call" | custom-call | flops 21474836480 | bytes 12582912 | tf_op jit(solution)/shard_map/pallas_call | solution.py:244
  578.8 7.8 %shard_map.263 = bf16[512,1024]{1,0:T(8,128)(2,1)} custom-call(bf16[512,1024]{1,0:T(8,128)(2,1)} %get-tuple-element.211.refs_0_, bf16[512,1024]{1,0:T(8,128)(2,1)} %get-tuple-element.212.refs_1_, bf16[3,1024,1024]{2,1,0:T(8,128)(2,1)} %get-tuple-element.213.refs_2_.refs_5_), custom_call_target="tpu_custom_call" | custom-call | flops 2147483648 | bytes 8388608 | tf_op jit(solution)/shard_map/pallas_call | solution.py:695
  600.6 7.7 %shard_map.264 = bf16[512,1024]{1,0:T(8,128)(2,1)} custom-call(bf16[512,1024]{1,0:T(8,128)(2,1)} %get-tuple-element.214.refs_0_, bf16[512,1024]{1,0:T(8,128)(2,1)} %get-tuple-element.215.refs_1_, bf16[3,1024,1024]{2,1,0:T(8,128)(2,1)} %get-tuple-element.216.refs_2_.refs_5_), custom_call_target="tpu_custom_call" | custom-call | flops 2147483648 | bytes 8388608 | tf_op jit(solution)/shard_map/pallas_call | solution.py:695
  613.9 11.2 %shard_map.265 = f32[512,1024]{1,0:T(8,128)} custom-call(f32[512,1024]{1,0:T(8,128)} %get-tuple-element.217.refs_0_, bf16[512,1024]{1,0:T(8,128)(2,1)} %copy-done.10, bf16[512,1024]{1,0:T(8,128)(2,1)} %get-tuple-element.200.refs_2_, bf16[512,1024]{1,0:T(8,128)(2,1)} %get-tuple-element.218.refs_3_, bf16[512,1024]{1,0:T(8,128)(2,1)} %get-tuple-element.219.refs_4_, ...), custom_call_target="tpu_custom_call" | custom-call | flops 3221225472 | bytes 12582912 | tf_op jit(solution)/shard_map/pallas_call | solution.py:695
  631.6 30.8 %shard_map.266 = f32[128,512]{1,0:T(8,128)} custom-call(f32[128,512]{1,0:T(8,128)} %copy-done.32, f32[128,512]{1,0:T(8,128)} %copy-done.47, f32[128,512]{1,0:T(8,128)} %collective-permute-done.31.refs_2_, f32[128,512]{1,0:T(8,128)} %collective-permute-done.32.refs_3_, f32[128,512]{1,0:T(8,128)} %collective-permute-done.33.refs_4_, f32[128,512]{1,0:T(8,128)} %copy-done.46, ...), custom_call_target="tpu_custom_call" | custom-call | flops 16106127360 | bytes 2097152 | tf_op jit(solution)/shard_map/pallas_call | solution.py:695
  672.6 11.1 %shard_map.267 = f32[512,1024]{1,0:T(8,128)} custom-call(f32[512,1024]{1,0:T(8,128)} %get-tuple-element.221.refs_0_, bf16[512,1024]{1,0:T(8,128)(2,1)} %copy-done.11, bf16[512,1024]{1,0:T(8,128)(2,1)} %get-tuple-element.207.refs_2_, bf16[512,1024]{1,0:T(8,128)(2,1)} %get-tuple-element.222.refs_3_, bf16[512,1024]{1,0:T(8,128)(2,1)} %get-tuple-element.223.refs_4_, ...), custom_call_target="tpu_custom_call" | custom-call | flops 3221225472 | bytes 12582912 | tf_op jit(solution)/shard_map/pallas_call | solution.py:695
  (252 shorter events, 143.5 us)
Async XLA Ops:
  3.6 41.0 %collective-permute-start.3 = (bf16[400,1024]{1,0:T(8,128)(2,1)}, bf16[400,1024]{1,0:T(8,128)(2,1)S(1)}, u32[]{:S(2)}, u32[]{:S(2)}) collective-permute-start(bf16[400,1024]{1,0:T(8,128)(2,1)} %pad_maximum_fusion.2.refs_0_), channel_id=1, source_target_pairs={{0,16},{4,20},{8,24},{12,28},{16,0},{20,4},{24,8},{28,12},{1,17},{... | collective-permute-start | bytes 2457608 | tf_op jit(solution)/shard_map/ppermute | solution.py:30
  6.5 38.0 %collective-permute-start.2 = (bf16[400,1024]{1,0:T(8,128)(2,1)}, bf16[400,1024]{1,0:T(8,128)(2,1)S(1)}, u32[]{:S(2)}, u32[]{:S(2)}) collective-permute-start(bf16[400,1024]{1,0:T(8,128)(2,1)} %pad_maximum_fusion.2.refs_0_), channel_id=1, source_target_pairs={{0,8},{4,12},{8,0},{12,4},{16,24},{20,28},{24,16},{28,20},{1,9},{5... | collective-permute-start | bytes 2457608 | tf_op jit(solution)/shard_map/ppermute | solution.py:30
  10.1 61.1 %collective-permute-start.1 = (bf16[512,1024]{1,0:T(8,128)(2,1)}, bf16[512,1024]{1,0:T(8,128)(2,1)}, u32[]{:S(2)}, u32[]{:S(2)}) collective-permute-start(bf16[512,1024]{1,0:T(8,128)(2,1)} %x_ref.5), channel_id=1, source_target_pairs={{0,1},{1,0},{2,3},{3,2},{4,5},{5,4},{6,7},{7,6},{8,9},{9,8},{10,11... | collective-permute-start | bytes 3145736 | tf_op jit(solution)/shard_map/ppermute | solution.py:30
  23.4 82.2 %collective-permute-start.5 = (bf16[512,1024]{1,0:T(8,128)(2,1)}, bf16[512,1024]{1,0:T(8,128)(2,1)}, u32[]{:S(2)}, u32[]{:S(2)}) collective-permute-start(bf16[512,1024]{1,0:T(8,128)(2,1)} %x_ref.6), channel_id=1, source_target_pairs={{0,1},{1,0},{2,3},{3,2},{4,5},{5,4},{6,7},{7,6},{8,9},{9,8},{10,11... | collective-permute-start | bytes 3145736 | tf_op jit(solution)/shard_map/ppermute | solution.py:30
  69.6 90.8 %collective-permute-start.11 = (bf16[640,1024]{1,0:T(8,128)(2,1)}, bf16[640,1024]{1,0:T(8,128)(2,1)S(1)}, u32[]{:S(2)}, u32[]{:S(2)}) collective-permute-start(bf16[640,1024]{1,0:T(8,128)(2,1)} %slice_dynamic-update-slice_fusion.refs_0_), channel_id=1, source_target_pairs={{0,16},{4,20},{8,24},{12,28},{16,0},{20,4},{24,8},{28,12},{1,17},{... | collective-permute-start | bytes 3932168 | tf_op jit(solution)/shard_map/ppermute | solution.py:30
  70.1 91.8 %collective-permute-start.10 = (bf16[640,1024]{1,0:T(8,128)(2,1)}, bf16[640,1024]{1,0:T(8,128)(2,1)S(1)}, u32[]{:S(2)}, u32[]{:S(2)}) collective-permute-start(bf16[640,1024]{1,0:T(8,128)(2,1)} %slice_dynamic-update-slice_fusion.refs_0_), channel_id=1, source_target_pairs={{0,8},{4,12},{8,0},{12,4},{16,24},{20,28},{24,16},{28,20},{1,9},{5... | collective-permute-start | bytes 3932168 | tf_op jit(solution)/shard_map/ppermute | solution.py:30
  71.0 36.2 %collective-permute-start.9 = (bf16[4,8,128]{2,1,0:T(8,128)(2,1)S(1)}, bf16[4,8,128]{2,1,0:T(8,128)(2,1)S(1)}, u32[]{:S(2)}, u32[]{:S(2)}) collective-permute-start(bf16[4,8,128]{2,1,0:T(8,128)(2,1)S(1)} %pad_maximum_fusion.6), channel_id=1, source_target_pairs={{0,4},{4,0},{8,12},{12,8},{16,20},{20,16},{24,28},{28,24},{1,5},{5... | collective-permute-start | bytes 24584 | tf_op jit(solution)/shard_map/ppermute | solution.py:30
  104.6 57.3 %collective-permute-start.16 = (bf16[640,1024]{1,0:T(8,128)(2,1)}, bf16[640,1024]{1,0:T(8,128)(2,1)}, u32[]{:S(2)}, u32[]{:S(2)}) collective-permute-start(bf16[640,1024]{1,0:T(8,128)(2,1)} %maximum_maximum_fusion.refs_0_), channel_id=1, source_target_pairs={{0,16},{4,20},{8,24},{12,28},{16,0},{20,4},{24,8},{28,12},{1,17},{... | collective-permute-start | bytes 3932168 | tf_op jit(solution)/shard_map/ppermute | solution.py:30
  105.6 56.2 %collective-permute-start.15 = (bf16[640,1024]{1,0:T(8,128)(2,1)}, bf16[640,1024]{1,0:T(8,128)(2,1)}, u32[]{:S(2)}, u32[]{:S(2)}) collective-permute-start(bf16[640,1024]{1,0:T(8,128)(2,1)} %maximum_maximum_fusion.refs_0_), channel_id=1, source_target_pairs={{0,8},{4,12},{8,0},{12,4},{16,24},{20,28},{24,16},{28,20},{1,9},{5... | collective-permute-start | bytes 3932168 | tf_op jit(solution)/shard_map/ppermute | solution.py:30
  107.1 37.2 %collective-permute-start.8 = (bf16[384,1024]{1,0:T(8,128)(2,1)S(1)}, bf16[384,1024]{1,0:T(8,128)(2,1)}, u32[]{:S(2)}, u32[]{:S(2)}) collective-permute-start(bf16[384,1024]{1,0:T(8,128)(2,1)S(1)} %broadcast_select_fusion.6), channel_id=1, source_target_pairs={{0,16},{4,12},{8,24},{12,4},{16,0},{20,28},{24,8},{28,20},{1,17},{... | collective-permute-start | bytes 2359304 | tf_op jit(solution)/shard_map/ppermute | solution.py:914
  159.3 31.2 %collective-permute-start.19 = (bf16[640,1024]{1,0:T(8,128)(2,1)S(1)}, bf16[640,1024]{1,0:T(8,128)(2,1)S(1)}, u32[]{:S(2)}, u32[]{:S(2)}) collective-permute-start(bf16[640,1024]{1,0:T(8,128)(2,1)S(1)} %copy-done.2), channel_id=1, source_target_pairs={{0,16},{4,20},{8,24},{12,28},{16,0},{20,4},{24,8},{28,12},{1,17},{... | collective-permute-start | bytes 3932168 | tf_op jit(solution)/shard_map/ppermute | solution.py:30
  160.3 31.7 %collective-permute-start.18 = (bf16[640,1024]{1,0:T(8,128)(2,1)S(1)}, bf16[640,1024]{1,0:T(8,128)(2,1)}, u32[]{:S(2)}, u32[]{:S(2)}) collective-permute-start(bf16[640,1024]{1,0:T(8,128)(2,1)S(1)} %copy-done.2), channel_id=1, source_target_pairs={{0,8},{4,12},{8,0},{12,4},{16,24},{20,28},{24,16},{28,20},{1,9},{5... | collective-permute-start | bytes 3932168 | tf_op jit(solution)/shard_map/ppermute | solution.py:30
  165.4 39.2 %collective-permute-start.12 = (bf16[640,1024]{1,0:T(8,128)(2,1)}, bf16[640,1024]{1,0:T(8,128)(2,1)S(1)}, u32[]{:S(2)}, u32[]{:S(2)}) collective-permute-start(bf16[640,1024]{1,0:T(8,128)(2,1)} %get-tuple-element.135), channel_id=1, source_target_pairs={{0,16},{4,12},{8,24},{12,4},{16,0},{20,28},{24,8},{28,20},{1,17},{... | collective-permute-start | bytes 3932168 | tf_op jit(solution)/shard_map/ppermute | solution.py:914
  184.6 50.4 %collective-permute-start.17 = (bf16[640,1024]{1,0:T(8,128)(2,1)}, bf16[640,1024]{1,0:T(8,128)(2,1)}, u32[]{:S(2)}, u32[]{:S(2)}) collective-permute-start(bf16[640,1024]{1,0:T(8,128)(2,1)} %get-tuple-element.139), channel_id=1, source_target_pairs={{0,16},{4,12},{8,24},{12,4},{16,0},{20,28},{24,8},{28,20},{1,17},{... | collective-permute-start | bytes 3932168 | tf_op jit(solution)/shard_map/ppermute | solution.py:914
  230.9 30.5 %collective-permute-start.20 = (bf16[640,1024]{1,0:T(8,128)(2,1)S(1)}, bf16[640,1024]{1,0:T(8,128)(2,1)S(1)}, u32[]{:S(2)}, u32[]{:S(2)}) collective-permute-start(bf16[640,1024]{1,0:T(8,128)(2,1)S(1)} %broadcast_select_fusion.1), channel_id=1, source_target_pairs={{0,16},{4,12},{8,24},{12,4},{16,0},{20,28},{24,8},{28,20},{1,17},{... | collective-permute-start | bytes 3932168 | tf_op jit(solution)/shard_map/ppermute | solution.py:914
  232.9 43.5 %collective-permute-start.23 = (bf16[512,1024]{1,0:T(8,128)(2,1)S(1)}, bf16[512,1024]{1,0:T(8,128)(2,1)}, u32[]{:S(2)}, u32[]{:S(2)}) collective-permute-start(bf16[512,1024]{1,0:T(8,128)(2,1)S(1)} %pad_maximum_fusion.1.refs_0_), channel_id=1, source_target_pairs={{0,16},{4,20},{8,24},{12,28},{16,0},{20,4},{24,8},{28,12},{1,17},{... | collective-permute-start | bytes 3145736 | tf_op jit(solution)/shard_map/ppermute | solution.py:30
  233.8 42.6 %collective-permute-start.22 = (bf16[512,1024]{1,0:T(8,128)(2,1)S(1)}, bf16[512,1024]{1,0:T(8,128)(2,1)}, u32[]{:S(2)}, u32[]{:S(2)}) collective-permute-start(bf16[512,1024]{1,0:T(8,128)(2,1)S(1)} %pad_maximum_fusion.1.refs_0_), channel_id=1, source_target_pairs={{0,8},{4,12},{8,0},{12,4},{16,24},{20,28},{24,16},{28,20},{1,9},{5... | collective-permute-start | bytes 3145736 | tf_op jit(solution)/shard_map/ppermute | solution.py:30
  256.1 28.0 %collective-permute-start.21 = (bf16[512,1024]{1,0:T(8,128)(2,1)}, bf16[512,1024]{1,0:T(8,128)(2,1)}, u32[]{:S(2)}, u32[]{:S(2)}) collective-permute-start(bf16[512,1024]{1,0:T(8,128)(2,1)} %get-tuple-element.252.x_ref), channel_id=1, source_target_pairs={{0,1},{1,0},{2,3},{3,2},{4,5},{5,4},{6,7},{7,6},{8,9},{9,8},{10,11... | collective-permute-start | bytes 3145736 | tf_op jit(solution)/shard_map/ppermute | solution.py:30
  274.4 41.8 %collective-permute-start.26 = (bf16[640,1024]{1,0:T(8,128)(2,1)S(1)}, bf16[640,1024]{1,0:T(8,128)(2,1)S(1)}, u32[]{:S(2)}, u32[]{:S(2)}) collective-permute-start(bf16[640,1024]{1,0:T(8,128)(2,1)S(1)} %maximum_maximum_fusion.1.refs_0_), channel_id=1, source_target_pairs={{0,16},{4,20},{8,24},{12,28},{16,0},{20,4},{24,8},{28,12},{1,17},{... | collective-permute-start | bytes 3932168 | tf_op jit(solution)/shard_map/ppermute | solution.py:30
  275.9 40.3 %collective-permute-start.25 = (bf16[640,1024]{1,0:T(8,128)(2,1)S(1)}, bf16[640,1024]{1,0:T(8,128)(2,1)S(1)}, u32[]{:S(2)}, u32[]{:S(2)}) collective-permute-start(bf16[640,1024]{1,0:T(8,128)(2,1)S(1)} %maximum_maximum_fusion.1.refs_0_), channel_id=1, source_target_pairs={{0,8},{4,12},{8,0},{12,4},{16,24},{20,28},{24,16},{28,20},{1,9},{5... | collective-permute-start | bytes 3932168 | tf_op jit(solution)/shard_map/ppermute | solution.py:30
  296.5 31.6 %collective-permute-start.24 = (bf16[512,1024]{1,0:T(8,128)(2,1)S(1)}, bf16[512,1024]{1,0:T(8,128)(2,1)S(1)}, u32[]{:S(2)}, u32[]{:S(2)}) collective-permute-start(bf16[512,1024]{1,0:T(8,128)(2,1)S(1)} %broadcast_select_fusion.4), channel_id=1, source_target_pairs={{0,16},{4,12},{8,24},{12,4},{16,0},{20,28},{24,8},{28,20},{1,17},{... | collective-permute-start | bytes 3145736 | tf_op jit(solution)/shard_map/ppermute | solution.py:914
  317.7 27.1 %collective-permute-start.27 = (bf16[640,1024]{1,0:T(8,128)(2,1)S(1)}, bf16[640,1024]{1,0:T(8,128)(2,1)S(1)}, u32[]{:S(2)}, u32[]{:S(2)}) collective-permute-start(bf16[640,1024]{1,0:T(8,128)(2,1)S(1)} %broadcast_select_fusion), channel_id=1, source_target_pairs={{0,16},{4,12},{8,24},{12,4},{16,0},{20,28},{24,8},{28,20},{1,17},{... | collective-permute-start | bytes 3932168 | tf_op jit(solution)/shard_map/ppermute | solution.py:914
  430.4 52.2 %collective-permute-start.28 = (bf16[512,1024]{1,0:T(8,128)(2,1)}, bf16[512,1024]{1,0:T(8,128)(2,1)}, u32[]{:S(2)}, u32[]{:S(2)}) collective-permute-start(bf16[512,1024]{1,0:T(8,128)(2,1)} %shard_map.257), channel_id=1, source_target_pairs={{0,1},{1,0},{2,3},{3,2},{4,5},{5,4},{6,7},{7,6},{8,9},{9,8},{10,11... | collective-permute-start | bytes 3145736 | tf_op jit(solution)/shard_map/ppermute | solution.py:30
  432.3 27.8 %all-to-all-start = ((f32[4,32,512]{2,1,0:T(8,128)}), f32[4,32,512]{2,1,0:T(8,128)S(1)}, u32[]{:S(2)}, u32[]{:S(2)}) async-start(f32[4,32,512]{2,1,0:T(8,128)} %param.35), calls=%async_computation | async-start | bytes 524288 | tf_op jit(solution)/shard_map/all_to_all | solution.py:1101
  460.0 50.3 %all-to-all-start.2 = ((bf16[8,256,512]{2,1,0:T(8,128)(2,1)}), bf16[8,256,512]{2,1,0:T(8,128)(2,1)S(1)}, u32[]{:S(2)}, u32[]{:S(2)}) async-start(bf16[8,256,512]{2,1,0:T(8,128)(2,1)} %get-tuple-element.202), calls=%async_computation.2 | async-start | bytes 4194304 | tf_op jit(solution)/shard_map/all_to_all | solution.py:1049
  510.3 33.2 %all-to-all-start.1 = ((bf16[8,256,512]{2,1,0:T(8,128)(2,1)}), bf16[8,256,512]{2,1,0:T(8,128)(2,1)}, u32[]{:S(2)}, u32[]{:S(2)}) async-start(bf16[8,256,512]{2,1,0:T(8,128)(2,1)} %get-tuple-element.196), calls=%async_computation.1 | async-start | bytes 4194304 | tf_op jit(solution)/shard_map/all_to_all | solution.py:1049
  546.3 32.3 %all-to-all-start.3 = ((bf16[4,128,512]{2,1,0:T(8,128)(2,1)}), bf16[4,128,512]{2,1,0:T(8,128)(2,1)S(1)}, u32[]{:S(2)}, u32[]{:S(2)}) async-start(bf16[4,128,512]{2,1,0:T(8,128)(2,1)} %bitcast.24), calls=%async_computation.3 | async-start | bytes 1048576 | tf_op jit(solution)/shard_map/all_to_all | solution.py:1049
  589.9 37.1 %all-to-all-start.4 = ((f32[32,1,128]{2,1,0:T(1,128)}), f32[32,1,128]{2,1,0:T(1,128)S(1)}, u32[]{:S(2)}, u32[]{:S(2)}) async-start(f32[32,1,128]{2,1,0:T(1,128)} %bitcast.29), calls=%async_computation.4 | async-start | bytes 32768 | tf_op jit(solution)/shard_map/all_to_all | solution.py:1049
  597.4 27.7 %collective-permute-start.35 = (f32[128,512]{1,0:T(8,128)S(1)}, f32[128,512]{1,0:T(8,128)S(1)}, u32[]{:S(2)}, u32[]{:S(2)}) collective-permute-start(f32[128,512]{1,0:T(8,128)S(1)} %bitcast_add_fusion.1.refs_0_), channel_id=1, source_target_pairs={{0,24},{4,28},{8,16},{12,20},{16,8},{20,12},{24,0},{28,4},{1,25},{... | collective-permute-start | bytes 786440 | tf_op jit(solution)/shard_map/ppermute | solution.py:30
  597.8 33.1 %collective-permute-start.34 = (f32[128,512]{1,0:T(8,128)S(1)}, f32[128,512]{1,0:T(8,128)S(1)}, u32[]{:S(2)}, u32[]{:S(2)}) collective-permute-start(f32[128,512]{1,0:T(8,128)S(1)} %bitcast_add_fusion.1.refs_0_), channel_id=1, source_target_pairs={{0,20},{4,16},{8,28},{12,24},{16,4},{20,0},{24,12},{28,8},{1,21},{... | collective-permute-start | bytes 786440 | tf_op jit(solution)/shard_map/ppermute | solution.py:30
  625.2 46.4 %collective-permute-start.37 = (bf16[512,1024]{1,0:T(8,128)(2,1)S(1)}, bf16[512,1024]{1,0:T(8,128)(2,1)S(1)}, u32[]{:S(2)}, u32[]{:S(2)}) collective-permute-start(bf16[512,1024]{1,0:T(8,128)(2,1)S(1)} %copy-done.12), channel_id=1, source_target_pairs={{0,1},{1,0},{2,3},{3,2},{4,5},{5,4},{6,7},{7,6},{8,9},{9,8},{10,11... | collective-permute-start | bytes 3145736 | tf_op jit(solution)/shard_map/ppermute | solution.py:30
  627.0 37.4 %all-to-all-start.5 = ((f32[1,128,512]{2,0,1:T(1,128)}), f32[1,128,512]{2,0,1:T(1,128)S(1)}, u32[]{:S(2)}, u32[]{:S(2)}) async-start(f32[1,128,512]{2,0,1:T(1,128)} %copy.76), calls=%async_computation.5 | async-start | bytes 524288 | tf_op jit(solution)/shard_map/all_to_all | solution.py:1104
  (61 other events, 678.5 us)

commit v3 on v2

--- a/solution.py
+++ b/solution.py
@@ -237,14 +237,14 @@
     )(*places, queries, *keys, *values)
 
 
-def attend_back(places, grad_out, queries, keys, values, mix, lse, causal):
+def attend_back(places, grad_out, queries, keys, values, mix, lse, causal, after=()):
     rows, width = queries.shape
     pairs = width // PAIR
     fixed, columns, stat = attention_specs(rows)
     return pl.pallas_call(
-        functools.partial(attend_back_kernel, causal, 256),
+        lambda *refs: attend_back_kernel(causal, 256, *refs[:12], *refs[12 + len(after) :]),
         grid=(pairs,),
-        in_specs=fixed + [columns] * 7 + [stat],
+        in_specs=fixed + [columns] * 7 + [stat] + [HBM] * len(after),
         out_specs=[columns] * 5,
         out_shape=[
             jax.ShapeDtypeStruct((rows, width), jnp.bfloat16),
@@ -255,7 +255,7 @@
         cost_estimate=pl.CostEstimate(
             flops=80 * rows * rows * width, bytes_accessed=24 * rows * width, transcendentals=0
         ),
-    )(*places, queries, *keys, *values, mix, grad_out, lse)
+    )(*places, queries, *keys, *values, mix, grad_out, lse, *after)
 
 
 def flipped(me, bits):
@@ -337,7 +337,7 @@
 
 
 ROWS = 64
-TILE = 256
+TILE = 512
 STAT = 128
 
 
@@ -498,8 +498,8 @@
     (up_hbm, down_hbm, adapt_hbm, wo_hbm), refs = refs[:4], refs[4:]
     if more:
         far_ref, refs = refs[0], refs[1:]
-    dz_ref, dmix_ref, matrices_ref, g_first_ref, g_second_ref = refs[:5]
-    up, down, adapt, wo, dt_ref, e_ref, low_ref, du_ref, dpre_ref, sem = refs[5:]
+    out_ref, dz_ref, dmix_ref, matrices_ref, g_first_ref, g_second_ref = refs[:6]
+    up, down, adapt, wo, dt_ref, e_ref, low_ref, du_ref, dpre_ref, sem = refs[6:]
     blocks = up.shape[0]
     load(
         [adapt_hbm, down_hbm, slope_hbm, up_hbm, wo_hbm.at[0]],
@@ -511,6 +511,7 @@
 
     def lower(rows):
         low_ref[rows, :] = bfloat(n1_ref[rows, :] * gain1)
+        out_ref[rows, :] = bfloat(n2_ref[rows, :] * gain2)
 
     tiles(lower, n1_ref.shape[0], ROWS)
 
@@ -691,7 +692,11 @@
 F32, BF16 = jnp.float32, jnp.bfloat16
 
 
-def call(kernel, ins, specs, outs, scratch, flops, collective_id=None):
+def call(kernel, ins, specs, outs, scratch, flops, collective_id=None, after=()):
+    if after:
+        inner, first = kernel, len(ins)
+        kernel = lambda *refs: inner(*refs[:first], *refs[first + len(after) :])
+        ins, specs = [*ins, *after], [*specs, *[HBM] * len(after)]
     return pl.pallas_call(
         kernel,
         in_specs=specs,
@@ -731,7 +736,7 @@
     )
 
 
-def settle(collective_id, x, mix, gains, pieces, wo_at, q_at, gain_rows):
+def settle(collective_id, x, mix, gains, pieces, wo_at, q_at, gain_rows, after=()):
     rows = x.shape[0]
     n = len(pieces.arrays)
     count = 1 if q_at is None else 2
@@ -748,6 +753,7 @@
         scratch + loader_sems(count, n),
         2 * rows * D * D * count,
         collective_id,
+        after,
     )
 
 
@@ -810,6 +816,7 @@
         [cot, *second, *first, gains, slope, pre_slope, adapt_low, *weights, *more],
         [IN_VMEM] * 6 + [HBM] + [IN_VMEM] * 2 + [HBM] * 4 + [IN_VMEM] * len(more),
         [
+            ((rows, D), BF16),
             ((rows, D), F32),
             ((rows, D), BF16),
             ((D // height, 2 * height, ADAPT), BF16),
@@ -910,9 +917,11 @@
         near, far = bits[1:3]
         pieces = self.pieces
         even = lax.axis_index("wide") % 2 == 0
-        chosen = jnp.where(even, pieces[near], pieces[far])
+        first, second = pieces[near], pieces[far]
+        if after:
+            first, second, *_ = lax.optimization_barrier((first, second, *after))
         pieces[near | far] = lax.ppermute(
-            tie(chosen, *after) if after else chosen,
+            jnp.where(even, first, second),
             "wide",
             [(i, i ^ (near if i % 2 else far)) for i in range(lax.axis_size("wide"))],
         )
@@ -957,70 +966,82 @@
     height = enc_wo.shape[0]
     stack = lambda *arrays: jnp.concatenate([a.reshape(-1, D) for a in arrays])
     columns = lambda array: [array[:, j * D : (j + 1) * D] for j in range(array.shape[1] // D)]
-    found = gather_any_order(bfloat(adapter_weights), "narrow")
-    found = found[lax.axis_index("narrow") ^ jnp.arange(lax.axis_size("narrow"))]
-    adapters = found.transpose(1, 0, 2, 3).reshape(4, height, ADAPT)
-    beside = lambda l: jnp.concatenate([adapters[2 * l], adapters[2 * l + 1]], axis=1)
     gain_rows = jnp.concatenate([enc_gains, dec_gains])
     gain_block = jnp.pad(gain_rows, ((0, 16 - gain_rows.shape[0]), (0, D - height)))
     gather = lambda array: Gather(array, height)
     enc_first = gather(stack(enc_qkv, gain_block))
     dec_first = gather(stack(dec_qkv[:3]))
     enc_up = gather(stack(enc_wo, *columns(enc_w_in)))
-    enc_down = gather(stack(enc_w_out, beside(0)))
     dec_second = gather(stack(dec_wo, dec_qkv[3:]))
     dec_up = gather(stack(*columns(dec_w_in)))
-    dec_down = gather(stack(dec_w_out, beside(1)))
-
+
+    count = lax.axis_size("wide")
     partner = lambda array: swap(array, "narrow", 1)
-    other_ids = partner(segment_ids)
     rows = enc_in.shape[0]
     half = (lax.axis_index("narrow") % 2).astype(jnp.int32).reshape(1)
+    at = lambda i: i * height
+
+    enc_first.begin()
+    enc_far = partner(enc_in)
+    enc_first.across()
+    begun = enc_first.arrays[-1]
+    dec_first.begin(begun)
+    dec_far = partner(tie(dec_in, begun))
+    other_ids = partner(tie(segment_ids, begun))
     places = (half, segment_ids.reshape(1, rows), segment_ids.reshape(rows, 1), other_ids.reshape(rows, 1))
-    at = lambda i: i * height
-
-    enc_first.begin()
-    enc_far, dec_far = partner(enc_in), partner(dec_in)
-    dec_first.begin(*enc_first.marks())
-    enc_first.across()
-    enc_up.begin(enc_first.arrays[-1])
+    found = gather_any_order(bfloat(tie(adapter_weights, begun)), "narrow")
+    found = found[lax.axis_index("narrow") ^ jnp.arange(lax.axis_size("narrow"))]
+    adapters = found.transpose(1, 0, 2, 3).reshape(4, height, ADAPT)
+    beside = lambda l: jnp.concatenate([adapters[2 * l], adapters[2 * l + 1]], axis=1)
     enc_query, enc_key, enc_value, enc_key_far, enc_value_far, enc_qkv_full = project(
-        0, enc_in, enc_far, enc_first, (at(0), at(1), at(2))
+        0, tie(enc_in, begun), enc_far, enc_first, (at(0), at(1), at(2))
     )
     enc_keys, enc_values = (enc_key, enc_key_far), (enc_value, enc_value_far)
-    count = lax.axis_size("wide")
+
+    repeat = lax.axis_size("narrow") // 4
+    spread = lambda array: jnp.repeat(array, repeat, axis=0) if repeat > 1 else array
+    to_matrix = lambda array: lax.all_to_all(
+        spread(array), "narrow", split_axis=0, concat_axis=1, tiled=True
+    )[0]
+    to_rows = lambda array: lax.all_to_all(
+        array[None], "narrow", split_axis=1, concat_axis=0, tiled=True
+    )[::repeat]
+
+    dec_first.across(enc_value)
+    enc_up.begin(enc_value)
+    enc_mix, enc_lse = attend(places, enc_query, enc_keys, enc_values, False)
     found = jnp.stack([p[at(3) : at(3) + 8, :height] for p in enc_first.arrays])
-    found = jnp.concatenate([found, swap(found, "wide", 1)])
+    found = jnp.concatenate([found, swap(tie(found, enc_mix), "wide", 1)])
     order = lax.axis_index("wide") ^ jnp.arange(count)
     order = order // 2 + order % 2 * (count // 2)
     gains = found[order].transpose(1, 0, 2).reshape(8, D).astype(jnp.float32)
-
-    dec_first.across(enc_value)
-    enc_mix, enc_lse = attend(places, enc_query, enc_keys, enc_values, False)
-    enc_up.across(enc_mix)
+    enc_down = gather(stack(enc_w_out, tie(beside(0), enc_mix)))
+    dec_down = gather(stack(dec_w_out, tie(beside(1), enc_mix)))
     enc_down.begin(enc_mix)
     self_query, self_key, self_value, self_key_far, self_value_far, dec_qkv_full = project(
         1, tie(dec_in, enc_mix), dec_far, dec_first, (at(0), at(1), at(2))
     )
     self_keys, self_values = (self_key, self_key_far), (self_value, self_value_far)
-    dec_second.begin(self_value)
+    enc_up.across(self_value)
     self_mix, self_lse = attend(places, self_query, self_keys, self_values, True)
-    enc_down.across(self_mix)
+    dec_second.begin(self_mix)
     *enc_norm1, enc_wo_full = settle(
         2, enc_in, tie(enc_mix, self_mix), gains, enc_up, at(0), None, (None, 0)
     )
+    enc_down.across(enc_norm1[0])
     enc_slope, enc_inner, enc_up_full = tail_up(3, enc_norm1[0], gains, enc_up, at(1), 0)
-    dec_second.across(enc_inner)
     dec_up.begin(enc_inner)
     enc_pre_slope, enc_adapt, *enc_norm2, enc_low, enc_down_full, enc_adapt_full = tail_down(
         4, enc_norm1[0], enc_inner, gains, bias_in[0], bias_out[0], enc_down, (0, at(4)), (0, 1)
     )
+    enc_low_far = partner(enc_low)
+    dec_second.across(enc_low)
     *dec_norm1, cross_query, dec_q_full = settle(
         5, dec_in, tie(self_mix, enc_low), gains, dec_second, at(0), at(2), (None, 2)
     )
     dec_down.begin(cross_query)
     cross_key, cross_value, cross_key_far, cross_value_far, dec_kv_full = project(
-        6, tie(enc_low, cross_query), partner(enc_low), dec_second, (at(3), at(4))
+        6, tie(enc_low, cross_query), enc_low_far, dec_second, (at(3), at(4))
     )
     cross_keys, cross_values = (cross_key, cross_key_far), (cross_value, cross_value_far)
     dec_up.across(cross_key)
@@ -1030,11 +1051,11 @@
         7, dec_norm1[0], cross_mix, gains, dec_second, at(1), None, (2, 3)
     )
     dec_slope, dec_inner, dec_up_full = tail_up(8, dec_norm2[0], gains, dec_up, at(0), 3)
-    dec_pre_slope, dec_adapt, *dec_norm3, dec_low, dec_down_full, dec_adapt_full = tail_down(
+    dec_pre_slope, dec_adapt, *dec_norm3, _, dec_down_full, dec_adapt_full = tail_down(
         9, dec_norm2[0], dec_inner, gains, bias_in[1], bias_out[1], dec_down, (0, at(4)), (3, 4)
     )
 
-    grad_z2, grad_cross_mix, dec_matrices, grad_dec_first, grad_dec_second = tail_back(
+    dec_out, grad_z2, grad_cross_mix, dec_matrices, grad_dec_first, grad_dec_second = tail_back(
         height,
         dec_cot,
         dec_norm3,
@@ -1052,12 +1073,12 @@
     cross_back = attend_back(
         places, grad_cross_mix, cross_query, cross_keys, cross_values, cross_mix, cross_lse, False
     )
-    far_encoded = back((), (cross_back[2], cross_back[4]), dec_kv_full, (0, 1), BF16)
+    dec_sums = total(tie(dec_matrices, cross_back[0]))
+    far_encoded = back((), (tie(cross_back[2], dec_sums), cross_back[4]), dec_kv_full, (0, 1), BF16)
     near_encoded = partner(far_encoded)
     grad_encoded = back(
         (tie(enc_cot, far_encoded),), (cross_back[1], cross_back[3]), dec_kv_full, (0, 1), F32
     )
-    dec_sums = total(tie(dec_matrices, cross_back[0]))
     grad_z1, grad_self_mix = query_back(
         tie(grad_z2, grad_encoded),
         cross_back[0],
@@ -1066,7 +1087,7 @@
         dec_q_full,
         2,
     )
-    grad_ez1, grad_enc_mix, enc_matrices, grad_enc_first, grad_enc_second = tail_back(
+    enc_out, grad_ez1, grad_enc_mix, enc_matrices, grad_enc_first, grad_enc_second = tail_back(
         height,
         tie(grad_encoded, grad_z1),
         enc_norm2,
@@ -1079,32 +1100,13 @@
         (0, 1),
         (near_encoded,),
     )
-    enc_matrices = exchange(enc_matrices, "wide")
-
-    devices = lax.axis_size("wide") * lax.axis_size("narrow")
-    slices = lambda first, second: jnp.concatenate([first, second]).reshape(2, devices, -1).transpose(1, 0, 2)
-    firsts = slices(grad_enc_first, grad_dec_first)
-    seconds = slices(grad_enc_second, grad_dec_second)
-    biases = jnp.concatenate([firsts.reshape(devices, -1), seconds.reshape(devices, -1)], axis=1)
-    used = biases.shape[1]
-    biases = jnp.pad(biases, ((0, 0), (0, -used % STAT)))
-    biases = jnp.sum(exchange(biases, ("wide", "narrow")), axis=0)[:used]
-    grad_bias_in = biases[: firsts[0].size].reshape(firsts.shape[1:])
-    grad_bias_out = biases[firsts[0].size :].reshape(seconds.shape[1:])
+    old_momentum = to_matrix(tie(adapter_momenta, grad_z1))
+    enc_matrices = exchange(tie(enc_matrices, old_momentum), "wide")
 
     self_back = attend_back(
-        places, tie(grad_self_mix, grad_ez1), self_query, self_keys, self_values, self_mix, self_lse, True
-    )
-
-    repeat = lax.axis_size("narrow") // 4
-    spread = lambda array: jnp.repeat(array, repeat, axis=0) if repeat > 1 else array
-    to_matrix = lambda array: lax.all_to_all(
-        spread(array), "narrow", split_axis=0, concat_axis=1, tiled=True
-    )[0]
-    to_rows = lambda array: lax.all_to_all(
-        array[None], "narrow", split_axis=1, concat_axis=0, tiled=True
-    )[::repeat]
-    old_momentum = to_matrix(tie(adapter_momenta, cross_back[0]))
+        places, tie(grad_self_mix, grad_ez1), self_query, self_keys, self_values, self_mix, self_lse, True, (old_momentum,)
+    )
+
     sums = jnp.concatenate([total(tie(enc_matrices, self_back[0])), dec_sums])
     sums = spread(bfloat(sums).reshape(4, height, ADAPT))
     enc_back = attend_back(
@@ -1128,6 +1130,17 @@
         (0, 1, 2),
         F32,
     )
+    devices = lax.axis_size("wide") * lax.axis_size("narrow")
+    slices = lambda first, second: jnp.concatenate([first, second]).reshape(2, devices, -1).transpose(1, 0, 2)
+    firsts = slices(tie(grad_enc_first, far_enc), grad_dec_first)
+    seconds = slices(tie(grad_enc_second, far_enc), grad_dec_second)
+    biases = jnp.concatenate([firsts.reshape(devices, -1), seconds.reshape(devices, -1)], axis=1)
+    used = biases.shape[1]
+    biases = jnp.pad(biases, ((0, 0), (0, -used % STAT)))
+    biases = jnp.sum(exchange(biases, ("wide", "narrow")), axis=0)[:used]
+    grad_bias_in = biases[: firsts[0].size].reshape(firsts.shape[1:])
+    grad_bias_out = biases[firsts[0].size :].reshape(seconds.shape[1:])
+
     orthogonal = muon([parts[0], tie(parts[1], grad_dec), *parts[2:]])
     grad_enc = back(
         (tie(grad_ez1, orthogonal), near_enc),
@@ -1138,8 +1151,8 @@
     )
     new_weights = adapter_weights - RATE * math.sqrt(max(1.0, D / ADAPT)) * to_rows(orthogonal)
     return (
-        enc_low,
-        dec_low,
+        enc_out,
+        dec_out,
         grad_enc,
         grad_dec,
         grad_bias_in,

time: 691 us -> 620 us (0.90); the launches traced: 687 us -> 609 us
  waiting for transfers between devices: 122 us -> 60.3 us
  Pallas kernels: 437 us -> 405 us
  local copies, waits for them, and re-layouts: 27.5 us -> 40.3 us
    ppermute x31, waiting for transfers between devices: 49.4 us -> 14.7 us  [swap(): lax.ppermute(array, axis, [(i, i ^ bit) for i in range(lax.axis_size(axis...]
    pallas_call x20, Pallas kernels: 297 us -> 266 us  [call(): pl.pallas_call(kernel, in_specs=specs, out_specs=[IN_VMEM if len(out) ==...]
    all_to_all x1, waiting for transfers between devices: 24.3 us -> 0.01 us  [shards(): lax.all_to_all(spread(array), 'narrow', split_axis=0, concat_axis=1, tile...]
    ppermute x31, starting transfers between devices: 40.6 us -> 48.2 us  [swap(): lax.ppermute(array, axis, [(i, i ^ bit) for i in range(lax.axis_size(axis...]
    unnamed x108 -> x90, local copies, waits for them, and re-layouts: 15.1 us -> 18.9 us
  transfers between devices with their start and end apart: 45 -> 45, of which waited for: 11 -> 10; matrix products, arithmetic and copies ran while one was open for 5% -> 7% of each run, Pallas kernels for 50% -> 57%
where the time goes in v3:
time: 620 us; the launch traced here: 609 us
  Pallas kernels  405 us (65%)
  starting transfers between devices  81.1 us (13%)
  waiting for transfers between devices  60.3 us (10%)
  local copies, waits for them, and re-layouts  40.3 us (6%)
  other arithmetic  19.5 us (3%)
    pallas_call x20, Pallas kernels, call(): pl.pallas_call(kernel, in_specs=specs, out_specs=[IN_VMEM if len(out) ==...  266 us
    pallas_call x3, Pallas kernels, attend_back(): pl.pallas_call(lambda *refs: attend_back_kernel(causal, 256, *refs[:12],...  84.7 us
    pallas_call x3, Pallas kernels, attend(): pl.pallas_call(functools.partial(attend_kernel, causal, 256), grid=(pairs...  54.7 us
    ppermute x31, starting transfers between devices, swap(): lax.ppermute(array, axis, [(i, i ^ bit) for i in range(lax.axis_size(axis...  48.2 us
    ppermute x7, waiting for transfers between devices, across(): lax.ppermute(jnp.where(even, first, second), 'wide', [(i, i ^ (near if i...  45.1 us
    unnamed x90, local copies, waits for them, and re-layouts  18.9 us
    all_to_all x4, starting transfers between devices, shards(): lax.all_to_all(array, axis, split_axis=0, concat_axis=0, tiled=True)  14.9 us
    ppermute x31, waiting for transfers between devices, swap(): lax.ppermute(array, axis, [(i, i ^ bit) for i in range(lax.axis_size(axis...  14.7 us
  transfers between devices with their start and end apart: 45, of which 10 were waited for; matrix products, arithmetic and copies ran while one was open for 7% of the time, Pallas kernels for 57%

profile of v3, /device:TPU:0, one launch (start us, length us, event | category | flops | bytes accessed | tf_op | source)
XLA Modules:
  0.0 608.6 jit_solution(5798713922611134498)
XLA Ops:
  30.8 9.4 %collective-permute-done.2.refs_3_ = bf16[400,1024]{1,0:T(8,128)(2,1)S(1)} collective-permute-done((bf16[400,1024]{1,0:T(8,128)(2,1)S(1)}, bf16[400,1024]{1,0:T(8,128)(2,1)S(1)}, u32[]{:S(2)}, u32[]{:S(2)}) %collective-permute-start.2) | collective-permute-done | bytes 819232 | tf_op jit(solution)/shard_map/ppermute | solution.py:923
  44.4 13.7 %shard_map.242 = (bf16[512,1024]{1,0:T(8,128)(2,1)}, bf16[512,1024]{1,0:T(8,128)(2,1)}, bf16[512,1024]{1,0:T(8,128)(2,1)}, bf16[512,1024]{1,0:T(8,128)(2,1)}, bf...) custom-call(bf16[512,1024]{1,0:T(8,128)(2,1)} %x_ref.4, bf16[512,1024]{1,0:T(8,128)(2,1)} %collective-permute-done.4.far_ref, ...), custom_call_target="tpu_custom_call" | custom-call | flops 5368709120 | bytes 5373952 | tf_op jit(solution)/shard_map/pallas_call | solution.py:700
  70.8 18.2 %shard_map.243 = (bf16[512,1024]{1,0:T(8,128)(2,1)}, f32[8,8,512]{2,1,0:T(8,128)}) custom-call(s32[1]{0:T(128)} %bitcast.half_ref.refs_0_, s32[1,512]{1,0:T(1,128)} %bitcast.1.qid_ref.refs_1_, s32[512,1]{1,0:T(8,128)} %copy.66.kid_own_ref.refs_2_, s32[512,1]{1,0:T(8,128)} %copy.67.kid_far_ref.refs_3_, bf16[512,1024]{1,0:T(8,128)(2,1)} %get-tuple-element.138.q_ref.refs_4_, ...), custom_call_target="tpu_custom_call" | custom-call | flops 8589934592 | bytes 6291456 | tf_op jit(solution)/shard_map/pallas_call | solution.py:220
  101.2 13.6 %shard_map.244 = (bf16[512,1024]{1,0:T(8,128)(2,1)}, bf16[512,1024]{1,0:T(8,128)(2,1)}, bf16[512,1024]{1,0:T(8,128)(2,1)}, bf16[512,1024]{1,0:T(8,128)(2,1)}, bf...) custom-call(bf16[512,1024]{1,0:T(8,128)(2,1)} %x_ref.5, bf16[512,1024]{1,0:T(8,128)(2,1)} %collective-permute-done.5.far_ref, ...), custom_call_target="tpu_custom_call" | custom-call | flops 5368709120 | bytes 5242880 | tf_op jit(solution)/shard_map/pallas_call | solution.py:700
  121.0 18.2 %shard_map.245 = (bf16[512,1024]{1,0:T(8,128)(2,1)}, f32[8,8,512]{2,1,0:T(8,128)}) custom-call(s32[1]{0:T(128)} %bitcast.half_ref.refs_0_, s32[1,512]{1,0:T(1,128)} %bitcast.1.qid_ref.refs_1_, s32[512,1]{1,0:T(8,128)} %copy.66.kid_own_ref.refs_2_, s32[512,1]{1,0:T(8,128)} %copy.67.kid_far_ref.refs_3_, bf16[512,1024]{1,0:T(8,128)(2,1)} %get-tuple-element.149.q_ref.refs_4_, ...), custom_call_target="tpu_custom_call" | custom-call | flops 8589934592 | bytes 6291456 | tf_op jit(solution)/shard_map/pallas_call | solution.py:220
  139.2 5.5 collective-permute-done.12.refs_3_
  144.7 9.0 %shard_map.246 = (f32[512,1024]{1,0:T(8,128)}, f32[512,128]{1,0:T(8,128)}, bf16[1,1024,1024]{2,1,0:T(8,128)(2,1)}) custom-call(bf16[512,1024]{1,0:T(8,128)(2,1)} %x_ref.4, bf16[512,1024]{1,0:T(8,128)(2,1)} %get-tuple-element.155.mix_ref.refs_9_, f32[8,1024]{1,0:T(8,128)} %convert_bitcast_fusion.1.gains_ref.refs_5_, ...), custom_call_target="tpu_custom_call" | custom-call | flops 1073741824 | bytes 7372800 | tf_op jit(solution)/shard_map/pallas_call | solution.py:700
  160.2 14.8 %shard_map.247 = (bf16[512,4096]{1,0:T(8,128)(2,1)}, bf16[512,4096]{1,0:T(8,128)(2,1)}, bf16[4,1024,1024]{2,1,0:T(8,128)(2,1)}) custom-call(f32[512,1024]{1,0:T(8,128)} %get-tuple-element.160.n_ref.refs_3_, f32[8,1024]{1,0:T(8,128)} %convert_bitcast_fusion.1.gains_ref.refs_5_, bf16[640,1024]{1,0:T(8,128)(2,1)} %slice_dynamic-update-slice_fusion.refs_0_, ...), custom_call_target="tpu_custom_call" | custom-call | flops 4294967296 | bytes 7372800 | tf_op jit(solution)/shard_map/pallas_call | solution.py:700
  175.1 11.5 %collective-permute-done.17.refs_3_ = bf16[640,1024]{1,0:T(8,128)(2,1)} collective-permute-done((bf16[640,1024]{1,0:T(8,128)(2,1)S(1)}, bf16[640,1024]{1,0:T(8,128)(2,1)}, u32[]{:S(2)}, u32[]{:S(2)}) %collective-permute-start.17) | collective-permute-done | bytes 1310752 | tf_op jit(solution)/shard_map/ppermute | solution.py:923
  186.6 18.6 %shard_map.248 = (bf16[512,512]{1,0:T(8,128)(2,1)}, bf16[512,512]{1,0:T(8,128)(2,1)}, f32[512,1024]{1,0:T(8,128)}, f32[512,128]{1,0:T(8,128)}, bf16[512,1024]{1,...) custom-call(f32[512,1024]{1,0:T(8,128)} %get-tuple-element.160.n_ref.refs_3_, ...), custom_call_target="tpu_custom_call" | custom-call | flops 5368709120 | bytes 11573248 | tf_op jit(solution)/shard_map/pallas_call | solution.py:700
  215.9 18.6 %collective-permute-done.20.refs_3_ = bf16[640,1024]{1,0:T(8,128)(2,1)S(1)} collective-permute-done((bf16[640,1024]{1,0:T(8,128)(2,1)S(1)}, bf16[640,1024]{1,0:T(8,128)(2,1)S(1)}, u32[]{:S(2)}, u32[]{:S(2)}) %collective-permute-start.20) | collective-permute-done | bytes 1310752 | tf_op jit(solution)/shard_map/ppermute | solution.py:923
  235.6 11.0 %shard_map.249 = (f32[512,1024]{1,0:T(8,128)}, f32[512,128]{1,0:T(8,128)}, bf16[512,1024]{1,0:T(8,128)(2,1)}, bf16[2,1024,1024]{2,1,0:T(8,128)(2,1)}) custom-call(bf16[512,1024]{1,0:T(8,128)(2,1)} %x_ref.5, bf16[512,1024]{1,0:T(8,128)(2,1)} %get-tuple-element.168.mix_ref.refs_9_, f32[8,1024]{1,0:T(8,128)} %convert_bitcast_fusion.1.gains_ref.refs_5_, ...), custom_call_target="tpu_custom_call" | custom-call | flops 2147483648 | bytes 7372800 | tf_op jit(solution)/shard_map/pallas_call | solution.py:700
  250.7 11.7 %shard_map.250 = (bf16[512,1024]{1,0:T(8,128)(2,1)}, bf16[512,1024]{1,0:T(8,128)(2,1)}, bf16[512,1024]{1,0:T(8,128)(2,1)}, bf16[512,1024]{1,0:T(8,128)(2,1)}, bf16[2,1024,1024]{2,1,0:T(8,128)(2,1)}) custom-call(bf16[512,1024]{1,0:T(8,128)(2,1)} %get-tuple-element.173.x_ref, bf16[512,1024]{1,0:T(8,128)(2,1)} %collective-permute-done.21.far_ref, ...), custom_call_target="tpu_custom_call" | custom-call | flops 4294967296 | bytes 7340032 | tf_op jit(solution)/shard_map/pallas_call | solution.py:700
  264.4 18.4 %shard_map.251 = (bf16[512,1024]{1,0:T(8,128)(2,1)}, f32[8,8,512]{2,1,0:T(8,128)}) custom-call(s32[1]{0:T(128)} %bitcast.half_ref.refs_0_, s32[1,512]{1,0:T(1,128)} %bitcast.1.qid_ref.refs_1_, s32[512,1]{1,0:T(8,128)} %copy.66.kid_own_ref.refs_2_, s32[512,1]{1,0:T(8,128)} %copy.67.kid_far_ref.refs_3_, bf16[512,1024]{1,0:T(8,128)(2,1)} %get-tuple-element.172.q_ref.refs_4_, ...), custom_call_target="tpu_custom_call" | custom-call | flops 8589934592 | bytes 6291456 | tf_op jit(solution)/shard_map/pallas_call | solution.py:220
  285.8 9.5 %shard_map.252 = (f32[512,1024]{1,0:T(8,128)}, f32[512,128]{1,0:T(8,128)}, bf16[1,1024,1024]{2,1,0:T(8,128)(2,1)}) custom-call(f32[512,1024]{1,0:T(8,128)} %get-tuple-element.179.x_ref.n_ref, bf16[512,1024]{1,0:T(8,128)(2,1)} %get-tuple-element.178.mix_ref.refs_9_, f32[8,1024]{1,0:T(8,128)} %convert_bitcast_fusion.1.gains_ref.refs_5_, ...), custom_call_target="tpu_custom_call" | custom-call | flops 1073741824 | bytes 8421376 | tf_op jit(solution)/shard_map/pallas_call | solution.py:700
  296.2 14.6 %shard_map.253 = (bf16[512,4096]{1,0:T(8,128)(2,1)}, bf16[512,4096]{1,0:T(8,128)(2,1)}, bf16[4,1024,1024]{2,1,0:T(8,128)(2,1)}) custom-call(f32[512,1024]{1,0:T(8,128)} %get-tuple-element.180.n_ref.refs_3_, f32[8,1024]{1,0:T(8,128)} %convert_bitcast_fusion.1.gains_ref.refs_5_, bf16[512,1024]{1,0:T(8,128)(2,1)} %copy-done.20, ...), custom_call_target="tpu_custom_call" | custom-call | flops 4294967296 | bytes 6324224 | tf_op jit(solution)/shard_map/pallas_call | solution.py:700
  310.9 18.6 %shard_map.254 = (bf16[512,512]{1,0:T(8,128)(2,1)}, bf16[512,512]{1,0:T(8,128)(2,1)}, f32[512,1024]{1,0:T(8,128)}, f32[512,128]{1,0:T(8,128)}, bf16[512,1024]{1,...) custom-call(f32[512,1024]{1,0:T(8,128)} %get-tuple-element.180.n_ref.refs_3_, ...), custom_call_target="tpu_custom_call" | custom-call | flops 5368709120 | bytes 11573248 | tf_op jit(solution)/shard_map/pallas_call | solution.py:700
  329.5 24.8 %shard_map.255 = (bf16[512,1024]{1,0:T(8,128)(2,1)}, f32[512,1024]{1,0:T(8,128)}, bf16[512,1024]{1,0:T(8,128)(2,1)}, bf16[8,256,512]{2,1,0:T(8,128)(2,1)}, f32[1,512]{1,0:T(1,128)}, /*index=5*/f32[1,1024]{1,0:T(1,128)}) custom-call(bf16[512,1024]{1,0:T(8,128)(2,1)} %refs_0_.1, f32[512,1024]{1,0:T(8,128)} %get-tuple-element.189.refs_1_, ...), custom_call_target="tpu_custom_call" | custom-call | flops 12884901888 | bytes 32014336 | tf_op jit(solution)/shard_map/pallas_call | solution.py:700
  357.9 28.2 %shard_map.256 = (bf16[512,1024]{1,0:T(8,128)(2,1)}, bf16[512,1024]{1,0:T(8,128)(2,1)}, bf16[512,1024]{1,0:T(8,128)(2,1)}, bf16[512,1024]{1,0:T(8,128)(2,1)}, bf16[512,1024]{1,0:T(8,128)(2,1)}) custom-call(s32[1]{0:T(128)} %bitcast.half_ref.refs_0_, s32[1,512]{1,0:T(1,128)} %bitcast.1.qid_ref.refs_1_, s32[512,1]{1,0:T(8,128)} %copy.66.kid_own_ref.refs_2_, ...), custom_call_target="tpu_custom_call" | custom-call | flops 21474836480 | bytes 12582912 | tf_op jit(solution)/shard_map/pallas_call | solution.py:244
  386.4 7.3 %shard_map.257 = bf16[512,1024]{1,0:T(8,128)(2,1)} custom-call(bf16[512,1024]{1,0:T(8,128)(2,1)} %get-tuple-element.205.refs_0_, bf16[512,1024]{1,0:T(8,128)(2,1)} %get-tuple-element.206.refs_1_, bf16[2,1024,1024]{2,1,0:T(8,128)(2,1)} %get-tuple-element.207.refs_2_.refs_3_), custom_call_target="tpu_custom_call" | custom-call | flops 2147483648 | bytes 6291456 | tf_op jit(solution)/shard_map/pallas_call | solution.py:700
  397.2 8.0 %shard_map.258.refs_0_ = f32[512,1024]{1,0:T(8,128)} custom-call(bf16[512,1024]{1,0:T(8,128)(2,1)} %refs_0_.2, bf16[512,1024]{1,0:T(8,128)(2,1)} %get-tuple-element.209.refs_1_, bf16[512,1024]{1,0:T(8,128)(2,1)} %get-tuple-element.210.refs_2_, bf16[2,1024,1024]{2,1,0:T(8,128)(2,1)} %get-tuple-element.207.refs_2_.refs_3_), custom_call_target="tpu_custom_call" | custom-call | flops 2147483648 | bytes 7340032 | tf_op jit(solution)/shard_map/pallas_call | solution.py:700
  405.2 9.5 %shard_map.259 = (f32[512,1024]{1,0:T(8,128)}, bf16[512,1024]{1,0:T(8,128)(2,1)}) custom-call(f32[512,1024]{1,0:T(8,128)} %get-tuple-element.212.dz_ref, bf16[512,1024]{1,0:T(8,128)(2,1)} %get-tuple-element.203.dq_ref, f32[512,1024]{1,0:T(8,128)} %get-tuple-element.179.x_ref.n_ref, f32[512,128]{1,0:T(8,128)} %get-tuple-element.213.r_ref, ...), custom_call_target="tpu_custom_call" | custom-call | flops 2147483648 | bytes 9732096 | tf_op jit(solution)/shard_map/pallas_call | solution.py:700
  422.0 25.0 %shard_map.260 = (bf16[512,1024]{1,0:T(8,128)(2,1)}, f32[512,1024]{1,0:T(8,128)}, bf16[512,1024]{1,0:T(8,128)(2,1)}, bf16[8,256,512]{2,1,0:T(8,128)(2,1)}, f32[1,512]{1,0:T(1,128)}, /*index=5*/f32[1,1024]{1,0:T(1,128)}) custom-call(f32[512,1024]{1,0:T(8,128)} %shard_map.258.refs_0_, f32[512,1024]{1,0:T(8,128)} %get-tuple-element.217.refs_1_, ...), custom_call_target="tpu_custom_call" | custom-call | flops 12884901888 | bytes 34111488 | tf_op jit(solution)/shard_map/pallas_call | solution.py:700
  447.8 4.0 all-to-all-start.2
  451.8 28.2 %shard_map.261 = (bf16[512,1024]{1,0:T(8,128)(2,1)}, bf16[512,1024]{1,0:T(8,128)(2,1)}, bf16[512,1024]{1,0:T(8,128)(2,1)}, bf16[512,1024]{1,0:T(8,128)(2,1)}, bf16[512,1024]{1,0:T(8,128)(2,1)}) custom-call(s32[1]{0:T(128)} %bitcast.half_ref.refs_0_, s32[1,512]{1,0:T(1,128)} %bitcast.1.qid_ref.refs_1_, s32[512,1]{1,0:T(8,128)} %copy.66.kid_own_ref.refs_2_, ...), custom_call_target="tpu_custom_call" | custom-call | flops 21474836480 | bytes 12582912 | tf_op jit(solution)/shard_map/pallas_call | solution.py:244
  485.2 28.2 %shard_map.262 = (bf16[512,1024]{1,0:T(8,128)(2,1)}, bf16[512,1024]{1,0:T(8,128)(2,1)}, bf16[512,1024]{1,0:T(8,128)(2,1)}, bf16[512,1024]{1,0:T(8,128)(2,1)}, bf16[512,1024]{1,0:T(8,128)(2,1)}) custom-call(s32[1]{0:T(128)} %bitcast.half_ref.refs_0_, s32[1,512]{1,0:T(1,128)} %bitcast.1.qid_ref.refs_1_, s32[512,1]{1,0:T(8,128)} %copy.66.kid_own_ref.refs_2_, ...), custom_call_target="tpu_custom_call" | custom-call | flops 21474836480 | bytes 12582912 | tf_op jit(solution)/shard_map/pallas_call | solution.py:244
  513.5 7.5 %shard_map.263 = bf16[512,1024]{1,0:T(8,128)(2,1)} custom-call(bf16[512,1024]{1,0:T(8,128)(2,1)} %get-tuple-element.245.refs_0_, bf16[512,1024]{1,0:T(8,128)(2,1)} %get-tuple-element.246.refs_1_, bf16[3,1024,1024]{2,1,0:T(8,128)(2,1)} %get-tuple-element.247.refs_2_.refs_5_), custom_call_target="tpu_custom_call" | custom-call | flops 2147483648 | bytes 8388608 | tf_op jit(solution)/shard_map/pallas_call | solution.py:700
  527.9 7.3 %shard_map.264 = bf16[512,1024]{1,0:T(8,128)(2,1)} custom-call(bf16[512,1024]{1,0:T(8,128)(2,1)} %get-tuple-element.248.refs_0_, bf16[512,1024]{1,0:T(8,128)(2,1)} %get-tuple-element.249.refs_1_, bf16[3,1024,1024]{2,1,0:T(8,128)(2,1)} %get-tuple-element.250.refs_2_.refs_5_), custom_call_target="tpu_custom_call" | custom-call | flops 2147483648 | bytes 8388608 | tf_op jit(solution)/shard_map/pallas_call | solution.py:700
  549.1 10.7 %shard_map.265 = f32[512,1024]{1,0:T(8,128)} custom-call(f32[512,1024]{1,0:T(8,128)} %get-tuple-element.251.refs_0_, bf16[512,1024]{1,0:T(8,128)(2,1)} %copy-done.11, bf16[512,1024]{1,0:T(8,128)(2,1)} %get-tuple-element.236.refs_2_, bf16[512,1024]{1,0:T(8,128)(2,1)} %get-tuple-element.252.refs_3_, bf16[512,1024]{1,0:T(8,128)(2,1)} %get-tuple-element.253.refs_4_, ...), custom_call_target="tpu_custom_call" | custom-call | flops 3221225472 | bytes 12582912 | tf_op jit(solution)/shard_map/pallas_call | solution.py:700
  566.1 20.2 %shard_map.266 = f32[128,512]{1,0:T(8,128)} custom-call(f32[128,512]{1,0:T(8,128)} %copy-done.23, f32[128,512]{1,0:T(8,128)} %copy-done.38, f32[128,512]{1,0:T(8,128)} %collective-permute-done.31.refs_2_, f32[128,512]{1,0:T(8,128)} %collective-permute-done.32.refs_3_, f32[128,512]{1,0:T(8,128)} %collective-permute-done.33.refs_4_, f32[128,512]{1,0:T(8,128)} %copy-done.37, ...), custom_call_target="tpu_custom_call" | custom-call | flops 16106127360 | bytes 2097152 | tf_op jit(solution)/shard_map/pallas_call | solution.py:700
  588.7 4.6 all-to-all-start.6
  596.4 10.7 %shard_map.267 = f32[512,1024]{1,0:T(8,128)} custom-call(f32[512,1024]{1,0:T(8,128)} %get-tuple-element.255.refs_0_, bf16[512,1024]{1,0:T(8,128)(2,1)} %copy-done.12, bf16[512,1024]{1,0:T(8,128)(2,1)} %get-tuple-element.241.refs_2_, bf16[512,1024]{1,0:T(8,128)(2,1)} %get-tuple-element.256.refs_3_, bf16[512,1024]{1,0:T(8,128)(2,1)} %get-tuple-element.257.refs_4_, ...), custom_call_target="tpu_custom_call" | custom-call | flops 3221225472 | bytes 12582912 | tf_op jit(solution)/shard_map/pallas_call | solution.py:700
  (237 shorter events, 147.5 us)
Async XLA Ops:
  8.1 36.3 %collective-permute-start.4 = (bf16[512,1024]{1,0:T(8,128)(2,1)S(1)}, bf16[512,1024]{1,0:T(8,128)(2,1)}, u32[]{:S(2)}, u32[]{:S(2)}) collective-permute-start(bf16[512,1024]{1,0:T(8,128)(2,1)S(1)} %copy-done.13), channel_id=1, source_target_pairs={{0,1},{1,0},{2,3},{3,2},{4,5},{5,4},{6,7},{7,6},{8,9},{9,8},{10,11... | collective-permute-start | bytes 3145736 | tf_op jit(solution)/shard_map/ppermute | solution.py:30
  40.5 27.6 %collective-permute-start.6 = (bf16[384,1024]{1,0:T(8,128)(2,1)}, bf16[384,1024]{1,0:T(8,128)(2,1)}, u32[]{:S(2)}, u32[]{:S(2)}) collective-permute-start(bf16[384,1024]{1,0:T(8,128)(2,1)} %bitcast.5.refs_0_), channel_id=1, source_target_pairs={{0,8},{4,12},{8,0},{12,4},{16,24},{20,28},{24,16},{28,20},{1,9},{5... | collective-permute-start | bytes 2359304 | tf_op jit(solution)/shard_map/ppermute | solution.py:30
  58.0 56.8 %collective-permute-start.11 = (bf16[640,1024]{1,0:T(8,128)(2,1)}, bf16[640,1024]{1,0:T(8,128)(2,1)S(1)}, u32[]{:S(2)}, u32[]{:S(2)}) collective-permute-start(bf16[640,1024]{1,0:T(8,128)(2,1)} %slice_dynamic-update-slice_fusion.refs_0_), channel_id=1, source_target_pairs={{0,16},{4,20},{8,24},{12,28},{16,0},{20,4},{24,8},{28,12},{1,17},{... | collective-permute-start | bytes 3932168 | tf_op jit(solution)/shard_map/ppermute | solution.py:30
  60.9 54.0 %collective-permute-start.10 = (bf16[640,1024]{1,0:T(8,128)(2,1)}, bf16[640,1024]{1,0:T(8,128)(2,1)S(1)}, u32[]{:S(2)}, u32[]{:S(2)}) collective-permute-start(bf16[640,1024]{1,0:T(8,128)(2,1)} %slice_dynamic-update-slice_fusion.refs_0_), channel_id=1, source_target_pairs={{0,8},{4,12},{8,0},{12,4},{16,24},{20,28},{24,16},{28,20},{1,9},{5... | collective-permute-start | bytes 3932168 | tf_op jit(solution)/shard_map/ppermute | solution.py:30
  63.0 36.2 %collective-permute-start.5 = (bf16[512,1024]{1,0:T(8,128)(2,1)}, bf16[512,1024]{1,0:T(8,128)(2,1)}, u32[]{:S(2)}, u32[]{:S(2)}) collective-permute-start(bf16[512,1024]{1,0:T(8,128)(2,1)} %x_ref.5), channel_id=1, source_target_pairs={{0,1},{1,0},{2,3},{3,2},{4,5},{5,4},{6,7},{7,6},{8,9},{9,8},{10,11... | collective-permute-start | bytes 3145736 | tf_op jit(solution)/shard_map/ppermute | solution.py:30
  65.5 26.9 %collective-permute-start.14 = (bf16[2,4,32,512]{3,2,1,0:T(8,128)(2,1)S(1)}, bf16[2,4,32,512]{3,2,1,0:T(8,128)(2,1)S(1)}, u32[]{:S(2)}, u32[]{:S(2)}) collective-permute-start(bf16[2,4,32,512]{3,2,1,0:T(8,128)(2,1)S(1)} %pad_maximum_fusion.5), channel_id=1, source_target_pairs={{0,2},{1,3},{2,0},{3,1},{4,6},{5,7},{6,4},{7,5},{8,10},{9,11},{10,... | collective-permute-start | bytes 786440 | tf_op jit(solution)/shard_map/ppermute | solution.py:30
  70.2 29.5 %collective-permute-start.8 = (bf16[384,1024]{1,0:T(8,128)(2,1)}, bf16[384,1024]{1,0:T(8,128)(2,1)}, u32[]{:S(2)}, u32[]{:S(2)}) collective-permute-start(bf16[384,1024]{1,0:T(8,128)(2,1)} %broadcast_select_fusion.6), channel_id=1, source_target_pairs={{0,16},{4,12},{8,24},{12,4},{16,0},{20,28},{24,8},{28,20},{1,17},{... | collective-permute-start | bytes 2359304 | tf_op jit(solution)/shard_map/ppermute | solution.py:923
  92.4 26.6 %collective-permute-start.9 = (bf16[4,8,128]{2,1,0:T(8,128)(2,1)}, bf16[4,8,128]{2,1,0:T(8,128)(2,1)}, u32[]{:S(2)}, u32[]{:S(2)}) collective-permute-start(bf16[4,8,128]{2,1,0:T(8,128)(2,1)} %pad_maximum_fusion.8), channel_id=1, source_target_pairs={{0,4},{4,0},{8,12},{12,8},{16,20},{20,16},{24,28},{28,24},{1,5},{5... | collective-permute-start | bytes 24584 | tf_op jit(solution)/shard_map/ppermute | solution.py:30
  99.2 54.5 %collective-permute-start.16 = (bf16[640,1024]{1,0:T(8,128)(2,1)}, bf16[640,1024]{1,0:T(8,128)(2,1)}, u32[]{:S(2)}, u32[]{:S(2)}) collective-permute-start(bf16[640,1024]{1,0:T(8,128)(2,1)} %constant_dynamic-update-slice_fusion.6.refs_0_), channel_id=1, source_target_pairs={{0,16},{4,20},{8,24},{12,28},{16,0},{20,4},{24,8},{28,12},{1,17},{... | collective-permute-start | bytes 3932168 | tf_op jit(solution)/shard_map/ppermute | solution.py:30
  99.7 54.0 %collective-permute-start.15 = (bf16[640,1024]{1,0:T(8,128)(2,1)}, bf16[640,1024]{1,0:T(8,128)(2,1)}, u32[]{:S(2)}, u32[]{:S(2)}) collective-permute-start(bf16[640,1024]{1,0:T(8,128)(2,1)} %constant_dynamic-update-slice_fusion.6.refs_0_), channel_id=1, source_target_pairs={{0,8},{4,12},{8,0},{12,4},{16,24},{20,28},{24,16},{28,20},{1,9},{5... | collective-permute-start | bytes 3932168 | tf_op jit(solution)/shard_map/ppermute | solution.py:30
  116.8 27.9 %collective-permute-start.12 = (bf16[640,1024]{1,0:T(8,128)(2,1)}, bf16[640,1024]{1,0:T(8,128)(2,1)}, u32[]{:S(2)}, u32[]{:S(2)}) collective-permute-start(bf16[640,1024]{1,0:T(8,128)(2,1)} %broadcast_select_fusion.3), channel_id=1, source_target_pairs={{0,16},{4,12},{8,24},{12,4},{16,0},{20,28},{24,8},{28,20},{1,17},{... | collective-permute-start | bytes 3932168 | tf_op jit(solution)/shard_map/ppermute | solution.py:923
  155.3 31.3 %collective-permute-start.17 = (bf16[640,1024]{1,0:T(8,128)(2,1)S(1)}, bf16[640,1024]{1,0:T(8,128)(2,1)}, u32[]{:S(2)}, u32[]{:S(2)}) collective-permute-start(bf16[640,1024]{1,0:T(8,128)(2,1)S(1)} %broadcast_select_fusion.2), channel_id=1, source_target_pairs={{0,16},{4,12},{8,24},{12,4},{16,0},{20,28},{24,8},{28,20},{1,17},{... | collective-permute-start | bytes 3932168 | tf_op jit(solution)/shard_map/ppermute | solution.py:923
  156.5 48.7 %collective-permute-start.19 = (bf16[640,1024]{1,0:T(8,128)(2,1)S(1)}, bf16[640,1024]{1,0:T(8,128)(2,1)S(1)}, u32[]{:S(2)}, u32[]{:S(2)}) collective-permute-start(bf16[640,1024]{1,0:T(8,128)(2,1)S(1)} %pad_maximum_fusion.refs_0_), channel_id=1, source_target_pairs={{0,16},{4,20},{8,24},{12,28},{16,0},{20,4},{24,8},{28,12},{1,17},{... | collective-permute-start | bytes 3932168 | tf_op jit(solution)/shard_map/ppermute | solution.py:30
  157.5 47.7 %collective-permute-start.18 = (bf16[640,1024]{1,0:T(8,128)(2,1)S(1)}, bf16[640,1024]{1,0:T(8,128)(2,1)S(1)}, u32[]{:S(2)}, u32[]{:S(2)}) collective-permute-start(bf16[640,1024]{1,0:T(8,128)(2,1)S(1)} %pad_maximum_fusion.refs_0_), channel_id=1, source_target_pairs={{0,8},{4,12},{8,0},{12,4},{16,24},{20,28},{24,16},{28,20},{1,9},{5... | collective-permute-start | bytes 3932168 | tf_op jit(solution)/shard_map/ppermute | solution.py:30
  206.7 27.8 %collective-permute-start.20 = (bf16[640,1024]{1,0:T(8,128)(2,1)S(1)}, bf16[640,1024]{1,0:T(8,128)(2,1)S(1)}, u32[]{:S(2)}, u32[]{:S(2)}) collective-permute-start(bf16[640,1024]{1,0:T(8,128)(2,1)S(1)} %broadcast_select_fusion.1), channel_id=1, source_target_pairs={{0,16},{4,12},{8,24},{12,4},{16,0},{20,28},{24,8},{28,20},{1,17},{... | collective-permute-start | bytes 3932168 | tf_op jit(solution)/shard_map/ppermute | solution.py:923
  207.3 43.4 %collective-permute-start.21 = (bf16[512,1024]{1,0:T(8,128)(2,1)}, bf16[512,1024]{1,0:T(8,128)(2,1)}, u32[]{:S(2)}, u32[]{:S(2)}) collective-permute-start(bf16[512,1024]{1,0:T(8,128)(2,1)} %get-tuple-element.173.x_ref), channel_id=1, source_target_pairs={{0,1},{1,0},{2,3},{3,2},{4,5},{5,4},{6,7},{7,6},{8,9},{9,8},{10,11... | collective-permute-start | bytes 3145736 | tf_op jit(solution)/shard_map/ppermute | solution.py:30
  211.0 51.4 %collective-permute-start.23 = (bf16[512,1024]{1,0:T(8,128)(2,1)S(1)}, bf16[512,1024]{1,0:T(8,128)(2,1)}, u32[]{:S(2)}, u32[]{:S(2)}) collective-permute-start(bf16[512,1024]{1,0:T(8,128)(2,1)S(1)} %pad_maximum_fusion.1.refs_0_), channel_id=1, source_target_pairs={{0,16},{4,20},{8,24},{12,28},{16,0},{20,4},{24,8},{28,12},{1,17},{... | collective-permute-start | bytes 3145736 | tf_op jit(solution)/shard_map/ppermute | solution.py:30
  212.5 50.0 %collective-permute-start.22 = (bf16[512,1024]{1,0:T(8,128)(2,1)S(1)}, bf16[512,1024]{1,0:T(8,128)(2,1)}, u32[]{:S(2)}, u32[]{:S(2)}) collective-permute-start(bf16[512,1024]{1,0:T(8,128)(2,1)S(1)} %pad_maximum_fusion.1.refs_0_), channel_id=1, source_target_pairs={{0,8},{4,12},{8,0},{12,4},{16,24},{20,28},{24,16},{28,20},{1,9},{5... | collective-permute-start | bytes 3145736 | tf_op jit(solution)/shard_map/ppermute | solution.py:30
  246.6 36.2 %collective-permute-start.26 = (bf16[640,1024]{1,0:T(8,128)(2,1)}, bf16[640,1024]{1,0:T(8,128)(2,1)S(1)}, u32[]{:S(2)}, u32[]{:S(2)}) collective-permute-start(bf16[640,1024]{1,0:T(8,128)(2,1)} %constant_dynamic-update-slice_fusion.8.refs_0_), channel_id=1, source_target_pairs={{0,16},{4,20},{8,24},{12,28},{16,0},{20,4},{24,8},{28,12},{1,17},{... | collective-permute-start | bytes 3932168 | tf_op jit(solution)/shard_map/ppermute | solution.py:30
  246.7 36.1 %collective-permute-start.25 = (bf16[640,1024]{1,0:T(8,128)(2,1)}, bf16[640,1024]{1,0:T(8,128)(2,1)S(1)}, u32[]{:S(2)}, u32[]{:S(2)}) collective-permute-start(bf16[640,1024]{1,0:T(8,128)(2,1)} %constant_dynamic-update-slice_fusion.8.refs_0_), channel_id=1, source_target_pairs={{0,8},{4,12},{8,0},{12,4},{16,24},{20,28},{24,16},{28,20},{1,9},{5... | collective-permute-start | bytes 3932168 | tf_op jit(solution)/shard_map/ppermute | solution.py:30
  263.8 31.4 %collective-permute-start.24 = (bf16[512,1024]{1,0:T(8,128)(2,1)S(1)}, bf16[512,1024]{1,0:T(8,128)(2,1)S(1)}, u32[]{:S(2)}, u32[]{:S(2)}) collective-permute-start(bf16[512,1024]{1,0:T(8,128)(2,1)S(1)} %broadcast_select_fusion.4), channel_id=1, source_target_pairs={{0,16},{4,12},{8,24},{12,4},{16,0},{20,28},{24,8},{28,20},{1,17},{... | collective-permute-start | bytes 3145736 | tf_op jit(solution)/shard_map/ppermute | solution.py:923
  284.3 26.6 %collective-permute-start.27 = (bf16[640,1024]{1,0:T(8,128)(2,1)S(1)}, bf16[640,1024]{1,0:T(8,128)(2,1)}, u32[]{:S(2)}, u32[]{:S(2)}) collective-permute-start(bf16[640,1024]{1,0:T(8,128)(2,1)S(1)} %broadcast_select_fusion), channel_id=1, source_target_pairs={{0,16},{4,12},{8,24},{12,4},{16,0},{20,28},{24,8},{28,20},{1,17},{... | collective-permute-start | bytes 3932168 | tf_op jit(solution)/shard_map/ppermute | solution.py:923
  354.3 31.9 %all-to-all-start = ((bf16[8,256,512]{2,1,0:T(8,128)(2,1)}), bf16[8,256,512]{2,1,0:T(8,128)(2,1)S(1)}, u32[]{:S(2)}, u32[]{:S(2)}) async-start(bf16[8,256,512]{2,1,0:T(8,128)(2,1)} %get-tuple-element.202), calls=%async_computation | async-start | bytes 4194304 | tf_op jit(solution)/shard_map/all_to_all | solution.py:1070
  393.8 27.3 %collective-permute-start.28 = (bf16[512,1024]{1,0:T(8,128)(2,1)}, bf16[512,1024]{1,0:T(8,128)(2,1)S(1)}, u32[]{:S(2)}, u32[]{:S(2)}) collective-permute-start(bf16[512,1024]{1,0:T(8,128)(2,1)} %shard_map.257), channel_id=1, source_target_pairs={{0,1},{1,0},{2,3},{3,2},{4,5},{5,4},{6,7},{7,6},{8,9},{9,8},{10,11... | collective-permute-start | bytes 3145736 | tf_op jit(solution)/shard_map/ppermute | solution.py:30
  414.7 32.4 %all-to-all-start.1 = ((f32[4,32,512]{2,1,0:T(8,128)}), f32[4,32,512]{2,1,0:T(8,128)S(1)}, u32[]{:S(2)}, u32[]{:S(2)}) async-start(f32[4,32,512]{2,1,0:T(8,128)} %param.35), calls=%async_computation.1 | async-start | bytes 524288 | tf_op jit(solution)/shard_map/all_to_all | solution.py:1003
  447.8 32.3 %all-to-all-start.2 = ((bf16[8,256,512]{2,1,0:T(8,128)(2,1)}), bf16[8,256,512]{2,1,0:T(8,128)(2,1)S(1)}, u32[]{:S(2)}, u32[]{:S(2)}) async-start(bf16[8,256,512]{2,1,0:T(8,128)(2,1)} %get-tuple-element.232), calls=%async_computation.2 | async-start | bytes 4194304 | tf_op jit(solution)/shard_map/all_to_all | solution.py:1070
  481.3 32.1 %all-to-all-start.3 = ((bf16[4,128,512]{2,1,0:T(8,128)(2,1)}), bf16[4,128,512]{2,1,0:T(8,128)(2,1)S(1)}, u32[]{:S(2)}, u32[]{:S(2)}) async-start(bf16[4,128,512]{2,1,0:T(8,128)(2,1)} %bitcast.24), calls=%async_computation.3 | async-start | bytes 1048576 | tf_op jit(solution)/shard_map/all_to_all | solution.py:1070
  521.0 26.4 %collective-permute-start.30 = (bf16[512,1024]{1,0:T(8,128)(2,1)}, bf16[512,1024]{1,0:T(8,128)(2,1)S(1)}, u32[]{:S(2)}, u32[]{:S(2)}) collective-permute-start(bf16[512,1024]{1,0:T(8,128)(2,1)} %shard_map.263), channel_id=1, source_target_pairs={{0,1},{1,0},{2,3},{3,2},{4,5},{5,4},{6,7},{7,6},{8,9},{9,8},{10,11... | collective-permute-start | bytes 3145736 | tf_op jit(solution)/shard_map/ppermute | solution.py:30
  525.8 34.1 %collective-permute-start.35 = (f32[128,512]{1,0:T(8,128)S(1)}, f32[128,512]{1,0:T(8,128)S(1)}, u32[]{:S(2)}, u32[]{:S(2)}) collective-permute-start(f32[128,512]{1,0:T(8,128)S(1)} %multiply_add_fusion.refs_0_), channel_id=1, source_target_pairs={{0,24},{4,28},{8,16},{12,20},{16,8},{20,12},{24,0},{28,4},{1,25},{... | collective-permute-start | bytes 786440 | tf_op jit(solution)/shard_map/ppermute | solution.py:30
  526.4 39.0 %collective-permute-start.34 = (f32[128,512]{1,0:T(8,128)S(1)}, f32[128,512]{1,0:T(8,128)S(1)}, u32[]{:S(2)}, u32[]{:S(2)}) collective-permute-start(f32[128,512]{1,0:T(8,128)S(1)} %multiply_add_fusion.refs_0_), channel_id=1, source_target_pairs={{0,20},{4,16},{8,28},{12,24},{16,4},{20,0},{24,12},{28,8},{1,21},{... | collective-permute-start | bytes 786440 | tf_op jit(solution)/shard_map/ppermute | solution.py:30
  559.9 35.5 %collective-permute-start.37 = (bf16[512,1024]{1,0:T(8,128)(2,1)S(1)}, bf16[512,1024]{1,0:T(8,128)(2,1)S(1)}, u32[]{:S(2)}, u32[]{:S(2)}) collective-permute-start(bf16[512,1024]{1,0:T(8,128)(2,1)S(1)} %copy-done.14), channel_id=1, source_target_pairs={{0,1},{1,0},{2,3},{3,2},{4,5},{5,4},{6,7},{7,6},{8,9},{9,8},{10,11... | collective-permute-start | bytes 3145736 | tf_op jit(solution)/shard_map/ppermute | solution.py:30
  561.7 27.0 %all-to-all-start.5 = ((f32[1,128,512]{2,0,1:T(1,128)}), f32[1,128,512]{2,0,1:T(1,128)S(1)}, u32[]{:S(2)}, u32[]{:S(2)}) async-start(f32[1,128,512]{2,0,1:T(1,128)} %copy.76), calls=%async_computation.5 | async-start | bytes 524288 | tf_op jit(solution)/shard_map/all_to_all | solution.py:1006
  (52 other events, 530.0 us)

commit v4 on v3

--- a/solution.py
+++ b/solution.py
@@ -268,6 +268,17 @@
     return place
 
 
+def place_of(me, piece):
+    odd = lax.rem(me, 2)
+    place = me
+    if piece % 4 in (1, 2):
+        first, second = (2, 4) if piece % 4 == 1 else (4, 2)
+        place = flipped(me, first) * (1 - odd) + flipped(me, second) * odd
+    elif piece % 4 == 3:
+        place = flipped(me, 6)
+    return place + (flipped(me, 2 * (piece - piece % 4)) - me)
+
+
 class Loader:
     def __init__(self, sems):
         self.local, self.send, self.recv, self.stored = sems
@@ -282,7 +293,7 @@
         block = len(self.copies)
         copies = []
         for i, piece in enumerate(pieces):
-            at = pl.multiple_of(flipped(self.me, 2 * i) * height, height)
+            at = pl.multiple_of(place_of(self.me, i) * height, height)
             source = piece.at[pl.ds(offset, height), columns]
             place = target.at[pl.ds(at, height), columns]
             near = pltpu.make_async_copy(source, place, self.local.at[block, i])
@@ -339,6 +350,7 @@
 ROWS = 64
 TILE = 512
 STAT = 128
+BIAS_ROWS = 16
 
 
 def normalise(z_ref, n_ref, r_ref, gain, low_ref):
@@ -498,8 +510,8 @@
     (up_hbm, down_hbm, adapt_hbm, wo_hbm), refs = refs[:4], refs[4:]
     if more:
         far_ref, refs = refs[0], refs[1:]
-    out_ref, dz_ref, dmix_ref, matrices_ref, g_first_ref, g_second_ref = refs[:6]
-    up, down, adapt, wo, dt_ref, e_ref, low_ref, du_ref, dpre_ref, sem = refs[6:]
+    out_ref, dz_ref, dmix_ref, matrices_ref = refs[:4]
+    up, down, adapt, wo, dt_ref, e_ref, low_ref, du_ref, dpre_ref, sem = refs[4:]
     blocks = up.shape[0]
     load(
         [adapt_hbm, down_hbm, slope_hbm, up_hbm, wo_hbm.at[0]],
@@ -527,8 +539,13 @@
         dpre_ref[:, columns] = bfloat(back * pre_slope_ref[:, columns].astype(jnp.float32))
 
     tiles(adapting, ADAPT, TILE)
-    g_first_ref[...] = jnp.sum(dpre_ref[...].astype(jnp.float32), axis=0, keepdims=True)
-    g_second_ref[...] = 4.0 * jnp.sum(e_ref[...].astype(jnp.float32), axis=0, keepdims=True)
+    first = jnp.sum(dpre_ref[...].astype(jnp.float32), axis=0, keepdims=True)
+    second = 4.0 * jnp.sum(e_ref[...].astype(jnp.float32), axis=0, keepdims=True)
+    row = lax.broadcasted_iota(jnp.int32, (BIAS_ROWS, ADAPT), 0)
+    biases = jnp.where(row == 1, second[:, :ADAPT], jnp.where(row == 2, second[:, ADAPT:], 0.0))
+    biases = bfloat(jnp.where(row == 0, first, biases))
+    for block in range(matrices_ref.shape[0]):
+        matrices_ref[block, 2 * height :, :] = biases
 
     wide = max(height, STAT)
 
@@ -538,7 +555,7 @@
         for i in range(wide // height):
             block, rows = columns.start // height + i, slice(i * height, (i + 1) * height)
             matrices_ref[block, :height, :] = down_grad[rows, :]
-            matrices_ref[block, height:, :] = up_grad[rows, :]
+            matrices_ref[block, height : 2 * height, :] = up_grad[rows, :]
 
     tiles(matrices, low_ref.shape[1], wide)
     loaded(down, sem.at[1])
@@ -635,7 +652,7 @@
 
 
 def muon_kernel(parts, *refs):
-    rows_refs, (out_ref, high, low, gram, poly, factor, left, right, rows_left) = refs[:parts], refs[parts:]
+    rows_refs, (out_ref, high, low, gram, poly, left, right, rows_left) = refs[:parts], refs[parts:]
     rows = rows_refs[0].shape[0]
     for i, ref in enumerate(rows_refs):
         high[i * rows : (i + 1) * rows, :], low[i * rows : (i + 1) * rows, :] = split(ref[...])
@@ -662,29 +679,22 @@
             jnp.where(eye, NEWTON_LINEAR, 0.0) + NEWTON_QUADRATIC * gram[...] + NEWTON_CUBIC * poly[...]
         )
         put_right(right, poly[...])
+        put_left(rows_left, out_ref[...])
+        multiply(out_ref, rows_left, right)
 
     def advance():
         multiply(gram, left, right)
         put_left(left, gram[...])
         multiply(gram, left, right)
 
-    polynomial()
-    factor[...] = poly[...]
-    advance()
-
-    @pl.loop(0, NS_ITERS - 2)
+    out_ref[...] = rows_refs[0][...] * scale
+
+    @pl.loop(0, NS_ITERS - 1)
     def _(i):
         polynomial()
         advance()
-        put_left(left, factor[...])
-        multiply(factor, left, right)
 
     polynomial()
-    put_left(left, factor[...])
-    multiply(factor, left, right)
-    put_right(right, factor[...])
-    put_left(rows_left, rows_refs[0][...] * scale)
-    multiply(out_ref, rows_left, right)
 
 
 HBM = pl.BlockSpec(memory_space=pltpu.HBM)
@@ -819,9 +829,7 @@
             ((rows, D), BF16),
             ((rows, D), F32),
             ((rows, D), BF16),
-            ((D // height, 2 * height, ADAPT), BF16),
-            ((1, ADAPT), F32),
-            ((1, D), F32),
+            ((D // height, 2 * height + BIAS_ROWS, ADAPT), BF16),
         ],
         [
             squares(hidden // D),
@@ -882,7 +890,6 @@
             pltpu.VMEM((rows * len(parts), ADAPT), BF16),
             full,
             full,
-            full,
             pltpu.VMEM((ADAPT, 3 * ADAPT), BF16),
             pltpu.VMEM((3 * ADAPT, ADAPT), BF16),
             pltpu.VMEM((rows, 3 * ADAPT), BF16),
@@ -906,33 +913,25 @@
 
     def begin(self, *after):
         array = tie(self.array, *after) if after else self.array
-        bits = axis_bits("wide")
-        self.pieces = {0: self.array}
-        for bit in bits[1:3]:
-            self.pieces[bit] = swap(array, "wide", bit)
+        steps = ((2, 4), (4, 2))
+        self.arrays = [self.array] + [
+            lax.ppermute(
+                array, "wide", [(i, i ^ steps[i % 2][which]) for i in range(lax.axis_size("wide"))]
+            )
+            for which in range(2)
+        ]
         return self
 
     def across(self, *after):
-        bits = axis_bits("wide")
-        near, far = bits[1:3]
-        pieces = self.pieces
-        even = lax.axis_index("wide") % 2 == 0
-        first, second = pieces[near], pieces[far]
-        if after:
-            first, second, *_ = lax.optimization_barrier((first, second, *after))
-        pieces[near | far] = lax.ppermute(
-            jnp.where(even, first, second),
-            "wide",
-            [(i, i ^ (near if i % 2 else far)) for i in range(lax.axis_size("wide"))],
+        first = tie(self.arrays[1], *after) if after else self.arrays[1]
+        self.arrays.append(
+            lax.ppermute(
+                first, "wide", [(i, i ^ (2 if i % 2 else 4)) for i in range(lax.axis_size("wide"))]
+            )
         )
-        for bit in bits[3:]:
-            for r in list(pieces):
-                pieces[r | bit] = swap(pieces[r], "wide", bit)
-        self.arrays = [pieces[r] for r in range(0, lax.axis_size("wide"), 2)]
+        for bit in axis_bits("wide")[3:]:
+            self.arrays += [swap(piece, "wide", bit) for piece in self.arrays]
         return self
-
-    def marks(self):
-        return list(self.pieces.values())[1:3]
 
 
 def gather_any_order(array, axis):
@@ -972,7 +971,8 @@
     enc_first = gather(stack(enc_qkv, gain_block))
     dec_first = gather(stack(dec_qkv[:3]))
     enc_up = gather(stack(enc_wo, *columns(enc_w_in)))
-    dec_second = gather(stack(dec_wo, dec_qkv[3:]))
+    dec_second = gather(stack(dec_wo[0], dec_qkv[3]))
+    dec_third = gather(stack(dec_qkv[4:], dec_wo[1]))
     dec_up = gather(stack(*columns(dec_w_in)))
 
     count = lax.axis_size("wide")
@@ -1000,11 +1000,10 @@
 
     repeat = lax.axis_size("narrow") // 4
     spread = lambda array: jnp.repeat(array, repeat, axis=0) if repeat > 1 else array
-    to_matrix = lambda array: lax.all_to_all(
-        spread(array), "narrow", split_axis=0, concat_axis=1, tiled=True
-    )[0]
-    to_rows = lambda array: lax.all_to_all(
-        array[None], "narrow", split_axis=1, concat_axis=0, tiled=True
+    exchange = lambda array, axis: lax.all_to_all(array, axis, split_axis=0, concat_axis=0, tiled=True)
+    to_matrix = lambda array: exchange(spread(array), "narrow").reshape(-1, ADAPT)
+    to_rows = lambda array: exchange(
+        array.reshape(lax.axis_size("narrow"), -1, ADAPT), "narrow"
     )[::repeat]
 
     dec_first.across(enc_value)
@@ -1012,8 +1011,12 @@
     enc_mix, enc_lse = attend(places, enc_query, enc_keys, enc_values, False)
     found = jnp.stack([p[at(3) : at(3) + 8, :height] for p in enc_first.arrays])
     found = jnp.concatenate([found, swap(tie(found, enc_mix), "wide", 1)])
-    order = lax.axis_index("wide") ^ jnp.arange(count)
-    order = order // 2 + order % 2 * (count // 2)
+    me = lax.axis_index("wide")
+    apart = me ^ jnp.arange(count)
+    odd = ((me ^ apart) & 1) == 1
+    low = apart & 6
+    piece = jnp.where(low == 0, 0, jnp.where(low == 6, 3, jnp.where((low == 2) ^ odd, 1, 2)))
+    order = (apart & 1) * (count // 2) + (apart >> 3) * 4 + piece
     gains = found[order].transpose(1, 0, 2).reshape(8, D).astype(jnp.float32)
     enc_down = gather(stack(enc_w_out, tie(beside(0), enc_mix)))
     dec_down = gather(stack(dec_w_out, tie(beside(1), enc_mix)))
@@ -1030,32 +1033,34 @@
     )
     enc_down.across(enc_norm1[0])
     enc_slope, enc_inner, enc_up_full = tail_up(3, enc_norm1[0], gains, enc_up, at(1), 0)
-    dec_up.begin(enc_inner)
+    dec_second.across(enc_inner)
+    dec_third.begin(enc_inner)
     enc_pre_slope, enc_adapt, *enc_norm2, enc_low, enc_down_full, enc_adapt_full = tail_down(
         4, enc_norm1[0], enc_inner, gains, bias_in[0], bias_out[0], enc_down, (0, at(4)), (0, 1)
     )
     enc_low_far = partner(enc_low)
-    dec_second.across(enc_low)
+    dec_third.across(enc_low)
     *dec_norm1, cross_query, dec_q_full = settle(
-        5, dec_in, tie(self_mix, enc_low), gains, dec_second, at(0), at(2), (None, 2)
-    )
+        5, dec_in, tie(self_mix, enc_low), gains, dec_second, at(0), at(1), (None, 2)
+    )
+    dec_up.begin(cross_query)
     dec_down.begin(cross_query)
     cross_key, cross_value, cross_key_far, cross_value_far, dec_kv_full = project(
-        6, tie(enc_low, cross_query), enc_low_far, dec_second, (at(3), at(4))
+        6, tie(enc_low, cross_query), enc_low_far, dec_third, (at(0), at(1))
     )
     cross_keys, cross_values = (cross_key, cross_key_far), (cross_value, cross_value_far)
     dec_up.across(cross_key)
     cross_mix, cross_lse = attend(places, cross_query, cross_keys, cross_values, False)
-    dec_down.across(cross_mix)
     *dec_norm2, dec_wo_full = settle(
-        7, dec_norm1[0], cross_mix, gains, dec_second, at(1), None, (2, 3)
-    )
+        7, dec_norm1[0], cross_mix, gains, dec_third, at(2), None, (2, 3)
+    )
+    dec_down.across(dec_norm2[0])
     dec_slope, dec_inner, dec_up_full = tail_up(8, dec_norm2[0], gains, dec_up, at(0), 3)
     dec_pre_slope, dec_adapt, *dec_norm3, _, dec_down_full, dec_adapt_full = tail_down(
         9, dec_norm2[0], dec_inner, gains, bias_in[1], bias_out[1], dec_down, (0, at(4)), (3, 4)
     )
 
-    dec_out, grad_z2, grad_cross_mix, dec_matrices, grad_dec_first, grad_dec_second = tail_back(
+    dec_out, grad_z2, grad_cross_mix, dec_matrices = tail_back(
         height,
         dec_cot,
         dec_norm3,
@@ -1067,7 +1072,6 @@
         (dec_up_full, dec_down_full, dec_adapt_full, dec_wo_full),
         (3, 4),
     )
-    exchange = lambda array, axis: lax.all_to_all(array, axis, split_axis=0, concat_axis=0, tiled=True)
     total = lambda array: jnp.sum(array.astype(jnp.float32), axis=0)
     dec_matrices = exchange(dec_matrices, "wide")
     cross_back = attend_back(
@@ -1087,7 +1091,7 @@
         dec_q_full,
         2,
     )
-    enc_out, grad_ez1, grad_enc_mix, enc_matrices, grad_enc_first, grad_enc_second = tail_back(
+    enc_out, grad_ez1, grad_enc_mix, enc_matrices = tail_back(
         height,
         tie(grad_encoded, grad_z1),
         enc_norm2,
@@ -1107,13 +1111,24 @@
         places, tie(grad_self_mix, grad_ez1), self_query, self_keys, self_values, self_mix, self_lse, True, (old_momentum,)
     )
 
-    sums = jnp.concatenate([total(tie(enc_matrices, self_back[0])), dec_sums])
-    sums = spread(bfloat(sums).reshape(4, height, ADAPT))
+    enc_sums = total(tie(enc_matrices, self_back[0]))
+    sums = [array[at(i) : at(i + 1)] for array in (enc_sums, dec_sums) for i in range(2)]
+    biases = jnp.concatenate([array[at(2) : at(2) + BIAS_ROWS // 2] for array in (enc_sums, dec_sums)])
+    sums = jnp.stack([jnp.concatenate([array, biases]) for array in sums])
+    sums = spread(bfloat(sums))
     enc_back = attend_back(
         places, tie(grad_enc_mix, sums), enc_query, enc_keys, enc_values, enc_mix, enc_lse, False
     )
     summed = exchange(sums, "narrow")
-    momentum = DECAY * old_momentum + total(tie(summed, enc_back[0]))
+    summed = total(tie(summed, enc_back[0]))
+    momentum = DECAY * old_momentum + summed[:height]
+    layers = summed[height:].reshape(2, -1, ADAPT)
+    place = lax.axis_index("wide") * lax.axis_size("narrow") + lax.axis_index("narrow")
+    devices = lax.axis_size("wide") * lax.axis_size("narrow")
+    own_part = lambda array: lax.dynamic_slice_in_dim(
+        array, place * (array.shape[1] // devices), array.shape[1] // devices, 1
+    )
+    grad_bias_in, grad_bias_out = own_part(layers[:, 0]), own_part(layers[:, 1:3].reshape(2, D))
     parts = [momentum] + [swap(momentum, "wide", r) for r in range(1, lax.axis_size("wide"))]
     new_momenta = to_rows(momentum)
 
@@ -1130,17 +1145,6 @@
         (0, 1, 2),
         F32,
     )
-    devices = lax.axis_size("wide") * lax.axis_size("narrow")
-    slices = lambda first, second: jnp.concatenate([first, second]).reshape(2, devices, -1).transpose(1, 0, 2)
-    firsts = slices(tie(grad_enc_first, far_enc), grad_dec_first)
-    seconds = slices(tie(grad_enc_second, far_enc), grad_dec_second)
-    biases = jnp.concatenate([firsts.reshape(devices, -1), seconds.reshape(devices, -1)], axis=1)
-    used = biases.shape[1]
-    biases = jnp.pad(biases, ((0, 0), (0, -used % STAT)))
-    biases = jnp.sum(exchange(biases, ("wide", "narrow")), axis=0)[:used]
-    grad_bias_in = biases[: firsts[0].size].reshape(firsts.shape[1:])
-    grad_bias_out = biases[firsts[0].size :].reshape(seconds.shape[1:])
-
     orthogonal = muon([parts[0], tie(parts[1], grad_dec), *parts[2:]])
     grad_enc = back(
         (tie(grad_ez1, orthogonal), near_enc),

time: 620 us -> 582 us (0.939)
  other arithmetic: 19.5 us -> 8.15 us
  waiting for transfers between devices: 60.3 us -> 49.9 us
  local copies, waits for them, and re-layouts: 40.3 us -> 31.2 us
    ppermute x31 -> x17, starting transfers between devices: 48.2 us -> 20.6 us  [swap(): lax.ppermute(array, axis, [(i, i ^ bit) for i in range(lax.axis_size(axis...]
    ppermute x7 -> x24, starting transfers between devices: 6.22 us -> 31.7 us  [the longest x16 23.3 us: begin(): lax.ppermute(array, 'wide', [(i, i ^ steps[i % 2][which]) for i in range(...]
    all_to_all x3 -> x0, starting transfers between devices: 11.8 us -> none  [the longest x2 8.23 us: shards(): lax.all_to_all(array[None], 'narrow', split_axis=1, concat_axis=0, tiled=...]
    all_to_all x4 -> x6, starting transfers between devices: 14.9 us -> 24 us  [shards(): lax.all_to_all(array, axis, split_axis=0, concat_axis=0, tiled=True)]
    select_n x7 -> x0, other arithmetic: 7.79 us -> none  [across(): jnp.where(even, first, second)]
    ppermute x7 -> x24, waiting for transfers between devices: 45.1 us -> 38 us  [the longest x8 34.9 us: across(): lax.ppermute(first, 'wide', [(i, i ^ (2 if i % 2 else 4)) for i in range(...]
    unnamed x90 -> x83, local copies, waits for them, and re-layouts: 18.9 us -> 16 us
    ppermute x31 -> x17, waiting for transfers between devices: 14.7 us -> 11.9 us  [swap(): lax.ppermute(array, axis, [(i, i ^ bit) for i in range(lax.axis_size(axis...]
  transfers between devices with their start and end apart: 45 -> 47, of which waited for: 10 -> 9; matrix products, arithmetic and copies ran while one was open for 7% -> 4% of each run, Pallas kernels for 57% -> 61%
where the time goes in v4:
time: 582 us; the launch traced here: 571 us
  Pallas kernels  403 us (69%)
  starting transfers between devices  76.3 us (13%)
  waiting for transfers between devices  49.9 us (9%)
  local copies, waits for them, and re-layouts  31.2 us (5%)
  other arithmetic  8.15 us (1%)
    pallas_call x20, Pallas kernels, call(): pl.pallas_call(kernel, in_specs=specs, out_specs=[IN_VMEM if len(out) ==...  264 us
    pallas_call x3, Pallas kernels, attend_back(): pl.pallas_call(lambda *refs: attend_back_kernel(causal, 256, *refs[:12],...  84.7 us
    pallas_call x3, Pallas kernels, attend(): pl.pallas_call(functools.partial(attend_kernel, causal, 256), grid=(pairs...  54.5 us
    ppermute x8, waiting for transfers between devices, across(): lax.ppermute(first, 'wide', [(i, i ^ (2 if i % 2 else 4)) for i in range(...  34.9 us
    all_to_all x6, starting transfers between devices, shards(): lax.all_to_all(array, axis, split_axis=0, concat_axis=0, tiled=True)  24 us
    ppermute x16, starting transfers between devices, begin(): lax.ppermute(array, 'wide', [(i, i ^ steps[i % 2][which]) for i in range(...  23.3 us
    ppermute x17, starting transfers between devices, swap(): lax.ppermute(array, axis, [(i, i ^ bit) for i in range(lax.axis_size(axis...  20.6 us
    unnamed x83, local copies, waits for them, and re-layouts  16 us
  transfers between devices with their start and end apart: 47, of which 9 were waited for; matrix products, arithmetic and copies ran while one was open for 4% of the time, Pallas kernels for 61%

profile of v4, /device:TPU:0, one launch (start us, length us, event | category | flops | bytes accessed | tf_op | source)
XLA Modules:
  0.0 570.7 jit_solution(14130124958168869737)
XLA Ops:
  29.6 8.0 %collective-permute-done.1.refs_3_ = bf16[400,1024]{1,0:T(8,128)(2,1)S(1)} collective-permute-done((bf16[400,1024]{1,0:T(8,128)(2,1)}, bf16[400,1024]{1,0:T(8,128)(2,1)S(1)}, u32[]{:S(2)}, u32[]{:S(2)}) %collective-permute-start.1) | collective-permute-done | bytes 819232 | tf_op jit(solution)/shard_map/ppermute | solution.py:928
  44.6 13.7 %shard_map.242 = (bf16[512,1024]{1,0:T(8,128)(2,1)}, bf16[512,1024]{1,0:T(8,128)(2,1)}, bf16[512,1024]{1,0:T(8,128)(2,1)}, bf16[512,1024]{1,0:T(8,128)(2,1)}, bf...) custom-call(bf16[512,1024]{1,0:T(8,128)(2,1)} %x_ref.4, bf16[512,1024]{1,0:T(8,128)(2,1)} %collective-permute-done.3.far_ref, ...), custom_call_target="tpu_custom_call" | custom-call | flops 5368709120 | bytes 5373952 | tf_op jit(solution)/shard_map/pallas_call | solution.py:710
  64.3 18.2 %shard_map.243 = (bf16[512,1024]{1,0:T(8,128)(2,1)}, f32[8,8,512]{2,1,0:T(8,128)}) custom-call(s32[1]{0:T(128)} %bitcast.half_ref.refs_0_, s32[1,512]{1,0:T(1,128)} %bitcast.1.qid_ref.refs_1_, s32[512,1]{1,0:T(8,128)} %copy.47.kid_own_ref.refs_2_, s32[512,1]{1,0:T(8,128)} %copy.48.kid_far_ref.refs_3_, bf16[512,1024]{1,0:T(8,128)(2,1)} %get-tuple-element.128.q_ref.refs_4_, ...), custom_call_target="tpu_custom_call" | custom-call | flops 8589934592 | bytes 6291456 | tf_op jit(solution)/shard_map/pallas_call | solution.py:220
  87.9 13.7 %shard_map.244 = (bf16[512,1024]{1,0:T(8,128)(2,1)}, bf16[512,1024]{1,0:T(8,128)(2,1)}, bf16[512,1024]{1,0:T(8,128)(2,1)}, bf16[512,1024]{1,0:T(8,128)(2,1)}, bf...) custom-call(bf16[512,1024]{1,0:T(8,128)(2,1)} %x_ref.5, bf16[512,1024]{1,0:T(8,128)(2,1)} %collective-permute-done.5.far_ref, ...), custom_call_target="tpu_custom_call" | custom-call | flops 5368709120 | bytes 5242880 | tf_op jit(solution)/shard_map/pallas_call | solution.py:710
  105.8 18.2 %shard_map.245 = (bf16[512,1024]{1,0:T(8,128)(2,1)}, f32[8,8,512]{2,1,0:T(8,128)}) custom-call(s32[1]{0:T(128)} %bitcast.half_ref.refs_0_, s32[1,512]{1,0:T(1,128)} %bitcast.1.qid_ref.refs_1_, s32[512,1]{1,0:T(8,128)} %copy.47.kid_own_ref.refs_2_, s32[512,1]{1,0:T(8,128)} %copy.48.kid_far_ref.refs_3_, bf16[512,1024]{1,0:T(8,128)(2,1)} %get-tuple-element.138.q_ref.refs_4_, ...), custom_call_target="tpu_custom_call" | custom-call | flops 8589934592 | bytes 6291456 | tf_op jit(solution)/shard_map/pallas_call | solution.py:220
  124.0 4.5 collective-permute-done.12.refs_3_
  129.5 9.0 %shard_map.246 = (f32[512,1024]{1,0:T(8,128)}, f32[512,128]{1,0:T(8,128)}, bf16[1,1024,1024]{2,1,0:T(8,128)(2,1)}) custom-call(bf16[512,1024]{1,0:T(8,128)(2,1)} %x_ref.4, bf16[512,1024]{1,0:T(8,128)(2,1)} %get-tuple-element.144.mix_ref.refs_9_, f32[8,1024]{1,0:T(8,128)} %convert_bitcast_fusion.1.gains_ref.refs_5_, ...), custom_call_target="tpu_custom_call" | custom-call | flops 1073741824 | bytes 7372800 | tf_op jit(solution)/shard_map/pallas_call | solution.py:710
  143.6 15.1 %shard_map.247 = (bf16[512,4096]{1,0:T(8,128)(2,1)}, bf16[512,4096]{1,0:T(8,128)(2,1)}, bf16[4,1024,1024]{2,1,0:T(8,128)(2,1)}) custom-call(f32[512,1024]{1,0:T(8,128)} %get-tuple-element.148.n_ref.refs_3_, f32[8,1024]{1,0:T(8,128)} %convert_bitcast_fusion.1.gains_ref.refs_5_, bf16[640,1024]{1,0:T(8,128)(2,1)} %slice_dynamic-update-slice_fusion.refs_0_, ...), custom_call_target="tpu_custom_call" | custom-call | flops 4294967296 | bytes 7372800 | tf_op jit(solution)/shard_map/pallas_call | solution.py:710
  162.6 18.6 %shard_map.248 = (bf16[512,512]{1,0:T(8,128)(2,1)}, bf16[512,512]{1,0:T(8,128)(2,1)}, f32[512,1024]{1,0:T(8,128)}, f32[512,128]{1,0:T(8,128)}, bf16[512,1024]{1,...) custom-call(f32[512,1024]{1,0:T(8,128)} %get-tuple-element.148.n_ref.refs_3_, ...), custom_call_target="tpu_custom_call" | custom-call | flops 5368709120 | bytes 11573248 | tf_op jit(solution)/shard_map/pallas_call | solution.py:710
  184.0 11.0 %shard_map.249 = (f32[512,1024]{1,0:T(8,128)}, f32[512,128]{1,0:T(8,128)}, bf16[512,1024]{1,0:T(8,128)(2,1)}, bf16[2,1024,1024]{2,1,0:T(8,128)(2,1)}) custom-call(bf16[512,1024]{1,0:T(8,128)(2,1)} %x_ref.5, bf16[512,1024]{1,0:T(8,128)(2,1)} %get-tuple-element.155.mix_ref.refs_9_, f32[8,1024]{1,0:T(8,128)} %convert_bitcast_fusion.1.gains_ref.refs_5_, ...), custom_call_target="tpu_custom_call" | custom-call | flops 2147483648 | bytes 4227072 | tf_op jit(solution)/shard_map/pallas_call | solution.py:710
  199.4 7.6 %collective-permute-done.24.refs_3_ = bf16[384,1024]{1,0:T(8,128)(2,1)} collective-permute-done((bf16[384,1024]{1,0:T(8,128)(2,1)S(1)}, bf16[384,1024]{1,0:T(8,128)(2,1)}, u32[]{:S(2)}, u32[]{:S(2)}) %collective-permute-start.24) | collective-permute-done | bytes 786464 | tf_op jit(solution)/shard_map/ppermute | solution.py:928
  208.7 11.7 %shard_map.250 = (bf16[512,1024]{1,0:T(8,128)(2,1)}, bf16[512,1024]{1,0:T(8,128)(2,1)}, bf16[512,1024]{1,0:T(8,128)(2,1)}, bf16[512,1024]{1,0:T(8,128)(2,1)}, bf16[2,1024,1024]{2,1,0:T(8,128)(2,1)}) custom-call(bf16[512,1024]{1,0:T(8,128)(2,1)} %get-tuple-element.159.x_ref, bf16[512,1024]{1,0:T(8,128)(2,1)} %collective-permute-done.21.far_ref, ...), custom_call_target="tpu_custom_call" | custom-call | flops 4294967296 | bytes 5242880 | tf_op jit(solution)/shard_map/pallas_call | solution.py:710
  223.0 18.2 %shard_map.251 = (bf16[512,1024]{1,0:T(8,128)(2,1)}, f32[8,8,512]{2,1,0:T(8,128)}) custom-call(s32[1]{0:T(128)} %bitcast.half_ref.refs_0_, s32[1,512]{1,0:T(1,128)} %bitcast.1.qid_ref.refs_1_, s32[512,1]{1,0:T(8,128)} %copy.47.kid_own_ref.refs_2_, s32[512,1]{1,0:T(8,128)} %copy.48.kid_far_ref.refs_3_, bf16[512,1024]{1,0:T(8,128)(2,1)} %get-tuple-element.158.q_ref.refs_4_, ...), custom_call_target="tpu_custom_call" | custom-call | flops 8589934592 | bytes 6291456 | tf_op jit(solution)/shard_map/pallas_call | solution.py:220
  241.2 9.6 %shard_map.252 = (f32[512,1024]{1,0:T(8,128)}, f32[512,128]{1,0:T(8,128)}, bf16[1,1024,1024]{2,1,0:T(8,128)(2,1)}) custom-call(f32[512,1024]{1,0:T(8,128)} %get-tuple-element.167.x_ref.n_ref, bf16[512,1024]{1,0:T(8,128)(2,1)} %get-tuple-element.166.mix_ref.refs_9_, f32[8,1024]{1,0:T(8,128)} %convert_bitcast_fusion.1.gains_ref.refs_5_, ...), custom_call_target="tpu_custom_call" | custom-call | flops 1073741824 | bytes 6324224 | tf_op jit(solution)/shard_map/pallas_call | solution.py:710
  251.1 13.1 %collective-permute-done.27.refs_3_ = bf16[512,1024]{1,0:T(8,128)(2,1)} collective-permute-done((bf16[512,1024]{1,0:T(8,128)(2,1)}, bf16[512,1024]{1,0:T(8,128)(2,1)}, u32[]{:S(2)}, u32[]{:S(2)}) %collective-permute-start.27) | collective-permute-done | bytes 1048608 | tf_op jit(solution)/shard_map/ppermute | solution.py:928
  264.2 14.7 %shard_map.253 = (bf16[512,4096]{1,0:T(8,128)(2,1)}, bf16[512,4096]{1,0:T(8,128)(2,1)}, bf16[4,1024,1024]{2,1,0:T(8,128)(2,1)}) custom-call(f32[512,1024]{1,0:T(8,128)} %get-tuple-element.168.n_ref.refs_3_, f32[8,1024]{1,0:T(8,128)} %convert_bitcast_fusion.1.gains_ref.refs_5_, bf16[512,1024]{1,0:T(8,128)(2,1)} %copy-done.15, ...), custom_call_target="tpu_custom_call" | custom-call | flops 4294967296 | bytes 6324224 | tf_op jit(solution)/shard_map/pallas_call | solution.py:710
  280.5 18.6 %shard_map.254 = (bf16[512,512]{1,0:T(8,128)(2,1)}, bf16[512,512]{1,0:T(8,128)(2,1)}, f32[512,1024]{1,0:T(8,128)}, f32[512,128]{1,0:T(8,128)}, bf16[512,1024]{1,...) custom-call(f32[512,1024]{1,0:T(8,128)} %get-tuple-element.168.n_ref.refs_3_, ...), custom_call_target="tpu_custom_call" | custom-call | flops 5368709120 | bytes 11573248 | tf_op jit(solution)/shard_map/pallas_call | solution.py:710
  299.1 24.6 %shard_map.255 = (bf16[512,1024]{1,0:T(8,128)(2,1)}, f32[512,1024]{1,0:T(8,128)}, bf16[512,1024]{1,0:T(8,128)(2,1)}, bf16[8,272,512]{2,1,0:T(8,128)(2,1)}) custom-call(bf16[512,1024]{1,0:T(8,128)(2,1)} %refs_0_.1, f32[512,1024]{1,0:T(8,128)} %get-tuple-element.175.refs_1_, f32[512,128]{1,0:T(8,128)} %get-tuple-element.176.refs_2_, ...), custom_call_target="tpu_custom_call" | custom-call | flops 12884901888 | bytes 32014336 | tf_op jit(solution)/shard_map/pallas_call | solution.py:710
  327.7 28.2 %shard_map.256 = (bf16[512,1024]{1,0:T(8,128)(2,1)}, bf16[512,1024]{1,0:T(8,128)(2,1)}, bf16[512,1024]{1,0:T(8,128)(2,1)}, bf16[512,1024]{1,0:T(8,128)(2,1)}, bf16[512,1024]{1,0:T(8,128)(2,1)}) custom-call(s32[1]{0:T(128)} %bitcast.half_ref.refs_0_, s32[1,512]{1,0:T(1,128)} %bitcast.1.qid_ref.refs_1_, s32[512,1]{1,0:T(8,128)} %copy.47.kid_own_ref.refs_2_, ...), custom_call_target="tpu_custom_call" | custom-call | flops 21474836480 | bytes 12582912 | tf_op jit(solution)/shard_map/pallas_call | solution.py:244
  356.2 7.4 %shard_map.257 = bf16[512,1024]{1,0:T(8,128)(2,1)} custom-call(bf16[512,1024]{1,0:T(8,128)(2,1)} %get-tuple-element.191.refs_0_, bf16[512,1024]{1,0:T(8,128)(2,1)} %get-tuple-element.192.refs_1_, bf16[2,1024,1024]{2,1,0:T(8,128)(2,1)} %get-tuple-element.193.refs_2_.refs_3_), custom_call_target="tpu_custom_call" | custom-call | flops 2147483648 | bytes 6291456 | tf_op jit(solution)/shard_map/pallas_call | solution.py:710
  365.3 8.0 %shard_map.258.refs_0_ = f32[512,1024]{1,0:T(8,128)} custom-call(bf16[512,1024]{1,0:T(8,128)(2,1)} %refs_0_.2, bf16[512,1024]{1,0:T(8,128)(2,1)} %get-tuple-element.195.refs_1_, bf16[512,1024]{1,0:T(8,128)(2,1)} %get-tuple-element.196.refs_2_, bf16[2,1024,1024]{2,1,0:T(8,128)(2,1)} %get-tuple-element.193.refs_2_.refs_3_), custom_call_target="tpu_custom_call" | custom-call | flops 2147483648 | bytes 7340032 | tf_op jit(solution)/shard_map/pallas_call | solution.py:710
  373.3 9.5 %shard_map.259 = (f32[512,1024]{1,0:T(8,128)}, bf16[512,1024]{1,0:T(8,128)(2,1)}) custom-call(f32[512,1024]{1,0:T(8,128)} %get-tuple-element.198.dz_ref, bf16[512,1024]{1,0:T(8,128)(2,1)} %get-tuple-element.189.dq_ref, f32[512,1024]{1,0:T(8,128)} %get-tuple-element.167.x_ref.n_ref, f32[512,128]{1,0:T(8,128)} %get-tuple-element.199.r_ref, ...), custom_call_target="tpu_custom_call" | custom-call | flops 2147483648 | bytes 9732096 | tf_op jit(solution)/shard_map/pallas_call | solution.py:710
  390.7 25.1 %shard_map.260 = (bf16[512,1024]{1,0:T(8,128)(2,1)}, f32[512,1024]{1,0:T(8,128)}, bf16[512,1024]{1,0:T(8,128)(2,1)}, bf16[8,272,512]{2,1,0:T(8,128)(2,1)}) custom-call(f32[512,1024]{1,0:T(8,128)} %shard_map.258.refs_0_, f32[512,1024]{1,0:T(8,128)} %get-tuple-element.203.refs_1_, f32[512,128]{1,0:T(8,128)} %get-tuple-element.204.refs_2_, ...), custom_call_target="tpu_custom_call" | custom-call | flops 12884901888 | bytes 34111488 | tf_op jit(solution)/shard_map/pallas_call | solution.py:710
  420.8 28.3 %shard_map.261 = (bf16[512,1024]{1,0:T(8,128)(2,1)}, bf16[512,1024]{1,0:T(8,128)(2,1)}, bf16[512,1024]{1,0:T(8,128)(2,1)}, bf16[512,1024]{1,0:T(8,128)(2,1)}, bf16[512,1024]{1,0:T(8,128)(2,1)}) custom-call(s32[1]{0:T(128)} %bitcast.half_ref.refs_0_, s32[1,512]{1,0:T(1,128)} %bitcast.1.qid_ref.refs_1_, s32[512,1]{1,0:T(8,128)} %copy.47.kid_own_ref.refs_2_, ...), custom_call_target="tpu_custom_call" | custom-call | flops 21474836480 | bytes 12582912 | tf_op jit(solution)/shard_map/pallas_call | solution.py:244
  454.3 28.2 %shard_map.262 = (bf16[512,1024]{1,0:T(8,128)(2,1)}, bf16[512,1024]{1,0:T(8,128)(2,1)}, bf16[512,1024]{1,0:T(8,128)(2,1)}, bf16[512,1024]{1,0:T(8,128)(2,1)}, bf16[512,1024]{1,0:T(8,128)(2,1)}) custom-call(s32[1]{0:T(128)} %bitcast.half_ref.refs_0_, s32[1,512]{1,0:T(1,128)} %bitcast.1.qid_ref.refs_1_, s32[512,1]{1,0:T(8,128)} %copy.47.kid_own_ref.refs_2_, ...), custom_call_target="tpu_custom_call" | custom-call | flops 21474836480 | bytes 12582912 | tf_op jit(solution)/shard_map/pallas_call | solution.py:244
  483.3 7.3 %shard_map.263 = bf16[512,1024]{1,0:T(8,128)(2,1)} custom-call(bf16[512,1024]{1,0:T(8,128)(2,1)} %get-tuple-element.231.refs_0_, bf16[512,1024]{1,0:T(8,128)(2,1)} %get-tuple-element.232.refs_1_, bf16[3,1024,1024]{2,1,0:T(8,128)(2,1)} %get-tuple-element.233.refs_2_.refs_5_), custom_call_target="tpu_custom_call" | custom-call | flops 2147483648 | bytes 8388608 | tf_op jit(solution)/shard_map/pallas_call | solution.py:710
  497.4 7.4 %shard_map.264 = bf16[512,1024]{1,0:T(8,128)(2,1)} custom-call(bf16[512,1024]{1,0:T(8,128)(2,1)} %get-tuple-element.234.refs_0_, bf16[512,1024]{1,0:T(8,128)(2,1)} %get-tuple-element.235.refs_1_, bf16[3,1024,1024]{2,1,0:T(8,128)(2,1)} %get-tuple-element.236.refs_2_.refs_5_), custom_call_target="tpu_custom_call" | custom-call | flops 2147483648 | bytes 8388608 | tf_op jit(solution)/shard_map/pallas_call | solution.py:710
  510.8 8.3 %collective-permute-done.33.refs_1_ = bf16[512,1024]{1,0:T(8,128)(2,1)S(1)} collective-permute-done((bf16[512,1024]{1,0:T(8,128)(2,1)}, bf16[512,1024]{1,0:T(8,128)(2,1)S(1)}, u32[]{:S(2)}, u32[]{:S(2)}) %collective-permute-start.33) | collective-permute-done | bytes 1048608 | tf_op jit(solution)/shard_map/ppermute | solution.py:30
  521.1 10.7 %shard_map.265 = f32[512,1024]{1,0:T(8,128)} custom-call(f32[512,1024]{1,0:T(8,128)} %get-tuple-element.237.refs_0_, bf16[512,1024]{1,0:T(8,128)(2,1)} %copy-done.4, bf16[512,1024]{1,0:T(8,128)(2,1)} %get-tuple-element.222.refs_2_, bf16[512,1024]{1,0:T(8,128)(2,1)} %get-tuple-element.238.refs_3_, bf16[512,1024]{1,0:T(8,128)(2,1)} %get-tuple-element.239.refs_4_, ...), custom_call_target="tpu_custom_call" | custom-call | flops 3221225472 | bytes 12582912 | tf_op jit(solution)/shard_map/pallas_call | solution.py:710
  533.5 17.9 %shard_map.266 = f32[128,512]{1,0:T(8,128)} custom-call(f32[128,512]{1,0:T(8,128)} %slice_add_fusion.refs_0_, f32[128,512]{1,0:T(8,128)} %copy-done.31, f32[128,512]{1,0:T(8,128)} %copy-done.34, f32[128,512]{1,0:T(8,128)} %copy-done.33, f32[128,512]{1,0:T(8,128)} %copy-done.32, f32[128,512]{1,0:T(8,128)} %collective-permute-done.37.refs_5_, ...), custom_call_target="tpu_custom_call" | custom-call | flops 16106127360 | bytes 2097152 | tf_op jit(solution)/shard_map/pallas_call | solution.py:710
  551.4 5.3 all-to-all-start.5
  558.4 10.7 %shard_map.267 = f32[512,1024]{1,0:T(8,128)} custom-call(f32[512,1024]{1,0:T(8,128)} %get-tuple-element.241.refs_0_, bf16[512,1024]{1,0:T(8,128)(2,1)} %copy-done.5, bf16[512,1024]{1,0:T(8,128)(2,1)} %get-tuple-element.227.refs_2_, bf16[512,1024]{1,0:T(8,128)(2,1)} %get-tuple-element.242.refs_3_, bf16[512,1024]{1,0:T(8,128)(2,1)} %get-tuple-element.243.refs_4_, ...), custom_call_target="tpu_custom_call" | custom-call | flops 3221225472 | bytes 12582912 | tf_op jit(solution)/shard_map/pallas_call | solution.py:710
  (225 shorter events, 118.7 us)
Async XLA Ops:
  3.6 24.0 %collective-permute-start.4 = (bf16[400,1024]{1,0:T(8,128)(2,1)}, bf16[400,1024]{1,0:T(8,128)(2,1)}, u32[]{:S(2)}, u32[]{:S(2)}) collective-permute-start(bf16[400,1024]{1,0:T(8,128)(2,1)} %pad_maximum_fusion.1.refs_0_), channel_id=1, source_target_pairs={{0,16},{4,12},{8,24},{12,4},{16,0},{20,28},{24,8},{28,20},{1,17},{... | collective-permute-start | bytes 2457608 | tf_op jit(solution)/shard_map/ppermute | solution.py:918
  8.0 35.0 %collective-permute-start.3 = (bf16[512,1024]{1,0:T(8,128)(2,1)S(1)}, bf16[512,1024]{1,0:T(8,128)(2,1)}, u32[]{:S(2)}, u32[]{:S(2)}) collective-permute-start(bf16[512,1024]{1,0:T(8,128)(2,1)S(1)} %copy-done.6), channel_id=1, source_target_pairs={{0,1},{1,0},{2,3},{3,2},{4,5},{5,4},{6,7},{7,6},{8,9},{9,8},{10,11... | collective-permute-start | bytes 3145736 | tf_op jit(solution)/shard_map/ppermute | solution.py:30
  37.6 48.7 %collective-permute-start.7 = (bf16[384,1024]{1,0:T(8,128)(2,1)}, bf16[384,1024]{1,0:T(8,128)(2,1)}, u32[]{:S(2)}, u32[]{:S(2)}) collective-permute-start(bf16[384,1024]{1,0:T(8,128)(2,1)} %bitcast.68), channel_id=1, source_target_pairs={{0,16},{4,12},{8,24},{12,4},{16,0},{20,28},{24,8},{28,20},{1,17},{... | collective-permute-start | bytes 2359304 | tf_op jit(solution)/shard_map/ppermute | solution.py:918
  39.4 24.4 %collective-permute-start.6 = (bf16[384,1024]{1,0:T(8,128)(2,1)}, bf16[384,1024]{1,0:T(8,128)(2,1)}, u32[]{:S(2)}, u32[]{:S(2)}) collective-permute-start(bf16[384,1024]{1,0:T(8,128)(2,1)} %bitcast.69), channel_id=1, source_target_pairs={{0,8},{4,20},{8,0},{12,28},{16,24},{20,4},{24,16},{28,12},{1,9},{5... | collective-permute-start | bytes 2359304 | tf_op jit(solution)/shard_map/ppermute | solution.py:918
  43.0 43.3 %collective-permute-start.5 = (bf16[512,1024]{1,0:T(8,128)(2,1)}, bf16[512,1024]{1,0:T(8,128)(2,1)}, u32[]{:S(2)}, u32[]{:S(2)}) collective-permute-start(bf16[512,1024]{1,0:T(8,128)(2,1)} %x_ref.5), channel_id=1, source_target_pairs={{0,1},{1,0},{2,3},{3,2},{4,5},{5,4},{6,7},{7,6},{8,9},{9,8},{10,11... | collective-permute-start | bytes 3145736 | tf_op jit(solution)/shard_map/ppermute | solution.py:30
  59.0 42.7 %collective-permute-start.10 = (bf16[640,1024]{1,0:T(8,128)(2,1)}, bf16[640,1024]{1,0:T(8,128)(2,1)}, u32[]{:S(2)}, u32[]{:S(2)}) collective-permute-start(bf16[640,1024]{1,0:T(8,128)(2,1)} %slice_dynamic-update-slice_fusion.refs_0_), channel_id=1, source_target_pairs={{0,8},{4,20},{8,0},{12,28},{16,24},{20,4},{24,16},{28,12},{1,9},{5... | collective-permute-start | bytes 3932168 | tf_op jit(solution)/shard_map/ppermute | solution.py:918
  63.8 24.1 %collective-permute-start.8 = (bf16[384,1024]{1,0:T(8,128)(2,1)}, bf16[384,1024]{1,0:T(8,128)(2,1)}, u32[]{:S(2)}, u32[]{:S(2)}) collective-permute-start(bf16[384,1024]{1,0:T(8,128)(2,1)} %collective-permute-done.6.refs_1_), channel_id=1, source_target_pairs={{0,16},{4,12},{8,24},{12,4},{16,0},{20,28},{24,8},{28,20},{1,17},{... | collective-permute-start | bytes 2359304 | tf_op jit(solution)/shard_map/ppermute | solution.py:928
  82.5 41.5 %collective-permute-start.11 = (bf16[640,1024]{1,0:T(8,128)(2,1)}, bf16[640,1024]{1,0:T(8,128)(2,1)}, u32[]{:S(2)}, u32[]{:S(2)}) collective-permute-start(bf16[640,1024]{1,0:T(8,128)(2,1)} %slice_dynamic-update-slice_fusion.refs_0_), channel_id=1, source_target_pairs={{0,16},{4,12},{8,24},{12,4},{16,0},{20,28},{24,8},{28,20},{1,17},{... | collective-permute-start | bytes 3932168 | tf_op jit(solution)/shard_map/ppermute | solution.py:918
  86.3 52.1 %collective-permute-start.15 = (bf16[640,1024]{1,0:T(8,128)(2,1)}, bf16[640,1024]{1,0:T(8,128)(2,1)}, u32[]{:S(2)}, u32[]{:S(2)}) collective-permute-start(bf16[640,1024]{1,0:T(8,128)(2,1)} %constant_dynamic-update-slice_fusion.6.refs_0_), channel_id=1, source_target_pairs={{0,8},{4,20},{8,0},{12,28},{16,24},{20,4},{24,16},{28,12},{1,9},{5... | collective-permute-start | bytes 3932168 | tf_op jit(solution)/shard_map/ppermute | solution.py:918
  101.7 26.8 %collective-permute-start.12 = (bf16[640,1024]{1,0:T(8,128)(2,1)}, bf16[640,1024]{1,0:T(8,128)(2,1)S(1)}, u32[]{:S(2)}, u32[]{:S(2)}) collective-permute-start(bf16[640,1024]{1,0:T(8,128)(2,1)} %collective-permute-done.10.refs_1_), channel_id=1, source_target_pairs={{0,16},{4,12},{8,24},{12,4},{16,0},{20,28},{24,8},{28,20},{1,17},{... | collective-permute-start | bytes 3932168 | tf_op jit(solution)/shard_map/ppermute | solution.py:928
  104.3 56.6 %collective-permute-start.16 = (bf16[640,1024]{1,0:T(8,128)(2,1)}, bf16[640,1024]{1,0:T(8,128)(2,1)}, u32[]{:S(2)}, u32[]{:S(2)}) collective-permute-start(bf16[640,1024]{1,0:T(8,128)(2,1)} %constant_dynamic-update-slice_fusion.6.refs_0_), channel_id=1, source_target_pairs={{0,16},{4,12},{8,24},{12,4},{16,0},{20,28},{24,8},{28,20},{1,17},{... | collective-permute-start | bytes 3932168 | tf_op jit(solution)/shard_map/ppermute | solution.py:918
  138.5 24.0 %collective-permute-start.17 = (bf16[640,1024]{1,0:T(8,128)(2,1)}, bf16[640,1024]{1,0:T(8,128)(2,1)}, u32[]{:S(2)}, u32[]{:S(2)}) collective-permute-start(bf16[640,1024]{1,0:T(8,128)(2,1)} %collective-permute-done.15.refs_1_), channel_id=1, source_target_pairs={{0,16},{4,12},{8,24},{12,4},{16,0},{20,28},{24,8},{28,20},{1,17},{... | collective-permute-start | bytes 3932168 | tf_op jit(solution)/shard_map/ppermute | solution.py:928
  143.0 41.0 %collective-permute-start.19 = (bf16[256,1024]{1,0:T(8,128)(2,1)S(1)}, bf16[256,1024]{1,0:T(8,128)(2,1)}, u32[]{:S(2)}, u32[]{:S(2)}) collective-permute-start(bf16[256,1024]{1,0:T(8,128)(2,1)S(1)} %pad_maximum_fusion.5.refs_0_), channel_id=1, source_target_pairs={{0,16},{4,12},{8,24},{12,4},{16,0},{20,28},{24,8},{28,20},{1,17},{... | collective-permute-start | bytes 1572872 | tf_op jit(solution)/shard_map/ppermute | solution.py:918
  158.7 25.3 %collective-permute-start.20 = (bf16[256,1024]{1,0:T(8,128)(2,1)S(1)}, bf16[256,1024]{1,0:T(8,128)(2,1)}, u32[]{:S(2)}, u32[]{:S(2)}) collective-permute-start(bf16[256,1024]{1,0:T(8,128)(2,1)S(1)} %collective-permute-done.18.refs_1_), channel_id=1, source_target_pairs={{0,16},{4,12},{8,24},{12,4},{16,0},{20,28},{24,8},{28,20},{1,17},{... | collective-permute-start | bytes 1572872 | tf_op jit(solution)/shard_map/ppermute | solution.py:928
  181.1 27.6 %collective-permute-start.21 = (bf16[512,1024]{1,0:T(8,128)(2,1)}, bf16[512,1024]{1,0:T(8,128)(2,1)}, u32[]{:S(2)}, u32[]{:S(2)}) collective-permute-start(bf16[512,1024]{1,0:T(8,128)(2,1)} %get-tuple-element.159.x_ref), channel_id=1, source_target_pairs={{0,1},{1,0},{2,3},{3,2},{4,5},{5,4},{6,7},{7,6},{8,9},{9,8},{10,11... | collective-permute-start | bytes 3145736 | tf_op jit(solution)/shard_map/ppermute | solution.py:30
  183.6 23.4 %collective-permute-start.24 = (bf16[384,1024]{1,0:T(8,128)(2,1)S(1)}, bf16[384,1024]{1,0:T(8,128)(2,1)}, u32[]{:S(2)}, u32[]{:S(2)}) collective-permute-start(bf16[384,1024]{1,0:T(8,128)(2,1)S(1)} %collective-permute-done.22.refs_1_), channel_id=1, source_target_pairs={{0,16},{4,12},{8,24},{12,4},{16,0},{20,28},{24,8},{28,20},{1,17},{... | collective-permute-start | bytes 2359304 | tf_op jit(solution)/shard_map/ppermute | solution.py:928
  195.0 26.3 %collective-permute-start.25 = (bf16[512,1024]{1,0:T(8,128)(2,1)S(1)}, bf16[512,1024]{1,0:T(8,128)(2,1)}, u32[]{:S(2)}, u32[]{:S(2)}) collective-permute-start(bf16[512,1024]{1,0:T(8,128)(2,1)S(1)} %pad_maximum_fusion.refs_0_), channel_id=1, source_target_pairs={{0,8},{4,20},{8,0},{12,28},{16,24},{20,4},{24,16},{28,12},{1,9},{5... | collective-permute-start | bytes 3145736 | tf_op jit(solution)/shard_map/ppermute | solution.py:918
  197.0 53.8 %collective-permute-start.28 = (bf16[640,1024]{1,0:T(8,128)(2,1)S(1)}, bf16[640,1024]{1,0:T(8,128)(2,1)}, u32[]{:S(2)}, u32[]{:S(2)}) collective-permute-start(bf16[640,1024]{1,0:T(8,128)(2,1)S(1)} %constant_dynamic-update-slice_fusion.8.refs_0_), channel_id=1, source_target_pairs={{0,8},{4,20},{8,0},{12,28},{16,24},{20,4},{24,16},{28,12},{1,9},{5... | collective-permute-start | bytes 3932168 | tf_op jit(solution)/shard_map/ppermute | solution.py:918
  197.8 53.3 %collective-permute-start.26 = (bf16[512,1024]{1,0:T(8,128)(2,1)S(1)}, bf16[512,1024]{1,0:T(8,128)(2,1)}, u32[]{:S(2)}, u32[]{:S(2)}) collective-permute-start(bf16[512,1024]{1,0:T(8,128)(2,1)S(1)} %pad_maximum_fusion.refs_0_), channel_id=1, source_target_pairs={{0,16},{4,12},{8,24},{12,4},{16,0},{20,28},{24,8},{28,20},{1,17},{... | collective-permute-start | bytes 3145736 | tf_op jit(solution)/shard_map/ppermute | solution.py:918
  207.0 72.0 %collective-permute-start.29 = (bf16[640,1024]{1,0:T(8,128)(2,1)S(1)}, bf16[640,1024]{1,0:T(8,128)(2,1)S(1)}, u32[]{:S(2)}, u32[]{:S(2)}) collective-permute-start(bf16[640,1024]{1,0:T(8,128)(2,1)S(1)} %constant_dynamic-update-slice_fusion.8.refs_0_), channel_id=1, source_target_pairs={{0,16},{4,12},{8,24},{12,4},{16,0},{20,28},{24,8},{28,20},{1,17},{... | collective-permute-start | bytes 3932168 | tf_op jit(solution)/shard_map/ppermute | solution.py:918
  221.3 42.9 %collective-permute-start.27 = (bf16[512,1024]{1,0:T(8,128)(2,1)}, bf16[512,1024]{1,0:T(8,128)(2,1)}, u32[]{:S(2)}, u32[]{:S(2)}) collective-permute-start(bf16[512,1024]{1,0:T(8,128)(2,1)} %collective-permute-done.25.refs_1_), channel_id=1, source_target_pairs={{0,16},{4,12},{8,24},{12,4},{16,0},{20,28},{24,8},{28,20},{1,17},{... | collective-permute-start | bytes 3145736 | tf_op jit(solution)/shard_map/ppermute | solution.py:928
  250.7 28.2 %collective-permute-start.30 = (bf16[640,1024]{1,0:T(8,128)(2,1)}, bf16[640,1024]{1,0:T(8,128)(2,1)S(1)}, u32[]{:S(2)}, u32[]{:S(2)}) collective-permute-start(bf16[640,1024]{1,0:T(8,128)(2,1)} %collective-permute-done.28.refs_1_), channel_id=1, source_target_pairs={{0,16},{4,12},{8,24},{12,4},{16,0},{20,28},{24,8},{28,20},{1,17},{... | collective-permute-start | bytes 3932168 | tf_op jit(solution)/shard_map/ppermute | solution.py:928
  323.7 32.2 %all-to-all-start = ((bf16[8,272,512]{2,1,0:T(8,128)(2,1)}), bf16[8,272,512]{2,1,0:T(8,128)(2,1)S(1)}, u32[]{:S(2)}, u32[]{:S(2)}) async-start(bf16[8,272,512]{2,1,0:T(8,128)(2,1)} %get-tuple-element.188), calls=%async_computation | async-start | bytes 4456448 | tf_op jit(solution)/shard_map/all_to_all | solution.py:1003
  363.6 26.1 %collective-permute-start.31 = (bf16[512,1024]{1,0:T(8,128)(2,1)}, bf16[512,1024]{1,0:T(8,128)(2,1)S(1)}, u32[]{:S(2)}, u32[]{:S(2)}) collective-permute-start(bf16[512,1024]{1,0:T(8,128)(2,1)} %shard_map.257), channel_id=1, source_target_pairs={{0,1},{1,0},{2,3},{3,2},{4,5},{5,4},{6,7},{7,6},{8,9},{9,8},{10,11... | collective-permute-start | bytes 3145736 | tf_op jit(solution)/shard_map/ppermute | solution.py:30
  382.8 33.1 %all-to-all-start.1 = ((f32[4,32,512]{2,1,0:T(8,128)}), f32[4,32,512]{2,1,0:T(8,128)S(1)}, u32[]{:S(2)}, u32[]{:S(2)}) async-start(f32[4,32,512]{2,1,0:T(8,128)} %param.35), calls=%async_computation.1 | async-start | bytes 524288 | tf_op jit(solution)/shard_map/all_to_all | solution.py:1003
  416.5 32.6 %all-to-all-start.2 = ((bf16[8,272,512]{2,1,0:T(8,128)(2,1)}), bf16[8,272,512]{2,1,0:T(8,128)(2,1)S(1)}, u32[]{:S(2)}, u32[]{:S(2)}) async-start(bf16[8,272,512]{2,1,0:T(8,128)(2,1)} %get-tuple-element.218), calls=%async_computation.2 | async-start | bytes 4456448 | tf_op jit(solution)/shard_map/all_to_all | solution.py:1003
  450.8 31.7 %all-to-all-start.3 = ((bf16[4,144,512]{2,1,0:T(8,128)(2,1)}), bf16[4,144,512]{2,1,0:T(8,128)(2,1)S(1)}, u32[]{:S(2)}, u32[]{:S(2)}) async-start(bf16[4,144,512]{2,1,0:T(8,128)(2,1)} %pad_maximum_fusion.3), calls=%async_computation.3 | async-start | bytes 1179648 | tf_op jit(solution)/shard_map/all_to_all | solution.py:1003
  490.7 28.4 %collective-permute-start.33 = (bf16[512,1024]{1,0:T(8,128)(2,1)}, bf16[512,1024]{1,0:T(8,128)(2,1)S(1)}, u32[]{:S(2)}, u32[]{:S(2)}) collective-permute-start(bf16[512,1024]{1,0:T(8,128)(2,1)} %shard_map.263), channel_id=1, source_target_pairs={{0,1},{1,0},{2,3},{3,2},{4,5},{5,4},{6,7},{7,6},{8,9},{9,8},{10,11... | collective-permute-start | bytes 3145736 | tf_op jit(solution)/shard_map/ppermute | solution.py:30
  495.2 36.7 %collective-permute-start.38 = (f32[128,512]{1,0:T(8,128)}, f32[128,512]{1,0:T(8,128)}, u32[]{:S(2)}, u32[]{:S(2)}) collective-permute-start(f32[128,512]{1,0:T(8,128)} %slice_add_fusion.refs_0_), channel_id=1, source_target_pairs={{0,24},{4,28},{8,16},{12,20},{16,8},{20,12},{24,0},{28,4},{1,25},{... | collective-permute-start | bytes 786440 | tf_op jit(solution)/shard_map/ppermute | solution.py:30
  495.8 36.2 %collective-permute-start.37 = (f32[128,512]{1,0:T(8,128)}, f32[128,512]{1,0:T(8,128)}, u32[]{:S(2)}, u32[]{:S(2)}) collective-permute-start(f32[128,512]{1,0:T(8,128)} %slice_add_fusion.refs_0_), channel_id=1, source_target_pairs={{0,20},{4,16},{8,28},{12,24},{16,4},{20,0},{24,12},{28,8},{1,21},{... | collective-permute-start | bytes 786440 | tf_op jit(solution)/shard_map/ppermute | solution.py:30
  504.8 46.6 %all-to-all-start.4 = ((f32[4,32,512]{2,1,0:T(8,128)}), f32[4,32,512]{2,1,0:T(8,128)S(1)}, u32[]{:S(2)}, u32[]{:S(2)}) async-start(f32[4,32,512]{2,1,0:T(8,128)} %bitcast.32), calls=%async_computation.4 | async-start | bytes 524288 | tf_op jit(solution)/shard_map/all_to_all | solution.py:1003
  531.9 25.5 %collective-permute-start.40 = (bf16[512,1024]{1,0:T(8,128)(2,1)S(1)}, bf16[512,1024]{1,0:T(8,128)(2,1)S(1)}, u32[]{:S(2)}, u32[]{:S(2)}) collective-permute-start(bf16[512,1024]{1,0:T(8,128)(2,1)S(1)} %copy-done.7), channel_id=1, source_target_pairs={{0,1},{1,0},{2,3},{3,2},{4,5},{5,4},{6,7},{7,6},{8,9},{9,8},{10,11... | collective-permute-start | bytes 3145736 | tf_op jit(solution)/shard_map/ppermute | solution.py:30
  (52 other events, 690.1 us)

commit v5 on v4

--- a/solution.py
+++ b/solution.py
@@ -347,7 +347,7 @@
         body(pl.ds(pl.multiple_of(i * step, step), step))
 
 
-ROWS = 64
+ROWS = 256
 TILE = 512
 STAT = 128
 BIAS_ROWS = 16
@@ -547,7 +547,7 @@
     for block in range(matrices_ref.shape[0]):
         matrices_ref[block, 2 * height :, :] = biases
 
-    wide = max(height, STAT)
+    wide = max(height, TILE)
 
     def matrices(columns):
         down_grad = bfloat(product_rows(low_ref[:, columns], dpre_ref[...]))
@@ -1116,8 +1116,12 @@
     biases = jnp.concatenate([array[at(2) : at(2) + BIAS_ROWS // 2] for array in (enc_sums, dec_sums)])
     sums = jnp.stack([jnp.concatenate([array, biases]) for array in sums])
     sums = spread(bfloat(sums))
+    far_dec = back(
+        (), (tie(self_back[2], sums), self_back[4]), dec_qkv_full, (1, 2), BF16
+    )
+    near_dec = partner(far_dec)
     enc_back = attend_back(
-        places, tie(grad_enc_mix, sums), enc_query, enc_keys, enc_values, enc_mix, enc_lse, False
+        places, tie(grad_enc_mix, far_dec), enc_query, enc_keys, enc_values, enc_mix, enc_lse, False
     )
     summed = exchange(sums, "narrow")
     summed = total(tie(summed, enc_back[0]))
@@ -1132,11 +1136,7 @@
     parts = [momentum] + [swap(momentum, "wide", r) for r in range(1, lax.axis_size("wide"))]
     new_momenta = to_rows(momentum)
 
-    far_dec = back(
-        (), (tie(self_back[2], momentum), self_back[4]), dec_qkv_full, (1, 2), BF16
-    )
-    near_dec = partner(far_dec)
-    far_enc = back((), (tie(enc_back[2], far_dec), enc_back[4]), enc_qkv_full, (1, 2), BF16)
+    far_enc = back((), (tie(enc_back[2], momentum), enc_back[4]), enc_qkv_full, (1, 2), BF16)
     near_enc = partner(far_enc)
     grad_dec = back(
         (tie(grad_z1, far_enc), near_dec),
@@ -1153,7 +1153,9 @@
         (0, 1, 2),
         F32,
     )
-    new_weights = adapter_weights - RATE * math.sqrt(max(1.0, D / ADAPT)) * to_rows(orthogonal)
+    new_weights = adapter_weights - RATE * math.sqrt(max(1.0, D / ADAPT)) * tie(
+        to_rows(orthogonal), grad_enc
+    )
     return (
         enc_out,
         dec_out,

time: 582 us -> 570 us (0.979)
  Pallas kernels: 403 us -> 397 us
    ppermute x17, waiting for transfers between devices: 11.9 us -> 3.85 us  [swap(): lax.ppermute(array, axis, [(i, i ^ bit) for i in range(lax.axis_size(axis...]
    pallas_call x20, Pallas kernels: 264 us -> 258 us  [call(): pl.pallas_call(kernel, in_specs=specs, out_specs=[IN_VMEM if len(out) ==...]
    unnamed x83 -> x85, local copies, waits for them, and re-layouts: 16 us -> 16 us
  transfers between devices with their start and end apart: 47 -> 47, of which waited for: 9 -> 7; matrix products, arithmetic and copies ran while one was open for 4% -> 5% of each run, Pallas kernels for 61% -> 62%
where the time goes in v5:
time: 570 us; the launch traced here: 560 us
  Pallas kernels  397 us (70%)
  starting transfers between devices  75.3 us (13%)
  waiting for transfers between devices  45.9 us (8%)
  local copies, waits for them, and re-layouts  31.2 us (5%)
  other arithmetic  8.2 us (1%)
    pallas_call x20, Pallas kernels, call(): pl.pallas_call(kernel, in_specs=specs, out_specs=[IN_VMEM if len(out) ==...  258 us
    pallas_call x3, Pallas kernels, attend_back(): pl.pallas_call(lambda *refs: attend_back_kernel(causal, 256, *refs[:12],...  84.6 us
    pallas_call x3, Pallas kernels, attend(): pl.pallas_call(functools.partial(attend_kernel, causal, 256), grid=(pairs...  54.9 us
    ppermute x8, waiting for transfers between devices, across(): lax.ppermute(first, 'wide', [(i, i ^ (2 if i % 2 else 4)) for i in range(...  39.9 us
    ppermute x16, starting transfers between devices, begin(): lax.ppermute(array, 'wide', [(i, i ^ steps[i % 2][which]) for i in range(...  23.3 us
    all_to_all x6, starting transfers between devices, shards(): lax.all_to_all(array, axis, split_axis=0, concat_axis=0, tiled=True)  22.9 us
    ppermute x17, starting transfers between devices, swap(): lax.ppermute(array, axis, [(i, i ^ bit) for i in range(lax.axis_size(axis...  20.8 us
    unnamed x85, local copies, waits for them, and re-layouts  16 us
  transfers between devices with their start and end apart: 47, of which 7 were waited for; matrix products, arithmetic and copies ran while one was open for 5% of the time, Pallas kernels for 62%

profile of v5, /device:TPU:0, one launch (start us, length us, event | category | flops | bytes accessed | tf_op | source)
XLA Modules:
  0.0 559.7 jit_solution(6803277142045902465)
XLA Ops:
  29.6 8.0 %collective-permute-done.1.refs_3_ = bf16[400,1024]{1,0:T(8,128)(2,1)S(1)} collective-permute-done((bf16[400,1024]{1,0:T(8,128)(2,1)}, bf16[400,1024]{1,0:T(8,128)(2,1)S(1)}, u32[]{:S(2)}, u32[]{:S(2)}) %collective-permute-start.1) | collective-permute-done | bytes 819232 | tf_op jit(solution)/shard_map/ppermute | solution.py:928
  44.6 13.7 %shard_map.242 = (bf16[512,1024]{1,0:T(8,128)(2,1)}, bf16[512,1024]{1,0:T(8,128)(2,1)}, bf16[512,1024]{1,0:T(8,128)(2,1)}, bf16[512,1024]{1,0:T(8,128)(2,1)}, bf...) custom-call(bf16[512,1024]{1,0:T(8,128)(2,1)} %x_ref.4, bf16[512,1024]{1,0:T(8,128)(2,1)} %collective-permute-done.3.far_ref, ...), custom_call_target="tpu_custom_call" | custom-call | flops 5368709120 | bytes 5373952 | tf_op jit(solution)/shard_map/pallas_call | solution.py:710
  64.3 18.2 %shard_map.243 = (bf16[512,1024]{1,0:T(8,128)(2,1)}, f32[8,8,512]{2,1,0:T(8,128)}) custom-call(s32[1]{0:T(128)} %bitcast.half_ref.refs_0_, s32[1,512]{1,0:T(1,128)} %bitcast.1.qid_ref.refs_1_, s32[512,1]{1,0:T(8,128)} %copy.47.kid_own_ref.refs_2_, s32[512,1]{1,0:T(8,128)} %copy.48.kid_far_ref.refs_3_, bf16[512,1024]{1,0:T(8,128)(2,1)} %get-tuple-element.129.q_ref.refs_4_, ...), custom_call_target="tpu_custom_call" | custom-call | flops 8589934592 | bytes 6291456 | tf_op jit(solution)/shard_map/pallas_call | solution.py:220
  87.9 13.8 %shard_map.244 = (bf16[512,1024]{1,0:T(8,128)(2,1)}, bf16[512,1024]{1,0:T(8,128)(2,1)}, bf16[512,1024]{1,0:T(8,128)(2,1)}, bf16[512,1024]{1,0:T(8,128)(2,1)}, bf...) custom-call(bf16[512,1024]{1,0:T(8,128)(2,1)} %x_ref.5, bf16[512,1024]{1,0:T(8,128)(2,1)} %collective-permute-done.5.far_ref, ...), custom_call_target="tpu_custom_call" | custom-call | flops 5368709120 | bytes 5242880 | tf_op jit(solution)/shard_map/pallas_call | solution.py:710
  105.8 18.2 %shard_map.245 = (bf16[512,1024]{1,0:T(8,128)(2,1)}, f32[8,8,512]{2,1,0:T(8,128)}) custom-call(s32[1]{0:T(128)} %bitcast.half_ref.refs_0_, s32[1,512]{1,0:T(1,128)} %bitcast.1.qid_ref.refs_1_, s32[512,1]{1,0:T(8,128)} %copy.47.kid_own_ref.refs_2_, s32[512,1]{1,0:T(8,128)} %copy.48.kid_far_ref.refs_3_, bf16[512,1024]{1,0:T(8,128)(2,1)} %get-tuple-element.139.q_ref.refs_4_, ...), custom_call_target="tpu_custom_call" | custom-call | flops 8589934592 | bytes 6291456 | tf_op jit(solution)/shard_map/pallas_call | solution.py:220
  124.0 4.4 collective-permute-done.12.refs_3_
  129.5 8.0 %shard_map.246 = (f32[512,1024]{1,0:T(8,128)}, f32[512,128]{1,0:T(8,128)}, bf16[1,1024,1024]{2,1,0:T(8,128)(2,1)}) custom-call(bf16[512,1024]{1,0:T(8,128)(2,1)} %x_ref.4, bf16[512,1024]{1,0:T(8,128)(2,1)} %get-tuple-element.145.mix_ref.refs_9_, f32[8,1024]{1,0:T(8,128)} %convert_bitcast_fusion.1.gains_ref.refs_5_, ...), custom_call_target="tpu_custom_call" | custom-call | flops 1073741824 | bytes 7372800 | tf_op jit(solution)/shard_map/pallas_call | solution.py:710
  142.6 14.9 %shard_map.247 = (bf16[512,4096]{1,0:T(8,128)(2,1)}, bf16[512,4096]{1,0:T(8,128)(2,1)}, bf16[4,1024,1024]{2,1,0:T(8,128)(2,1)}) custom-call(f32[512,1024]{1,0:T(8,128)} %get-tuple-element.149.n_ref.refs_3_, f32[8,1024]{1,0:T(8,128)} %convert_bitcast_fusion.1.gains_ref.refs_5_, bf16[640,1024]{1,0:T(8,128)(2,1)} %slice_dynamic-update-slice_fusion.refs_0_, ...), custom_call_target="tpu_custom_call" | custom-call | flops 4294967296 | bytes 7372800 | tf_op jit(solution)/shard_map/pallas_call | solution.py:710
  159.6 4.2 collective-permute-done.17.refs_3_
  163.8 17.6 %shard_map.248 = (bf16[512,512]{1,0:T(8,128)(2,1)}, bf16[512,512]{1,0:T(8,128)(2,1)}, f32[512,1024]{1,0:T(8,128)}, f32[512,128]{1,0:T(8,128)}, bf16[512,1024]{1,...) custom-call(f32[512,1024]{1,0:T(8,128)} %get-tuple-element.149.n_ref.refs_3_, ...), custom_call_target="tpu_custom_call" | custom-call | flops 5368709120 | bytes 11573248 | tf_op jit(solution)/shard_map/pallas_call | solution.py:710
  184.2 10.0 %shard_map.249 = (f32[512,1024]{1,0:T(8,128)}, f32[512,128]{1,0:T(8,128)}, bf16[512,1024]{1,0:T(8,128)(2,1)}, bf16[2,1024,1024]{2,1,0:T(8,128)(2,1)}) custom-call(bf16[512,1024]{1,0:T(8,128)(2,1)} %x_ref.5, bf16[512,1024]{1,0:T(8,128)(2,1)} %get-tuple-element.156.mix_ref.refs_9_, f32[8,1024]{1,0:T(8,128)} %convert_bitcast_fusion.1.gains_ref.refs_5_, ...), custom_call_target="tpu_custom_call" | custom-call | flops 2147483648 | bytes 4227072 | tf_op jit(solution)/shard_map/pallas_call | solution.py:710
  198.6 9.6 %collective-permute-done.24.refs_3_ = bf16[384,1024]{1,0:T(8,128)(2,1)} collective-permute-done((bf16[384,1024]{1,0:T(8,128)(2,1)S(1)}, bf16[384,1024]{1,0:T(8,128)(2,1)}, u32[]{:S(2)}, u32[]{:S(2)}) %collective-permute-start.24) | collective-permute-done | bytes 786464 | tf_op jit(solution)/shard_map/ppermute | solution.py:928
  210.0 11.7 %shard_map.250 = (bf16[512,1024]{1,0:T(8,128)(2,1)}, bf16[512,1024]{1,0:T(8,128)(2,1)}, bf16[512,1024]{1,0:T(8,128)(2,1)}, bf16[512,1024]{1,0:T(8,128)(2,1)}, bf16[2,1024,1024]{2,1,0:T(8,128)(2,1)}) custom-call(bf16[512,1024]{1,0:T(8,128)(2,1)} %get-tuple-element.160.x_ref, bf16[512,1024]{1,0:T(8,128)(2,1)} %collective-permute-done.21.far_ref, ...), custom_call_target="tpu_custom_call" | custom-call | flops 4294967296 | bytes 5242880 | tf_op jit(solution)/shard_map/pallas_call | solution.py:710
  222.3 18.6 %shard_map.251 = (bf16[512,1024]{1,0:T(8,128)(2,1)}, f32[8,8,512]{2,1,0:T(8,128)}) custom-call(s32[1]{0:T(128)} %bitcast.half_ref.refs_0_, s32[1,512]{1,0:T(1,128)} %bitcast.1.qid_ref.refs_1_, s32[512,1]{1,0:T(8,128)} %copy.47.kid_own_ref.refs_2_, s32[512,1]{1,0:T(8,128)} %copy.48.kid_far_ref.refs_3_, bf16[512,1024]{1,0:T(8,128)(2,1)} %get-tuple-element.159.q_ref.refs_4_, ...), custom_call_target="tpu_custom_call" | custom-call | flops 8589934592 | bytes 6291456 | tf_op jit(solution)/shard_map/pallas_call | solution.py:220
  240.8 8.6 %shard_map.252 = (f32[512,1024]{1,0:T(8,128)}, f32[512,128]{1,0:T(8,128)}, bf16[1,1024,1024]{2,1,0:T(8,128)(2,1)}) custom-call(f32[512,1024]{1,0:T(8,128)} %get-tuple-element.168.x_ref.n_ref, bf16[512,1024]{1,0:T(8,128)(2,1)} %get-tuple-element.167.mix_ref.refs_9_, f32[8,1024]{1,0:T(8,128)} %convert_bitcast_fusion.1.gains_ref.refs_5_, ...), custom_call_target="tpu_custom_call" | custom-call | flops 1073741824 | bytes 6324224 | tf_op jit(solution)/shard_map/pallas_call | solution.py:710
  250.8 13.7 %collective-permute-done.27.refs_3_ = bf16[512,1024]{1,0:T(8,128)(2,1)} collective-permute-done((bf16[512,1024]{1,0:T(8,128)(2,1)}, bf16[512,1024]{1,0:T(8,128)(2,1)}, u32[]{:S(2)}, u32[]{:S(2)}) %collective-permute-start.27) | collective-permute-done | bytes 1048608 | tf_op jit(solution)/shard_map/ppermute | solution.py:928
  264.5 14.6 %shard_map.253 = (bf16[512,4096]{1,0:T(8,128)(2,1)}, bf16[512,4096]{1,0:T(8,128)(2,1)}, bf16[4,1024,1024]{2,1,0:T(8,128)(2,1)}) custom-call(f32[512,1024]{1,0:T(8,128)} %get-tuple-element.169.n_ref.refs_3_, f32[8,1024]{1,0:T(8,128)} %convert_bitcast_fusion.1.gains_ref.refs_5_, bf16[512,1024]{1,0:T(8,128)(2,1)} %copy-done.15, ...), custom_call_target="tpu_custom_call" | custom-call | flops 4294967296 | bytes 6324224 | tf_op jit(solution)/shard_map/pallas_call | solution.py:710
  280.7 17.6 %shard_map.254 = (bf16[512,512]{1,0:T(8,128)(2,1)}, bf16[512,512]{1,0:T(8,128)(2,1)}, f32[512,1024]{1,0:T(8,128)}, f32[512,128]{1,0:T(8,128)}, bf16[512,1024]{1,...) custom-call(f32[512,1024]{1,0:T(8,128)} %get-tuple-element.169.n_ref.refs_3_, ...), custom_call_target="tpu_custom_call" | custom-call | flops 5368709120 | bytes 11573248 | tf_op jit(solution)/shard_map/pallas_call | solution.py:710
  298.3 24.0 %shard_map.255 = (bf16[512,1024]{1,0:T(8,128)(2,1)}, f32[512,1024]{1,0:T(8,128)}, bf16[512,1024]{1,0:T(8,128)(2,1)}, bf16[8,272,512]{2,1,0:T(8,128)(2,1)}) custom-call(bf16[512,1024]{1,0:T(8,128)(2,1)} %refs_0_.1, f32[512,1024]{1,0:T(8,128)} %get-tuple-element.176.refs_1_, f32[512,128]{1,0:T(8,128)} %get-tuple-element.177.refs_2_, ...), custom_call_target="tpu_custom_call" | custom-call | flops 12884901888 | bytes 32014336 | tf_op jit(solution)/shard_map/pallas_call | solution.py:710
  326.2 28.2 %shard_map.256 = (bf16[512,1024]{1,0:T(8,128)(2,1)}, bf16[512,1024]{1,0:T(8,128)(2,1)}, bf16[512,1024]{1,0:T(8,128)(2,1)}, bf16[512,1024]{1,0:T(8,128)(2,1)}, bf16[512,1024]{1,0:T(8,128)(2,1)}) custom-call(s32[1]{0:T(128)} %bitcast.half_ref.refs_0_, s32[1,512]{1,0:T(1,128)} %bitcast.1.qid_ref.refs_1_, s32[512,1]{1,0:T(8,128)} %copy.47.kid_own_ref.refs_2_, ...), custom_call_target="tpu_custom_call" | custom-call | flops 21474836480 | bytes 12582912 | tf_op jit(solution)/shard_map/pallas_call | solution.py:244
  354.8 7.4 %shard_map.257 = bf16[512,1024]{1,0:T(8,128)(2,1)} custom-call(bf16[512,1024]{1,0:T(8,128)(2,1)} %get-tuple-element.192.refs_0_, bf16[512,1024]{1,0:T(8,128)(2,1)} %get-tuple-element.193.refs_1_, bf16[2,1024,1024]{2,1,0:T(8,128)(2,1)} %get-tuple-element.194.refs_2_.refs_3_), custom_call_target="tpu_custom_call" | custom-call | flops 2147483648 | bytes 6291456 | tf_op jit(solution)/shard_map/pallas_call | solution.py:710
  363.9 8.0 %shard_map.258.refs_0_ = f32[512,1024]{1,0:T(8,128)} custom-call(bf16[512,1024]{1,0:T(8,128)(2,1)} %refs_0_.2, bf16[512,1024]{1,0:T(8,128)(2,1)} %get-tuple-element.196.refs_1_, bf16[512,1024]{1,0:T(8,128)(2,1)} %get-tuple-element.197.refs_2_, bf16[2,1024,1024]{2,1,0:T(8,128)(2,1)} %get-tuple-element.194.refs_2_.refs_3_), custom_call_target="tpu_custom_call" | custom-call | flops 2147483648 | bytes 7340032 | tf_op jit(solution)/shard_map/pallas_call | solution.py:710
  371.9 9.1 %shard_map.259 = (f32[512,1024]{1,0:T(8,128)}, bf16[512,1024]{1,0:T(8,128)(2,1)}) custom-call(f32[512,1024]{1,0:T(8,128)} %get-tuple-element.199.dz_ref, bf16[512,1024]{1,0:T(8,128)(2,1)} %get-tuple-element.190.dq_ref, f32[512,1024]{1,0:T(8,128)} %get-tuple-element.168.x_ref.n_ref, f32[512,128]{1,0:T(8,128)} %get-tuple-element.200.r_ref, ...), custom_call_target="tpu_custom_call" | custom-call | flops 2147483648 | bytes 9732096 | tf_op jit(solution)/shard_map/pallas_call | solution.py:710
  389.4 24.6 %shard_map.260 = (bf16[512,1024]{1,0:T(8,128)(2,1)}, f32[512,1024]{1,0:T(8,128)}, bf16[512,1024]{1,0:T(8,128)(2,1)}, bf16[8,272,512]{2,1,0:T(8,128)(2,1)}) custom-call(f32[512,1024]{1,0:T(8,128)} %shard_map.258.refs_0_, f32[512,1024]{1,0:T(8,128)} %get-tuple-element.204.refs_1_, f32[512,128]{1,0:T(8,128)} %get-tuple-element.205.refs_2_, ...), custom_call_target="tpu_custom_call" | custom-call | flops 12884901888 | bytes 34111488 | tf_op jit(solution)/shard_map/pallas_call | solution.py:710
  418.6 28.2 %shard_map.261 = (bf16[512,1024]{1,0:T(8,128)(2,1)}, bf16[512,1024]{1,0:T(8,128)(2,1)}, bf16[512,1024]{1,0:T(8,128)(2,1)}, bf16[512,1024]{1,0:T(8,128)(2,1)}, bf16[512,1024]{1,0:T(8,128)(2,1)}) custom-call(s32[1]{0:T(128)} %bitcast.half_ref.refs_0_, s32[1,512]{1,0:T(1,128)} %bitcast.1.qid_ref.refs_1_, s32[512,1]{1,0:T(8,128)} %copy.47.kid_own_ref.refs_2_, ...), custom_call_target="tpu_custom_call" | custom-call | flops 21474836480 | bytes 12582912 | tf_op jit(solution)/shard_map/pallas_call | solution.py:244
  452.0 7.3 %shard_map.262 = bf16[512,1024]{1,0:T(8,128)(2,1)} custom-call(bf16[512,1024]{1,0:T(8,128)(2,1)} %get-tuple-element.227.refs_0_, bf16[512,1024]{1,0:T(8,128)(2,1)} %get-tuple-element.228.refs_1_, bf16[3,1024,1024]{2,1,0:T(8,128)(2,1)} %get-tuple-element.229.refs_2_.refs_5_), custom_call_target="tpu_custom_call" | custom-call | flops 2147483648 | bytes 8388608 | tf_op jit(solution)/shard_map/pallas_call | solution.py:710
  461.3 28.2 %shard_map.263 = (bf16[512,1024]{1,0:T(8,128)(2,1)}, bf16[512,1024]{1,0:T(8,128)(2,1)}, bf16[512,1024]{1,0:T(8,128)(2,1)}, bf16[512,1024]{1,0:T(8,128)(2,1)}, bf16[512,1024]{1,0:T(8,128)(2,1)}) custom-call(s32[1]{0:T(128)} %bitcast.half_ref.refs_0_, s32[1,512]{1,0:T(1,128)} %bitcast.1.qid_ref.refs_1_, s32[512,1]{1,0:T(8,128)} %copy.47.kid_own_ref.refs_2_, ...), custom_call_target="tpu_custom_call" | custom-call | flops 21474836480 | bytes 12582912 | tf_op jit(solution)/shard_map/pallas_call | solution.py:244
  494.9 7.4 %shard_map.264 = bf16[512,1024]{1,0:T(8,128)(2,1)} custom-call(bf16[512,1024]{1,0:T(8,128)(2,1)} %get-tuple-element.235.refs_0_, bf16[512,1024]{1,0:T(8,128)(2,1)} %get-tuple-element.236.refs_1_, bf16[3,1024,1024]{2,1,0:T(8,128)(2,1)} %get-tuple-element.237.refs_2_.refs_5_), custom_call_target="tpu_custom_call" | custom-call | flops 2147483648 | bytes 8388608 | tf_op jit(solution)/shard_map/pallas_call | solution.py:710
  508.9 10.7 %shard_map.265 = f32[512,1024]{1,0:T(8,128)} custom-call(f32[512,1024]{1,0:T(8,128)} %get-tuple-element.238.refs_0_, bf16[512,1024]{1,0:T(8,128)(2,1)} %copy-done.4, bf16[512,1024]{1,0:T(8,128)(2,1)} %get-tuple-element.223.refs_2_, bf16[512,1024]{1,0:T(8,128)(2,1)} %get-tuple-element.239.refs_3_, bf16[512,1024]{1,0:T(8,128)(2,1)} %get-tuple-element.240.refs_4_, ...), custom_call_target="tpu_custom_call" | custom-call | flops 3221225472 | bytes 12582912 | tf_op jit(solution)/shard_map/pallas_call | solution.py:710
  523.3 17.8 %shard_map.266 = f32[128,512]{1,0:T(8,128)} custom-call(f32[128,512]{1,0:T(8,128)} %slice_add_fusion.refs_0_, f32[128,512]{1,0:T(8,128)} %copy-done.32, f32[128,512]{1,0:T(8,128)} %copy-done.35, f32[128,512]{1,0:T(8,128)} %copy-done.34, f32[128,512]{1,0:T(8,128)} %copy-done.33, f32[128,512]{1,0:T(8,128)} %collective-permute-done.37.refs_5_, ...), custom_call_target="tpu_custom_call" | custom-call | flops 16106127360 | bytes 2097152 | tf_op jit(solution)/shard_map/pallas_call | solution.py:710
  541.2 4.2 all-to-all-start.5
  547.1 10.7 %shard_map.267 = f32[512,1024]{1,0:T(8,128)} custom-call(f32[512,1024]{1,0:T(8,128)} %get-tuple-element.242.refs_0_, bf16[512,1024]{1,0:T(8,128)(2,1)} %copy-done.5, bf16[512,1024]{1,0:T(8,128)(2,1)} %get-tuple-element.232.refs_2_, bf16[512,1024]{1,0:T(8,128)(2,1)} %get-tuple-element.243.refs_3_, bf16[512,1024]{1,0:T(8,128)(2,1)} %get-tuple-element.244.refs_4_, ...), custom_call_target="tpu_custom_call" | custom-call | flops 3221225472 | bytes 12582912 | tf_op jit(solution)/shard_map/pallas_call | solution.py:710
  (227 shorter events, 116.5 us)
Async XLA Ops:
  8.0 35.0 %collective-permute-start.3 = (bf16[512,1024]{1,0:T(8,128)(2,1)S(1)}, bf16[512,1024]{1,0:T(8,128)(2,1)}, u32[]{:S(2)}, u32[]{:S(2)}) collective-permute-start(bf16[512,1024]{1,0:T(8,128)(2,1)S(1)} %copy-done.6), channel_id=1, source_target_pairs={{0,1},{1,0},{2,3},{3,2},{4,5},{5,4},{6,7},{7,6},{8,9},{9,8},{10,11... | collective-permute-start | bytes 3145736 | tf_op jit(solution)/shard_map/ppermute | solution.py:30
  37.6 48.7 %collective-permute-start.7 = (bf16[384,1024]{1,0:T(8,128)(2,1)}, bf16[384,1024]{1,0:T(8,128)(2,1)}, u32[]{:S(2)}, u32[]{:S(2)}) collective-permute-start(bf16[384,1024]{1,0:T(8,128)(2,1)} %bitcast.68), channel_id=1, source_target_pairs={{0,16},{4,12},{8,24},{12,4},{16,0},{20,28},{24,8},{28,20},{1,17},{... | collective-permute-start | bytes 2359304 | tf_op jit(solution)/shard_map/ppermute | solution.py:918
  39.4 24.4 %collective-permute-start.6 = (bf16[384,1024]{1,0:T(8,128)(2,1)}, bf16[384,1024]{1,0:T(8,128)(2,1)}, u32[]{:S(2)}, u32[]{:S(2)}) collective-permute-start(bf16[384,1024]{1,0:T(8,128)(2,1)} %bitcast.69), channel_id=1, source_target_pairs={{0,8},{4,20},{8,0},{12,28},{16,24},{20,4},{24,16},{28,12},{1,9},{5... | collective-permute-start | bytes 2359304 | tf_op jit(solution)/shard_map/ppermute | solution.py:918
  43.0 43.3 %collective-permute-start.5 = (bf16[512,1024]{1,0:T(8,128)(2,1)}, bf16[512,1024]{1,0:T(8,128)(2,1)}, u32[]{:S(2)}, u32[]{:S(2)}) collective-permute-start(bf16[512,1024]{1,0:T(8,128)(2,1)} %x_ref.5), channel_id=1, source_target_pairs={{0,1},{1,0},{2,3},{3,2},{4,5},{5,4},{6,7},{7,6},{8,9},{9,8},{10,11... | collective-permute-start | bytes 3145736 | tf_op jit(solution)/shard_map/ppermute | solution.py:30
  59.0 42.7 %collective-permute-start.10 = (bf16[640,1024]{1,0:T(8,128)(2,1)}, bf16[640,1024]{1,0:T(8,128)(2,1)}, u32[]{:S(2)}, u32[]{:S(2)}) collective-permute-start(bf16[640,1024]{1,0:T(8,128)(2,1)} %slice_dynamic-update-slice_fusion.refs_0_), channel_id=1, source_target_pairs={{0,8},{4,20},{8,0},{12,28},{16,24},{20,4},{24,16},{28,12},{1,9},{5... | collective-permute-start | bytes 3932168 | tf_op jit(solution)/shard_map/ppermute | solution.py:918
  63.8 24.1 %collective-permute-start.8 = (bf16[384,1024]{1,0:T(8,128)(2,1)}, bf16[384,1024]{1,0:T(8,128)(2,1)}, u32[]{:S(2)}, u32[]{:S(2)}) collective-permute-start(bf16[384,1024]{1,0:T(8,128)(2,1)} %collective-permute-done.6.refs_1_), channel_id=1, source_target_pairs={{0,16},{4,12},{8,24},{12,4},{16,0},{20,28},{24,8},{28,20},{1,17},{... | collective-permute-start | bytes 2359304 | tf_op jit(solution)/shard_map/ppermute | solution.py:928
  82.5 41.5 %collective-permute-start.11 = (bf16[640,1024]{1,0:T(8,128)(2,1)}, bf16[640,1024]{1,0:T(8,128)(2,1)}, u32[]{:S(2)}, u32[]{:S(2)}) collective-permute-start(bf16[640,1024]{1,0:T(8,128)(2,1)} %slice_dynamic-update-slice_fusion.refs_0_), channel_id=1, source_target_pairs={{0,16},{4,12},{8,24},{12,4},{16,0},{20,28},{24,8},{28,20},{1,17},{... | collective-permute-start | bytes 3932168 | tf_op jit(solution)/shard_map/ppermute | solution.py:918
  86.4 51.2 %collective-permute-start.15 = (bf16[640,1024]{1,0:T(8,128)(2,1)}, bf16[640,1024]{1,0:T(8,128)(2,1)}, u32[]{:S(2)}, u32[]{:S(2)}) collective-permute-start(bf16[640,1024]{1,0:T(8,128)(2,1)} %constant_dynamic-update-slice_fusion.6.refs_0_), channel_id=1, source_target_pairs={{0,8},{4,20},{8,0},{12,28},{16,24},{20,4},{24,16},{28,12},{1,9},{5... | collective-permute-start | bytes 3932168 | tf_op jit(solution)/shard_map/ppermute | solution.py:918
  101.7 26.8 %collective-permute-start.12 = (bf16[640,1024]{1,0:T(8,128)(2,1)}, bf16[640,1024]{1,0:T(8,128)(2,1)S(1)}, u32[]{:S(2)}, u32[]{:S(2)}) collective-permute-start(bf16[640,1024]{1,0:T(8,128)(2,1)} %collective-permute-done.10.refs_1_), channel_id=1, source_target_pairs={{0,16},{4,12},{8,24},{12,4},{16,0},{20,28},{24,8},{28,20},{1,17},{... | collective-permute-start | bytes 3932168 | tf_op jit(solution)/shard_map/ppermute | solution.py:928
  104.3 55.3 %collective-permute-start.16 = (bf16[640,1024]{1,0:T(8,128)(2,1)}, bf16[640,1024]{1,0:T(8,128)(2,1)}, u32[]{:S(2)}, u32[]{:S(2)}) collective-permute-start(bf16[640,1024]{1,0:T(8,128)(2,1)} %constant_dynamic-update-slice_fusion.6.refs_0_), channel_id=1, source_target_pairs={{0,16},{4,12},{8,24},{12,4},{16,0},{20,28},{24,8},{28,20},{1,17},{... | collective-permute-start | bytes 3932168 | tf_op jit(solution)/shard_map/ppermute | solution.py:918
  137.5 26.3 %collective-permute-start.17 = (bf16[640,1024]{1,0:T(8,128)(2,1)}, bf16[640,1024]{1,0:T(8,128)(2,1)}, u32[]{:S(2)}, u32[]{:S(2)}) collective-permute-start(bf16[640,1024]{1,0:T(8,128)(2,1)} %collective-permute-done.15.refs_1_), channel_id=1, source_target_pairs={{0,16},{4,12},{8,24},{12,4},{16,0},{20,28},{24,8},{28,20},{1,17},{... | collective-permute-start | bytes 3932168 | tf_op jit(solution)/shard_map/ppermute | solution.py:928
  142.0 42.2 %collective-permute-start.19 = (bf16[256,1024]{1,0:T(8,128)(2,1)S(1)}, bf16[256,1024]{1,0:T(8,128)(2,1)}, u32[]{:S(2)}, u32[]{:S(2)}) collective-permute-start(bf16[256,1024]{1,0:T(8,128)(2,1)S(1)} %pad_maximum_fusion.5.refs_0_), channel_id=1, source_target_pairs={{0,16},{4,12},{8,24},{12,4},{16,0},{20,28},{24,8},{28,20},{1,17},{... | collective-permute-start | bytes 1572872 | tf_op jit(solution)/shard_map/ppermute | solution.py:918
  157.5 26.7 %collective-permute-start.20 = (bf16[256,1024]{1,0:T(8,128)(2,1)S(1)}, bf16[256,1024]{1,0:T(8,128)(2,1)}, u32[]{:S(2)}, u32[]{:S(2)}) collective-permute-start(bf16[256,1024]{1,0:T(8,128)(2,1)S(1)} %collective-permute-done.18.refs_1_), channel_id=1, source_target_pairs={{0,16},{4,12},{8,24},{12,4},{16,0},{20,28},{24,8},{28,20},{1,17},{... | collective-permute-start | bytes 1572872 | tf_op jit(solution)/shard_map/ppermute | solution.py:928
  159.1 24.8 %collective-permute-start.22 = (bf16[384,1024]{1,0:T(8,128)(2,1)S(1)}, bf16[384,1024]{1,0:T(8,128)(2,1)S(1)}, u32[]{:S(2)}, u32[]{:S(2)}) collective-permute-start(bf16[384,1024]{1,0:T(8,128)(2,1)S(1)} %pad_maximum_fusion.2.refs_0_), channel_id=1, source_target_pairs={{0,8},{4,20},{8,0},{12,28},{16,24},{20,4},{24,16},{28,12},{1,9},{5... | collective-permute-start | bytes 2359304 | tf_op jit(solution)/shard_map/ppermute | solution.py:918
  181.4 28.6 %collective-permute-start.21 = (bf16[512,1024]{1,0:T(8,128)(2,1)}, bf16[512,1024]{1,0:T(8,128)(2,1)}, u32[]{:S(2)}, u32[]{:S(2)}) collective-permute-start(bf16[512,1024]{1,0:T(8,128)(2,1)} %get-tuple-element.160.x_ref), channel_id=1, source_target_pairs={{0,1},{1,0},{2,3},{3,2},{4,5},{5,4},{6,7},{7,6},{8,9},{9,8},{10,11... | collective-permute-start | bytes 3145736 | tf_op jit(solution)/shard_map/ppermute | solution.py:30
  183.9 24.4 %collective-permute-start.24 = (bf16[384,1024]{1,0:T(8,128)(2,1)S(1)}, bf16[384,1024]{1,0:T(8,128)(2,1)}, u32[]{:S(2)}, u32[]{:S(2)}) collective-permute-start(bf16[384,1024]{1,0:T(8,128)(2,1)S(1)} %collective-permute-done.22.refs_1_), channel_id=1, source_target_pairs={{0,16},{4,12},{8,24},{12,4},{16,0},{20,28},{24,8},{28,20},{1,17},{... | collective-permute-start | bytes 2359304 | tf_op jit(solution)/shard_map/ppermute | solution.py:928
  194.3 27.4 %collective-permute-start.25 = (bf16[512,1024]{1,0:T(8,128)(2,1)S(1)}, bf16[512,1024]{1,0:T(8,128)(2,1)}, u32[]{:S(2)}, u32[]{:S(2)}) collective-permute-start(bf16[512,1024]{1,0:T(8,128)(2,1)S(1)} %pad_maximum_fusion.refs_0_), channel_id=1, source_target_pairs={{0,8},{4,20},{8,0},{12,28},{16,24},{20,4},{24,16},{28,12},{1,9},{5... | collective-permute-start | bytes 3145736 | tf_op jit(solution)/shard_map/ppermute | solution.py:918
  196.2 53.2 %collective-permute-start.28 = (bf16[640,1024]{1,0:T(8,128)(2,1)S(1)}, bf16[640,1024]{1,0:T(8,128)(2,1)}, u32[]{:S(2)}, u32[]{:S(2)}) collective-permute-start(bf16[640,1024]{1,0:T(8,128)(2,1)S(1)} %constant_dynamic-update-slice_fusion.8.refs_0_), channel_id=1, source_target_pairs={{0,8},{4,20},{8,0},{12,28},{16,24},{20,4},{24,16},{28,12},{1,9},{5... | collective-permute-start | bytes 3932168 | tf_op jit(solution)/shard_map/ppermute | solution.py:918
  197.0 53.8 %collective-permute-start.26 = (bf16[512,1024]{1,0:T(8,128)(2,1)S(1)}, bf16[512,1024]{1,0:T(8,128)(2,1)}, u32[]{:S(2)}, u32[]{:S(2)}) collective-permute-start(bf16[512,1024]{1,0:T(8,128)(2,1)S(1)} %pad_maximum_fusion.refs_0_), channel_id=1, source_target_pairs={{0,16},{4,12},{8,24},{12,4},{16,0},{20,28},{24,8},{28,20},{1,17},{... | collective-permute-start | bytes 3145736 | tf_op jit(solution)/shard_map/ppermute | solution.py:918
  208.3 70.9 %collective-permute-start.29 = (bf16[640,1024]{1,0:T(8,128)(2,1)S(1)}, bf16[640,1024]{1,0:T(8,128)(2,1)S(1)}, u32[]{:S(2)}, u32[]{:S(2)}) collective-permute-start(bf16[640,1024]{1,0:T(8,128)(2,1)S(1)} %constant_dynamic-update-slice_fusion.8.refs_0_), channel_id=1, source_target_pairs={{0,16},{4,12},{8,24},{12,4},{16,0},{20,28},{24,8},{28,20},{1,17},{... | collective-permute-start | bytes 3932168 | tf_op jit(solution)/shard_map/ppermute | solution.py:918
  221.7 42.8 %collective-permute-start.27 = (bf16[512,1024]{1,0:T(8,128)(2,1)}, bf16[512,1024]{1,0:T(8,128)(2,1)}, u32[]{:S(2)}, u32[]{:S(2)}) collective-permute-start(bf16[512,1024]{1,0:T(8,128)(2,1)} %collective-permute-done.25.refs_1_), channel_id=1, source_target_pairs={{0,16},{4,12},{8,24},{12,4},{16,0},{20,28},{24,8},{28,20},{1,17},{... | collective-permute-start | bytes 3145736 | tf_op jit(solution)/shard_map/ppermute | solution.py:928
  249.4 29.7 %collective-permute-start.30 = (bf16[640,1024]{1,0:T(8,128)(2,1)}, bf16[640,1024]{1,0:T(8,128)(2,1)S(1)}, u32[]{:S(2)}, u32[]{:S(2)}) collective-permute-start(bf16[640,1024]{1,0:T(8,128)(2,1)} %collective-permute-done.28.refs_1_), channel_id=1, source_target_pairs={{0,16},{4,12},{8,24},{12,4},{16,0},{20,28},{24,8},{28,20},{1,17},{... | collective-permute-start | bytes 3932168 | tf_op jit(solution)/shard_map/ppermute | solution.py:928
  322.3 32.2 %all-to-all-start = ((bf16[8,272,512]{2,1,0:T(8,128)(2,1)}), bf16[8,272,512]{2,1,0:T(8,128)(2,1)S(1)}, u32[]{:S(2)}, u32[]{:S(2)}) async-start(bf16[8,272,512]{2,1,0:T(8,128)(2,1)} %get-tuple-element.189), calls=%async_computation | async-start | bytes 4456448 | tf_op jit(solution)/shard_map/all_to_all | solution.py:1003
  362.2 26.2 %collective-permute-start.31 = (bf16[512,1024]{1,0:T(8,128)(2,1)}, bf16[512,1024]{1,0:T(8,128)(2,1)S(1)}, u32[]{:S(2)}, u32[]{:S(2)}) collective-permute-start(bf16[512,1024]{1,0:T(8,128)(2,1)} %shard_map.257), channel_id=1, source_target_pairs={{0,1},{1,0},{2,3},{3,2},{4,5},{5,4},{6,7},{7,6},{8,9},{9,8},{10,11... | collective-permute-start | bytes 3145736 | tf_op jit(solution)/shard_map/ppermute | solution.py:30
  381.0 33.1 %all-to-all-start.1 = ((f32[4,32,512]{2,1,0:T(8,128)}), f32[4,32,512]{2,1,0:T(8,128)S(1)}, u32[]{:S(2)}, u32[]{:S(2)}) async-start(f32[4,32,512]{2,1,0:T(8,128)} %param.35), calls=%async_computation.1 | async-start | bytes 524288 | tf_op jit(solution)/shard_map/all_to_all | solution.py:1003
  414.7 32.1 %all-to-all-start.2 = ((bf16[8,272,512]{2,1,0:T(8,128)(2,1)}), bf16[8,272,512]{2,1,0:T(8,128)(2,1)S(1)}, u32[]{:S(2)}, u32[]{:S(2)}) async-start(bf16[8,272,512]{2,1,0:T(8,128)(2,1)} %get-tuple-element.219), calls=%async_computation.2 | async-start | bytes 4456448 | tf_op jit(solution)/shard_map/all_to_all | solution.py:1003
  448.5 41.1 %all-to-all-start.3 = ((bf16[4,144,512]{2,1,0:T(8,128)(2,1)}), bf16[4,144,512]{2,1,0:T(8,128)(2,1)S(1)}, u32[]{:S(2)}, u32[]{:S(2)}) async-start(bf16[4,144,512]{2,1,0:T(8,128)(2,1)} %pad_maximum_fusion.3), calls=%async_computation.3 | async-start | bytes 1179648 | tf_op jit(solution)/shard_map/all_to_all | solution.py:1003
  459.3 47.5 %collective-permute-start.33 = (bf16[512,1024]{1,0:T(8,128)(2,1)}, bf16[512,1024]{1,0:T(8,128)(2,1)S(1)}, u32[]{:S(2)}, u32[]{:S(2)}) collective-permute-start(bf16[512,1024]{1,0:T(8,128)(2,1)} %shard_map.262), channel_id=1, source_target_pairs={{0,1},{1,0},{2,3},{3,2},{4,5},{5,4},{6,7},{7,6},{8,9},{9,8},{10,11... | collective-permute-start | bytes 3145736 | tf_op jit(solution)/shard_map/ppermute | solution.py:30
  492.7 27.0 %collective-permute-start.38 = (f32[128,512]{1,0:T(8,128)}, f32[128,512]{1,0:T(8,128)S(1)}, u32[]{:S(2)}, u32[]{:S(2)}) collective-permute-start(f32[128,512]{1,0:T(8,128)} %slice_add_fusion.refs_0_), channel_id=1, source_target_pairs={{0,24},{4,28},{8,16},{12,20},{16,8},{20,12},{24,0},{28,4},{1,25},{... | collective-permute-start | bytes 786440 | tf_op jit(solution)/shard_map/ppermute | solution.py:30
  493.4 28.5 %collective-permute-start.37 = (f32[128,512]{1,0:T(8,128)}, f32[128,512]{1,0:T(8,128)}, u32[]{:S(2)}, u32[]{:S(2)}) collective-permute-start(f32[128,512]{1,0:T(8,128)} %slice_add_fusion.refs_0_), channel_id=1, source_target_pairs={{0,20},{4,16},{8,28},{12,24},{16,4},{20,0},{24,12},{28,8},{1,21},{... | collective-permute-start | bytes 786440 | tf_op jit(solution)/shard_map/ppermute | solution.py:30
  502.3 38.8 %all-to-all-start.4 = ((f32[4,32,512]{2,1,0:T(8,128)}), f32[4,32,512]{2,1,0:T(8,128)S(1)}, u32[]{:S(2)}, u32[]{:S(2)}) async-start(f32[4,32,512]{2,1,0:T(8,128)} %bitcast.32), calls=%async_computation.4 | async-start | bytes 524288 | tf_op jit(solution)/shard_map/all_to_all | solution.py:1003
  519.7 26.3 %collective-permute-start.40 = (bf16[512,1024]{1,0:T(8,128)(2,1)S(1)}, bf16[512,1024]{1,0:T(8,128)(2,1)S(1)}, u32[]{:S(2)}, u32[]{:S(2)}) collective-permute-start(bf16[512,1024]{1,0:T(8,128)(2,1)S(1)} %copy-done.7), channel_id=1, source_target_pairs={{0,1},{1,0},{2,3},{3,2},{4,5},{5,4},{6,7},{7,6},{8,9},{9,8},{10,11... | collective-permute-start | bytes 3145736 | tf_op jit(solution)/shard_map/ppermute | solution.py:30
  (53 other events, 656.0 us)

commit v6 on v5

--- a/solution.py
+++ b/solution.py
@@ -111,27 +111,31 @@
     ]
     keys = (k_own_ref, k_far_ref)
     values = (v_own_ref, v_far_ref)
-    mixes = []
-    for head in range(2):
-        q_head = jnp.where(head_mask(rows, head), queries, jnp.zeros_like(queries))
-        peak = None
-        for part, at in steps:
-            place = pl.ds(part * rows + at, chunk)
-            scores = product_t(keys[part][pl.ds(at, chunk), :], q_head)
-            scores = scores * LOG2E + bias_ref[place, :]
-            score_ref[head, place, :] = scores
-            top = jnp.max(scores, axis=0, keepdims=True)
-            peak = top if peak is None else jnp.maximum(peak, top)
-        total, mix = None, None
-        for part, at in steps:
-            place = pl.ds(part * rows + at, chunk)
-            raised = jnp.exp2(score_ref[head, place, :] - peak)
-            share = jnp.sum(raised, axis=0, keepdims=True)
-            piece = product_rows(values[part][pl.ds(at, chunk), :], bfloat(raised))
-            total = share if total is None else total + share
-            mix = piece if mix is None else mix + piece
-        mixes.append((mix * (1.0 / total))[head * HD : (head + 1) * HD, :])
-        lse_ref[0, pl.ds(head, 1), :] = peak + jnp.log2(total)
+    q_both = jnp.concatenate(
+        [jnp.where(head_mask(rows, h), queries, jnp.zeros_like(queries)) for h in range(2)], axis=0
+    )
+    peak = None
+    for part, at in steps:
+        place = pl.ds(part * rows + at, chunk)
+        bias = bias_ref[place, :]
+        scores = product_t(keys[part][pl.ds(at, chunk), :], q_both)
+        scores = scores * LOG2E + jnp.concatenate([bias, bias], axis=1)
+        score_ref[place, :] = scores
+        top = jnp.max(scores, axis=0, keepdims=True)
+        peak = top if peak is None else jnp.maximum(peak, top)
+    total, mix = None, None
+    for part, at in steps:
+        place = pl.ds(part * rows + at, chunk)
+        raised = jnp.exp2(score_ref[place, :] - peak)
+        share = jnp.sum(raised, axis=0, keepdims=True)
+        piece = product_rows(values[part][pl.ds(at, chunk), :], bfloat(raised))
+        total = share if total is None else total + share
+        mix = piece if mix is None else mix + piece
+    mix = mix * (1.0 / total)
+    mixes = [mix[:HD, :rows], mix[HD:, rows:]]
+    lse = peak + jnp.log2(total)
+    lse_ref[0, pl.ds(0, 1), :] = lse[:, :rows]
+    lse_ref[0, pl.ds(1, 1), :] = lse[:, rows:]
     out_ref[...] = bfloat(jnp.concatenate(mixes, axis=0).T)
 
 
@@ -173,7 +177,9 @@
         g_heads.append(jnp.where(chosen, grads, jnp.zeros_like(grads)))
         deltas.append(jnp.sum(products[head * HD : (head + 1) * HD, :], axis=0, keepdims=True))
         lses.append(lse_ref[0, pl.ds(head, 1), :])
-    grad_q = [None, None]
+    q_both, g_both = jnp.concatenate(q_heads, axis=0), jnp.concatenate(g_heads, axis=0)
+    lse, delta = jnp.concatenate(lses, axis=1), jnp.concatenate(deltas, axis=1)
+    grad_q = None
     for part in range(2):
         key_ref = (k_own_ref, k_far_ref)[part]
         value_ref = (v_own_ref, v_far_ref)[part]
@@ -182,22 +188,15 @@
         for at in range(0, rows, chunk):
             here = pl.ds(at, chunk)
             keys, values = key_ref[here, :], value_ref[here, :]
-            grad_k, grad_v = None, None
-            for head in range(2):
-                scores = product_t(keys, q_heads[head])
-                bias = bias_ref[pl.ds(part * rows + at, chunk), :]
-                weights = jnp.exp2(scores * LOG2E + (bias - lses[head]))
-                grad_w = product_t(values, g_heads[head])
-                grad_s = bfloat(weights * (grad_w - deltas[head]))
-                piece_v = product(bfloat(weights), g_heads[head])
-                piece_k = product(grad_s, q_heads[head])
-                piece_q = product_rows(keys, grad_s)
-                grad_v = piece_v if grad_v is None else grad_v + piece_v
-                grad_k = piece_k if grad_k is None else grad_k + piece_k
-                grad_q[head] = piece_q if grad_q[head] is None else grad_q[head] + piece_q
-            dk_ref[here, :] = grad_k.astype(dk_ref.dtype)
-            dv_ref[here, :] = grad_v.astype(dv_ref.dtype)
-    joined = jnp.concatenate([grad_q[h][h * HD : (h + 1) * HD, :] for h in range(2)], axis=0)
+            bias = bias_ref[pl.ds(part * rows + at, chunk), :]
+            scores = product_t(keys, q_both)
+            weights = jnp.exp2(scores * LOG2E + (jnp.concatenate([bias, bias], axis=1) - lse))
+            grad_s = bfloat(weights * (product_t(values, g_both) - delta))
+            dv_ref[here, :] = product(bfloat(weights), g_both).astype(dv_ref.dtype)
+            dk_ref[here, :] = product(grad_s, q_both).astype(dk_ref.dtype)
+            piece = product_rows(keys, grad_s)
+            grad_q = piece if grad_q is None else grad_q + piece
+    joined = jnp.concatenate([grad_q[:HD, :rows], grad_q[HD:, rows:]], axis=0)
     dq_ref[...] = bfloat((joined * 0.125).T)
 
 
@@ -218,7 +217,7 @@
     pairs = width // PAIR
     fixed, columns, stat = attention_specs(rows)
     return pl.pallas_call(
-        functools.partial(attend_kernel, causal, 256),
+        functools.partial(attend_kernel, causal, 512),
         grid=(pairs,),
         in_specs=fixed + [columns] * 5,
         out_specs=[columns, stat],
@@ -228,7 +227,7 @@
         ],
         scratch_shapes=[
             pltpu.VMEM((2 * rows, rows), jnp.float32),
-            pltpu.VMEM((2, 2 * rows, rows), jnp.float32),
+            pltpu.VMEM((2 * rows, 2 * rows), jnp.float32),
         ],
         compiler_params=pltpu.CompilerParams(vmem_limit_bytes=VMEM_LIMIT),
         cost_estimate=pl.CostEstimate(
@@ -242,7 +241,7 @@
     pairs = width // PAIR
     fixed, columns, stat = attention_specs(rows)
     return pl.pallas_call(
-        lambda *refs: attend_back_kernel(causal, 256, *refs[:12], *refs[12 + len(after) :]),
+        lambda *refs: attend_back_kernel(causal, 512, *refs[:12], *refs[12 + len(after) :]),
         grid=(pairs,),
         in_specs=fixed + [columns] * 7 + [stat] + [HBM] * len(after),
         out_specs=[columns] * 5,

time: 570 us -> 564 us (0.989)
  Pallas kernels: 397 us -> 387 us
    pallas_call x6, Pallas kernels: 140 us -> 130 us  [the longest x3 76.7 us: attend_back(): pl.pallas_call(lambda *refs: attend_back_kernel(causal, 512, *refs[:12],...]
  transfers between devices with their start and end apart: 47 -> 47, of which waited for: 7 -> 9; matrix products, arithmetic and copies ran while one was open for 5% -> 5% of each run, Pallas kernels for 62% -> 61%
where the time goes in v6:
time: 564 us; the launch traced here: 553 us
  Pallas kernels  387 us (69%)
  starting transfers between devices  74.9 us (13%)
  waiting for transfers between devices  49.9 us (9%)
  local copies, waits for them, and re-layouts  30.9 us (5%)
  other arithmetic  8.2 us (1%)
    pallas_call x20, Pallas kernels, call(): pl.pallas_call(kernel, in_specs=specs, out_specs=[IN_VMEM if len(out) ==...  258 us
    pallas_call x3, Pallas kernels, attend_back(): pl.pallas_call(lambda *refs: attend_back_kernel(causal, 512, *refs[:12],...  76.7 us
    pallas_call x3, Pallas kernels, attend(): pl.pallas_call(functools.partial(attend_kernel, causal, 512), grid=(pairs...  53.1 us
    ppermute x8, waiting for transfers between devices, across(): lax.ppermute(first, 'wide', [(i, i ^ (2 if i % 2 else 4)) for i in range(...  41 us
    ppermute x16, starting transfers between devices, begin(): lax.ppermute(array, 'wide', [(i, i ^ steps[i % 2][which]) for i in range(...  23.3 us
    all_to_all x6, starting transfers between devices, shards(): lax.all_to_all(array, axis, split_axis=0, concat_axis=0, tiled=True)  22.9 us
    ppermute x17, starting transfers between devices, swap(): lax.ppermute(array, axis, [(i, i ^ bit) for i in range(lax.axis_size(axis...  20.3 us
    unnamed x85, local copies, waits for them, and re-layouts  16 us
  transfers between devices with their start and end apart: 47, of which 9 were waited for; matrix products, arithmetic and copies ran while one was open for 5% of the time, Pallas kernels for 61%

profile of v6, /device:TPU:0, one launch (start us, length us, event | category | flops | bytes accessed | tf_op | source)
XLA Modules:
  0.0 553.1 jit_solution(9015872854403991094)
XLA Ops:
  29.6 8.0 %collective-permute-done.1.refs_3_ = bf16[400,1024]{1,0:T(8,128)(2,1)S(1)} collective-permute-done((bf16[400,1024]{1,0:T(8,128)(2,1)}, bf16[400,1024]{1,0:T(8,128)(2,1)S(1)}, u32[]{:S(2)}, u32[]{:S(2)}) %collective-permute-start.1) | collective-permute-done | bytes 819232 | tf_op jit(solution)/shard_map/ppermute | solution.py:927
  44.6 13.7 %shard_map.242 = (bf16[512,1024]{1,0:T(8,128)(2,1)}, bf16[512,1024]{1,0:T(8,128)(2,1)}, bf16[512,1024]{1,0:T(8,128)(2,1)}, bf16[512,1024]{1,0:T(8,128)(2,1)}, bf...) custom-call(bf16[512,1024]{1,0:T(8,128)(2,1)} %x_ref.4, bf16[512,1024]{1,0:T(8,128)(2,1)} %collective-permute-done.3.far_ref, ...), custom_call_target="tpu_custom_call" | custom-call | flops 5368709120 | bytes 5373952 | tf_op jit(solution)/shard_map/pallas_call | solution.py:709
  64.3 17.6 %shard_map.243 = (bf16[512,1024]{1,0:T(8,128)(2,1)}, f32[8,8,512]{2,1,0:T(8,128)}) custom-call(s32[1]{0:T(128)} %bitcast.half_ref.refs_0_, s32[1,512]{1,0:T(1,128)} %bitcast.1.qid_ref.refs_1_, s32[512,1]{1,0:T(8,128)} %copy.47.kid_own_ref.refs_2_, s32[512,1]{1,0:T(8,128)} %copy.48.kid_far_ref.refs_3_, bf16[512,1024]{1,0:T(8,128)(2,1)} %get-tuple-element.129.q_ref.refs_4_, ...), custom_call_target="tpu_custom_call" | custom-call | flops 8589934592 | bytes 6291456 | tf_op jit(solution)/shard_map/pallas_call | solution.py:219
  87.3 13.8 %shard_map.244 = (bf16[512,1024]{1,0:T(8,128)(2,1)}, bf16[512,1024]{1,0:T(8,128)(2,1)}, bf16[512,1024]{1,0:T(8,128)(2,1)}, bf16[512,1024]{1,0:T(8,128)(2,1)}, bf...) custom-call(bf16[512,1024]{1,0:T(8,128)(2,1)} %x_ref.5, bf16[512,1024]{1,0:T(8,128)(2,1)} %collective-permute-done.5.far_ref, ...), custom_call_target="tpu_custom_call" | custom-call | flops 5368709120 | bytes 5242880 | tf_op jit(solution)/shard_map/pallas_call | solution.py:709
  105.2 17.6 %shard_map.245 = (bf16[512,1024]{1,0:T(8,128)(2,1)}, f32[8,8,512]{2,1,0:T(8,128)}) custom-call(s32[1]{0:T(128)} %bitcast.half_ref.refs_0_, s32[1,512]{1,0:T(1,128)} %bitcast.1.qid_ref.refs_1_, s32[512,1]{1,0:T(8,128)} %copy.47.kid_own_ref.refs_2_, s32[512,1]{1,0:T(8,128)} %copy.48.kid_far_ref.refs_3_, bf16[512,1024]{1,0:T(8,128)(2,1)} %get-tuple-element.139.q_ref.refs_4_, ...), custom_call_target="tpu_custom_call" | custom-call | flops 8589934592 | bytes 6291456 | tf_op jit(solution)/shard_map/pallas_call | solution.py:219
  122.8 5.0 collective-permute-done.12.refs_3_
  128.9 8.0 %shard_map.246 = (f32[512,1024]{1,0:T(8,128)}, f32[512,128]{1,0:T(8,128)}, bf16[1,1024,1024]{2,1,0:T(8,128)(2,1)}) custom-call(bf16[512,1024]{1,0:T(8,128)(2,1)} %x_ref.4, bf16[512,1024]{1,0:T(8,128)(2,1)} %get-tuple-element.145.mix_ref.refs_9_, f32[8,1024]{1,0:T(8,128)} %convert_bitcast_fusion.1.gains_ref.refs_5_, ...), custom_call_target="tpu_custom_call" | custom-call | flops 1073741824 | bytes 7372800 | tf_op jit(solution)/shard_map/pallas_call | solution.py:709
  142.0 14.9 %shard_map.247 = (bf16[512,4096]{1,0:T(8,128)(2,1)}, bf16[512,4096]{1,0:T(8,128)(2,1)}, bf16[4,1024,1024]{2,1,0:T(8,128)(2,1)}) custom-call(f32[512,1024]{1,0:T(8,128)} %get-tuple-element.149.n_ref.refs_3_, f32[8,1024]{1,0:T(8,128)} %convert_bitcast_fusion.1.gains_ref.refs_5_, bf16[640,1024]{1,0:T(8,128)(2,1)} %slice_dynamic-update-slice_fusion.refs_0_, ...), custom_call_target="tpu_custom_call" | custom-call | flops 4294967296 | bytes 7372800 | tf_op jit(solution)/shard_map/pallas_call | solution.py:709
  159.0 4.2 collective-permute-done.17.refs_3_
  163.2 17.6 %shard_map.248 = (bf16[512,512]{1,0:T(8,128)(2,1)}, bf16[512,512]{1,0:T(8,128)(2,1)}, f32[512,1024]{1,0:T(8,128)}, f32[512,128]{1,0:T(8,128)}, bf16[512,1024]{1,...) custom-call(f32[512,1024]{1,0:T(8,128)} %get-tuple-element.149.n_ref.refs_3_, ...), custom_call_target="tpu_custom_call" | custom-call | flops 5368709120 | bytes 11573248 | tf_op jit(solution)/shard_map/pallas_call | solution.py:709
  183.6 10.0 %shard_map.249 = (f32[512,1024]{1,0:T(8,128)}, f32[512,128]{1,0:T(8,128)}, bf16[512,1024]{1,0:T(8,128)(2,1)}, bf16[2,1024,1024]{2,1,0:T(8,128)(2,1)}) custom-call(bf16[512,1024]{1,0:T(8,128)(2,1)} %x_ref.5, bf16[512,1024]{1,0:T(8,128)(2,1)} %get-tuple-element.156.mix_ref.refs_9_, f32[8,1024]{1,0:T(8,128)} %convert_bitcast_fusion.1.gains_ref.refs_5_, ...), custom_call_target="tpu_custom_call" | custom-call | flops 2147483648 | bytes 4227072 | tf_op jit(solution)/shard_map/pallas_call | solution.py:709
  198.0 9.6 %collective-permute-done.24.refs_3_ = bf16[384,1024]{1,0:T(8,128)(2,1)} collective-permute-done((bf16[384,1024]{1,0:T(8,128)(2,1)S(1)}, bf16[384,1024]{1,0:T(8,128)(2,1)}, u32[]{:S(2)}, u32[]{:S(2)}) %collective-permute-start.24) | collective-permute-done | bytes 786464 | tf_op jit(solution)/shard_map/ppermute | solution.py:927
  209.3 11.7 %shard_map.250 = (bf16[512,1024]{1,0:T(8,128)(2,1)}, bf16[512,1024]{1,0:T(8,128)(2,1)}, bf16[512,1024]{1,0:T(8,128)(2,1)}, bf16[512,1024]{1,0:T(8,128)(2,1)}, bf16[2,1024,1024]{2,1,0:T(8,128)(2,1)}) custom-call(bf16[512,1024]{1,0:T(8,128)(2,1)} %get-tuple-element.160.x_ref, bf16[512,1024]{1,0:T(8,128)(2,1)} %collective-permute-done.21.far_ref, ...), custom_call_target="tpu_custom_call" | custom-call | flops 4294967296 | bytes 5242880 | tf_op jit(solution)/shard_map/pallas_call | solution.py:709
  221.6 17.9 %shard_map.251 = (bf16[512,1024]{1,0:T(8,128)(2,1)}, f32[8,8,512]{2,1,0:T(8,128)}) custom-call(s32[1]{0:T(128)} %bitcast.half_ref.refs_0_, s32[1,512]{1,0:T(1,128)} %bitcast.1.qid_ref.refs_1_, s32[512,1]{1,0:T(8,128)} %copy.47.kid_own_ref.refs_2_, s32[512,1]{1,0:T(8,128)} %copy.48.kid_far_ref.refs_3_, bf16[512,1024]{1,0:T(8,128)(2,1)} %get-tuple-element.159.q_ref.refs_4_, ...), custom_call_target="tpu_custom_call" | custom-call | flops 8589934592 | bytes 6291456 | tf_op jit(solution)/shard_map/pallas_call | solution.py:219
  239.6 8.6 %shard_map.252 = (f32[512,1024]{1,0:T(8,128)}, f32[512,128]{1,0:T(8,128)}, bf16[1,1024,1024]{2,1,0:T(8,128)(2,1)}) custom-call(f32[512,1024]{1,0:T(8,128)} %get-tuple-element.168.x_ref.n_ref, bf16[512,1024]{1,0:T(8,128)(2,1)} %get-tuple-element.167.mix_ref.refs_9_, f32[8,1024]{1,0:T(8,128)} %convert_bitcast_fusion.1.gains_ref.refs_5_, ...), custom_call_target="tpu_custom_call" | custom-call | flops 1073741824 | bytes 6324224 | tf_op jit(solution)/shard_map/pallas_call | solution.py:709
  249.7 14.1 %collective-permute-done.27.refs_3_ = bf16[512,1024]{1,0:T(8,128)(2,1)} collective-permute-done((bf16[512,1024]{1,0:T(8,128)(2,1)}, bf16[512,1024]{1,0:T(8,128)(2,1)}, u32[]{:S(2)}, u32[]{:S(2)}) %collective-permute-start.27) | collective-permute-done | bytes 1048608 | tf_op jit(solution)/shard_map/ppermute | solution.py:927
  263.9 14.6 %shard_map.253 = (bf16[512,4096]{1,0:T(8,128)(2,1)}, bf16[512,4096]{1,0:T(8,128)(2,1)}, bf16[4,1024,1024]{2,1,0:T(8,128)(2,1)}) custom-call(f32[512,1024]{1,0:T(8,128)} %get-tuple-element.169.n_ref.refs_3_, f32[8,1024]{1,0:T(8,128)} %convert_bitcast_fusion.1.gains_ref.refs_5_, bf16[512,1024]{1,0:T(8,128)(2,1)} %copy-done.15, ...), custom_call_target="tpu_custom_call" | custom-call | flops 4294967296 | bytes 6324224 | tf_op jit(solution)/shard_map/pallas_call | solution.py:709
  280.1 17.6 %shard_map.254 = (bf16[512,512]{1,0:T(8,128)(2,1)}, bf16[512,512]{1,0:T(8,128)(2,1)}, f32[512,1024]{1,0:T(8,128)}, f32[512,128]{1,0:T(8,128)}, bf16[512,1024]{1,...) custom-call(f32[512,1024]{1,0:T(8,128)} %get-tuple-element.169.n_ref.refs_3_, ...), custom_call_target="tpu_custom_call" | custom-call | flops 5368709120 | bytes 11573248 | tf_op jit(solution)/shard_map/pallas_call | solution.py:709
  297.7 24.0 %shard_map.255 = (bf16[512,1024]{1,0:T(8,128)(2,1)}, f32[512,1024]{1,0:T(8,128)}, bf16[512,1024]{1,0:T(8,128)(2,1)}, bf16[8,272,512]{2,1,0:T(8,128)(2,1)}) custom-call(bf16[512,1024]{1,0:T(8,128)(2,1)} %refs_0_.1, f32[512,1024]{1,0:T(8,128)} %get-tuple-element.176.refs_1_, f32[512,128]{1,0:T(8,128)} %get-tuple-element.177.refs_2_, ...), custom_call_target="tpu_custom_call" | custom-call | flops 12884901888 | bytes 32014336 | tf_op jit(solution)/shard_map/pallas_call | solution.py:709
  325.6 25.5 %shard_map.256 = (bf16[512,1024]{1,0:T(8,128)(2,1)}, bf16[512,1024]{1,0:T(8,128)(2,1)}, bf16[512,1024]{1,0:T(8,128)(2,1)}, bf16[512,1024]{1,0:T(8,128)(2,1)}, bf16[512,1024]{1,0:T(8,128)(2,1)}) custom-call(s32[1]{0:T(128)} %bitcast.half_ref.refs_0_, s32[1,512]{1,0:T(1,128)} %bitcast.1.qid_ref.refs_1_, s32[512,1]{1,0:T(8,128)} %copy.47.kid_own_ref.refs_2_, ...), custom_call_target="tpu_custom_call" | custom-call | flops 21474836480 | bytes 12582912 | tf_op jit(solution)/shard_map/pallas_call | solution.py:243
  354.0 7.4 %shard_map.257 = bf16[512,1024]{1,0:T(8,128)(2,1)} custom-call(bf16[512,1024]{1,0:T(8,128)(2,1)} %get-tuple-element.192.refs_0_, bf16[512,1024]{1,0:T(8,128)(2,1)} %get-tuple-element.193.refs_1_, bf16[2,1024,1024]{2,1,0:T(8,128)(2,1)} %get-tuple-element.194.refs_2_.refs_3_), custom_call_target="tpu_custom_call" | custom-call | flops 2147483648 | bytes 6291456 | tf_op jit(solution)/shard_map/pallas_call | solution.py:709
  363.1 8.0 %shard_map.258.refs_0_ = f32[512,1024]{1,0:T(8,128)} custom-call(bf16[512,1024]{1,0:T(8,128)(2,1)} %refs_0_.2, bf16[512,1024]{1,0:T(8,128)(2,1)} %get-tuple-element.196.refs_1_, bf16[512,1024]{1,0:T(8,128)(2,1)} %get-tuple-element.197.refs_2_, bf16[2,1024,1024]{2,1,0:T(8,128)(2,1)} %get-tuple-element.194.refs_2_.refs_3_), custom_call_target="tpu_custom_call" | custom-call | flops 2147483648 | bytes 7340032 | tf_op jit(solution)/shard_map/pallas_call | solution.py:709
  371.1 9.1 %shard_map.259 = (f32[512,1024]{1,0:T(8,128)}, bf16[512,1024]{1,0:T(8,128)(2,1)}) custom-call(f32[512,1024]{1,0:T(8,128)} %get-tuple-element.199.dz_ref, bf16[512,1024]{1,0:T(8,128)(2,1)} %get-tuple-element.190.dq_ref, f32[512,1024]{1,0:T(8,128)} %get-tuple-element.168.x_ref.n_ref, f32[512,128]{1,0:T(8,128)} %get-tuple-element.200.r_ref, ...), custom_call_target="tpu_custom_call" | custom-call | flops 2147483648 | bytes 9732096 | tf_op jit(solution)/shard_map/pallas_call | solution.py:709
  386.6 24.6 %shard_map.260 = (bf16[512,1024]{1,0:T(8,128)(2,1)}, f32[512,1024]{1,0:T(8,128)}, bf16[512,1024]{1,0:T(8,128)(2,1)}, bf16[8,272,512]{2,1,0:T(8,128)(2,1)}) custom-call(f32[512,1024]{1,0:T(8,128)} %shard_map.258.refs_0_, f32[512,1024]{1,0:T(8,128)} %get-tuple-element.204.refs_1_, f32[512,128]{1,0:T(8,128)} %get-tuple-element.205.refs_2_, ...), custom_call_target="tpu_custom_call" | custom-call | flops 12884901888 | bytes 34111488 | tf_op jit(solution)/shard_map/pallas_call | solution.py:709
  415.5 25.6 %shard_map.261 = (bf16[512,1024]{1,0:T(8,128)(2,1)}, bf16[512,1024]{1,0:T(8,128)(2,1)}, bf16[512,1024]{1,0:T(8,128)(2,1)}, bf16[512,1024]{1,0:T(8,128)(2,1)}, bf16[512,1024]{1,0:T(8,128)(2,1)}) custom-call(s32[1]{0:T(128)} %bitcast.half_ref.refs_0_, s32[1,512]{1,0:T(1,128)} %bitcast.1.qid_ref.refs_1_, s32[512,1]{1,0:T(8,128)} %copy.47.kid_own_ref.refs_2_, ...), custom_call_target="tpu_custom_call" | custom-call | flops 21474836480 | bytes 12582912 | tf_op jit(solution)/shard_map/pallas_call | solution.py:243
  448.5 7.3 %shard_map.262 = bf16[512,1024]{1,0:T(8,128)(2,1)} custom-call(bf16[512,1024]{1,0:T(8,128)(2,1)} %get-tuple-element.227.refs_0_, bf16[512,1024]{1,0:T(8,128)(2,1)} %get-tuple-element.228.refs_1_, bf16[3,1024,1024]{2,1,0:T(8,128)(2,1)} %get-tuple-element.229.refs_2_.refs_5_), custom_call_target="tpu_custom_call" | custom-call | flops 2147483648 | bytes 8388608 | tf_op jit(solution)/shard_map/pallas_call | solution.py:709
  458.1 25.6 %shard_map.263 = (bf16[512,1024]{1,0:T(8,128)(2,1)}, bf16[512,1024]{1,0:T(8,128)(2,1)}, bf16[512,1024]{1,0:T(8,128)(2,1)}, bf16[512,1024]{1,0:T(8,128)(2,1)}, bf16[512,1024]{1,0:T(8,128)(2,1)}) custom-call(s32[1]{0:T(128)} %bitcast.half_ref.refs_0_, s32[1,512]{1,0:T(1,128)} %bitcast.1.qid_ref.refs_1_, s32[512,1]{1,0:T(8,128)} %copy.47.kid_own_ref.refs_2_, ...), custom_call_target="tpu_custom_call" | custom-call | flops 21474836480 | bytes 12582912 | tf_op jit(solution)/shard_map/pallas_call | solution.py:243
  487.5 7.4 %shard_map.264 = bf16[512,1024]{1,0:T(8,128)(2,1)} custom-call(bf16[512,1024]{1,0:T(8,128)(2,1)} %get-tuple-element.235.refs_0_, bf16[512,1024]{1,0:T(8,128)(2,1)} %get-tuple-element.236.refs_1_, bf16[3,1024,1024]{2,1,0:T(8,128)(2,1)} %get-tuple-element.237.refs_2_.refs_5_), custom_call_target="tpu_custom_call" | custom-call | flops 2147483648 | bytes 8388608 | tf_op jit(solution)/shard_map/pallas_call | solution.py:709
  502.6 10.7 %shard_map.265 = f32[512,1024]{1,0:T(8,128)} custom-call(f32[512,1024]{1,0:T(8,128)} %get-tuple-element.238.refs_0_, bf16[512,1024]{1,0:T(8,128)(2,1)} %copy-done.4, bf16[512,1024]{1,0:T(8,128)(2,1)} %get-tuple-element.223.refs_2_, bf16[512,1024]{1,0:T(8,128)(2,1)} %get-tuple-element.239.refs_3_, bf16[512,1024]{1,0:T(8,128)(2,1)} %get-tuple-element.240.refs_4_, ...), custom_call_target="tpu_custom_call" | custom-call | flops 3221225472 | bytes 12582912 | tf_op jit(solution)/shard_map/pallas_call | solution.py:709
  516.7 17.8 %shard_map.266 = f32[128,512]{1,0:T(8,128)} custom-call(f32[128,512]{1,0:T(8,128)} %slice_add_fusion.refs_0_, f32[128,512]{1,0:T(8,128)} %copy-done.32, f32[128,512]{1,0:T(8,128)} %copy-done.35, f32[128,512]{1,0:T(8,128)} %copy-done.34, f32[128,512]{1,0:T(8,128)} %copy-done.33, f32[128,512]{1,0:T(8,128)} %collective-permute-done.37.refs_5_, ...), custom_call_target="tpu_custom_call" | custom-call | flops 16106127360 | bytes 2097152 | tf_op jit(solution)/shard_map/pallas_call | solution.py:709
  534.5 4.3 all-to-all-start.5
  540.5 10.7 %shard_map.267 = f32[512,1024]{1,0:T(8,128)} custom-call(f32[512,1024]{1,0:T(8,128)} %get-tuple-element.242.refs_0_, bf16[512,1024]{1,0:T(8,128)(2,1)} %copy-done.5, bf16[512,1024]{1,0:T(8,128)(2,1)} %get-tuple-element.232.refs_2_, bf16[512,1024]{1,0:T(8,128)(2,1)} %get-tuple-element.243.refs_3_, bf16[512,1024]{1,0:T(8,128)(2,1)} %get-tuple-element.244.refs_4_, ...), custom_call_target="tpu_custom_call" | custom-call | flops 3221225472 | bytes 12582912 | tf_op jit(solution)/shard_map/pallas_call | solution.py:709
  (227 shorter events, 118.6 us)
Async XLA Ops:
  3.6 24.0 %collective-permute-start.4 = (bf16[400,1024]{1,0:T(8,128)(2,1)}, bf16[400,1024]{1,0:T(8,128)(2,1)}, u32[]{:S(2)}, u32[]{:S(2)}) collective-permute-start(bf16[400,1024]{1,0:T(8,128)(2,1)} %pad_maximum_fusion.1.refs_0_), channel_id=1, source_target_pairs={{0,16},{4,12},{8,24},{12,4},{16,0},{20,28},{24,8},{28,20},{1,17},{... | collective-permute-start | bytes 2457608 | tf_op jit(solution)/shard_map/ppermute | solution.py:917
  8.0 35.0 %collective-permute-start.3 = (bf16[512,1024]{1,0:T(8,128)(2,1)S(1)}, bf16[512,1024]{1,0:T(8,128)(2,1)}, u32[]{:S(2)}, u32[]{:S(2)}) collective-permute-start(bf16[512,1024]{1,0:T(8,128)(2,1)S(1)} %copy-done.6), channel_id=1, source_target_pairs={{0,1},{1,0},{2,3},{3,2},{4,5},{5,4},{6,7},{7,6},{8,9},{9,8},{10,11... | collective-permute-start | bytes 3145736 | tf_op jit(solution)/shard_map/ppermute | solution.py:30
  37.6 48.1 %collective-permute-start.7 = (bf16[384,1024]{1,0:T(8,128)(2,1)}, bf16[384,1024]{1,0:T(8,128)(2,1)}, u32[]{:S(2)}, u32[]{:S(2)}) collective-permute-start(bf16[384,1024]{1,0:T(8,128)(2,1)} %bitcast.68), channel_id=1, source_target_pairs={{0,16},{4,12},{8,24},{12,4},{16,0},{20,28},{24,8},{28,20},{1,17},{... | collective-permute-start | bytes 2359304 | tf_op jit(solution)/shard_map/ppermute | solution.py:917
  39.4 24.4 %collective-permute-start.6 = (bf16[384,1024]{1,0:T(8,128)(2,1)}, bf16[384,1024]{1,0:T(8,128)(2,1)}, u32[]{:S(2)}, u32[]{:S(2)}) collective-permute-start(bf16[384,1024]{1,0:T(8,128)(2,1)} %bitcast.69), channel_id=1, source_target_pairs={{0,8},{4,20},{8,0},{12,28},{16,24},{20,4},{24,16},{28,12},{1,9},{5... | collective-permute-start | bytes 2359304 | tf_op jit(solution)/shard_map/ppermute | solution.py:917
  43.0 42.7 %collective-permute-start.5 = (bf16[512,1024]{1,0:T(8,128)(2,1)}, bf16[512,1024]{1,0:T(8,128)(2,1)}, u32[]{:S(2)}, u32[]{:S(2)}) collective-permute-start(bf16[512,1024]{1,0:T(8,128)(2,1)} %x_ref.5), channel_id=1, source_target_pairs={{0,1},{1,0},{2,3},{3,2},{4,5},{5,4},{6,7},{7,6},{8,9},{9,8},{10,11... | collective-permute-start | bytes 3145736 | tf_op jit(solution)/shard_map/ppermute | solution.py:30
  59.0 42.1 %collective-permute-start.10 = (bf16[640,1024]{1,0:T(8,128)(2,1)}, bf16[640,1024]{1,0:T(8,128)(2,1)}, u32[]{:S(2)}, u32[]{:S(2)}) collective-permute-start(bf16[640,1024]{1,0:T(8,128)(2,1)} %slice_dynamic-update-slice_fusion.refs_0_), channel_id=1, source_target_pairs={{0,8},{4,20},{8,0},{12,28},{16,24},{20,4},{24,16},{28,12},{1,9},{5... | collective-permute-start | bytes 3932168 | tf_op jit(solution)/shard_map/ppermute | solution.py:917
  81.9 40.9 %collective-permute-start.11 = (bf16[640,1024]{1,0:T(8,128)(2,1)}, bf16[640,1024]{1,0:T(8,128)(2,1)}, u32[]{:S(2)}, u32[]{:S(2)}) collective-permute-start(bf16[640,1024]{1,0:T(8,128)(2,1)} %slice_dynamic-update-slice_fusion.refs_0_), channel_id=1, source_target_pairs={{0,16},{4,12},{8,24},{12,4},{16,0},{20,28},{24,8},{28,20},{1,17},{... | collective-permute-start | bytes 3932168 | tf_op jit(solution)/shard_map/ppermute | solution.py:917
  85.7 51.2 %collective-permute-start.15 = (bf16[640,1024]{1,0:T(8,128)(2,1)}, bf16[640,1024]{1,0:T(8,128)(2,1)}, u32[]{:S(2)}, u32[]{:S(2)}) collective-permute-start(bf16[640,1024]{1,0:T(8,128)(2,1)} %constant_dynamic-update-slice_fusion.6.refs_0_), channel_id=1, source_target_pairs={{0,8},{4,20},{8,0},{12,28},{16,24},{20,4},{24,16},{28,12},{1,9},{5... | collective-permute-start | bytes 3932168 | tf_op jit(solution)/shard_map/ppermute | solution.py:917
  101.1 26.8 %collective-permute-start.12 = (bf16[640,1024]{1,0:T(8,128)(2,1)}, bf16[640,1024]{1,0:T(8,128)(2,1)S(1)}, u32[]{:S(2)}, u32[]{:S(2)}) collective-permute-start(bf16[640,1024]{1,0:T(8,128)(2,1)} %collective-permute-done.10.refs_1_), channel_id=1, source_target_pairs={{0,16},{4,12},{8,24},{12,4},{16,0},{20,28},{24,8},{28,20},{1,17},{... | collective-permute-start | bytes 3932168 | tf_op jit(solution)/shard_map/ppermute | solution.py:927
  103.7 55.3 %collective-permute-start.16 = (bf16[640,1024]{1,0:T(8,128)(2,1)}, bf16[640,1024]{1,0:T(8,128)(2,1)}, u32[]{:S(2)}, u32[]{:S(2)}) collective-permute-start(bf16[640,1024]{1,0:T(8,128)(2,1)} %constant_dynamic-update-slice_fusion.6.refs_0_), channel_id=1, source_target_pairs={{0,16},{4,12},{8,24},{12,4},{16,0},{20,28},{24,8},{28,20},{1,17},{... | collective-permute-start | bytes 3932168 | tf_op jit(solution)/shard_map/ppermute | solution.py:917
  136.9 26.3 %collective-permute-start.17 = (bf16[640,1024]{1,0:T(8,128)(2,1)}, bf16[640,1024]{1,0:T(8,128)(2,1)}, u32[]{:S(2)}, u32[]{:S(2)}) collective-permute-start(bf16[640,1024]{1,0:T(8,128)(2,1)} %collective-permute-done.15.refs_1_), channel_id=1, source_target_pairs={{0,16},{4,12},{8,24},{12,4},{16,0},{20,28},{24,8},{28,20},{1,17},{... | collective-permute-start | bytes 3932168 | tf_op jit(solution)/shard_map/ppermute | solution.py:927
  141.4 42.2 %collective-permute-start.19 = (bf16[256,1024]{1,0:T(8,128)(2,1)S(1)}, bf16[256,1024]{1,0:T(8,128)(2,1)}, u32[]{:S(2)}, u32[]{:S(2)}) collective-permute-start(bf16[256,1024]{1,0:T(8,128)(2,1)S(1)} %pad_maximum_fusion.5.refs_0_), channel_id=1, source_target_pairs={{0,16},{4,12},{8,24},{12,4},{16,0},{20,28},{24,8},{28,20},{1,17},{... | collective-permute-start | bytes 1572872 | tf_op jit(solution)/shard_map/ppermute | solution.py:917
  156.9 26.7 %collective-permute-start.20 = (bf16[256,1024]{1,0:T(8,128)(2,1)S(1)}, bf16[256,1024]{1,0:T(8,128)(2,1)}, u32[]{:S(2)}, u32[]{:S(2)}) collective-permute-start(bf16[256,1024]{1,0:T(8,128)(2,1)S(1)} %collective-permute-done.18.refs_1_), channel_id=1, source_target_pairs={{0,16},{4,12},{8,24},{12,4},{16,0},{20,28},{24,8},{28,20},{1,17},{... | collective-permute-start | bytes 1572872 | tf_op jit(solution)/shard_map/ppermute | solution.py:927
  158.5 24.8 %collective-permute-start.22 = (bf16[384,1024]{1,0:T(8,128)(2,1)S(1)}, bf16[384,1024]{1,0:T(8,128)(2,1)S(1)}, u32[]{:S(2)}, u32[]{:S(2)}) collective-permute-start(bf16[384,1024]{1,0:T(8,128)(2,1)S(1)} %pad_maximum_fusion.2.refs_0_), channel_id=1, source_target_pairs={{0,8},{4,20},{8,0},{12,28},{16,24},{20,4},{24,16},{28,12},{1,9},{5... | collective-permute-start | bytes 2359304 | tf_op jit(solution)/shard_map/ppermute | solution.py:917
  180.8 28.6 %collective-permute-start.21 = (bf16[512,1024]{1,0:T(8,128)(2,1)}, bf16[512,1024]{1,0:T(8,128)(2,1)}, u32[]{:S(2)}, u32[]{:S(2)}) collective-permute-start(bf16[512,1024]{1,0:T(8,128)(2,1)} %get-tuple-element.160.x_ref), channel_id=1, source_target_pairs={{0,1},{1,0},{2,3},{3,2},{4,5},{5,4},{6,7},{7,6},{8,9},{9,8},{10,11... | collective-permute-start | bytes 3145736 | tf_op jit(solution)/shard_map/ppermute | solution.py:30
  183.3 24.4 %collective-permute-start.24 = (bf16[384,1024]{1,0:T(8,128)(2,1)S(1)}, bf16[384,1024]{1,0:T(8,128)(2,1)}, u32[]{:S(2)}, u32[]{:S(2)}) collective-permute-start(bf16[384,1024]{1,0:T(8,128)(2,1)S(1)} %collective-permute-done.22.refs_1_), channel_id=1, source_target_pairs={{0,16},{4,12},{8,24},{12,4},{16,0},{20,28},{24,8},{28,20},{1,17},{... | collective-permute-start | bytes 2359304 | tf_op jit(solution)/shard_map/ppermute | solution.py:927
  193.7 27.4 %collective-permute-start.25 = (bf16[512,1024]{1,0:T(8,128)(2,1)S(1)}, bf16[512,1024]{1,0:T(8,128)(2,1)}, u32[]{:S(2)}, u32[]{:S(2)}) collective-permute-start(bf16[512,1024]{1,0:T(8,128)(2,1)S(1)} %pad_maximum_fusion.refs_0_), channel_id=1, source_target_pairs={{0,8},{4,20},{8,0},{12,28},{16,24},{20,4},{24,16},{28,12},{1,9},{5... | collective-permute-start | bytes 3145736 | tf_op jit(solution)/shard_map/ppermute | solution.py:917
  195.6 52.6 %collective-permute-start.28 = (bf16[640,1024]{1,0:T(8,128)(2,1)S(1)}, bf16[640,1024]{1,0:T(8,128)(2,1)}, u32[]{:S(2)}, u32[]{:S(2)}) collective-permute-start(bf16[640,1024]{1,0:T(8,128)(2,1)S(1)} %constant_dynamic-update-slice_fusion.8.refs_0_), channel_id=1, source_target_pairs={{0,8},{4,20},{8,0},{12,28},{16,24},{20,4},{24,16},{28,12},{1,9},{5... | collective-permute-start | bytes 3932168 | tf_op jit(solution)/shard_map/ppermute | solution.py:917
  196.4 53.3 %collective-permute-start.26 = (bf16[512,1024]{1,0:T(8,128)(2,1)S(1)}, bf16[512,1024]{1,0:T(8,128)(2,1)}, u32[]{:S(2)}, u32[]{:S(2)}) collective-permute-start(bf16[512,1024]{1,0:T(8,128)(2,1)S(1)} %pad_maximum_fusion.refs_0_), channel_id=1, source_target_pairs={{0,16},{4,12},{8,24},{12,4},{16,0},{20,28},{24,8},{28,20},{1,17},{... | collective-permute-start | bytes 3145736 | tf_op jit(solution)/shard_map/ppermute | solution.py:917
  207.6 70.9 %collective-permute-start.29 = (bf16[640,1024]{1,0:T(8,128)(2,1)S(1)}, bf16[640,1024]{1,0:T(8,128)(2,1)S(1)}, u32[]{:S(2)}, u32[]{:S(2)}) collective-permute-start(bf16[640,1024]{1,0:T(8,128)(2,1)S(1)} %constant_dynamic-update-slice_fusion.8.refs_0_), channel_id=1, source_target_pairs={{0,16},{4,12},{8,24},{12,4},{16,0},{20,28},{24,8},{28,20},{1,17},{... | collective-permute-start | bytes 3932168 | tf_op jit(solution)/shard_map/ppermute | solution.py:917
  221.0 42.8 %collective-permute-start.27 = (bf16[512,1024]{1,0:T(8,128)(2,1)}, bf16[512,1024]{1,0:T(8,128)(2,1)}, u32[]{:S(2)}, u32[]{:S(2)}) collective-permute-start(bf16[512,1024]{1,0:T(8,128)(2,1)} %collective-permute-done.25.refs_1_), channel_id=1, source_target_pairs={{0,16},{4,12},{8,24},{12,4},{16,0},{20,28},{24,8},{28,20},{1,17},{... | collective-permute-start | bytes 3145736 | tf_op jit(solution)/shard_map/ppermute | solution.py:927
  248.2 30.3 %collective-permute-start.30 = (bf16[640,1024]{1,0:T(8,128)(2,1)}, bf16[640,1024]{1,0:T(8,128)(2,1)S(1)}, u32[]{:S(2)}, u32[]{:S(2)}) collective-permute-start(bf16[640,1024]{1,0:T(8,128)(2,1)} %collective-permute-done.28.refs_1_), channel_id=1, source_target_pairs={{0,16},{4,12},{8,24},{12,4},{16,0},{20,28},{24,8},{28,20},{1,17},{... | collective-permute-start | bytes 3932168 | tf_op jit(solution)/shard_map/ppermute | solution.py:927
  321.7 32.0 %all-to-all-start = ((bf16[8,272,512]{2,1,0:T(8,128)(2,1)}), bf16[8,272,512]{2,1,0:T(8,128)(2,1)S(1)}, u32[]{:S(2)}, u32[]{:S(2)}) async-start(bf16[8,272,512]{2,1,0:T(8,128)(2,1)} %get-tuple-element.189), calls=%async_computation | async-start | bytes 4456448 | tf_op jit(solution)/shard_map/all_to_all | solution.py:1002
  361.4 24.2 %collective-permute-start.31 = (bf16[512,1024]{1,0:T(8,128)(2,1)}, bf16[512,1024]{1,0:T(8,128)(2,1)S(1)}, u32[]{:S(2)}, u32[]{:S(2)}) collective-permute-start(bf16[512,1024]{1,0:T(8,128)(2,1)} %shard_map.257), channel_id=1, source_target_pairs={{0,1},{1,0},{2,3},{3,2},{4,5},{5,4},{6,7},{7,6},{8,9},{9,8},{10,11... | collective-permute-start | bytes 3145736 | tf_op jit(solution)/shard_map/ppermute | solution.py:30
  380.2 31.0 %all-to-all-start.1 = ((f32[4,32,512]{2,1,0:T(8,128)}), f32[4,32,512]{2,1,0:T(8,128)S(1)}, u32[]{:S(2)}, u32[]{:S(2)}) async-start(f32[4,32,512]{2,1,0:T(8,128)} %param.35), calls=%async_computation.1 | async-start | bytes 524288 | tf_op jit(solution)/shard_map/all_to_all | solution.py:1002
  411.9 31.6 %all-to-all-start.2 = ((bf16[8,272,512]{2,1,0:T(8,128)(2,1)}), bf16[8,272,512]{2,1,0:T(8,128)(2,1)S(1)}, u32[]{:S(2)}, u32[]{:S(2)}) async-start(bf16[8,272,512]{2,1,0:T(8,128)(2,1)} %get-tuple-element.219), calls=%async_computation.2 | async-start | bytes 4456448 | tf_op jit(solution)/shard_map/all_to_all | solution.py:1002
  444.9 38.8 %all-to-all-start.3 = ((bf16[4,144,512]{2,1,0:T(8,128)(2,1)}), bf16[4,144,512]{2,1,0:T(8,128)(2,1)S(1)}, u32[]{:S(2)}, u32[]{:S(2)}) async-start(bf16[4,144,512]{2,1,0:T(8,128)(2,1)} %pad_maximum_fusion.3), calls=%async_computation.3 | async-start | bytes 1179648 | tf_op jit(solution)/shard_map/all_to_all | solution.py:1002
  455.9 43.4 %collective-permute-start.33 = (bf16[512,1024]{1,0:T(8,128)(2,1)}, bf16[512,1024]{1,0:T(8,128)(2,1)S(1)}, u32[]{:S(2)}, u32[]{:S(2)}) collective-permute-start(bf16[512,1024]{1,0:T(8,128)(2,1)} %shard_map.262), channel_id=1, source_target_pairs={{0,1},{1,0},{2,3},{3,2},{4,5},{5,4},{6,7},{7,6},{8,9},{9,8},{10,11... | collective-permute-start | bytes 3145736 | tf_op jit(solution)/shard_map/ppermute | solution.py:30
  484.8 28.6 %collective-permute-start.38 = (f32[128,512]{1,0:T(8,128)}, f32[128,512]{1,0:T(8,128)S(1)}, u32[]{:S(2)}, u32[]{:S(2)}) collective-permute-start(f32[128,512]{1,0:T(8,128)} %slice_add_fusion.refs_0_), channel_id=1, source_target_pairs={{0,24},{4,28},{8,16},{12,20},{16,8},{20,12},{24,0},{28,4},{1,25},{... | collective-permute-start | bytes 786440 | tf_op jit(solution)/shard_map/ppermute | solution.py:30
  485.4 29.8 %collective-permute-start.37 = (f32[128,512]{1,0:T(8,128)}, f32[128,512]{1,0:T(8,128)}, u32[]{:S(2)}, u32[]{:S(2)}) collective-permute-start(f32[128,512]{1,0:T(8,128)} %slice_add_fusion.refs_0_), channel_id=1, source_target_pairs={{0,20},{4,16},{8,28},{12,24},{16,4},{20,0},{24,12},{28,8},{1,21},{... | collective-permute-start | bytes 786440 | tf_op jit(solution)/shard_map/ppermute | solution.py:30
  494.9 39.6 %all-to-all-start.4 = ((f32[4,32,512]{2,1,0:T(8,128)}), f32[4,32,512]{2,1,0:T(8,128)S(1)}, u32[]{:S(2)}, u32[]{:S(2)}) async-start(f32[4,32,512]{2,1,0:T(8,128)} %bitcast.32), calls=%async_computation.4 | async-start | bytes 524288 | tf_op jit(solution)/shard_map/all_to_all | solution.py:1002
  513.4 26.1 %collective-permute-start.40 = (bf16[512,1024]{1,0:T(8,128)(2,1)S(1)}, bf16[512,1024]{1,0:T(8,128)(2,1)S(1)}, u32[]{:S(2)}, u32[]{:S(2)}) collective-permute-start(bf16[512,1024]{1,0:T(8,128)(2,1)S(1)} %copy-done.7), channel_id=1, source_target_pairs={{0,1},{1,0},{2,3},{3,2},{4,5},{5,4},{6,7},{7,6},{8,9},{9,8},{10,11... | collective-permute-start | bytes 3145736 | tf_op jit(solution)/shard_map/ppermute | solution.py:30
  (53 other events, 658.9 us)

commit v7 on v6

--- a/solution.py
+++ b/solution.py
@@ -1039,16 +1039,16 @@
     )
     enc_low_far = partner(enc_low)
     dec_third.across(enc_low)
+    dec_up.begin(enc_low)
     *dec_norm1, cross_query, dec_q_full = settle(
         5, dec_in, tie(self_mix, enc_low), gains, dec_second, at(0), at(1), (None, 2)
     )
-    dec_up.begin(cross_query)
-    dec_down.begin(cross_query)
     cross_key, cross_value, cross_key_far, cross_value_far, dec_kv_full = project(
         6, tie(enc_low, cross_query), enc_low_far, dec_third, (at(0), at(1))
     )
     cross_keys, cross_values = (cross_key, cross_key_far), (cross_value, cross_value_far)
     dec_up.across(cross_key)
+    dec_down.begin(cross_key)
     cross_mix, cross_lse = attend(places, cross_query, cross_keys, cross_values, False)
     *dec_norm2, dec_wo_full = settle(
         7, dec_norm1[0], cross_mix, gains, dec_third, at(2), None, (2, 3)

time: 564 us -> 588 us (1.043)
  waiting for transfers between devices: 49.9 us -> 70.2 us
    ppermute x8, waiting for transfers between devices: 41 us -> 55 us  [across(): lax.ppermute(first, 'wide', [(i, i ^ (2 if i % 2 else 4)) for i in range(...]
    ppermute x16, waiting for transfers between devices: 2.16 us -> 8.28 us  [begin(): lax.ppermute(array, 'wide', [(i, i ^ steps[i % 2][which]) for i in range(...]
  transfers between devices with their start and end apart: 47 -> 47, of which waited for: 9 -> 11; matrix products, arithmetic and copies ran while one was open for 5% -> 5% of each run, Pallas kernels for 61% -> 59%
where the time goes in v7:
time: 588 us; the launch traced here: 577 us
  Pallas kernels  387 us (66%)
  starting transfers between devices  73.3 us (12%)
  waiting for transfers between devices  70.2 us (12%)
  local copies, waits for them, and re-layouts  36 us (6%)
  other arithmetic  8.4 us (1%)
    pallas_call x20, Pallas kernels, call(): pl.pallas_call(kernel, in_specs=specs, out_specs=[IN_VMEM if len(out) ==...  257 us
    pallas_call x3, Pallas kernels, attend_back(): pl.pallas_call(lambda *refs: attend_back_kernel(causal, 512, *refs[:12],...  76.7 us
    ppermute x8, waiting for transfers between devices, across(): lax.ppermute(first, 'wide', [(i, i ^ (2 if i % 2 else 4)) for i in range(...  55 us
    pallas_call x3, Pallas kernels, attend(): pl.pallas_call(functools.partial(attend_kernel, causal, 512), grid=(pairs...  53.1 us
    all_to_all x6, starting transfers between devices, shards(): lax.all_to_all(array, axis, split_axis=0, concat_axis=0, tiled=True)  23.5 us
    ppermute x16, starting transfers between devices, begin(): lax.ppermute(array, 'wide', [(i, i ^ steps[i % 2][which]) for i in range(...  22.2 us
    unnamed x85, local copies, waits for them, and re-layouts  20.5 us
    ppermute x17, starting transfers between devices, swap(): lax.ppermute(array, axis, [(i, i ^ bit) for i in range(lax.axis_size(axis...  19.9 us
  transfers between devices with their start and end apart: 47, of which 11 were waited for; matrix products, arithmetic and copies ran while one was open for 5% of the time, Pallas kernels for 59%

profile of v7, /device:TPU:0, one launch (start us, length us, event | category | flops | bytes accessed | tf_op | source)
XLA Modules:
  0.0 576.9 jit_solution(1085869838740576715)
XLA Ops:
  30.7 6.9 %collective-permute-done.1.refs_3_ = bf16[400,1024]{1,0:T(8,128)(2,1)S(1)} collective-permute-done((bf16[400,1024]{1,0:T(8,128)(2,1)}, bf16[400,1024]{1,0:T(8,128)(2,1)S(1)}, u32[]{:S(2)}, u32[]{:S(2)}) %collective-permute-start.1) | collective-permute-done | bytes 819232 | tf_op jit(solution)/shard_map/ppermute | solution.py:927
  44.6 13.7 %shard_map.242 = (bf16[512,1024]{1,0:T(8,128)(2,1)}, bf16[512,1024]{1,0:T(8,128)(2,1)}, bf16[512,1024]{1,0:T(8,128)(2,1)}, bf16[512,1024]{1,0:T(8,128)(2,1)}, bf...) custom-call(bf16[512,1024]{1,0:T(8,128)(2,1)} %x_ref.4, bf16[512,1024]{1,0:T(8,128)(2,1)} %collective-permute-done.3.far_ref, ...), custom_call_target="tpu_custom_call" | custom-call | flops 5368709120 | bytes 5373952 | tf_op jit(solution)/shard_map/pallas_call | solution.py:709
  64.3 17.6 %shard_map.243 = (bf16[512,1024]{1,0:T(8,128)(2,1)}, f32[8,8,512]{2,1,0:T(8,128)}) custom-call(s32[1]{0:T(128)} %bitcast.half_ref.refs_0_, s32[1,512]{1,0:T(1,128)} %bitcast.1.qid_ref.refs_1_, s32[512,1]{1,0:T(8,128)} %copy.47.kid_own_ref.refs_2_, s32[512,1]{1,0:T(8,128)} %copy.48.kid_far_ref.refs_3_, bf16[512,1024]{1,0:T(8,128)(2,1)} %get-tuple-element.129.q_ref.refs_4_, ...), custom_call_target="tpu_custom_call" | custom-call | flops 8589934592 | bytes 6291456 | tf_op jit(solution)/shard_map/pallas_call | solution.py:219
  87.1 13.8 %shard_map.244 = (bf16[512,1024]{1,0:T(8,128)(2,1)}, bf16[512,1024]{1,0:T(8,128)(2,1)}, bf16[512,1024]{1,0:T(8,128)(2,1)}, bf16[512,1024]{1,0:T(8,128)(2,1)}, bf...) custom-call(bf16[512,1024]{1,0:T(8,128)(2,1)} %x_ref.5, bf16[512,1024]{1,0:T(8,128)(2,1)} %collective-permute-done.5.far_ref, ...), custom_call_target="tpu_custom_call" | custom-call | flops 5368709120 | bytes 5242880 | tf_op jit(solution)/shard_map/pallas_call | solution.py:709
  106.9 17.6 %shard_map.245 = (bf16[512,1024]{1,0:T(8,128)(2,1)}, f32[8,8,512]{2,1,0:T(8,128)}) custom-call(s32[1]{0:T(128)} %bitcast.half_ref.refs_0_, s32[1,512]{1,0:T(1,128)} %bitcast.1.qid_ref.refs_1_, s32[512,1]{1,0:T(8,128)} %copy.47.kid_own_ref.refs_2_, s32[512,1]{1,0:T(8,128)} %copy.48.kid_far_ref.refs_3_, bf16[512,1024]{1,0:T(8,128)(2,1)} %get-tuple-element.139.q_ref.refs_4_, ...), custom_call_target="tpu_custom_call" | custom-call | flops 8589934592 | bytes 6291456 | tf_op jit(solution)/shard_map/pallas_call | solution.py:219
  128.9 8.0 %shard_map.246 = (f32[512,1024]{1,0:T(8,128)}, f32[512,128]{1,0:T(8,128)}, bf16[1,1024,1024]{2,1,0:T(8,128)(2,1)}) custom-call(bf16[512,1024]{1,0:T(8,128)(2,1)} %x_ref.4, bf16[512,1024]{1,0:T(8,128)(2,1)} %get-tuple-element.145.mix_ref.refs_9_, f32[8,1024]{1,0:T(8,128)} %convert_bitcast_fusion.1.gains_ref.refs_5_, ...), custom_call_target="tpu_custom_call" | custom-call | flops 1073741824 | bytes 7372800 | tf_op jit(solution)/shard_map/pallas_call | solution.py:709
  140.1 14.9 %shard_map.247 = (bf16[512,4096]{1,0:T(8,128)(2,1)}, bf16[512,4096]{1,0:T(8,128)(2,1)}, bf16[4,1024,1024]{2,1,0:T(8,128)(2,1)}) custom-call(f32[512,1024]{1,0:T(8,128)} %get-tuple-element.149.n_ref.refs_3_, f32[8,1024]{1,0:T(8,128)} %convert_bitcast_fusion.1.gains_ref.refs_5_, bf16[640,1024]{1,0:T(8,128)(2,1)} %slice_dynamic-update-slice_fusion.refs_0_, ...), custom_call_target="tpu_custom_call" | custom-call | flops 4294967296 | bytes 7372800 | tf_op jit(solution)/shard_map/pallas_call | solution.py:709
  158.7 17.6 %shard_map.248 = (bf16[512,512]{1,0:T(8,128)(2,1)}, bf16[512,512]{1,0:T(8,128)(2,1)}, f32[512,1024]{1,0:T(8,128)}, f32[512,128]{1,0:T(8,128)}, bf16[512,1024]{1,...) custom-call(f32[512,1024]{1,0:T(8,128)} %get-tuple-element.149.n_ref.refs_3_, ...), custom_call_target="tpu_custom_call" | custom-call | flops 5368709120 | bytes 11573248 | tf_op jit(solution)/shard_map/pallas_call | solution.py:709
  181.9 4.3 collective-permute-done.19.refs_2_
  187.8 23.8 %collective-permute-done.20.refs_3_ = bf16[256,1024]{1,0:T(8,128)(2,1)} collective-permute-done((bf16[256,1024]{1,0:T(8,128)(2,1)S(1)}, bf16[256,1024]{1,0:T(8,128)(2,1)}, u32[]{:S(2)}, u32[]{:S(2)}) %collective-permute-start.20) | collective-permute-done | bytes 524320 | tf_op jit(solution)/shard_map/ppermute | solution.py:927
  211.6 10.0 %shard_map.249 = (f32[512,1024]{1,0:T(8,128)}, f32[512,128]{1,0:T(8,128)}, bf16[512,1024]{1,0:T(8,128)(2,1)}, bf16[2,1024,1024]{2,1,0:T(8,128)(2,1)}) custom-call(bf16[512,1024]{1,0:T(8,128)(2,1)} %x_ref.5, bf16[512,1024]{1,0:T(8,128)(2,1)} %get-tuple-element.156.mix_ref.refs_9_, f32[8,1024]{1,0:T(8,128)} %convert_bitcast_fusion.1.gains_ref.refs_5_, ...), custom_call_target="tpu_custom_call" | custom-call | flops 2147483648 | bytes 4227072 | tf_op jit(solution)/shard_map/pallas_call | solution.py:709
  222.8 11.7 %shard_map.250 = (bf16[512,1024]{1,0:T(8,128)(2,1)}, bf16[512,1024]{1,0:T(8,128)(2,1)}, bf16[512,1024]{1,0:T(8,128)(2,1)}, bf16[512,1024]{1,0:T(8,128)(2,1)}, bf16[2,1024,1024]{2,1,0:T(8,128)(2,1)}) custom-call(bf16[512,1024]{1,0:T(8,128)(2,1)} %get-tuple-element.160.x_ref, bf16[512,1024]{1,0:T(8,128)(2,1)} %collective-permute-done.21.far_ref, ...), custom_call_target="tpu_custom_call" | custom-call | flops 4294967296 | bytes 5242880 | tf_op jit(solution)/shard_map/pallas_call | solution.py:709
  238.6 17.9 %shard_map.251 = (bf16[512,1024]{1,0:T(8,128)(2,1)}, f32[8,8,512]{2,1,0:T(8,128)}) custom-call(s32[1]{0:T(128)} %bitcast.half_ref.refs_0_, s32[1,512]{1,0:T(1,128)} %bitcast.1.qid_ref.refs_1_, s32[512,1]{1,0:T(8,128)} %copy.47.kid_own_ref.refs_2_, s32[512,1]{1,0:T(8,128)} %copy.48.kid_far_ref.refs_3_, bf16[512,1024]{1,0:T(8,128)(2,1)} %get-tuple-element.159.q_ref.refs_4_, ...), custom_call_target="tpu_custom_call" | custom-call | flops 8589934592 | bytes 6291456 | tf_op jit(solution)/shard_map/pallas_call | solution.py:219
  256.5 8.4 %shard_map.252 = (f32[512,1024]{1,0:T(8,128)}, f32[512,128]{1,0:T(8,128)}, bf16[1,1024,1024]{2,1,0:T(8,128)(2,1)}) custom-call(f32[512,1024]{1,0:T(8,128)} %get-tuple-element.168.x_ref.n_ref, bf16[512,1024]{1,0:T(8,128)(2,1)} %get-tuple-element.167.mix_ref.refs_9_, f32[8,1024]{1,0:T(8,128)} %convert_bitcast_fusion.1.gains_ref.refs_5_, ...), custom_call_target="tpu_custom_call" | custom-call | flops 1073741824 | bytes 6324224 | tf_op jit(solution)/shard_map/pallas_call | solution.py:709
  266.9 20.9 %collective-permute-done.27.refs_3_ = bf16[512,1024]{1,0:T(8,128)(2,1)} collective-permute-done((bf16[512,1024]{1,0:T(8,128)(2,1)}, bf16[512,1024]{1,0:T(8,128)(2,1)}, u32[]{:S(2)}, u32[]{:S(2)}) %collective-permute-start.27) | collective-permute-done | bytes 1048608 | tf_op jit(solution)/shard_map/ppermute | solution.py:927
  287.8 14.7 %shard_map.253 = (bf16[512,4096]{1,0:T(8,128)(2,1)}, bf16[512,4096]{1,0:T(8,128)(2,1)}, bf16[4,1024,1024]{2,1,0:T(8,128)(2,1)}) custom-call(f32[512,1024]{1,0:T(8,128)} %get-tuple-element.169.n_ref.refs_3_, f32[8,1024]{1,0:T(8,128)} %convert_bitcast_fusion.1.gains_ref.refs_5_, bf16[512,1024]{1,0:T(8,128)(2,1)} %copy-done.15, ...), custom_call_target="tpu_custom_call" | custom-call | flops 4294967296 | bytes 6324224 | tf_op jit(solution)/shard_map/pallas_call | solution.py:709
  303.6 17.6 %shard_map.254 = (bf16[512,512]{1,0:T(8,128)(2,1)}, bf16[512,512]{1,0:T(8,128)(2,1)}, f32[512,1024]{1,0:T(8,128)}, f32[512,128]{1,0:T(8,128)}, bf16[512,1024]{1,...) custom-call(f32[512,1024]{1,0:T(8,128)} %get-tuple-element.169.n_ref.refs_3_, ...), custom_call_target="tpu_custom_call" | custom-call | flops 5368709120 | bytes 11573248 | tf_op jit(solution)/shard_map/pallas_call | solution.py:709
  321.3 24.0 %shard_map.255 = (bf16[512,1024]{1,0:T(8,128)(2,1)}, f32[512,1024]{1,0:T(8,128)}, bf16[512,1024]{1,0:T(8,128)(2,1)}, bf16[8,272,512]{2,1,0:T(8,128)(2,1)}) custom-call(bf16[512,1024]{1,0:T(8,128)(2,1)} %refs_0_.1, f32[512,1024]{1,0:T(8,128)} %get-tuple-element.176.refs_1_, f32[512,128]{1,0:T(8,128)} %get-tuple-element.177.refs_2_, ...), custom_call_target="tpu_custom_call" | custom-call | flops 12884901888 | bytes 32014336 | tf_op jit(solution)/shard_map/pallas_call | solution.py:709
  348.9 25.6 %shard_map.256 = (bf16[512,1024]{1,0:T(8,128)(2,1)}, bf16[512,1024]{1,0:T(8,128)(2,1)}, bf16[512,1024]{1,0:T(8,128)(2,1)}, bf16[512,1024]{1,0:T(8,128)(2,1)}, bf16[512,1024]{1,0:T(8,128)(2,1)}) custom-call(s32[1]{0:T(128)} %bitcast.half_ref.refs_0_, s32[1,512]{1,0:T(1,128)} %bitcast.1.qid_ref.refs_1_, s32[512,1]{1,0:T(8,128)} %copy.47.kid_own_ref.refs_2_, ...), custom_call_target="tpu_custom_call" | custom-call | flops 21474836480 | bytes 12582912 | tf_op jit(solution)/shard_map/pallas_call | solution.py:243
  377.2 7.4 %shard_map.257 = bf16[512,1024]{1,0:T(8,128)(2,1)} custom-call(bf16[512,1024]{1,0:T(8,128)(2,1)} %get-tuple-element.192.refs_0_, bf16[512,1024]{1,0:T(8,128)(2,1)} %get-tuple-element.193.refs_1_, bf16[2,1024,1024]{2,1,0:T(8,128)(2,1)} %get-tuple-element.194.refs_2_.refs_3_), custom_call_target="tpu_custom_call" | custom-call | flops 2147483648 | bytes 6291456 | tf_op jit(solution)/shard_map/pallas_call | solution.py:709
  386.2 8.0 %shard_map.258.refs_0_ = f32[512,1024]{1,0:T(8,128)} custom-call(bf16[512,1024]{1,0:T(8,128)(2,1)} %refs_0_.2, bf16[512,1024]{1,0:T(8,128)(2,1)} %get-tuple-element.196.refs_1_, bf16[512,1024]{1,0:T(8,128)(2,1)} %get-tuple-element.197.refs_2_, bf16[2,1024,1024]{2,1,0:T(8,128)(2,1)} %get-tuple-element.194.refs_2_.refs_3_), custom_call_target="tpu_custom_call" | custom-call | flops 2147483648 | bytes 7340032 | tf_op jit(solution)/shard_map/pallas_call | solution.py:709
  394.2 9.1 %shard_map.259 = (f32[512,1024]{1,0:T(8,128)}, bf16[512,1024]{1,0:T(8,128)(2,1)}) custom-call(f32[512,1024]{1,0:T(8,128)} %get-tuple-element.199.dz_ref, bf16[512,1024]{1,0:T(8,128)(2,1)} %get-tuple-element.190.dq_ref, f32[512,1024]{1,0:T(8,128)} %get-tuple-element.168.x_ref.n_ref, f32[512,128]{1,0:T(8,128)} %get-tuple-element.200.r_ref, ...), custom_call_target="tpu_custom_call" | custom-call | flops 2147483648 | bytes 9732096 | tf_op jit(solution)/shard_map/pallas_call | solution.py:709
  409.9 24.6 %shard_map.260 = (bf16[512,1024]{1,0:T(8,128)(2,1)}, f32[512,1024]{1,0:T(8,128)}, bf16[512,1024]{1,0:T(8,128)(2,1)}, bf16[8,272,512]{2,1,0:T(8,128)(2,1)}) custom-call(f32[512,1024]{1,0:T(8,128)} %shard_map.258.refs_0_, f32[512,1024]{1,0:T(8,128)} %get-tuple-element.204.refs_1_, f32[512,128]{1,0:T(8,128)} %get-tuple-element.205.refs_2_, ...), custom_call_target="tpu_custom_call" | custom-call | flops 12884901888 | bytes 34111488 | tf_op jit(solution)/shard_map/pallas_call | solution.py:709
  438.8 25.6 %shard_map.261 = (bf16[512,1024]{1,0:T(8,128)(2,1)}, bf16[512,1024]{1,0:T(8,128)(2,1)}, bf16[512,1024]{1,0:T(8,128)(2,1)}, bf16[512,1024]{1,0:T(8,128)(2,1)}, bf16[512,1024]{1,0:T(8,128)(2,1)}) custom-call(s32[1]{0:T(128)} %bitcast.half_ref.refs_0_, s32[1,512]{1,0:T(1,128)} %bitcast.1.qid_ref.refs_1_, s32[512,1]{1,0:T(8,128)} %copy.47.kid_own_ref.refs_2_, ...), custom_call_target="tpu_custom_call" | custom-call | flops 21474836480 | bytes 12582912 | tf_op jit(solution)/shard_map/pallas_call | solution.py:243
  468.1 4.4 all-to-all-start.3
  472.5 7.3 %shard_map.262 = bf16[512,1024]{1,0:T(8,128)(2,1)} custom-call(bf16[512,1024]{1,0:T(8,128)(2,1)} %get-tuple-element.227.refs_0_, bf16[512,1024]{1,0:T(8,128)(2,1)} %get-tuple-element.228.refs_1_, bf16[3,1024,1024]{2,1,0:T(8,128)(2,1)} %get-tuple-element.229.refs_2_.refs_5_), custom_call_target="tpu_custom_call" | custom-call | flops 2147483648 | bytes 8388608 | tf_op jit(solution)/shard_map/pallas_call | solution.py:709
  482.0 25.6 %shard_map.263 = (bf16[512,1024]{1,0:T(8,128)(2,1)}, bf16[512,1024]{1,0:T(8,128)(2,1)}, bf16[512,1024]{1,0:T(8,128)(2,1)}, bf16[512,1024]{1,0:T(8,128)(2,1)}, bf16[512,1024]{1,0:T(8,128)(2,1)}) custom-call(s32[1]{0:T(128)} %bitcast.half_ref.refs_0_, s32[1,512]{1,0:T(1,128)} %bitcast.1.qid_ref.refs_1_, s32[512,1]{1,0:T(8,128)} %copy.47.kid_own_ref.refs_2_, ...), custom_call_target="tpu_custom_call" | custom-call | flops 21474836480 | bytes 12582912 | tf_op jit(solution)/shard_map/pallas_call | solution.py:243
  511.3 7.4 %shard_map.264 = bf16[512,1024]{1,0:T(8,128)(2,1)} custom-call(bf16[512,1024]{1,0:T(8,128)(2,1)} %get-tuple-element.235.refs_0_, bf16[512,1024]{1,0:T(8,128)(2,1)} %get-tuple-element.236.refs_1_, bf16[3,1024,1024]{2,1,0:T(8,128)(2,1)} %get-tuple-element.237.refs_2_.refs_5_), custom_call_target="tpu_custom_call" | custom-call | flops 2147483648 | bytes 8388608 | tf_op jit(solution)/shard_map/pallas_call | solution.py:709
  526.4 10.7 %shard_map.265 = f32[512,1024]{1,0:T(8,128)} custom-call(f32[512,1024]{1,0:T(8,128)} %get-tuple-element.238.refs_0_, bf16[512,1024]{1,0:T(8,128)(2,1)} %copy-done.4, bf16[512,1024]{1,0:T(8,128)(2,1)} %get-tuple-element.223.refs_2_, bf16[512,1024]{1,0:T(8,128)(2,1)} %get-tuple-element.239.refs_3_, bf16[512,1024]{1,0:T(8,128)(2,1)} %get-tuple-element.240.refs_4_, ...), custom_call_target="tpu_custom_call" | custom-call | flops 3221225472 | bytes 12582912 | tf_op jit(solution)/shard_map/pallas_call | solution.py:709
  540.5 17.8 %shard_map.266 = f32[128,512]{1,0:T(8,128)} custom-call(f32[128,512]{1,0:T(8,128)} %slice_add_fusion.refs_0_, f32[128,512]{1,0:T(8,128)} %copy-done.32, f32[128,512]{1,0:T(8,128)} %copy-done.35, f32[128,512]{1,0:T(8,128)} %copy-done.34, f32[128,512]{1,0:T(8,128)} %copy-done.33, f32[128,512]{1,0:T(8,128)} %collective-permute-done.37.refs_5_, ...), custom_call_target="tpu_custom_call" | custom-call | flops 16106127360 | bytes 2097152 | tf_op jit(solution)/shard_map/pallas_call | solution.py:709
  558.4 4.3 all-to-all-start.5
  564.3 10.7 %shard_map.267 = f32[512,1024]{1,0:T(8,128)} custom-call(f32[512,1024]{1,0:T(8,128)} %get-tuple-element.242.refs_0_, bf16[512,1024]{1,0:T(8,128)(2,1)} %copy-done.5, bf16[512,1024]{1,0:T(8,128)(2,1)} %get-tuple-element.232.refs_2_, bf16[512,1024]{1,0:T(8,128)(2,1)} %get-tuple-element.243.refs_3_, bf16[512,1024]{1,0:T(8,128)(2,1)} %get-tuple-element.244.refs_4_, ...), custom_call_target="tpu_custom_call" | custom-call | flops 3221225472 | bytes 12582912 | tf_op jit(solution)/shard_map/pallas_call | solution.py:709
  (227 shorter events, 123.2 us)
Async XLA Ops:
  3.6 24.0 %collective-permute-start.4 = (bf16[400,1024]{1,0:T(8,128)(2,1)}, bf16[400,1024]{1,0:T(8,128)(2,1)}, u32[]{:S(2)}, u32[]{:S(2)}) collective-permute-start(bf16[400,1024]{1,0:T(8,128)(2,1)} %pad_maximum_fusion.1.refs_0_), channel_id=1, source_target_pairs={{0,16},{4,12},{8,24},{12,4},{16,0},{20,28},{24,8},{28,20},{1,17},{... | collective-permute-start | bytes 2457608 | tf_op jit(solution)/shard_map/ppermute | solution.py:917
  8.0 35.0 %collective-permute-start.3 = (bf16[512,1024]{1,0:T(8,128)(2,1)S(1)}, bf16[512,1024]{1,0:T(8,128)(2,1)}, u32[]{:S(2)}, u32[]{:S(2)}) collective-permute-start(bf16[512,1024]{1,0:T(8,128)(2,1)S(1)} %copy-done.6), channel_id=1, source_target_pairs={{0,1},{1,0},{2,3},{3,2},{4,5},{5,4},{6,7},{7,6},{8,9},{9,8},{10,11... | collective-permute-start | bytes 3145736 | tf_op jit(solution)/shard_map/ppermute | solution.py:30
  37.6 47.9 %collective-permute-start.7 = (bf16[384,1024]{1,0:T(8,128)(2,1)}, bf16[384,1024]{1,0:T(8,128)(2,1)}, u32[]{:S(2)}, u32[]{:S(2)}) collective-permute-start(bf16[384,1024]{1,0:T(8,128)(2,1)} %bitcast.68), channel_id=1, source_target_pairs={{0,16},{4,12},{8,24},{12,4},{16,0},{20,28},{24,8},{28,20},{1,17},{... | collective-permute-start | bytes 2359304 | tf_op jit(solution)/shard_map/ppermute | solution.py:917
  39.4 24.4 %collective-permute-start.6 = (bf16[384,1024]{1,0:T(8,128)(2,1)}, bf16[384,1024]{1,0:T(8,128)(2,1)}, u32[]{:S(2)}, u32[]{:S(2)}) collective-permute-start(bf16[384,1024]{1,0:T(8,128)(2,1)} %bitcast.69), channel_id=1, source_target_pairs={{0,8},{4,20},{8,0},{12,28},{16,24},{20,4},{24,16},{28,12},{1,9},{5... | collective-permute-start | bytes 2359304 | tf_op jit(solution)/shard_map/ppermute | solution.py:917
  43.0 42.5 %collective-permute-start.5 = (bf16[512,1024]{1,0:T(8,128)(2,1)}, bf16[512,1024]{1,0:T(8,128)(2,1)}, u32[]{:S(2)}, u32[]{:S(2)}) collective-permute-start(bf16[512,1024]{1,0:T(8,128)(2,1)} %x_ref.5), channel_id=1, source_target_pairs={{0,1},{1,0},{2,3},{3,2},{4,5},{5,4},{6,7},{7,6},{8,9},{9,8},{10,11... | collective-permute-start | bytes 3145736 | tf_op jit(solution)/shard_map/ppermute | solution.py:30
  59.0 41.9 %collective-permute-start.10 = (bf16[640,1024]{1,0:T(8,128)(2,1)}, bf16[640,1024]{1,0:T(8,128)(2,1)}, u32[]{:S(2)}, u32[]{:S(2)}) collective-permute-start(bf16[640,1024]{1,0:T(8,128)(2,1)} %slice_dynamic-update-slice_fusion.refs_0_), channel_id=1, source_target_pairs={{0,8},{4,20},{8,0},{12,28},{16,24},{20,4},{24,16},{28,12},{1,9},{5... | collective-permute-start | bytes 3932168 | tf_op jit(solution)/shard_map/ppermute | solution.py:917
  63.8 23.4 %collective-permute-start.8 = (bf16[384,1024]{1,0:T(8,128)(2,1)}, bf16[384,1024]{1,0:T(8,128)(2,1)}, u32[]{:S(2)}, u32[]{:S(2)}) collective-permute-start(bf16[384,1024]{1,0:T(8,128)(2,1)} %collective-permute-done.6.refs_1_), channel_id=1, source_target_pairs={{0,16},{4,12},{8,24},{12,4},{16,0},{20,28},{24,8},{28,20},{1,17},{... | collective-permute-start | bytes 2359304 | tf_op jit(solution)/shard_map/ppermute | solution.py:927
  81.9 42.6 %collective-permute-start.11 = (bf16[640,1024]{1,0:T(8,128)(2,1)}, bf16[640,1024]{1,0:T(8,128)(2,1)}, u32[]{:S(2)}, u32[]{:S(2)}) collective-permute-start(bf16[640,1024]{1,0:T(8,128)(2,1)} %slice_dynamic-update-slice_fusion.refs_0_), channel_id=1, source_target_pairs={{0,16},{4,12},{8,24},{12,4},{16,0},{20,28},{24,8},{28,20},{1,17},{... | collective-permute-start | bytes 3932168 | tf_op jit(solution)/shard_map/ppermute | solution.py:917
  85.6 51.3 %collective-permute-start.15 = (bf16[640,1024]{1,0:T(8,128)(2,1)}, bf16[640,1024]{1,0:T(8,128)(2,1)}, u32[]{:S(2)}, u32[]{:S(2)}) collective-permute-start(bf16[640,1024]{1,0:T(8,128)(2,1)} %constant_dynamic-update-slice_fusion.6.refs_0_), channel_id=1, source_target_pairs={{0,8},{4,20},{8,0},{12,28},{16,24},{20,4},{24,16},{28,12},{1,9},{5... | collective-permute-start | bytes 3932168 | tf_op jit(solution)/shard_map/ppermute | solution.py:917
  100.9 26.9 %collective-permute-start.12 = (bf16[640,1024]{1,0:T(8,128)(2,1)}, bf16[640,1024]{1,0:T(8,128)(2,1)S(1)}, u32[]{:S(2)}, u32[]{:S(2)}) collective-permute-start(bf16[640,1024]{1,0:T(8,128)(2,1)} %collective-permute-done.10.refs_1_), channel_id=1, source_target_pairs={{0,16},{4,12},{8,24},{12,4},{16,0},{20,28},{24,8},{28,20},{1,17},{... | collective-permute-start | bytes 3932168 | tf_op jit(solution)/shard_map/ppermute | solution.py:927
  105.4 52.3 %collective-permute-start.16 = (bf16[640,1024]{1,0:T(8,128)(2,1)}, bf16[640,1024]{1,0:T(8,128)(2,1)}, u32[]{:S(2)}, u32[]{:S(2)}) collective-permute-start(bf16[640,1024]{1,0:T(8,128)(2,1)} %constant_dynamic-update-slice_fusion.6.refs_0_), channel_id=1, source_target_pairs={{0,16},{4,12},{8,24},{12,4},{16,0},{20,28},{24,8},{28,20},{1,17},{... | collective-permute-start | bytes 3932168 | tf_op jit(solution)/shard_map/ppermute | solution.py:917
  155.0 24.6 %collective-permute-start.22 = (bf16[384,1024]{1,0:T(8,128)(2,1)S(1)}, bf16[384,1024]{1,0:T(8,128)(2,1)S(1)}, u32[]{:S(2)}, u32[]{:S(2)}) collective-permute-start(bf16[384,1024]{1,0:T(8,128)(2,1)S(1)} %pad_maximum_fusion.2.refs_0_), channel_id=1, source_target_pairs={{0,8},{4,20},{8,0},{12,28},{16,24},{20,4},{24,16},{28,12},{1,9},{5... | collective-permute-start | bytes 2359304 | tf_op jit(solution)/shard_map/ppermute | solution.py:917
  176.3 45.4 %collective-permute-start.21 = (bf16[512,1024]{1,0:T(8,128)(2,1)}, bf16[512,1024]{1,0:T(8,128)(2,1)}, u32[]{:S(2)}, u32[]{:S(2)}) collective-permute-start(bf16[512,1024]{1,0:T(8,128)(2,1)} %get-tuple-element.160.x_ref), channel_id=1, source_target_pairs={{0,1},{1,0},{2,3},{3,2},{4,5},{5,4},{6,7},{7,6},{8,9},{9,8},{10,11... | collective-permute-start | bytes 3145736 | tf_op jit(solution)/shard_map/ppermute | solution.py:30
  177.5 44.1 %collective-permute-start.23 = (bf16[384,1024]{1,0:T(8,128)(2,1)S(1)}, bf16[384,1024]{1,0:T(8,128)(2,1)S(1)}, u32[]{:S(2)}, u32[]{:S(2)}) collective-permute-start(bf16[384,1024]{1,0:T(8,128)(2,1)S(1)} %pad_maximum_fusion.2.refs_0_), channel_id=1, source_target_pairs={{0,16},{4,12},{8,24},{12,4},{16,0},{20,28},{24,8},{28,20},{1,17},{... | collective-permute-start | bytes 2359304 | tf_op jit(solution)/shard_map/ppermute | solution.py:917
  178.9 32.7 %collective-permute-start.20 = (bf16[256,1024]{1,0:T(8,128)(2,1)S(1)}, bf16[256,1024]{1,0:T(8,128)(2,1)}, u32[]{:S(2)}, u32[]{:S(2)}) collective-permute-start(bf16[256,1024]{1,0:T(8,128)(2,1)S(1)} %collective-permute-done.18.refs_1_), channel_id=1, source_target_pairs={{0,16},{4,12},{8,24},{12,4},{16,0},{20,28},{24,8},{28,20},{1,17},{... | collective-permute-start | bytes 1572872 | tf_op jit(solution)/shard_map/ppermute | solution.py:927
  179.6 42.1 %collective-permute-start.24 = (bf16[384,1024]{1,0:T(8,128)(2,1)S(1)}, bf16[384,1024]{1,0:T(8,128)(2,1)S(1)}, u32[]{:S(2)}, u32[]{:S(2)}) collective-permute-start(bf16[384,1024]{1,0:T(8,128)(2,1)S(1)} %collective-permute-done.22.refs_1_), channel_id=1, source_target_pairs={{0,16},{4,12},{8,24},{12,4},{16,0},{20,28},{24,8},{28,20},{1,17},{... | collective-permute-start | bytes 2359304 | tf_op jit(solution)/shard_map/ppermute | solution.py:927
  186.2 51.9 %collective-permute-start.25 = (bf16[512,1024]{1,0:T(8,128)(2,1)S(1)}, bf16[512,1024]{1,0:T(8,128)(2,1)}, u32[]{:S(2)}, u32[]{:S(2)}) collective-permute-start(bf16[512,1024]{1,0:T(8,128)(2,1)S(1)} %pad_maximum_fusion.refs_0_), channel_id=1, source_target_pairs={{0,8},{4,20},{8,0},{12,28},{16,24},{20,4},{24,16},{28,12},{1,9},{5... | collective-permute-start | bytes 3145736 | tf_op jit(solution)/shard_map/ppermute | solution.py:917
  234.5 31.6 %collective-permute-start.28 = (bf16[640,1024]{1,0:T(8,128)(2,1)S(1)}, bf16[640,1024]{1,0:T(8,128)(2,1)S(1)}, u32[]{:S(2)}, u32[]{:S(2)}) collective-permute-start(bf16[640,1024]{1,0:T(8,128)(2,1)S(1)} %constant_dynamic-update-slice_fusion.8.refs_0_), channel_id=1, source_target_pairs={{0,8},{4,20},{8,0},{12,28},{16,24},{20,4},{24,16},{28,12},{1,9},{5... | collective-permute-start | bytes 3932168 | tf_op jit(solution)/shard_map/ppermute | solution.py:917
  236.1 30.8 %collective-permute-start.26 = (bf16[512,1024]{1,0:T(8,128)(2,1)S(1)}, bf16[512,1024]{1,0:T(8,128)(2,1)}, u32[]{:S(2)}, u32[]{:S(2)}) collective-permute-start(bf16[512,1024]{1,0:T(8,128)(2,1)S(1)} %pad_maximum_fusion.refs_0_), channel_id=1, source_target_pairs={{0,16},{4,12},{8,24},{12,4},{16,0},{20,28},{24,8},{28,20},{1,17},{... | collective-permute-start | bytes 3145736 | tf_op jit(solution)/shard_map/ppermute | solution.py:917
  236.6 66.0 %collective-permute-start.29 = (bf16[640,1024]{1,0:T(8,128)(2,1)S(1)}, bf16[640,1024]{1,0:T(8,128)(2,1)S(1)}, u32[]{:S(2)}, u32[]{:S(2)}) collective-permute-start(bf16[640,1024]{1,0:T(8,128)(2,1)S(1)} %constant_dynamic-update-slice_fusion.8.refs_0_), channel_id=1, source_target_pairs={{0,16},{4,12},{8,24},{12,4},{16,0},{20,28},{24,8},{28,20},{1,17},{... | collective-permute-start | bytes 3932168 | tf_op jit(solution)/shard_map/ppermute | solution.py:917
  238.1 49.7 %collective-permute-start.27 = (bf16[512,1024]{1,0:T(8,128)(2,1)}, bf16[512,1024]{1,0:T(8,128)(2,1)}, u32[]{:S(2)}, u32[]{:S(2)}) collective-permute-start(bf16[512,1024]{1,0:T(8,128)(2,1)} %collective-permute-done.25.refs_1_), channel_id=1, source_target_pairs={{0,16},{4,12},{8,24},{12,4},{16,0},{20,28},{24,8},{28,20},{1,17},{... | collective-permute-start | bytes 3145736 | tf_op jit(solution)/shard_map/ppermute | solution.py:927
  266.1 36.4 %collective-permute-start.30 = (bf16[640,1024]{1,0:T(8,128)(2,1)S(1)}, bf16[640,1024]{1,0:T(8,128)(2,1)}, u32[]{:S(2)}, u32[]{:S(2)}) collective-permute-start(bf16[640,1024]{1,0:T(8,128)(2,1)S(1)} %collective-permute-done.28.refs_1_), channel_id=1, source_target_pairs={{0,16},{4,12},{8,24},{12,4},{16,0},{20,28},{24,8},{28,20},{1,17},{... | collective-permute-start | bytes 3932168 | tf_op jit(solution)/shard_map/ppermute | solution.py:927
  345.3 31.6 %all-to-all-start = ((bf16[8,272,512]{2,1,0:T(8,128)(2,1)}), bf16[8,272,512]{2,1,0:T(8,128)(2,1)S(1)}, u32[]{:S(2)}, u32[]{:S(2)}) async-start(bf16[8,272,512]{2,1,0:T(8,128)(2,1)} %get-tuple-element.189), calls=%async_computation | async-start | bytes 4456448 | tf_op jit(solution)/shard_map/all_to_all | solution.py:1002
  384.6 24.3 %collective-permute-start.31 = (bf16[512,1024]{1,0:T(8,128)(2,1)}, bf16[512,1024]{1,0:T(8,128)(2,1)S(1)}, u32[]{:S(2)}, u32[]{:S(2)}) collective-permute-start(bf16[512,1024]{1,0:T(8,128)(2,1)} %shard_map.257), channel_id=1, source_target_pairs={{0,1},{1,0},{2,3},{3,2},{4,5},{5,4},{6,7},{7,6},{8,9},{9,8},{10,11... | collective-permute-start | bytes 3145736 | tf_op jit(solution)/shard_map/ppermute | solution.py:30
  403.4 31.1 %all-to-all-start.1 = ((f32[4,32,512]{2,1,0:T(8,128)}), f32[4,32,512]{2,1,0:T(8,128)S(1)}, u32[]{:S(2)}, u32[]{:S(2)}) async-start(f32[4,32,512]{2,1,0:T(8,128)} %param.35), calls=%async_computation.1 | async-start | bytes 524288 | tf_op jit(solution)/shard_map/all_to_all | solution.py:1002
  435.2 31.6 %all-to-all-start.2 = ((bf16[8,272,512]{2,1,0:T(8,128)(2,1)}), bf16[8,272,512]{2,1,0:T(8,128)(2,1)S(1)}, u32[]{:S(2)}, u32[]{:S(2)}) async-start(bf16[8,272,512]{2,1,0:T(8,128)(2,1)} %get-tuple-element.219), calls=%async_computation.2 | async-start | bytes 4456448 | tf_op jit(solution)/shard_map/all_to_all | solution.py:1002
  468.1 39.4 %all-to-all-start.3 = ((bf16[4,144,512]{2,1,0:T(8,128)(2,1)}), bf16[4,144,512]{2,1,0:T(8,128)(2,1)S(1)}, u32[]{:S(2)}, u32[]{:S(2)}) async-start(bf16[4,144,512]{2,1,0:T(8,128)(2,1)} %pad_maximum_fusion.3), calls=%async_computation.3 | async-start | bytes 1179648 | tf_op jit(solution)/shard_map/all_to_all | solution.py:1002
  479.9 43.4 %collective-permute-start.33 = (bf16[512,1024]{1,0:T(8,128)(2,1)}, bf16[512,1024]{1,0:T(8,128)(2,1)S(1)}, u32[]{:S(2)}, u32[]{:S(2)}) collective-permute-start(bf16[512,1024]{1,0:T(8,128)(2,1)} %shard_map.262), channel_id=1, source_target_pairs={{0,1},{1,0},{2,3},{3,2},{4,5},{5,4},{6,7},{7,6},{8,9},{9,8},{10,11... | collective-permute-start | bytes 3145736 | tf_op jit(solution)/shard_map/ppermute | solution.py:30
  508.4 28.8 %collective-permute-start.38 = (f32[128,512]{1,0:T(8,128)}, f32[128,512]{1,0:T(8,128)S(1)}, u32[]{:S(2)}, u32[]{:S(2)}) collective-permute-start(f32[128,512]{1,0:T(8,128)} %slice_add_fusion.refs_0_), channel_id=1, source_target_pairs={{0,24},{4,28},{8,16},{12,20},{16,8},{20,12},{24,0},{28,4},{1,25},{... | collective-permute-start | bytes 786440 | tf_op jit(solution)/shard_map/ppermute | solution.py:30
  509.2 29.8 %collective-permute-start.37 = (f32[128,512]{1,0:T(8,128)}, f32[128,512]{1,0:T(8,128)}, u32[]{:S(2)}, u32[]{:S(2)}) collective-permute-start(f32[128,512]{1,0:T(8,128)} %slice_add_fusion.refs_0_), channel_id=1, source_target_pairs={{0,20},{4,16},{8,28},{12,24},{16,4},{20,0},{24,12},{28,8},{1,21},{... | collective-permute-start | bytes 786440 | tf_op jit(solution)/shard_map/ppermute | solution.py:30
  518.7 39.6 %all-to-all-start.4 = ((f32[4,32,512]{2,1,0:T(8,128)}), f32[4,32,512]{2,1,0:T(8,128)S(1)}, u32[]{:S(2)}, u32[]{:S(2)}) async-start(f32[4,32,512]{2,1,0:T(8,128)} %bitcast.32), calls=%async_computation.4 | async-start | bytes 524288 | tf_op jit(solution)/shard_map/all_to_all | solution.py:1002
  537.2 26.0 %collective-permute-start.40 = (bf16[512,1024]{1,0:T(8,128)(2,1)S(1)}, bf16[512,1024]{1,0:T(8,128)(2,1)S(1)}, u32[]{:S(2)}, u32[]{:S(2)}) collective-permute-start(bf16[512,1024]{1,0:T(8,128)(2,1)S(1)} %copy-done.7), channel_id=1, source_target_pairs={{0,1},{1,0},{2,3},{3,2},{4,5},{5,4},{6,7},{7,6},{8,9},{9,8},{10,11... | collective-permute-start | bytes 3145736 | tf_op jit(solution)/shard_map/ppermute | solution.py:30
  (53 other events, 654.9 us)
